TPU v7x, 256 devices: a whole 4x4x8 slice. The times are simulated.
256 devices in a mesh: branch: 4 (over y), seq: 64 (over x, z, core).
Axes of the slice: x: 4, y: 4, z: 8, core: 2. Of those that a mesh axis runs over, the one named last changes fastest.
Arguments:
- queries: bfloat16 [4, 2048, 40, 256], P('branch', 'seq'), may hold values from -6 to 6
- keys_values: bfloat16 [4, 8192, 40, 256], P('branch', 'seq'), may hold values from -6 to 6
- prompt_bank: bfloat16 [8, 512, 4096], P('branch', 'seq'), may hold values from -6 to 6
- prompt_lengths: int32 [8], replicated, may hold values from 16 to 512
- requests: int32 [4], replicated, may hold values from 0 to 7
- w_text: bfloat16 [4096, 40, 256], P('seq'), may hold values from -0.09375 to 0.09375
- q_gain: float32 [40, 128], replicated, may hold values from 1.2 to 2
- k_gain: float32 [40, 128], replicated, may hold values from 1.2 to 2
- cq_gain: float32 [40, 128], replicated, may hold values from 1.2 to 2
- ck_gain: float32 [40, 128], replicated, may hold values from 1.2 to 2
Outputs:
- self_out: bfloat16 [4, 2048, 5120], P('branch', 'seq')
- cross_out: bfloat16 [4, 2048, 5120], P('branch', 'seq')
All inputs are finite; a program needn't handle non-finite values.
Results may differ from a plain program's by a relative error of at most 0.011.
Values may be sent and summed in bfloat16 or wider, within the bound.
No kernel may reach another device: no remote copies, remote signals or barrier semaphores. Data moves between devices by JAX's collectives and lax.ppermute only.
A program may use at most 128 MiB of HBM per device.

v0:
```python
import math

import jax
import jax.numpy as jnp
from jax import lax
from jax.sharding import PartitionSpec as P

EPSILON = 1e-06


def head_norm(values, gains):
    values = values.astype(jnp.float32)
    return values * lax.rsqrt(jnp.mean(values * values, axis=-1, keepdims=True) + EPSILON) * gains


def attend(query_rows, key_rows, value_rows, live, scale):
    scores = (
        jnp.einsum("qd,kd->qk", query_rows, key_rows, preferred_element_type=jnp.float32) * scale
    )
    powers = jnp.exp(scores)
    if live is not None:
        powers = jnp.where(live[None, :], powers, jnp.float32(0.0))
    weights = (powers / jnp.sum(powers, axis=-1, keepdims=True)).astype(jnp.bfloat16)
    return jnp.dot(weights, value_rows, preferred_element_type=jnp.float32).astype(jnp.bfloat16)


def local(
    queries,
    keys_values,
    prompt_bank,
    prompt_lengths,
    requests,
    w_text,
    q_gain,
    k_gain,
    cq_gain,
    ck_gain,
):
    shards = lax.axis_size("seq")
    device = lax.axis_index("seq")
    group = lax.axis_index("branch")
    heads, head_dim = q_gain.shape
    scale = 1.0 / math.sqrt(head_dim)
    tok_local = queries.shape[1]
    blocks = shards // 8
    block_rows = 8 * tok_local
    slots = (heads + shards - 1) // shards
    per_device = slots * blocks
    owners = jnp.arange(shards, dtype=jnp.int32)
    first_heads = owners * per_device // blocks
    slot_range = jnp.arange(slots, dtype=jnp.int32)
    head_lists = jnp.minimum(first_heads[:, None] + slot_range[None, :], heads - 1).reshape(-1)
    local_queries = queries[0]
    normed_queries = jnp.concatenate(
        [
            head_norm(local_queries[..., :head_dim], q_gain),
            head_norm(local_queries[..., head_dim:], cq_gain),
        ],
        axis=-1,
    ).astype(jnp.bfloat16)
    local_pairs = keys_values[0]
    normed_pairs = jnp.concatenate(
        [
            head_norm(local_pairs[..., :head_dim], k_gain).astype(jnp.bfloat16),
            local_pairs[..., head_dim:],
        ],
        axis=-1,
    )
    send_queries = jnp.take(normed_queries, head_lists, axis=1)
    send_pairs = jnp.take(normed_pairs, head_lists, axis=1)
    send_weights = jnp.take(w_text, head_lists, axis=1)
    head_queries, head_pairs, head_weights = (
        lax.all_to_all(send_queries, "seq", split_axis=1, concat_axis=0, tiled=True),
        lax.all_to_all(send_pairs, "seq", split_axis=1, concat_axis=0, tiled=True),
        lax.all_to_all(send_weights, "seq", split_axis=1, concat_axis=0, tiled=True),
    )
    per_branch = prompt_bank.shape[0]
    held = requests // per_branch == group
    picked = jnp.take(prompt_bank, jnp.remainder(requests, per_branch), axis=0)
    outgoing = jnp.where(held[:, None, None], picked, jnp.zeros_like(picked))
    incoming = lax.all_to_all(outgoing, "branch", split_axis=0, concat_axis=0, tiled=True)
    context_rows = jnp.sum(incoming.astype(jnp.float32), axis=0).astype(jnp.bfloat16)
    my_first = device * per_device // blocks
    my_heads = jnp.minimum(my_first + slot_range, heads - 1)
    key_gains = jnp.take(ck_gain, my_heads, axis=0)
    mapped = jnp.einsum(
        "rf,fsc->rsc",
        lax.all_gather(context_rows, "seq", axis=0, tiled=True),
        head_weights,
        preferred_element_type=jnp.float32,
    )
    text_keys = head_norm(mapped[..., :head_dim], key_gains)
    text_pairs = jnp.concatenate([text_keys, mapped[..., head_dim:]], axis=-1).astype(jnp.bfloat16)
    text_total = text_pairs.shape[0]
    prompt_length = jnp.take(prompt_lengths, jnp.take(requests, group))
    live = jnp.arange(text_total, dtype=jnp.int32) < prompt_length
    count = jnp.clip(heads * blocks - device * per_device, 0, per_device)
    results = jnp.zeros((head_queries.shape[0], slots, 2 * head_dim), jnp.bfloat16)

    def one_unit(position, buffer):
        unit = device * per_device + position
        head = unit // blocks
        block = unit % blocks
        slot = head - my_first
        rows_start = block * block_rows
        query_rows = lax.dynamic_slice(
            head_queries, (rows_start, slot, 0), (block_rows, 1, 2 * head_dim)
        )[:, 0, :]
        pairs = lax.dynamic_index_in_dim(head_pairs, slot, 1, keepdims=False)
        texts = lax.dynamic_index_in_dim(text_pairs, slot, 1, keepdims=False)
        self_part = attend(
            query_rows[:, :head_dim], pairs[:, :head_dim], pairs[:, head_dim:], None, scale
        )
        cross_part = attend(
            query_rows[:, head_dim:], texts[:, :head_dim], texts[:, head_dim:], live, scale
        )
        update = jnp.concatenate([self_part, cross_part], axis=-1)[:, None, :]
        return lax.dynamic_update_slice(buffer, update, (rows_start, slot, 0))

    results = lax.fori_loop(0, count, one_unit, results)
    returned = lax.all_to_all(results, "seq", split_axis=0, concat_axis=1, tiled=True)
    placement_table = (head_lists[:, None] == jnp.arange(heads, dtype=jnp.int32)[None, :]).astype(
        jnp.bfloat16
    )
    placed = jnp.einsum(
        "tmc,mh->thc", returned, placement_table, preferred_element_type=jnp.float32
    ).astype(jnp.bfloat16)
    self_out = placed[:, :, :head_dim].reshape(tok_local, heads * head_dim)[None]
    cross_out = placed[:, :, head_dim:].reshape(tok_local, heads * head_dim)[None]
    return (self_out, cross_out)


def solution(mesh):
    in_specs = (
        P("branch", "seq", None, None),
        P("branch", "seq", None, None),
        P("branch", "seq", None),
        P(),
        P(),
        P("seq", None, None),
        P(),
        P(),
        P(),
        P(),
    )
    out_specs = (P("branch", "seq", None), P("branch", "seq", None))
    return jax.shard_map(local, mesh=mesh, in_specs=in_specs, out_specs=out_specs, check_vma=False)
```

profile of v0, /device:TPU:1, one launch (start us, length us, event | category | flops | bytes accessed | tf_op | source)
XLA Modules:
  0.0 351.5 jit_solution(12747718191494631701)
XLA Ops:
  7.2 0.8 compare_and_fusion
  8.0 1.5 gather_fusion.2
  9.5 0.8 select_select_fusion
  10.3 5.0 %all-to-all-start.2 = ((bf16[4,8,4096]{2,1,0:T(8,128)(2,1)}), bf16[4,8,4096]{2,1,0:T(8,128)(2,1)S(1)}, u32[]{:S(2)}, u32[]{:S(2)}) async-start(bf16[4,8,4096]{2,1,0:T(8,128)(2,1)} %select_select_fusion), calls=%async_computation.2 | async-start | bytes 524288 | tf_op jit(solution)/shard_map/all_to_all | solution.py:81
  15.3 1.2 copy.35
  17.5 0.6 gather_fusion
  18.2 1.2 select_bitcast_fusion.2
  19.3 1.5 all-to-all-done.2
  20.8 0.7 copy-done.2
  21.5 13.8 %all-to-all-start = ((bf16[32,64,256]{2,0,1:T(8,128)(2,1)}), bf16[32,64,256]{2,0,1:T(8,128)(2,1)}, u32[]{:S(2)}, u32[]{:S(2)}) async-start(bf16[32,64,256]{2,0,1:T(8,128)(2,1)} %select_bitcast_fusion.2), calls=%async_computation | async-start | bytes 2097152 | tf_op jit(solution)/shard_map/all_to_all | solution.py:73
  35.3 6.6 %gather_fusion.3 = bf16[64,64,256]{2,0,1:T(8,128)(2,1)S(1)} fusion(bf16[64,40,256]{2,1,0:T(8,128)(2,1)S(1)} %copy-done, s32[1024]{0:T(1024)S(1)} %pad_clamp_fusion.1), kind=kCustom, calls=%fused_computation.3 | custom fusion | bytes 4194560 | tf_op jit(solution)/shard_map/jit(_take)/gather | solution.py:71
  42.2 2.5 copy.23
  44.6 19.1 %all-to-all-done = bf16[32,64,256]{2,0,1:T(8,128)(2,1)} async-done(((bf16[32,64,256]{2,0,1:T(8,128)(2,1)}), bf16[32,64,256]{2,0,1:T(8,128)(2,1)}, u32[]{:S(2)}, u32[]{:S(2)}) %all-to-all-start) | async-done | bytes 1048608 | tf_op jit(solution)/shard_map/all_to_all | solution.py:73
  63.8 6.2 %all-to-all-start.3 = ((bf16[64,64,256]{2,0,1:T(8,128)(2,1)}), bf16[64,64,256]{2,0,1:T(8,128)(2,1)S(1)}, u32[]{:S(2)}, u32[]{:S(2)}) async-start(bf16[64,64,256]{2,0,1:T(8,128)(2,1)} %copy.23), calls=%async_computation.3 | async-start | bytes 4194304 | tf_op jit(solution)/shard_map/all_to_all | solution.py:75
  70.2 3.8 %copy.34 = bf16[1,128,40,256]{3,1,2,0:T(8,128)(2,1)} copy(bf16[1,128,40,256]{3,2,1,0:T(8,128)(2,1)} %param.13) | data formatting | bytes 5242880 | tf_op args[1]
  74.1 1.6 reduce_sum.77
  75.7 2.2 fusion.16
  77.9 1.5 slice.115
  79.4 0.9 fusion.18
  80.4 1.9 pad_maximum_fusion
  82.3 4.6 %gather_fusion.1 = bf16[64,128,256]{2,1,0:T(8,128)(2,1)} fusion(bf16[128,40,256]{2,0,1:T(8,128)(2,1)} %pad_maximum_fusion, s32[1024]{0:T(1024)S(1)} %pad_clamp_fusion.1), kind=kCustom, calls=%fused_computation.1 | custom fusion | bytes 8388864 | tf_op jit(solution)/shard_map/jit(_take)/gather | solution.py:70
  86.9 4.7 %select_bitcast_fusion = bf16[128,64,256]{2,0,1:T(8,128)(2,1)} fusion(bf16[64,128,256]{2,1,0:T(8,128)(2,1)} %gather_fusion.1, pred[64]{0:T(512)(128)(4,1)S(1)} %compare_and_fusion.1), kind=kLoop, calls=%fused_computation.25 | loop fusion | flops 2097152 | bytes 8388672 | tf_op jit(solution)/shard_map/jit(_take)/select_n | solution.py:70
  91.6 32.1 %all-to-all-done.3 = bf16[64,64,256]{2,0,1:T(8,128)(2,1)S(1)} async-done(((bf16[64,64,256]{2,0,1:T(8,128)(2,1)}), bf16[64,64,256]{2,0,1:T(8,128)(2,1)S(1)}, u32[]{:S(2)}, u32[]{:S(2)}) %all-to-all-start.3) | async-done | bytes 2097184 | tf_op jit(solution)/shard_map/all_to_all | solution.py:75
  123.7 6.0 %all-to-all-start.1 = ((bf16[128,64,256]{2,0,1:T(8,128)(2,1)}), bf16[128,64,256]{2,0,1:T(8,128)(2,1)}, u32[]{:S(2)}, u32[]{:S(2)}) async-start(bf16[128,64,256]{2,0,1:T(8,128)(2,1)} %select_bitcast_fusion), calls=%async_computation.1 | async-start | bytes 8388608 | tf_op jit(solution)/shard_map/all_to_all | solution.py:74
  129.7 0.6 dynamic-slice.7
  130.9 0.6 dynamic-slice.8
  132.0 0.7 fusion.31
  132.7 40.5 %all-gather.2.cloned.1.call-done = bf16[512,4096]{1,0:T(8,128)(2,1)} async-done(((bf16[8,4096]{1,0:T(8,128)(2,1)}), bf16[512,4096]{1,0:T(8,128)(2,1)}) %all-gather.2.cloned.1.call-update) | async-done | bytes 4194320 | tf_op jit(solution)/shard_map/all_gather | solution.py:88
  173.2 3.5 convolution_bitcast_fusion
  177.0 57.0 %all-to-all-done.1 = bf16[128,64,256]{2,0,1:T(8,128)(2,1)} async-done(((bf16[128,64,256]{2,0,1:T(8,128)(2,1)}), bf16[128,64,256]{2,0,1:T(8,128)(2,1)}, u32[]{:S(2)}, u32[]{:S(2)}) %all-to-all-start.1) | async-done | bytes 4194336 | tf_op jit(solution)/shard_map/all_to_all | solution.py:74
  234.1 63.4 %while.17 = (s32[]{:T(128)}, bf16[2048,1,256]{0,2,1:T(8,128)(2,1)S(1)}, s32[]{:T(128)}, s32[]{:T(128)}, bf16[2048,1,256]{2,0,1:T(8,128)(2,1)}, /*index=5*/bf16[8...) while((s32[]{:T(128)}, ...), condition=%wide.region_8.9_spmd.clone, body=%wide.region_5.8_spmd.clone.sunk | while | flops 1150222336 | bytes 23074104 | solution.py:120
  234.2 0.9 dynamic-slice_bitcast_fusion.2
  235.1 3.0 fusion.49
  238.1 3.3 fusion.50
  242.1 0.9 dynamic-slice_bitcast_fusion.2
  243.0 3.0 fusion.49
  246.0 3.3 fusion.50
  250.0 0.9 dynamic-slice_bitcast_fusion.2
  250.9 3.0 fusion.49
  253.9 3.3 fusion.50
  257.9 0.9 dynamic-slice_bitcast_fusion.2
  258.9 3.0 fusion.49
  261.9 3.3 fusion.50
  265.9 0.9 dynamic-slice_bitcast_fusion.2
  266.8 3.0 fusion.49
  269.8 3.3 fusion.50
  273.8 0.9 dynamic-slice_bitcast_fusion.2
  274.7 3.0 fusion.49
  277.7 3.3 fusion.50
  281.7 0.9 dynamic-slice_bitcast_fusion.2
  282.6 3.0 fusion.49
  285.6 3.3 fusion.50
  289.6 0.9 dynamic-slice_bitcast_fusion.2
  290.6 3.0 fusion.49
  293.6 3.3 fusion.50
  298.0 1.4 reduce.2
  299.5 0.5 copy.36
  300.0 1.2 reshape.297
  301.2 5.7 %all-to-all-start.4 = ((bf16[64,2,4096]{2,1,0:T(2,128)(2,1)}), bf16[64,2,4096]{2,1,0:T(2,128)(2,1)}, u32[]{:S(2)}, u32[]{:S(2)}) async-start(bf16[64,2,4096]{2,1,0:T(2,128)(2,1)} %reshape.297), calls=%async_computation.4 | async-start | bytes 2097152 | tf_op jit(solution)/shard_map/all_to_all | solution.py:121
  306.9 28.5 %all-to-all-done.4 = bf16[64,2,4096]{2,1,0:T(2,128)(2,1)} async-done(((bf16[64,2,4096]{2,1,0:T(2,128)(2,1)}), bf16[64,2,4096]{2,1,0:T(2,128)(2,1)}, u32[]{:S(2)}, u32[]{:S(2)}) %all-to-all-start.4) | async-done | bytes 1048608 | tf_op jit(solution)/shard_map/all_to_all | solution.py:121
  335.4 6.5 %reshape.298 = bf16[2048,1,256]{2,1,0:T(2,128)(2,1)S(1)} reshape(bf16[64,2,4096]{2,1,0:T(2,128)(2,1)} %all-to-all-done.4) | data formatting | bytes 2097152
  342.0 0.8 fusion.19
  343.0 0.9 broadcast_in_dim_reshape.6
  343.8 0.9 broadcast_in_dim_reshape.7
  (70 shorter events, 8.0 us)
Async XLA Ops:
  7.2 28.1 %copy-start = (bf16[64,40,256]{2,1,0:T(8,128)(2,1)S(1)}, bf16[64,40,256]{2,1,0:T(8,128)(2,1)}, u32[]{:S(2)}) copy-start(bf16[64,40,256]{2,1,0:T(8,128)(2,1)} %param.17) | copy-start | bytes 3932164
  7.2 9.8 %copy-start.3 = (f32[40,128]{1,0:T(8,128)S(1)}, f32[40,128]{1,0:T(8,128)}, u32[]{:S(2)}) copy-start(f32[40,128]{1,0:T(8,128)} %param.18) | copy-start | bytes 61444
  7.2 9.8 %copy-start.4 = (f32[40,128]{1,0:T(8,128)S(1)}, f32[40,128]{1,0:T(8,128)}, u32[]{:S(2)}) copy-start(f32[40,128]{1,0:T(8,128)} %param.20) | copy-start | bytes 61444
  10.3 10.5 %all-to-all-start.2 = ((bf16[4,8,4096]{2,1,0:T(8,128)(2,1)}), bf16[4,8,4096]{2,1,0:T(8,128)(2,1)S(1)}, u32[]{:S(2)}, u32[]{:S(2)}) async-start(bf16[4,8,4096]{2,1,0:T(8,128)(2,1)} %select_select_fusion), calls=%async_computation.2 | async-start | bytes 524288 | tf_op jit(solution)/shard_map/all_to_all | solution.py:81
  20.8 0.7 copy-start.2
  21.5 42.3 %all-to-all-start = ((bf16[32,64,256]{2,0,1:T(8,128)(2,1)}), bf16[32,64,256]{2,0,1:T(8,128)(2,1)}, u32[]{:S(2)}, u32[]{:S(2)}) async-start(bf16[32,64,256]{2,0,1:T(8,128)(2,1)} %select_bitcast_fusion.2), calls=%async_computation | async-start | bytes 2097152 | tf_op jit(solution)/shard_map/all_to_all | solution.py:73
  63.8 59.9 %all-to-all-start.3 = ((bf16[64,64,256]{2,0,1:T(8,128)(2,1)}), bf16[64,64,256]{2,0,1:T(8,128)(2,1)S(1)}, u32[]{:S(2)}, u32[]{:S(2)}) async-start(bf16[64,64,256]{2,0,1:T(8,128)(2,1)} %copy.23), calls=%async_computation.3 | async-start | bytes 4194304 | tf_op jit(solution)/shard_map/all_to_all | solution.py:75
  70.0 103.2 %all-gather.2.cloned.1.call-start = ((), (), s32[]{:S(2)}) async-start(), calls=%async_computation.5 | async-start | bytes 4259840 | tf_op jit(solution)/shard_map/all_gather | solution.py:88
  74.1 5.4 %copy-start.5 = (f32[40,128]{1,0:T(8,128)S(1)}, f32[40,128]{1,0:T(8,128)}, u32[]{:S(2)}) copy-start(f32[40,128]{1,0:T(8,128)} %param.19) | copy-start | bytes 61444
  75.7 3.7 %copy-start.1 = (bf16[1,128,40,256]{3,1,2,0:T(8,128)(2,1)S(1)}, bf16[1,128,40,256]{3,1,2,0:T(8,128)(2,1)}, u32[]{:S(2)}) copy-start(bf16[1,128,40,256]{3,1,2,0:T(8,128)(2,1)} %copy.34) | copy-start | bytes 7864324
  91.6 38.1 %copy-start.6 = (s32[4]{0:T(128)S(1)}, s32[4]{0:T(128)}, u32[]{:S(2)}) copy-start(s32[4]{0:T(128)} %param.16) | copy-start | bytes 52
  91.6 39.3 %copy-start.7 = (s32[8]{0:T(128)S(1)}, s32[8]{0:T(128)}, u32[]{:S(2)}) copy-start(s32[8]{0:T(128)} %param.15) | copy-start | bytes 100
  123.7 110.3 %all-to-all-start.1 = ((bf16[128,64,256]{2,0,1:T(8,128)(2,1)}), bf16[128,64,256]{2,0,1:T(8,128)(2,1)}, u32[]{:S(2)}, u32[]{:S(2)}) async-start(bf16[128,64,256]{2,0,1:T(8,128)(2,1)} %select_bitcast_fusion), calls=%async_computation.1 | async-start | bytes 8388608 | tf_op jit(solution)/shard_map/all_to_all | solution.py:74
  301.2 34.2 %all-to-all-start.4 = ((bf16[64,2,4096]{2,1,0:T(2,128)(2,1)}), bf16[64,2,4096]{2,1,0:T(2,128)(2,1)}, u32[]{:S(2)}, u32[]{:S(2)}) async-start(bf16[64,2,4096]{2,1,0:T(2,128)(2,1)} %reshape.297), calls=%async_computation.4 | async-start | bytes 2097152 | tf_op jit(solution)/shard_map/all_to_all | solution.py:121
Sparse Core Ops, SparseCore 0:
  75.8 97.3 all-gather.1
where the time goes:
time: 353 us; the launch traced here: 352 us
  waiting for transfers between devices  179 us (51%)
  matrix products  59.5 us (17%)
  local copies, waits for them, and re-layouts  42.4 us (12%)
  starting transfers between devices  36.9 us (10%)
  other arithmetic  17.9 us (5%)
  between operations  15.5 us (4%)
    all_to_all x1, waiting for transfers between devices, local(): lax.all_to_all(send_pairs, 'seq', split_axis=1, concat_axis=0, tiled=True)  57 us
    all_gather x1, waiting for transfers between devices, local(): lax.all_gather(context_rows, 'seq', axis=0, tiled=True)  40.5 us
    all_to_all x1, waiting for transfers between devices, local(): lax.all_to_all(send_weights, 'seq', split_axis=1, concat_axis=0, tiled=True)  32.1 us
    dot_general x16, matrix products, attend(): jnp.dot(weights, value_rows, preferred_element_type=jnp.float32)  28.5 us
    all_to_all x1, waiting for transfers between devices, local(): lax.all_to_all(results, 'seq', split_axis=0, concat_axis=1, tiled=True)  28.5 us
    dot_general x16, matrix products, attend(): jnp.einsum('qd,kd->qk', query_rows, key_rows, preferred_element_type=jnp....  26.7 us
    all_to_all x1, waiting for transfers between devices, local(): lax.all_to_all(send_queries, 'seq', split_axis=1, concat_axis=0, tiled=True)  19.1 us
    unnamed x23, local copies, waits for them, and re-layouts  14.3 us
  transfers between devices with their start and end apart: 6, of which 6 were waited for; matrix products, arithmetic and copies ran while one was open for 11% of the time, Pallas kernels for 0%

commit v1 on v0

v1 whole, which is shorter than its diff:
```python
import functools
import math

import jax
import jax.numpy as jnp
from jax import lax
from jax.experimental import pallas as pl
from jax.experimental.pallas import tpu as pltpu
from jax.sharding import Mesh
from jax.sharding import PartitionSpec as P

EPSILON = 1e-06
BF16 = jnp.bfloat16
F32 = jnp.float32
NX, NZ, NC = 4, 8, 2
GROUP = ("x", "c")


def head_norm(values, gains):
    values = values.astype(F32)
    return values * lax.rsqrt(jnp.mean(values * values, axis=-1, keepdims=True) + EPSILON) * gains


def ring(size, step):
    return [(i, (i + step) % size) for i in range(size)]


def columns_to_rows(sums):
    eye = lax.broadcasted_iota(jnp.int32, (128, 128), 0) == lax.broadcasted_iota(
        jnp.int32, (128, 128), 1
    )
    return [
        jnp.sum(jnp.where(eye, sums[a * 128 : (a + 1) * 128], 0.0), axis=0, keepdims=True)
        for a in range(sums.shape[0] // 128)
    ]


def self_kernel(order, q_ref, k_ref, v_ref, *refs, chunks, rows, keys, scale):
    q_refs = (q_ref,) + refs[: chunks - 1]
    o_ref, l_ref = refs[chunks - 1 :]
    values = v_ref[...].reshape(1024, 256)[:, 128:]
    values = jnp.concatenate([values, jnp.ones((1024, 128), BF16)], axis=1)
    queries = jnp.concatenate([ref[...].reshape(256, 128) for ref in q_refs], axis=0)
    for i in range(chunks * 256 // rows):
        part = queries[i * rows : (i + 1) * rows]
        total = None
        for j in range(1024 // keys):
            scores = lax.dot_general(
                part,
                k_ref[0, j * keys : (j + 1) * keys],
                (((1,), (1,)), ((), ())),
                preferred_element_type=F32,
            )
            powers = jnp.exp2(scores * scale).astype(BF16)
            term = jnp.dot(
                powers, values[j * keys : (j + 1) * keys], preferred_element_type=F32
            )
            total = term if total is None else total + term
        for a in range(rows // 256):
            chunk = i * rows // 256 + a
            piece = total[a * 256 : (a + 1) * 256]
            o_ref[chunk] = piece[:, :128].reshape(8, 1, 32, 128).astype(o_ref.dtype)
            l_ref[chunk, 0] = jnp.concatenate(
                columns_to_rows(piece[:, 128:]) + [jnp.zeros((6, 128), F32)], axis=0
            )


def self_part(order, gathered, keys, pairs, scale, out_type):
    chunks = order.shape[0]
    slots = keys.shape[0]

    def q_spec(n):
        return pl.BlockSpec((1, 8, 1, 32, 128), lambda h, order: (order[n], 0, h, 0, 0))

    grid_spec = pltpu.PrefetchScalarGridSpec(
        num_scalar_prefetch=1,
        grid=(slots,),
        in_specs=[
            q_spec(0),
            pl.BlockSpec((1, 1024, 128), lambda h, order: (h, 0, 0)),
            pl.BlockSpec((8, 1, 128, 256), lambda h, order: (0, h, 0, 0)),
        ]
        + [q_spec(n) for n in range(1, chunks)],
        out_specs=[
            pl.BlockSpec((chunks, 8, 1, 32, 128), lambda h, order: (0, 0, h, 0, 0)),
            pl.BlockSpec((chunks, 1, 8, 128), lambda h, order: (0, h, 0, 0)),
        ],
    )
    pairs_count = slots * chunks * 256 * 1024
    return pl.pallas_call(
        functools.partial(
            self_kernel, chunks=chunks, rows=256 * chunks, keys=512, scale=scale
        ),
        grid_spec=grid_spec,
        out_shape=[
            jax.ShapeDtypeStruct((chunks, 8, slots, 32, 128), out_type),
            jax.ShapeDtypeStruct((chunks, slots, 8, 128), F32),
        ],
        compiler_params=pltpu.CompilerParams(vmem_limit_bytes=48 << 20),
        cost_estimate=pl.CostEstimate(
            flops=pairs_count * 128 * 6, bytes_accessed=6 << 20, transcendentals=pairs_count
        ),
        name="self_part",
    )(order, gathered, keys, pairs, *([gathered] * (chunks - 1)))


def norm_kernel(kv_ref, gain_ref, out_ref):
    keys = kv_ref[...].reshape(1024, 256)[:, :128]
    out_ref[0] = head_norm(keys, gain_ref[0]).astype(BF16)


def norm_keys(pairs, gains):
    slots = pairs.shape[1]
    return pl.pallas_call(
        norm_kernel,
        grid=(slots,),
        in_specs=[
            pl.BlockSpec((8, 1, 128, 256), lambda h: (0, h, 0, 0)),
            pl.BlockSpec((1, 1, 128), lambda h: (h, 0, 0)),
        ],
        out_specs=pl.BlockSpec((1, 1024, 128), lambda h: (h, 0, 0)),
        out_shape=jax.ShapeDtypeStruct((slots, 1024, 128), BF16),
        compiler_params=pltpu.CompilerParams(vmem_limit_bytes=48 << 20),
        name="norm_keys",
    )(pairs, gains[:, None, :])


def cross_kernel(q_ref, text_ref, live_ref, o_ref, *, scale):
    text = text_ref[...].reshape(512, 256)
    queries = q_ref[...].reshape(256, 128)
    scores = lax.dot_general(
        queries, text[:, :128], (((1,), (1,)), ((), ())), preferred_element_type=F32
    )
    powers = jnp.where(live_ref[...] > 0.0, jnp.exp2(scores * scale), 0.0)
    weights = powers / jnp.sum(powers, axis=1, keepdims=True)
    result = jnp.dot(weights.astype(BF16), text[:, 128:], preferred_element_type=F32)
    o_ref[...] = result.astype(BF16).reshape(8, 1, 32, 128)


def cross_part(queries, text, live, scale):
    slots = queries.shape[1]
    return pl.pallas_call(
        functools.partial(cross_kernel, scale=scale),
        grid=(slots,),
        in_specs=[
            pl.BlockSpec((8, 1, 32, 128), lambda h: (0, h, 0, 0)),
            pl.BlockSpec((8, 1, 64, 256), lambda h: (0, h, 0, 0)),
            pl.BlockSpec((1, 512), lambda h: (0, 0)),
        ],
        out_specs=pl.BlockSpec((8, 1, 32, 128), lambda h: (0, h, 0, 0)),
        out_shape=jax.ShapeDtypeStruct(queries.shape, BF16),
        compiler_params=pltpu.CompilerParams(vmem_limit_bytes=48 << 20),
        name="cross_part",
    )(queries, text, live)


def local(
    queries,
    keys_values,
    prompt_bank,
    prompt_lengths,
    requests,
    w_text,
    q_gain,
    k_gain,
    cq_gain,
    ck_gain,
):
    branch = lax.axis_index("branch")
    x = lax.axis_index("x")
    z = lax.axis_index("z")
    c = lax.axis_index("c")
    heads, head_dim = q_gain.shape
    slots = heads // (NX * NC)
    scale = math.log2(math.e) / math.sqrt(head_dim)
    tokens = queries.shape[1]

    def head_major(values):
        return jnp.transpose(values, (1, 0, 2)).reshape(
            8, slots, values.shape[0], values.shape[2]
        )

    local_queries = queries[0]
    self_queries = head_major(head_norm(local_queries[..., :head_dim], q_gain).astype(BF16))
    self_queries = lax.all_to_all(self_queries, GROUP, 0, 0, tiled=True)
    gathered = lax.all_gather(self_queries, "z", axis=0)

    pairs = lax.all_to_all(head_major(keys_values[0]), GROUP, 0, 0, tiled=True)
    group = x * NC + c
    my_gains = lax.dynamic_slice_in_dim(k_gain, group * slots, slots, 0)
    keys = norm_keys(pairs, my_gains)

    per_branch = prompt_bank.shape[0]
    held = requests // per_branch == branch
    picked = jnp.take(prompt_bank, jnp.remainder(requests, per_branch), axis=0)
    outgoing = jnp.where(held[:, None, None], picked, jnp.zeros_like(picked))
    incoming = lax.all_to_all(outgoing, "branch", split_axis=0, concat_axis=0, tiled=True)
    source = jnp.take(requests, branch) // per_branch
    rows = lax.dynamic_index_in_dim(incoming, source, 0, keepdims=False)
    count = rows.shape[0]
    rows = rows.reshape(count, NX, NZ, NC, 4, 16)
    rows = jnp.transpose(rows, (1, 3, 0, 4, 2, 5)).reshape(8, count, 512)
    rows = lax.all_to_all(rows, GROUP, 0, 0, tiled=True).reshape(8 * count, 512)
    context = lax.all_gather(rows, "z", axis=0)

    part = lax.dynamic_slice_in_dim(w_text, branch * 16, 16, 0)
    part = lax.all_to_all(head_major(part), "z", 0, 0, tiled=True)
    planes = [part] + [lax.ppermute(part, "branch", ring(4, k)) for k in (1, 2, 3)]
    planes = jnp.stack(planes + planes)
    planes = jnp.flip(planes, 0)
    weights = lax.dynamic_slice_in_dim(planes, 3 - branch, 4, 0)

    partial = jnp.einsum(
        "btk,hkc->bhtc",
        context,
        jnp.transpose(weights, (2, 0, 1, 3, 4)).reshape(slots, 512, 2 * head_dim),
        preferred_element_type=F32,
    ).astype(BF16)
    projected = lax.psum_scatter(partial, GROUP, scatter_dimension=0, tiled=True)[0]
    text_gains = lax.dynamic_slice_in_dim(ck_gain, z * slots, slots, 0)
    text_keys = head_norm(projected[..., :head_dim], text_gains[:, None, :]).astype(BF16)
    text = jnp.concatenate([text_keys, projected[..., head_dim:]], axis=-1)
    text = lax.all_gather(text, GROUP, axis=0)

    entry = jnp.arange(512, dtype=jnp.int32)
    of_z, of_x, of_c, of_row = entry // 64, entry // 16 % 4, entry // 8 % 2, entry % 8
    text_row = ((of_x * NZ + of_z) * NC + of_c) * 8 + of_row
    prompt_length = jnp.take(prompt_lengths, jnp.take(requests, branch))
    live = (text_row < prompt_length).astype(F32)[None, :]

    cross_queries = head_major(head_norm(local_queries[..., head_dim:], cq_gain).astype(BF16))
    cross_queries = lax.all_to_all(cross_queries, "z", 0, 0, tiled=True)
    cross = cross_part(cross_queries, text, live, scale)
    cross = lax.all_to_all(cross, "z", 0, 0, tiled=True)

    def chunk_order(*steps):
        return jnp.stack([(z + step) % NZ for step in steps]).astype(jnp.int32)

    far, far_sums = self_part(chunk_order(4), gathered, keys, pairs, scale, BF16)
    right = lax.ppermute(far[0, :4], "z", ring(NZ, 1))
    left = lax.ppermute(far[0, 4:], "z", ring(NZ, -1))
    sums = {4: far_sums[0]}
    for step in (3, 2, 1):
        own, own_sums = self_part(chunk_order(step, -step), gathered, keys, pairs, scale, F32)
        sums[step], sums[8 - step] = own_sums[0], own_sums[1]
        if step == 3:
            to_right = jnp.concatenate([own[0, :4] + right.astype(F32), own[0, 4:]], axis=0)
            to_left = jnp.concatenate([own[1, :4], own[1, 4:] + left.astype(F32)], axis=0)
        else:
            to_right = own[0] + right.astype(F32)
            to_left = own[1] + left.astype(F32)
        right = lax.ppermute(to_right.astype(BF16), "z", ring(NZ, 1))
        left = lax.ppermute(to_left.astype(BF16), "z", ring(NZ, -1))
    own, own_sums = self_part(chunk_order(0), gathered, keys, pairs, scale, F32)
    sums[0] = own_sums[0]
    by_step = jnp.stack([sums[k] for k in range(8)])[:, :, :2]
    by_step = jnp.concatenate([by_step, by_step], axis=0)
    by_chunk = lax.dynamic_slice_in_dim(by_step, NZ - z, NZ, 0)
    total = jnp.sum(lax.all_to_all(by_chunk, "z", 0, 0, tiled=True), axis=0)
    total = jnp.transpose(total.reshape(slots, 8, 32), (1, 0, 2))[..., None]
    mine = (own[0] + right.astype(F32) + left.astype(F32)) / total
    mine = lax.all_to_all(mine.astype(BF16), GROUP, 0, 0, tiled=True)

    def token_major(values):
        values = values.reshape(heads, tokens, head_dim)
        return jnp.transpose(values, (1, 0, 2)).reshape(1, tokens, heads * head_dim)

    return token_major(mine), token_major(cross)


def solution(mesh):
    fine = Mesh(mesh.devices.reshape(4, NX, NZ, NC), ("branch", "x", "z", "c"))
    seq = ("x", "z", "c")
    in_specs = (
        P("branch", seq, None, None),
        P("branch", seq, None, None),
        P("branch", seq, None),
        P(),
        P(),
        P(seq, None, None),
        P(),
        P(),
        P(),
        P(),
    )
    out_specs = (P("branch", seq, None), P("branch", seq, None))
    return jax.shard_map(local, mesh=fine, in_specs=in_specs, out_specs=out_specs, check_vma=False)
```

time: 353 us -> 302 us (0.86)
  waiting for transfers between devices: 179 us -> 89.4 us
  matrix products: 59.5 us -> 1.91 us
  Pallas kernels: 0 us -> 40 us
  blocking collectives: 0 us -> 39.5 us
  starting transfers between devices: 36.9 us -> 74.4 us
  local copies, waits for them, and re-layouts: 42.4 us -> 30.2 us
  other arithmetic: 17.9 us -> 7.59 us
    all_to_all x4 -> x7, waiting for transfers between devices: 137 us -> 27.6 us  [the longest x1 8.29 us: local(): cross = lax.all_to_all(cross, 'z', 0, 0, tiled=True)]
    dot_general x34 -> x1, matrix products: 59.5 us -> 1.91 us  [local(): jnp.einsum('btk,hkc->bhtc', context, jnp.transpose(weights, (2, 0, 1, 3,...]
    unnamed x1 -> x4, waiting for transfers between devices: 0.02 us -> 43.5 us
    all_gather x1 -> x2, waiting for transfers between devices: 40.5 us -> 0.05 us  [the longest x1 0.03 us: local(): gathered = lax.all_gather(self_queries, 'z', axis=0)]
    pallas_call x0 -> x7, Pallas kernels: none -> 40 us  [the longest x5 32.8 us: self_part(): pl.pallas_call(functools.partial(self_kernel, chunks=chunks, rows=256 * c...]
    all_to_all x4 -> x7, starting transfers between devices: 31.7 us -> 54.5 us  [the longest x1 15.7 us: local(): mine = lax.all_to_all(mine.astype(BF16), GROUP, 0, 0, tiled=True)]
    all_to_all x0 -> x1, blocking collectives: none -> 19.9 us  [local(): self_queries = lax.all_to_all(self_queries, GROUP, 0, 0, tiled=True)]
    all_gather x0 -> x1, blocking collectives: none -> 19.7 us  [local(): context = lax.all_gather(rows, 'z', axis=0)]
  transfers between devices with their start and end apart: 6 -> 22, of which waited for: 6 -> 11; matrix products, arithmetic and copies ran while one was open for 11% -> 7% of each run, Pallas kernels for 0% -> 13%
where the time goes in v1:
time: 302 us; the launch traced here: 300 us
  waiting for transfers between devices  89.4 us (30%)
  starting transfers between devices  74.4 us (25%)
  Pallas kernels  40 us (13%)
  blocking collectives  39.5 us (13%)
  local copies, waits for them, and re-layouts  30.2 us (10%)
  between operations  17.1 us (6%)
  other arithmetic  7.59 us (3%)
    unnamed x4, waiting for transfers between devices  43.5 us
    pallas_call x5, Pallas kernels, self_part(): pl.pallas_call(functools.partial(self_kernel, chunks=chunks, rows=256 * c...  32.8 us
    all_to_all x1, blocking collectives, local(): self_queries = lax.all_to_all(self_queries, GROUP, 0, 0, tiled=True)  19.9 us
    all_gather x1, blocking collectives, local(): context = lax.all_gather(rows, 'z', axis=0)  19.7 us
    all_to_all x1, starting transfers between devices, local(): mine = lax.all_to_all(mine.astype(BF16), GROUP, 0, 0, tiled=True)  15.7 us
    unnamed x41, local copies, waits for them, and re-layouts  10.8 us
    ppermute x3, waiting for transfers between devices, local(): right = lax.ppermute(to_right.astype(BF16), 'z', ring(NZ, 1))  9.07 us
    all_to_all x1, starting transfers between devices, local(): rows = lax.all_to_all(rows, GROUP, 0, 0, tiled=True).reshape(8 * count, 512)  8.54 us
  transfers between devices with their start and end apart: 22, of which 11 were waited for; matrix products, arithmetic and copies ran while one was open for 7% of the time, Pallas kernels for 13%

profile of v1, /device:TPU:1, one launch (start us, length us, event | category | flops | bytes accessed | tf_op | source)
XLA Modules:
  0.0 300.2 jit_solution(9688167689737019092)
XLA Ops:
  8.0 0.8 compare_and_fusion
  8.9 1.5 gather_fusion
  10.3 0.8 select_select_fusion
  11.1 5.0 %all-to-all-start.6 = ((bf16[4,8,4096]{2,1,0:T(8,128)(2,1)}), bf16[4,8,4096]{2,1,0:T(8,128)(2,1)S(1)}, u32[]{:S(2)}, u32[]{:S(2)}) async-start(bf16[4,8,4096]{2,1,0:T(8,128)(2,1)} %select_select_fusion), calls=%async_computation.6 | async-start | bytes 524288 | tf_op jit(solution)/shard_map/all_to_all | solution.py:197
  16.2 0.8 copy.50
  17.0 4.7 %all-to-all-done.6 = bf16[4,8,4096]{2,1,0:T(8,128)(2,1)S(1)} async-done(((bf16[4,8,4096]{2,1,0:T(8,128)(2,1)}), bf16[4,8,4096]{2,1,0:T(8,128)(2,1)S(1)}, u32[]{:S(2)}, u32[]{:S(2)}) %all-to-all-start.6) | async-done | bytes 262176 | tf_op jit(solution)/shard_map/all_to_all | solution.py:197
  21.7 8.2 %all-to-all-start.5 = ((bf16[8,5,16,256]{3,2,1,0:T(8,128)(2,1)}), bf16[8,5,16,256]{3,2,1,0:T(8,128)(2,1)S(1)}, u32[]{:S(2)}, u32[]{:S(2)}) async-start(bf16[8,5,16,256]{3,2,1,0:T(8,128)(2,1)} %bitcast.32), calls=%async_computation.5 | async-start | bytes 655360 | tf_op jit(solution)/shard_map/all_to_all | solution.py:207
  31.7 1.4 reshape.273
  33.1 6.8 %all-to-all-done.5 = bf16[8,5,16,256]{3,2,1,0:T(8,128)(2,1)S(1)} async-done(((bf16[8,5,16,256]{3,2,1,0:T(8,128)(2,1)}), bf16[8,5,16,256]{3,2,1,0:T(8,128)(2,1)S(1)}, u32[]{:S(2)}, u32[]{:S(2)}) %all-to-all-start.5) | async-done | bytes 327712 | tf_op jit(solution)/shard_map/all_to_all | solution.py:207
  39.9 8.5 %all-to-all-start.7 = ((bf16[8,8,512]{2,1,0:T(8,128)(2,1)}), bf16[8,8,512]{2,1,0:T(8,128)(2,1)S(1)}, u32[]{:S(2)}, u32[]{:S(2)}) async-start(bf16[8,8,512]{2,1,0:T(8,128)(2,1)} %reshape.273), calls=%async_computation.7 | async-start | bytes 131072 | tf_op jit(solution)/shard_map/all_to_all | solution.py:203
  49.2 4.0 %all-to-all-done.7 = bf16[8,8,512]{2,1,0:T(8,128)(2,1)S(1)} async-done(((bf16[8,8,512]{2,1,0:T(8,128)(2,1)}), bf16[8,8,512]{2,1,0:T(8,128)(2,1)S(1)}, u32[]{:S(2)}, u32[]{:S(2)}) %all-to-all-start.7) | async-done | bytes 65568 | tf_op jit(solution)/shard_map/all_to_all | solution.py:203
  53.3 19.7 %all_gather.17 = bf16[8,64,512]{2,1,0:T(8,128)(2,1)S(1)} all-gather(bf16[1,64,512]{2,1,0:T(8,128)(2,1)S(1)} %bitcast.133), channel_id=1, replica_groups=mesh['branch'=4,'x'=4,'z'=8,'c'=2] {'z'}, dimensions={0}, use_global_device_ids=true | all-gather | bytes 589824 | tf_op jit(solution)/shard_map/all_gather | solution.py:204
  73.0 0.7 bitcast_dynamic-update-slice_fusion.6
  73.7 2.5 collective-permute-start.10
  76.2 0.8 bitcast_dynamic-update-slice_fusion.4
  77.0 3.4 %collective-permute-done.9 = bf16[8,5,16,256]{3,2,1,0:T(8,128)(2,1)S(1)} collective-permute-done((bf16[8,5,16,256]{3,2,1,0:T(8,128)(2,1)S(1)}, bf16[8,5,16,256]{3,2,1,0:T(8,128)(2,1)S(1)}, u32[]{:S(2)}, u32[]{:S(2)}) %collective-permute-start.9) | collective-permute-done | bytes 327712 | tf_op jit(solution)/shard_map/ppermute | solution.py:208
  80.4 0.8 bitcast_dynamic-update-slice_fusion.2
  81.1 1.0 collective-permute-done.10
  82.2 0.8 bitcast_dynamic-update-slice_fusion
  82.9 0.8 bitcast_dynamic-update-slice_fusion.7
  83.7 0.7 bitcast_dynamic-update-slice_fusion.5
  84.4 0.8 bitcast_dynamic-update-slice_fusion.3
  85.2 0.8 bitcast_dynamic-update-slice_fusion.1
  86.0 3.5 %rev.4 = bf16[8,8,5,16,256]{4,3,2,1,0:T(8,128)(2,1)} reverse(bf16[8,8,5,16,256]{4,3,2,1,0:T(8,128)(2,1)} %bitcast_dynamic-update-slice_fusion.1), dimensions={0} | reverse | bytes 5242880 | tf_op jit(solution)/shard_map/jit(_flip)/rev | solution.py:210
  89.5 1.4 dynamic-slice_bitcast_fusion
  91.0 1.9 fusion
  93.1 1.1 fusion.6
  94.2 19.9 %all_to_all.45 = bf16[8,5,32,128]{3,2,1,0:T(8,128)(2,1)} all-to-all(bf16[8,5,32,128]{3,2,1,0:T(8,128)(2,1)S(1)} %bitcast.132), channel_id=1, replica_groups=mesh['branch'=4,'x'=4,'z'=8,'c'=2] {'x','c'}, dimensions={0} | all-to-all | bytes 655360 | tf_op jit(solution)/shard_map/all_to_all | solution.py:185
  114.1 3.9 %copy.40 = bf16[40,128,256]{2,1,0:T(8,128)(2,1)} copy(bf16[40,128,256]{2,0,1:T(8,128)(2,1)} %bitcast.127) | data formatting | bytes 5242880 | tf_op jit(solution)/shard_map/transpose | solution.py:179
  118.0 5.2 %all-to-all-start.1 = ((bf16[8,5,128,256]{3,2,1,0:T(8,128)(2,1)}), bf16[8,5,128,256]{3,2,1,0:T(8,128)(2,1)}, u32[]{:S(2)}, u32[]{:S(2)}) async-start(bf16[8,5,128,256]{3,2,1,0:T(8,128)(2,1)} %bitcast.124), calls=%async_computation.1 | async-start | bytes 5242880 | tf_op jit(solution)/shard_map/all_to_all | solution.py:188
  123.2 0.7 constant_dynamic-slice_fusion.3
  125.9 0.7 constant_dynamic-slice_fusion
  126.6 43.5 %all-reduce.3.cloned.1.call-done = bf16[8,5,64,256]{3,2,0,1:T(8,128)(2,1)} async-done(((bf16[8,5,64,256]{3,2,0,1:T(8,128)(2,1)}), bf16[8,5,64,256]{3,2,0,1:T(8,128)(2,1)}) %all-reduce.3.cloned.1.call-update) | async-done | bytes 1310736
  170.1 1.6 dynamic-slice_bitcast_fusion.1
  171.9 0.7 pad_maximum_fusion.2
  172.7 5.7 %all-to-all-start.4 = ((bf16[8,5,32,128]{3,2,1,0:T(8,128)(2,1)}), bf16[8,5,32,128]{3,2,1,0:T(8,128)(2,1)S(1)}, u32[]{:S(2)}, u32[]{:S(2)}) async-start(bf16[8,5,32,128]{3,2,1,0:T(8,128)(2,1)} %bitcast.30), calls=%async_computation.4 | async-start | bytes 655360 | tf_op jit(solution)/shard_map/all_to_all | solution.py:232
  178.3 3.8 %norm_keys.1.k_ref = bf16[5,1024,128]{2,1,0:T(8,128)(2,1)S(1)} custom-call(bf16[8,5,128,256]{3,2,1,0:T(8,128)(2,1)} %all-to-all-done.1.kv_ref.v_ref, f32[5,1,128]{2,1,0:T(1,128)S(1)} %broadcast_in_dim.44.gain_ref), custom_call_target="tpu_custom_call" | custom-call | tf_op jit(solution)/shard_map/norm_keys/pallas_call | solution.py:114
  182.2 1.7 copy-done.1
  184.0 7.4 %self_part.8 = (f32[2,8,5,32,128]{4,3,2,1,0:T(8,128)S(1)}, f32[2,5,8,128]{3,2,1,0:T(8,128)S(1)}) custom-call(s32[2]{0:T(128)S(1)} %pad_add_fusion.2.order, bf16[8,8,5,32,128]{4,3,2,1,0:T(8,128)(2,1)S(1)} %bitcast.115, bf16[5,1024,128]{2,1,0:T(8,128)(2,1)S(1)} %norm_keys.1.k_ref, bf16[8,5,128,256]{3,2,1,0:T(8,128)(2,1)} %all-to-all-done.1.kv_ref.v_ref, ...), custom_call_target="tpu_custom_call" | custom-call | flops 2013265920 | bytes 6291456 | tf_op jit(solution)/shard_map/self_part/pallas_call | solution.py:90
  191.5 5.5 %self_part.9 = (bf16[1,8,5,32,128]{4,3,2,1,0:T(8,128)(2,1)S(1)}, f32[1,5,8,128]{3,2,1,0:T(8,128)S(1)}) custom-call(s32[1]{0:T(128)} %bitcast.18.order, bf16[8,8,5,32,128]{4,3,2,1,0:T(8,128)(2,1)S(1)} %bitcast.117, bf16[5,1024,128]{2,1,0:T(8,128)(2,1)S(1)} %norm_keys.1.k_ref, bf16[8,5,128,256]{3,2,1,0:T(8,128)(2,1)} %all-to-all-done.1.kv_ref.v_ref), custom_call_target="tpu_custom_call" | custom-call | flops 1006632960 | bytes 6291456 | tf_op jit(solution)/shard_map/self_part/pallas_call | solution.py:90
  197.0 1.6 collective-permute-start
  198.6 1.4 collective-permute-start.4
  200.0 5.3 %self_part.5 = (f32[1,8,5,32,128]{4,3,2,1,0:T(8,128)S(1)}, f32[1,5,8,128]{3,2,1,0:T(8,128)S(1)}) custom-call(s32[1]{0:T(128)} %bitcast.order, bf16[8,8,5,32,128]{4,3,2,1,0:T(8,128)(2,1)S(1)} %bitcast.118, bf16[5,1024,128]{2,1,0:T(8,128)(2,1)S(1)} %norm_keys.1.k_ref, bf16[8,5,128,256]{3,2,1,0:T(8,128)(2,1)} %all-to-all-done.1.kv_ref.v_ref), custom_call_target="tpu_custom_call" | custom-call | flops 1006632960 | bytes 6291456 | tf_op jit(solution)/shard_map/self_part/pallas_call | solution.py:90
  205.3 0.8 copy-done.4
  206.2 7.3 %self_part.6 = (f32[2,8,5,32,128]{4,3,2,1,0:T(8,128)S(1)}, f32[2,5,8,128]{3,2,1,0:T(8,128)S(1)}) custom-call(s32[2]{0:T(128)S(1)} %get-tuple-element.61.order, bf16[8,8,5,32,128]{4,3,2,1,0:T(8,128)(2,1)S(1)} %bitcast.119, bf16[5,1024,128]{2,1,0:T(8,128)(2,1)S(1)} %norm_keys.1.k_ref, bf16[8,5,128,256]{3,2,1,0:T(8,128)(2,1)} %all-to-all-done.1.kv_ref.v_ref, ...), custom_call_target="tpu_custom_call" | custom-call | flops 2013265920 | bytes 6291456 | tf_op jit(solution)/shard_map/self_part/pallas_call | solution.py:90
  213.5 7.3 %self_part.7 = (f32[2,8,5,32,128]{4,3,2,1,0:T(8,128)S(1)}, f32[2,5,8,128]{3,2,1,0:T(8,128)S(1)}) custom-call(s32[2]{0:T(128)S(1)} %get-tuple-element.62.order, bf16[8,8,5,32,128]{4,3,2,1,0:T(8,128)(2,1)S(1)} %bitcast.121, bf16[5,1024,128]{2,1,0:T(8,128)(2,1)S(1)} %norm_keys.1.k_ref, bf16[8,5,128,256]{3,2,1,0:T(8,128)(2,1)} %all-to-all-done.1.kv_ref.v_ref, ...), custom_call_target="tpu_custom_call" | custom-call | flops 2013265920 | bytes 6291456 | tf_op jit(solution)/shard_map/self_part/pallas_call | solution.py:90
  221.2 2.7 collective-permute-start.5
  224.0 4.3 %collective-permute-done.1 = bf16[8,5,32,128]{3,2,1,0:T(8,128)(2,1)S(1)} collective-permute-done((bf16[8,5,32,128]{3,2,1,0:T(8,128)(2,1)S(1)}, bf16[8,5,32,128]{3,2,1,0:T(8,128)(2,1)S(1)}, u32[]{:S(2)}, u32[]{:S(2)}) %collective-permute-start.1) | collective-permute-done | bytes 327712 | tf_op jit(solution)/shard_map/ppermute | solution.py:252
  228.5 1.1 collective-permute-start.2
  229.6 1.9 collective-permute-start.6
  231.5 0.7 fusion.20
  232.1 4.7 %collective-permute-done.2 = bf16[8,5,32,128]{3,2,1,0:T(8,128)(2,1)S(1)} collective-permute-done((bf16[8,5,32,128]{3,2,1,0:T(8,128)(2,1)S(1)}, bf16[8,5,32,128]{3,2,1,0:T(8,128)(2,1)S(1)}, u32[]{:S(2)}, u32[]{:S(2)}) %collective-permute-start.2) | collective-permute-done | bytes 327712 | tf_op jit(solution)/shard_map/ppermute | solution.py:252
  237.1 3.1 %collective-permute-start.7 = (bf16[8,5,32,128]{3,2,1,0:T(8,128)(2,1)S(1)}, bf16[8,5,32,128]{3,2,1,0:T(8,128)(2,1)S(1)}, u32[]{:S(2)}, u32[]{:S(2)}) collective-permute-start(bf16[8,5,32,128]{3,2,1,0:T(8,128)(2,1)S(1)} %get-tuple-element.49), channel_id=1, source_target_pairs={{0,14},{2,0},{4,2},{6,4},{8,6},{10,8},{12,10},{14,12},{1,15},{3,1}... | collective-permute-start | bytes 983048 | tf_op jit(solution)/shard_map/ppermute | solution.py:253
  240.2 6.9 %all-to-all-start.2 = ((f32[8,5,2,128]{3,2,1,0:T(2,128)}), f32[8,5,2,128]{3,2,1,0:T(2,128)S(1)}, u32[]{:S(2)}, u32[]{:S(2)}) async-start(f32[8,5,2,128]{3,2,1,0:T(2,128)} %fusion.20), calls=%async_computation.2 | async-start | bytes 81920 | tf_op jit(solution)/shard_map/all_to_all | solution.py:259
  247.2 1.3 copy-done.3
  248.5 3.4 %cross_part.1 = bf16[8,5,32,128]{3,2,1,0:T(8,128)(2,1)} custom-call(bf16[8,5,32,128]{3,2,1,0:T(8,128)(2,1)S(1)} %all-to-all-done.4.q_ref, bf16[8,5,64,256]{3,2,1,0:T(8,128)(2,1)S(1)} %bitcast.123, f32[1,512]{1,0:T(1,128)S(1)} %compare_convert_fusion.live_ref), custom_call_target="tpu_custom_call" | custom-call | tf_op jit(solution)/shard_map/cross_part/pallas_call | solution.py:142
  251.8 2.3 all-to-all-done.2
  254.2 4.3 %all-to-all-start.8 = ((bf16[8,5,32,128]{3,2,1,0:T(8,128)(2,1)}), bf16[8,5,32,128]{3,2,1,0:T(8,128)(2,1)S(1)}, u32[]{:S(2)}, u32[]{:S(2)}) async-start(bf16[8,5,32,128]{3,2,1,0:T(8,128)(2,1)} %cross_part.1), calls=%async_computation.8 | async-start | bytes 655360 | tf_op jit(solution)/shard_map/all_to_all | solution.py:234
  258.6 1.9 fusion.13
  260.6 8.3 %all-to-all-done.8 = bf16[8,5,32,128]{3,2,1,0:T(8,128)(2,1)S(1)} async-done(((bf16[8,5,32,128]{3,2,1,0:T(8,128)(2,1)}), bf16[8,5,32,128]{3,2,1,0:T(8,128)(2,1)S(1)}, u32[]{:S(2)}, u32[]{:S(2)}) %all-to-all-start.8) | async-done | bytes 327712 | tf_op jit(solution)/shard_map/all_to_all | solution.py:234
  268.9 15.7 %all-to-all-start.3 = ((bf16[8,5,32,128]{3,2,1,0:T(8,128)(2,1)}), bf16[8,5,32,128]{3,2,1,0:T(8,128)(2,1)S(1)}, u32[]{:S(2)}, u32[]{:S(2)}) async-start(bf16[8,5,32,128]{3,2,1,0:T(8,128)(2,1)} %fusion.13), calls=%async_computation.3 | async-start | bytes 655360 | tf_op jit(solution)/shard_map/all_to_all | solution.py:262
  284.8 0.9 reshape.275
  285.6 6.1 %all-to-all-done.3 = bf16[8,5,32,128]{3,2,1,0:T(8,128)(2,1)S(1)} async-done(((bf16[8,5,32,128]{3,2,1,0:T(8,128)(2,1)}), bf16[8,5,32,128]{3,2,1,0:T(8,128)(2,1)S(1)}, u32[]{:S(2)}, u32[]{:S(2)}) %all-to-all-start.3) | async-done | bytes 327712 | tf_op jit(solution)/shard_map/all_to_all | solution.py:262
  291.9 0.9 reshape.268
  (84 shorter events, 5.4 us)
Async XLA Ops:
  8.0 8.2 %copy-start = (bf16[64,40,256]{2,1,0:T(8,128)(2,1)S(1)}, bf16[64,40,256]{2,1,0:T(8,128)(2,1)}, u32[]{:S(2)}) copy-start(bf16[64,40,256]{2,1,0:T(8,128)(2,1)} %param.15) | copy-start | bytes 3932164
  8.0 21.9 %copy-start.9 = (s32[4]{0:T(128)S(1)}, s32[4]{0:T(128)}, u32[]{:S(2)}) copy-start(s32[4]{0:T(128)} %param.14) | copy-start | bytes 52
  8.0 23.0 %copy-start.6 = (bf16[1,32,40,256]{3,2,1,0:T(8,128)(2,1)S(1)}, bf16[1,32,40,256]{3,2,1,0:T(8,128)(2,1)}, u32[]{:S(2)}) copy-start(bf16[1,32,40,256]{3,2,1,0:T(8,128)(2,1)} %param.10) | copy-start | bytes 1966084
  11.1 10.5 %all-to-all-start.6 = ((bf16[4,8,4096]{2,1,0:T(8,128)(2,1)}), bf16[4,8,4096]{2,1,0:T(8,128)(2,1)S(1)}, u32[]{:S(2)}, u32[]{:S(2)}) async-start(bf16[4,8,4096]{2,1,0:T(8,128)(2,1)} %select_select_fusion), calls=%async_computation.6 | async-start | bytes 524288 | tf_op jit(solution)/shard_map/all_to_all | solution.py:197
  21.7 18.2 %all-to-all-start.5 = ((bf16[8,5,16,256]{3,2,1,0:T(8,128)(2,1)}), bf16[8,5,16,256]{3,2,1,0:T(8,128)(2,1)S(1)}, u32[]{:S(2)}, u32[]{:S(2)}) async-start(bf16[8,5,16,256]{3,2,1,0:T(8,128)(2,1)} %bitcast.32), calls=%async_computation.5 | async-start | bytes 655360 | tf_op jit(solution)/shard_map/all_to_all | solution.py:207
  39.9 13.4 %all-to-all-start.7 = ((bf16[8,8,512]{2,1,0:T(8,128)(2,1)}), bf16[8,8,512]{2,1,0:T(8,128)(2,1)S(1)}, u32[]{:S(2)}, u32[]{:S(2)}) async-start(bf16[8,8,512]{2,1,0:T(8,128)(2,1)} %reshape.273), calls=%async_computation.7 | async-start | bytes 131072 | tf_op jit(solution)/shard_map/all_to_all | solution.py:203
  48.4 121.7 %all-reduce.3.cloned.1.call-start = ((), (), s32[]{:S(2)}) async-start(), calls=%async_computation.11 | async-start | bytes 2621440
  48.8 27.4 %collective-permute-start.8 = (bf16[8,5,16,256]{3,2,1,0:T(8,128)(2,1)S(1)}, bf16[8,5,16,256]{3,2,1,0:T(8,128)(2,1)S(1)}, u32[]{:S(2)}, u32[]{:S(2)}) collective-permute-start(bf16[8,5,16,256]{3,2,1,0:T(8,128)(2,1)S(1)} %all-to-all-done.5), channel_id=1, source_target_pairs={{0,64},{64,128},{128,192},{192,0},{1,65},{65,129},{129,193},{193,1... | collective-permute-start | bytes 983048 | tf_op jit(solution)/shard_map/ppermute | solution.py:208
  73.0 7.4 %collective-permute-start.9 = (bf16[8,5,16,256]{3,2,1,0:T(8,128)(2,1)S(1)}, bf16[8,5,16,256]{3,2,1,0:T(8,128)(2,1)S(1)}, u32[]{:S(2)}, u32[]{:S(2)}) collective-permute-start(bf16[8,5,16,256]{3,2,1,0:T(8,128)(2,1)S(1)} %all-to-all-done.5), channel_id=1, source_target_pairs={{0,128},{64,192},{128,0},{192,64},{1,129},{65,193},{129,1},{193,65... | collective-permute-start | bytes 983048 | tf_op jit(solution)/shard_map/ppermute | solution.py:208
  73.7 8.4 %collective-permute-start.10 = (bf16[8,5,16,256]{3,2,1,0:T(8,128)(2,1)S(1)}, bf16[8,5,16,256]{3,2,1,0:T(8,128)(2,1)S(1)}, u32[]{:S(2)}, u32[]{:S(2)}) collective-permute-start(bf16[8,5,16,256]{3,2,1,0:T(8,128)(2,1)S(1)} %all-to-all-done.5), channel_id=1, source_target_pairs={{0,192},{64,0},{128,64},{192,128},{1,193},{65,1},{129,65},{193,129... | collective-permute-start | bytes 983048 | tf_op jit(solution)/shard_map/ppermute | solution.py:208
  91.0 2.0 copy-start.7
  91.0 2.0 copy-start.8
  93.0 89.2 %all-gather.5.cloned.1.call-start = ((), (), s32[]{:S(2)}) async-start(), calls=%async_computation.9 | async-start | bytes 2949120 | tf_op jit(solution)/shard_map/all_gather | solution.py:186
  118.0 5.9 %copy-start.10 = (s32[8]{0:T(128)S(1)}, s32[8]{0:T(128)}, u32[]{:S(2)}) copy-start(s32[8]{0:T(128)} %param.13) | copy-start | bytes 100
  118.0 6.6 %copy-start.11 = (u32[256]{0:T(256)S(1)}, u32[256]{0:T(256)}, u32[]{:S(2)}) copy-start(u32[256]{0:T(256)} %constant.286) | copy-start | bytes 3076
  118.0 54.7 %all-to-all-start.1 = ((bf16[8,5,128,256]{3,2,1,0:T(8,128)(2,1)}), bf16[8,5,128,256]{3,2,1,0:T(8,128)(2,1)}, u32[]{:S(2)}, u32[]{:S(2)}) async-start(bf16[8,5,128,256]{3,2,1,0:T(8,128)(2,1)} %bitcast.124), calls=%async_computation.1 | async-start | bytes 5242880 | tf_op jit(solution)/shard_map/all_to_all | solution.py:188
  123.2 124.0 %all-gather.7.cloned.1.call-start = ((), (), s32[]{:S(2)}) async-start(), calls=%async_computation.10 | async-start | bytes 1474560 | tf_op jit(solution)/shard_map/all_gather | solution.py:223
  172.7 67.6 %all-to-all-start.4 = ((bf16[8,5,32,128]{3,2,1,0:T(8,128)(2,1)}), bf16[8,5,32,128]{3,2,1,0:T(8,128)(2,1)S(1)}, u32[]{:S(2)}, u32[]{:S(2)}) async-start(bf16[8,5,32,128]{3,2,1,0:T(8,128)(2,1)} %bitcast.30), calls=%async_computation.4 | async-start | bytes 655360 | tf_op jit(solution)/shard_map/all_to_all | solution.py:232
  182.2 1.7 copy-start.1
  191.5 8.5 %copy-start.2 = (bf16[64,5,32,128]{3,2,1,0:T(8,128)(2,1)S(1)}, bf16[64,5,32,128]{3,2,1,0:T(8,128)(2,1)}, u32[]{:S(2)}) copy-start(bf16[64,5,32,128]{3,2,1,0:T(8,128)(2,1)} %all-gather.5.cloned.1.call-done) | copy-start | bytes 7864324
  197.0 23.9 %collective-permute-start = (bf16[4,5,32,128]{3,2,1,0:T(8,128)(2,1)S(1)}, bf16[4,5,32,128]{3,2,1,0:T(8,128)(2,1)S(1)}, u32[]{:S(2)}, u32[]{:S(2)}) collective-permute-start(bf16[4,5,32,128]{3,2,1,0:T(8,128)(2,1)S(1)} %get-tuple-element.58), channel_id=1, source_target_pairs={{0,2},{2,4},{4,6},{6,8},{8,10},{10,12},{12,14},{14,0},{1,3},{3,5},... | collective-permute-start | bytes 491528 | tf_op jit(solution)/shard_map/ppermute | solution.py:240
  198.6 22.4 %collective-permute-start.4 = (bf16[4,5,32,128]{3,2,1,0:T(8,128)(2,1)S(1)}, bf16[4,5,32,128]{3,2,1,0:T(8,128)(2,1)S(1)}, u32[]{:S(2)}, u32[]{:S(2)}) collective-permute-start(bf16[4,5,32,128]{3,2,1,0:T(8,128)(2,1)S(1)} %get-tuple-element.59), channel_id=1, source_target_pairs={{0,14},{2,0},{4,2},{6,4},{8,6},{10,8},{12,10},{14,12},{1,15},{3,1}... | collective-permute-start | bytes 491528 | tf_op jit(solution)/shard_map/ppermute | solution.py:241
  205.3 0.8 copy-start.4
  221.1 7.2 %collective-permute-start.1 = (bf16[8,5,32,128]{3,2,1,0:T(8,128)(2,1)S(1)}, bf16[8,5,32,128]{3,2,1,0:T(8,128)(2,1)S(1)}, u32[]{:S(2)}, u32[]{:S(2)}) collective-permute-start(bf16[8,5,32,128]{3,2,1,0:T(8,128)(2,1)S(1)} %pad_maximum_fusion), channel_id=1, source_target_pairs={{0,2},{2,4},{4,6},{6,8},{8,10},{10,12},{12,14},{14,0},{1,3},{3,5},... | collective-permute-start | bytes 983048 | tf_op jit(solution)/shard_map/ppermute | solution.py:252
  221.2 7.1 %collective-permute-start.5 = (bf16[8,5,32,128]{3,2,1,0:T(8,128)(2,1)S(1)}, bf16[8,5,32,128]{3,2,1,0:T(8,128)(2,1)S(1)}, u32[]{:S(2)}, u32[]{:S(2)}) collective-permute-start(bf16[8,5,32,128]{3,2,1,0:T(8,128)(2,1)S(1)} %pad_maximum_fusion.1), channel_id=1, source_target_pairs={{0,14},{2,0},{4,2},{6,4},{8,6},{10,8},{12,10},{14,12},{1,15},{3,1}... | collective-permute-start | bytes 983048 | tf_op jit(solution)/shard_map/ppermute | solution.py:253
  228.5 8.4 %collective-permute-start.2 = (bf16[8,5,32,128]{3,2,1,0:T(8,128)(2,1)S(1)}, bf16[8,5,32,128]{3,2,1,0:T(8,128)(2,1)S(1)}, u32[]{:S(2)}, u32[]{:S(2)}) collective-permute-start(bf16[8,5,32,128]{3,2,1,0:T(8,128)(2,1)S(1)} %get-tuple-element.50), channel_id=1, source_target_pairs={{0,2},{2,4},{4,6},{6,8},{8,10},{10,12},{12,14},{14,0},{1,3},{3,5},... | collective-permute-start | bytes 983048 | tf_op jit(solution)/shard_map/ppermute | solution.py:252
  229.6 7.3 %collective-permute-start.6 = (bf16[8,5,32,128]{3,2,1,0:T(8,128)(2,1)S(1)}, bf16[8,5,32,128]{3,2,1,0:T(8,128)(2,1)S(1)}, u32[]{:S(2)}, u32[]{:S(2)}) collective-permute-start(bf16[8,5,32,128]{3,2,1,0:T(8,128)(2,1)S(1)} %get-tuple-element.51), channel_id=1, source_target_pairs={{0,14},{2,0},{4,2},{6,4},{8,6},{10,8},{12,10},{14,12},{1,15},{3,1}... | collective-permute-start | bytes 983048 | tf_op jit(solution)/shard_map/ppermute | solution.py:253
  236.9 21.8 %copy-start.5 = (f32[1,8,5,32,128]{4,3,2,1,0:T(8,128)S(1)}, f32[1,8,5,32,128]{4,3,2,1,0:T(8,128)}, u32[]{:S(2)}) copy-start(f32[1,8,5,32,128]{4,3,2,1,0:T(8,128)} %copy-done.4) | copy-start | bytes 1966084
  237.1 21.5 %collective-permute-start.7 = (bf16[8,5,32,128]{3,2,1,0:T(8,128)(2,1)S(1)}, bf16[8,5,32,128]{3,2,1,0:T(8,128)(2,1)S(1)}, u32[]{:S(2)}, u32[]{:S(2)}) collective-permute-start(bf16[8,5,32,128]{3,2,1,0:T(8,128)(2,1)S(1)} %get-tuple-element.49), channel_id=1, source_target_pairs={{0,14},{2,0},{4,2},{6,4},{8,6},{10,8},{12,10},{14,12},{1,15},{3,1}... | collective-permute-start | bytes 983048 | tf_op jit(solution)/shard_map/ppermute | solution.py:253
  240.2 18.4 %collective-permute-start.3 = (bf16[8,5,32,128]{3,2,1,0:T(8,128)(2,1)S(1)}, bf16[8,5,32,128]{3,2,1,0:T(8,128)(2,1)}, u32[]{:S(2)}, u32[]{:S(2)}) collective-permute-start(bf16[8,5,32,128]{3,2,1,0:T(8,128)(2,1)S(1)} %get-tuple-element.48), channel_id=1, source_target_pairs={{0,2},{2,4},{4,6},{6,8},{8,10},{10,12},{12,14},{14,0},{1,3},{3,5},... | collective-permute-start | bytes 983048 | tf_op jit(solution)/shard_map/ppermute | solution.py:252
  240.2 13.9 %all-to-all-start.2 = ((f32[8,5,2,128]{3,2,1,0:T(2,128)}), f32[8,5,2,128]{3,2,1,0:T(2,128)S(1)}, u32[]{:S(2)}, u32[]{:S(2)}) async-start(f32[8,5,2,128]{3,2,1,0:T(2,128)} %fusion.20), calls=%async_computation.2 | async-start | bytes 81920 | tf_op jit(solution)/shard_map/all_to_all | solution.py:259
  247.2 1.3 copy-start.3
  254.2 14.7 %all-to-all-start.8 = ((bf16[8,5,32,128]{3,2,1,0:T(8,128)(2,1)}), bf16[8,5,32,128]{3,2,1,0:T(8,128)(2,1)S(1)}, u32[]{:S(2)}, u32[]{:S(2)}) async-start(bf16[8,5,32,128]{3,2,1,0:T(8,128)(2,1)} %cross_part.1), calls=%async_computation.8 | async-start | bytes 655360 | tf_op jit(solution)/shard_map/all_to_all | solution.py:234
  268.9 22.9 %all-to-all-start.3 = ((bf16[8,5,32,128]{3,2,1,0:T(8,128)(2,1)}), bf16[8,5,32,128]{3,2,1,0:T(8,128)(2,1)S(1)}, u32[]{:S(2)}, u32[]{:S(2)}) async-start(bf16[8,5,32,128]{3,2,1,0:T(8,128)(2,1)} %fusion.13), calls=%async_computation.3 | async-start | bytes 655360 | tf_op jit(solution)/shard_map/all_to_all | solution.py:262
Sparse Core Ops, SparseCore 0:
  93.1 76.9 all-reduce.2
Sparse Core Ops, SparseCore 1:
  114.2 33.8 all-gather.4
  172.7 27.1 all-gather.6

commit v2 on v1

v2 whole, which is shorter than its diff:
```python
import functools
import math

import jax
import jax.numpy as jnp
from jax import lax
from jax.experimental import pallas as pl
from jax.experimental.pallas import tpu as pltpu
from jax.sharding import Mesh
from jax.sharding import PartitionSpec as P

EPSILON = 1e-06
BF16 = jnp.bfloat16
F32 = jnp.float32
NX, NZ, NC = 4, 8, 2
GROUP = ("x", "c")
SUMS = 16
ROWS = 256
VMEM = 24 << 20
ALL_VMEM = 60 << 20


def head_norm(values, gains):
    values = values.astype(F32)
    return values * lax.rsqrt(jnp.mean(values * values, axis=-1, keepdims=True) + EPSILON) * gains


def ring(size, step):
    return [(i, (i + step) % size) for i in range(size)]


def eye_mask():
    first = lax.broadcasted_iota(jnp.int32, (128, 128), 0)
    return first == lax.broadcasted_iota(jnp.int32, (128, 128), 1)


def self_kernel(q_ref, kv_ref, o_ref, *, rows, keys, scale):
    pairs = kv_ref[...].reshape(1024, 256)
    values = jnp.concatenate([pairs[:, 128:], jnp.ones((1024, 128), BF16)], axis=1)
    queries = q_ref[...].reshape(NZ * ROWS, 128)
    eye = eye_mask()
    for i in range(NZ * ROWS // rows):
        total = None
        for j in range(1024 // keys):
            scores = lax.dot_general(
                queries[i * rows : (i + 1) * rows],
                pairs[j * keys : (j + 1) * keys, :128],
                (((1,), (1,)), ((), ())),
                preferred_element_type=F32,
            )
            powers = jnp.exp2(scores * scale).astype(BF16)
            term = jnp.dot(powers, values[j * keys : (j + 1) * keys], preferred_element_type=F32)
            total = term if total is None else total + term
        for a in range(rows // ROWS):
            piece = total[a * ROWS : (a + 1) * ROWS]
            sums = [
                jnp.sum(jnp.where(eye, piece[b * 128 : (b + 1) * 128, 128:], 0.0), axis=0, keepdims=True)
                for b in range(2)
            ]
            sums = jnp.concatenate(sums + [jnp.zeros((6, 128), F32)], axis=0)
            high = sums.astype(BF16).astype(F32)
            result = jnp.concatenate([high, sums - high, piece[:, :128]], axis=0)
            o_ref[i * rows // ROWS + a, 0] = result.astype(BF16)


def self_part(gathered, pairs, scale):
    slots = pairs.shape[1]
    pairs_count = slots * NZ * ROWS * 1024
    return pl.pallas_call(
        functools.partial(self_kernel, rows=512, keys=512, scale=scale),
        grid=(slots,),
        in_specs=[
            pl.BlockSpec((NZ, 8, 32, 128), lambda h: (0, 0, h, 0)),
            pl.BlockSpec((8, 1, 128, 256), lambda h: (0, h, 0, 0)),
        ],
        out_specs=pl.BlockSpec((NZ, 1, SUMS + ROWS, 128), lambda h: (0, h, 0, 0)),
        out_shape=jax.ShapeDtypeStruct((NZ, slots, SUMS + ROWS, 128), BF16),
        compiler_params=pltpu.CompilerParams(vmem_limit_bytes=ALL_VMEM),
        cost_estimate=pl.CostEstimate(
            flops=pairs_count * 128 * 6, bytes_accessed=6 << 20, transcendentals=pairs_count
        ),
        name="self_part",
    )(gathered, pairs)


def last_kernel(total_ref, out_ref):
    eye = eye_mask()
    for h in range(out_ref.shape[1]):
        sums = total_ref[h, :SUMS].astype(F32)
        sums = sums[:8] + sums[8:]
        for b in range(2):
            rows = slice(SUMS + b * 128, SUMS + (b + 1) * 128)
            line = jnp.broadcast_to(sums[b : b + 1], (128, 128))
            column = jnp.sum(jnp.where(eye, line, 0.0), axis=1, keepdims=True)
            value = total_ref[h, rows].astype(F32)
            out_ref[b * 4 : (b + 1) * 4, h] = (value / column).astype(BF16).reshape(4, 32, 128)


def last_part(total):
    slots = total.shape[0]
    return pl.pallas_call(
        last_kernel,
        out_shape=jax.ShapeDtypeStruct((8, slots, 32, 128), BF16),
        compiler_params=pltpu.CompilerParams(vmem_limit_bytes=VMEM),
        name="last_part",
    )(total)


def norm_kernel(kv_ref, gain_ref, out_ref):
    out_ref[..., :128] = head_norm(kv_ref[..., :128], gain_ref[...]).astype(BF16)
    out_ref[..., 128:] = kv_ref[..., 128:]


def norm_keys(pairs, gains):
    heads, rows, width = pairs.shape
    block = heads // 8
    return pl.pallas_call(
        norm_kernel,
        grid=(8,),
        in_specs=[
            pl.BlockSpec((block, rows, width), lambda g: (g, 0, 0)),
            pl.BlockSpec((block, 1, 128), lambda g: (g, 0, 0)),
        ],
        out_specs=pl.BlockSpec((block, rows, width), lambda g: (g, 0, 0)),
        out_shape=jax.ShapeDtypeStruct(pairs.shape, BF16),
        compiler_params=pltpu.CompilerParams(vmem_limit_bytes=VMEM),
        name="norm_keys",
    )(pairs, gains[:, None, :])


def nothing(*refs):
    del refs


def after(value, *others):
    anywhere = pl.BlockSpec(memory_space=pl.ANY)
    return pl.pallas_call(
        nothing,
        in_specs=[anywhere] * (1 + len(others)),
        out_specs=anywhere,
        out_shape=jax.ShapeDtypeStruct(value.shape, value.dtype),
        input_output_aliases={0: 0},
        name="after",
    )(value, *others)


def pick_kernel(which_ref, b0, b1, b2, b3, out_ref):
    plane, prompt = which_ref[0], which_ref[1]
    rows = None
    for k, ref in enumerate((b0, b1, b2, b3)):
        for p in range(ref.shape[0]):
            value = ref[p].astype(F32)
            here = jnp.logical_and(plane == k, prompt == p)
            rows = value if rows is None else jnp.where(here, value, rows)
    count = rows.shape[0]
    rows = rows.astype(BF16)
    for x in range(NX):
        for block in range(8):
            first = (x * 8 + block) * 128
            for c in range(NC):
                at = slice(block * count, (block + 1) * count)
                out_ref[x * NC + c, at] = rows[:, first : first + 128]


def pick_part(which, banks):
    per_branch, count, width = banks[0].shape
    return pl.pallas_call(
        pick_kernel,
        grid_spec=pltpu.PrefetchScalarGridSpec(
            num_scalar_prefetch=1,
            grid=(1,),
            in_specs=[pl.BlockSpec(banks[0].shape, lambda i, w: (0, 0, 0))] * 4,
            out_specs=pl.BlockSpec((8, 8 * count, 128), lambda i, w: (0, 0, 0)),
        ),
        out_shape=jax.ShapeDtypeStruct((8, 8 * count, 128), BF16),
        compiler_params=pltpu.CompilerParams(vmem_limit_bytes=VMEM),
        name="pick_part",
    )(which, *banks)


def text_sum_kernel(where_ref, p0, p1, p2, p3, gain_ref, out_ref):
    total = p0[...].astype(F32)
    for ref in (p1, p2, p3):
        total = total + ref[...].astype(F32)
    keys = head_norm(total, gain_ref[0])
    out_ref[...] = jnp.where(where_ref[3] == 0, keys, total).astype(BF16)


def text_sum(where, parts, gains):
    slots, rows, width = parts[0].shape
    return pl.pallas_call(
        text_sum_kernel,
        grid_spec=pltpu.PrefetchScalarGridSpec(
            num_scalar_prefetch=1,
            grid=(1,),
            in_specs=[pl.BlockSpec((slots, rows, width), lambda i, w: (0, 0, 0))] * 4
            + [pl.BlockSpec((1, slots, 1, width), lambda i, w: (w[1], 0, 0, 0))],
            out_specs=pl.BlockSpec((slots, rows, width), lambda i, w: (0, 0, 0)),
        ),
        out_shape=jax.ShapeDtypeStruct((slots, rows, width), BF16),
        compiler_params=pltpu.CompilerParams(vmem_limit_bytes=VMEM),
        name="text_sum",
    )(where, *parts, gains.reshape(NZ, slots, 1, width))


def text_kernel(where_ref, low_ref, high_ref, w0, w1, w2, w3, o0, o1, o2, o3, held, context):
    branch, z, x, c = where_ref[0], where_ref[1], where_ref[2], where_ref[3]
    for k, ref in enumerate((w0, w1, w2, w3)):
        held[lax.rem(branch - k + 4, 4)] = ref[:, :, 0]
    weights = jnp.concatenate(
        [
            held[plane, lax.rem(of_c + c, NC), lax.rem(z - of_z + NZ, NZ)]
            for of_z in range(NZ)
            for of_c in range(NC)
            for plane in range(4)
        ],
        axis=0,
    )

    @pl.when(pl.program_id(0) == 0)
    def _():
        for i, ref in enumerate((low_ref, high_ref)):
            rows = ref[...].astype(F32)
            for j in range(4):
                part = rows[:, :, j * 8 : (j + 1) * 8].reshape(512, 128)
                first = (i * 4 + j) * 128
                context[:, first : first + 128] = part.astype(BF16)

    for k, ref in enumerate((o0, o1, o2, o3)):
        first = pl.multiple_of(lax.rem(x + k, NX) * 128, 128)
        result = jnp.dot(context[pl.ds(first, 128)], weights, preferred_element_type=F32)
        ref[0] = result.astype(BF16)


def text_part(where, gathered, weights):
    slots = weights[0].shape[2]
    first = slots
    grid_spec = pltpu.PrefetchScalarGridSpec(
        num_scalar_prefetch=1,
        grid=(slots,),
        in_specs=[
            pl.BlockSpec((NZ, 8, 32, 128), lambda h, w: (0, 0, first, 0)),
            pl.BlockSpec((NZ, 8, 32, 128), lambda h, w: (0, 0, first + 1, 0)),
        ]
        + [pl.BlockSpec((NC, NZ, 1, 16, 128), lambda h, w: (0, 0, h, 0, 0))] * 4,
        out_specs=[pl.BlockSpec((1, 128, 128), lambda h, w: (h, 0, 0))] * NX,
        scratch_shapes=[pltpu.VMEM((4, NC, NZ, 16, 128), BF16), pltpu.VMEM((512, 1024), BF16)],
    )
    return pl.pallas_call(
        text_kernel,
        grid_spec=grid_spec,
        out_shape=[jax.ShapeDtypeStruct((slots, 128, 128), BF16)] * NX,
        compiler_params=pltpu.CompilerParams(vmem_limit_bytes=ALL_VMEM),
        name="text_part",
    )(where, gathered, gathered, *weights)


def cross_kernel(where_ref, q_ref, mine_ref, other_ref, live_ref, o_ref, *, scale):
    mine, other = mine_ref[...].reshape(512, 128), other_ref[...].reshape(512, 128)
    first = where_ref[3] == 0
    keys, values = jnp.where(first, mine, other), jnp.where(first, other, mine)
    queries = q_ref[...].reshape(ROWS, 128)
    scores = lax.dot_general(
        queries, keys, (((1,), (1,)), ((), ())), preferred_element_type=F32
    )
    powers = jnp.where(live_ref[...] > 0.0, jnp.exp2(scores * scale), 0.0)
    weights = powers / jnp.sum(powers, axis=1, keepdims=True)
    result = jnp.dot(weights.astype(BF16), values, preferred_element_type=F32)
    o_ref[...] = result.astype(BF16).reshape(8, 1, 32, 128)


def cross_part(where, queries, mine, other, live, scale):
    slots = queries.shape[1]
    half = pl.BlockSpec((NX, 1, 128, 128), lambda h, w: (0, h, 0, 0))
    grid_spec = pltpu.PrefetchScalarGridSpec(
        num_scalar_prefetch=1,
        grid=(slots,),
        in_specs=[
            pl.BlockSpec((8, 1, 32, 128), lambda h, w: (0, h, 0, 0)),
            half,
            half,
            pl.BlockSpec((1, 512), lambda h, w: (0, 0)),
        ],
        out_specs=pl.BlockSpec((8, 1, 32, 128), lambda h, w: (0, h, 0, 0)),
    )
    return pl.pallas_call(
        functools.partial(cross_kernel, scale=scale),
        grid_spec=grid_spec,
        out_shape=jax.ShapeDtypeStruct(queries.shape, BF16),
        compiler_params=pltpu.CompilerParams(vmem_limit_bytes=VMEM),
        name="cross_part",
    )(where, queries, mine, other, live)


def local(
    queries,
    keys_values,
    prompt_bank,
    prompt_lengths,
    requests,
    w_text,
    q_gain,
    k_gain,
    cq_gain,
    ck_gain,
):
    branch = lax.axis_index("branch")
    z = lax.axis_index("z")
    x = lax.axis_index("x")
    c = lax.axis_index("c")
    where = jnp.stack([branch, z, x, c]).astype(jnp.int32)
    heads, head_dim = q_gain.shape
    slots = heads // (NX * NC)
    scale = math.log2(math.e) / math.sqrt(head_dim)
    tokens = queries.shape[1]
    per_branch, count, width = prompt_bank.shape

    def head_major(values):
        return jnp.transpose(values, (1, 0, 2)).reshape(
            8, slots, values.shape[0], values.shape[2]
        )

    wanted = jnp.take(requests, branch)
    which = jnp.stack([(branch - wanted // per_branch) % 4, wanted % per_branch])
    banks = [prompt_bank] + [lax.ppermute(prompt_bank, "branch", ring(4, k)) for k in (1, 2, 3)]
    columns = pick_part(which.astype(jnp.int32), banks)

    local_queries = queries[0]
    self_queries = head_major(head_norm(local_queries[..., :head_dim], q_gain).astype(BF16))
    self_queries = self_queries.reshape(8, slots * tokens, 128)
    got = lax.all_to_all(
        jnp.concatenate([self_queries, columns], axis=1), GROUP, 0, 0, tiled=True
    )

    pairs = norm_keys(jnp.transpose(keys_values[0], (1, 0, 2)), k_gain)
    got = after(got, pairs)
    pairs = pairs.reshape(8, slots, keys_values.shape[1], 2 * head_dim)
    pairs = lax.all_to_all(pairs, GROUP, 0, 0, tiled=True)
    gathered = lax.all_gather(got, "z", axis=0)

    part = after(head_major(lax.dynamic_slice_in_dim(w_text, branch * 16, 16, 0)), got)
    moved = [lax.dynamic_index_in_dim(part, z, 0, keepdims=False)]
    for k in range(1, NZ):
        piece = lax.dynamic_index_in_dim(part, (z + k) % NZ, 0, keepdims=False)
        moved.append(lax.ppermute(piece, "z", ring(NZ, k)))
    moved = jnp.stack(moved)
    halves = moved[..., :head_dim], moved[..., head_dim:]
    mine = jnp.where(c == 0, halves[0], halves[1])
    other = lax.ppermute(jnp.where(c == 0, halves[1], halves[0]), "c", ring(NC, 1))
    moved = jnp.stack([mine, other])
    weights = [moved] + [lax.ppermute(moved, "branch", ring(4, k)) for k in (1, 2, 3)]

    cross_queries = head_major(head_norm(local_queries[..., head_dim:], cq_gain).astype(BF16))
    cross_queries = lax.all_to_all(after(cross_queries, pairs), "z", 0, 0, tiled=True)

    entry = jnp.arange(512, dtype=jnp.int32)
    of_z = 2 * ((x - entry // 128 + NX) % NX) + entry % 128 // 64
    of_x, of_c, of_row = entry // 16 % 4, entry // 8 % 2, entry % 8
    text_row = ((of_x * NZ + of_z) * NC + of_c) * 8 + of_row
    live = (text_row < jnp.take(prompt_lengths, wanted)).astype(F32)[None, :]

    def to_others(pieces):
        return [pieces[0]] + [lax.ppermute(pieces[k], "x", ring(NX, k)) for k in (1, 2, 3)]

    gathered = after(gathered, cross_queries, *weights)
    own = self_part(gathered, pairs, scale)
    total = lax.psum_scatter(own, "z", scatter_dimension=0)

    parts = to_others(text_part(where, after(gathered, own), weights))
    text = jnp.stack(to_others([text_sum(where, parts, ck_gain)] * NX))
    other = lax.ppermute(text, "c", ring(NC, 1))
    cross = cross_part(where, cross_queries, text, other, live, scale)
    cross = lax.all_to_all(cross, "z", 0, 0, tiled=True)
    mine = last_part(total)
    mine = lax.all_to_all(mine, GROUP, 0, 0, tiled=True)

    def token_major(values):
        values = values.reshape(heads, tokens, head_dim)
        return jnp.transpose(values, (1, 0, 2)).reshape(1, tokens, heads * head_dim)

    return token_major(mine), token_major(cross)


def solution(mesh):
    fine = Mesh(mesh.devices.reshape(4, NX, NZ, NC), ("branch", "x", "z", "c"))
    seq = ("x", "z", "c")
    in_specs = (
        P("branch", seq, None, None),
        P("branch", seq, None, None),
        P("branch", seq, None),
        P(),
        P(),
        P(seq, None, None),
        P(),
        P(),
        P(),
        P(),
    )
    out_specs = (P("branch", seq, None), P("branch", seq, None))
    return jax.shard_map(local, mesh=fine, in_specs=in_specs, out_specs=out_specs, check_vma=False)
```

time: 302 us -> 197 us (0.65)
  blocking collectives: 39.5 us -> 0 us
  waiting for transfers between devices: 89.4 us -> 70.7 us
  local copies, waits for them, and re-layouts: 30.2 us -> 13.8 us
  starting transfers between devices: 74.4 us -> 61 us
  Pallas kernels: 40 us -> 30.3 us
    unnamed x4 -> x2, waiting for transfers between devices: 43.5 us -> 0.03 us
    ppermute x11 -> x21, waiting for transfers between devices: 13.5 us -> 49.5 us  [the longest x6 17.4 us: to_others(): lax.ppermute(pieces[k], 'x', ring(NX, k))]
    all_to_all x7 -> x4, starting transfers between devices: 55.2 us -> 22.2 us  [the longest x1 7.31 us: local(): lax.all_to_all(after(cross_queries, pairs), 'z', 0, 0, tiled=True)]
    all_to_all x1 -> x0, blocking collectives: 19.9 us -> none  [local(): self_queries = lax.all_to_all(self_queries, GROUP, 0, 0, tiled=True)]
    all_gather x1 -> x0, blocking collectives: 19.7 us -> none  [local(): context = lax.all_gather(rows, 'z', axis=0)]
    ppermute x11 -> x21, starting transfers between devices: 14.8 us -> 32.2 us  [the longest x7 12.5 us: local(): moved.append(lax.ppermute(piece, 'z', ring(NZ, k)))]
    all_to_all x7 -> x4, waiting for transfers between devices: 24 us -> 9.47 us  [the longest x1 6.14 us: local(): mine = lax.all_to_all(mine, GROUP, 0, 0, tiled=True)]
    pallas_call x7 -> x12, Pallas kernels: 40 us -> 30.3 us  [the longest x1 15.9 us: self_part(): pl.pallas_call(functools.partial(self_kernel, rows=512, keys=512, scale=s...]
  transfers between devices with their start and end apart: 22 -> 28, of which waited for: 11 -> 14; matrix products, arithmetic and copies ran while one was open for 7% -> 6% of each run, Pallas kernels for 13% -> 7%
where the time goes in v2:
time: 197 us; the launch traced here: 196 us
  waiting for transfers between devices  70.7 us (36%)
  starting transfers between devices  61 us (31%)
  Pallas kernels  30.3 us (15%)
  between operations  15.7 us (8%)
  local copies, waits for them, and re-layouts  13.8 us (7%)
  other arithmetic  4.67 us (2%)
    ppermute x6, waiting for transfers between devices, to_others(): lax.ppermute(pieces[k], 'x', ring(NX, k))  17.4 us
    ppermute x3, waiting for transfers between devices, local(): lax.ppermute(moved, 'branch', ring(4, k))  17 us
    pallas_call x1, Pallas kernels, self_part(): pl.pallas_call(functools.partial(self_kernel, rows=512, keys=512, scale=s...  15.9 us
    ppermute x7, waiting for transfers between devices, local(): moved.append(lax.ppermute(piece, 'z', ring(NZ, k)))  14.6 us
    ppermute x7, starting transfers between devices, local(): moved.append(lax.ppermute(piece, 'z', ring(NZ, k)))  12.5 us
    all_to_all x1, waiting for transfers between devices, local(): cross = lax.all_to_all(cross, 'z', 0, 0, tiled=True)  11.6 us
    unnamed x39, local copies, waits for them, and re-layouts  7.37 us
    all_to_all x1, starting transfers between devices, local(): lax.all_to_all(after(cross_queries, pairs), 'z', 0, 0, tiled=True)  7.31 us
  transfers between devices with their start and end apart: 28, of which 14 were waited for; matrix products, arithmetic and copies ran while one was open for 6% of the time, Pallas kernels for 7%

profile of v2, /device:TPU:1, one launch (start us, length us, event | category | flops | bytes accessed | tf_op | source)
XLA Modules:
  0.0 196.1 jit_solution(6589277697582535162)
XLA Ops:
  7.2 3.8 %collective-permute-start.1 = (bf16[2,8,4096]{2,1,0:T(8,128)(2,1)}, bf16[2,8,4096]{2,1,0:T(8,128)(2,1)S(1)}, u32[]{:S(2)}, u32[]{:S(2)}) collective-permute-start(bf16[2,8,4096]{2,1,0:T(8,128)(2,1)} %b0.1), channel_id=1, source_target_pairs={{0,128},{64,192},{128,0},{192,64},{1,129},{65,193},{129,1},{193,65... | collective-permute-start | bytes 393224 | tf_op jit(solution)/shard_map/ppermute | solution.py:325
  11.0 0.4 collective-permute-start
  11.4 2.3 %collective-permute-start.2 = (bf16[2,8,4096]{2,1,0:T(8,128)(2,1)}, bf16[2,8,4096]{2,1,0:T(8,128)(2,1)S(1)}, u32[]{:S(2)}, u32[]{:S(2)}) collective-permute-start(bf16[2,8,4096]{2,1,0:T(8,128)(2,1)} %b0.1), channel_id=1, source_target_pairs={{0,192},{64,0},{128,64},{192,128},{1,193},{65,1},{129,65},{193,129... | collective-permute-start | bytes 393224 | tf_op jit(solution)/shard_map/ppermute | solution.py:325
  13.7 1.5 fusion.3
  15.2 1.5 fusion.6
  16.7 1.2 dynamic-slice.4
  18.8 0.6 pick_part.1
  19.4 0.8 pad_maximum_fusion.1
  20.3 5.8 %all-to-all-start = ((bf16[8,224,128]{2,1,0:T(8,128)(2,1)}), bf16[8,224,128]{2,1,0:T(8,128)(2,1)S(1)}, u32[]{:S(2)}, u32[]{:S(2)}) async-start(bf16[8,224,128]{2,1,0:T(8,128)(2,1)} %pad_maximum_fusion.1), calls=%async_computation | async-start | bytes 917504 | tf_op jit(solution)/shard_map/all_to_all | solution.py:331
  26.1 2.4 %copy.30 = bf16[1,128,40,256]{3,1,2,0:T(8,128)(2,1)S(1)} copy(bf16[1,128,40,256]{3,2,1,0:T(8,128)(2,1)} %param.11) | data formatting | bytes 5242880 | tf_op args[1]
  28.5 1.6 norm_keys.1.refs_1_
  30.0 1.5 copy-done.1
  31.5 3.3 %all-to-all-done.refs_0_ = bf16[8,224,128]{2,1,0:T(8,128)(2,1)S(1)} async-done(((bf16[8,224,128]{2,1,0:T(8,128)(2,1)}), bf16[8,224,128]{2,1,0:T(8,128)(2,1)S(1)}, u32[]{:S(2)}, u32[]{:S(2)}) %all-to-all-start) | async-done | bytes 458784 | tf_op jit(solution)/shard_map/all_to_all | solution.py:331
  34.9 0.8 copy-done.10
  35.7 5.2 %all-to-all-start.1 = ((bf16[8,5,128,256]{3,2,1,0:T(8,128)(2,1)}), bf16[8,5,128,256]{3,2,1,0:T(8,128)(2,1)}, u32[]{:S(2)}, u32[]{:S(2)}) async-start(bf16[8,5,128,256]{3,2,1,0:T(8,128)(2,1)} %bitcast.71), calls=%async_computation.1 | async-start | bytes 5242880 | tf_op jit(solution)/shard_map/all_to_all | solution.py:338
  40.8 0.8 copy.26
  41.6 0.9 dynamic-slice_bitcast_fusion.1
  42.6 1.7 collective-permute-start.3
  44.3 4.0 %collective-permute-start.9 = (bf16[5,16,256]{2,1,0:T(8,128)(2,1)S(1)}, bf16[5,16,256]{2,1,0:T(8,128)(2,1)S(1)}, u32[]{:S(2)}, u32[]{:S(2)}) collective-permute-start(bf16[5,16,256]{2,1,0:T(8,128)(2,1)S(1)} %get-tuple-element.38), channel_id=1, source_target_pairs={{0,14},{2,0},{4,2},{6,4},{8,6},{10,8},{12,10},{14,12},{1,15},{3,1}... | collective-permute-start | bytes 122888 | tf_op jit(solution)/shard_map/ppermute | solution.py:345
  48.3 1.8 collective-permute-start.8
  50.1 2.1 %collective-permute-start.7 = (bf16[5,16,256]{2,1,0:T(8,128)(2,1)S(1)}, bf16[5,16,256]{2,1,0:T(8,128)(2,1)S(1)}, u32[]{:S(2)}, u32[]{:S(2)}) collective-permute-start(bf16[5,16,256]{2,1,0:T(8,128)(2,1)S(1)} %get-tuple-element.40), channel_id=1, source_target_pairs={{0,10},{2,12},{4,14},{6,0},{8,2},{10,4},{12,6},{14,8},{1,11},{3,13... | collective-permute-start | bytes 122888 | tf_op jit(solution)/shard_map/ppermute | solution.py:345
  52.2 2.8 %collective-permute-start.6 = (bf16[5,16,256]{2,1,0:T(8,128)(2,1)S(1)}, bf16[5,16,256]{2,1,0:T(8,128)(2,1)S(1)}, u32[]{:S(2)}, u32[]{:S(2)}) collective-permute-start(bf16[5,16,256]{2,1,0:T(8,128)(2,1)S(1)} %get-tuple-element.41), channel_id=1, source_target_pairs={{0,8},{2,10},{4,12},{6,14},{8,0},{10,2},{12,4},{14,6},{1,9},{3,11}... | collective-permute-start | bytes 122888 | tf_op jit(solution)/shard_map/ppermute | solution.py:345
  55.1 7.7 %collective-permute-done.4 = bf16[5,16,256]{2,1,0:T(8,128)(2,1)S(1)} collective-permute-done((bf16[5,16,256]{2,1,0:T(8,128)(2,1)S(1)}, bf16[5,16,256]{2,1,0:T(8,128)(2,1)S(1)}, u32[]{:S(2)}, u32[]{:S(2)}) %collective-permute-start.4) | collective-permute-done | bytes 40992 | tf_op jit(solution)/shard_map/ppermute | solution.py:345
  62.8 6.9 %collective-permute-done.5 = bf16[5,16,256]{2,1,0:T(8,128)(2,1)S(1)} collective-permute-done((bf16[5,16,256]{2,1,0:T(8,128)(2,1)S(1)}, bf16[5,16,256]{2,1,0:T(8,128)(2,1)S(1)}, u32[]{:S(2)}, u32[]{:S(2)}) %collective-permute-start.5) | collective-permute-done | bytes 40992 | tf_op jit(solution)/shard_map/ppermute | solution.py:345
  69.8 3.2 %collective-permute-start.10 = (bf16[8,5,16,128]{3,2,1,0:T(8,128)(2,1)S(1)}, bf16[8,5,16,128]{3,2,1,0:T(8,128)(2,1)S(1)}, u32[]{:S(2)}, u32[]{:S(2)}) collective-permute-start(bf16[8,5,16,128]{3,2,1,0:T(8,128)(2,1)S(1)} %get-tuple-element.37), channel_id=1, source_target_pairs={{0,1},{1,0},{2,3},{3,2},{4,5},{5,4},{6,7},{7,6},{8,9},{9,8},{10,11... | collective-permute-start | bytes 491528 | tf_op jit(solution)/shard_map/ppermute | solution.py:349
  73.0 0.8 copy.25
  73.8 7.3 %all-to-all-start.2 = ((bf16[8,5,32,128]{3,2,1,0:T(8,128)(2,1)}), bf16[8,5,32,128]{3,2,1,0:T(8,128)(2,1)S(1)}, u32[]{:S(2)}, u32[]{:S(2)}) async-start(bf16[8,5,32,128]{3,2,1,0:T(8,128)(2,1)} %after.6), calls=%async_computation.2 | async-start | bytes 655360 | tf_op jit(solution)/shard_map/all_to_all | solution.py:354
  81.2 1.5 collective-permute-start.13
  82.7 0.6 collective-permute-start.11
  83.3 6.1 %collective-permute-done.13.refs_5_.w3 = bf16[2,8,5,16,128]{4,3,2,1,0:T(8,128)(2,1)S(1)} collective-permute-done((bf16[2,8,5,16,128]{4,3,2,1,0:T(8,128)(2,1)S(1)}, bf16[2,8,5,16,128]{4,3,2,1,0:T(8,128)(2,1)S(1)}, u32[]{:S(2)}, u32[]{:S(2)}) %collective-permute-start.13) | collective-permute-done | bytes 327712 | tf_op jit(solution)/shard_map/ppermute | solution.py:351
  89.4 2.6 %collective-permute-done.12.refs_4_.w2 = bf16[2,8,5,16,128]{4,3,2,1,0:T(8,128)(2,1)S(1)} collective-permute-done((bf16[2,8,5,16,128]{4,3,2,1,0:T(8,128)(2,1)S(1)}, bf16[2,8,5,16,128]{4,3,2,1,0:T(8,128)(2,1)S(1)}, u32[]{:S(2)}, u32[]{:S(2)}) %collective-permute-start.12) | collective-permute-done | bytes 327712 | tf_op jit(solution)/shard_map/ppermute | solution.py:351
  92.0 8.3 %collective-permute-done.11.refs_3_.w1 = bf16[2,8,5,16,128]{4,3,2,1,0:T(8,128)(2,1)S(1)} collective-permute-done((bf16[2,8,5,16,128]{4,3,2,1,0:T(8,128)(2,1)S(1)}, bf16[2,8,5,16,128]{4,3,2,1,0:T(8,128)(2,1)S(1)}, u32[]{:S(2)}, u32[]{:S(2)}) %collective-permute-start.11) | collective-permute-done | bytes 327712 | tf_op jit(solution)/shard_map/ppermute | solution.py:351
  100.4 0.7 copy-done.14
  101.1 0.1 copy-done.2
  101.2 15.9 %self_part.1.refs_1_ = bf16[8,5,272,128]{3,2,1,0:T(8,128)(2,1)} custom-call(bf16[8,8,224,128]{3,2,1,0:T(8,128)(2,1)} %after.8.q_ref.refs_0_, bf16[8,5,128,256]{3,2,1,0:T(8,128)(2,1)} %all-to-all-done.1.refs_1_.kv_ref), custom_call_target="tpu_custom_call" | custom-call | flops 8053063680 | bytes 6291456 | tf_op jit(solution)/shard_map/self_part/pallas_call | solution.py:69
  117.1 0.6 pad_add_fusion.1.where_ref
  117.7 6.6 %text_part.1 = (bf16[5,128,128]{2,1,0:T(8,128)(2,1)}, bf16[5,128,128]{2,1,0:T(8,128)(2,1)}, bf16[5,128,128]{2,1,0:T(8,128)(2,1)}, bf16[5,128,128]{2,1,0:T(8,128)(2,1)}) custom-call(s32[4]{0:T(128)} %pad_add_fusion.1.where_ref, bf16[8,8,224,128]{3,2,1,0:T(8,128)(2,1)} %after.9.low_ref.high_ref, bf16[8,8,224,128]{3,2,1,0:T(8,128)(2,1)} %after.9.low_ref.high_ref, ...), custom_call_target="tpu_custom_call" | custom-call | tf_op jit(solution)/shard_map/text_part/pallas_call | solution.py:249
  124.3 0.3 collective-permute-start.14
  124.6 1.8 collective-permute-start.15
  126.4 0.7 collective-permute-start.16
  127.1 4.4 %collective-permute-done.14.p1 = bf16[5,128,128]{2,1,0:T(8,128)(2,1)S(1)} collective-permute-done((bf16[5,128,128]{2,1,0:T(8,128)(2,1)}, bf16[5,128,128]{2,1,0:T(8,128)(2,1)S(1)}, u32[]{:S(2)}, u32[]{:S(2)}) %collective-permute-start.14) | collective-permute-done | bytes 163872 | tf_op jit(solution)/shard_map/ppermute | solution.py:363
  131.5 2.2 %collective-permute-done.15.p2 = bf16[5,128,128]{2,1,0:T(8,128)(2,1)S(1)} collective-permute-done((bf16[5,128,128]{2,1,0:T(8,128)(2,1)}, bf16[5,128,128]{2,1,0:T(8,128)(2,1)S(1)}, u32[]{:S(2)}, u32[]{:S(2)}) %collective-permute-start.15) | collective-permute-done | bytes 163872 | tf_op jit(solution)/shard_map/ppermute | solution.py:363
  133.7 1.0 collective-permute-done.16.p3
  134.7 0.9 copy-done.5
  135.6 0.7 text_sum.1
  136.3 3.4 %collective-permute-start.19 = (bf16[5,128,128]{2,1,0:T(8,128)(2,1)S(1)}, bf16[5,128,128]{2,1,0:T(8,128)(2,1)S(1)}, u32[]{:S(2)}, u32[]{:S(2)}) collective-permute-start(bf16[5,128,128]{2,1,0:T(8,128)(2,1)S(1)} %text_sum.1), channel_id=1, source_target_pairs={{0,48},{16,0},{32,16},{48,32},{1,49},{17,1},{33,17},{49,33},{2,50}... | collective-permute-start | bytes 491528 | tf_op jit(solution)/shard_map/ppermute | solution.py:363
  139.8 0.7 collective-permute-start.17
  140.5 6.0 %collective-permute-done.19 = bf16[5,128,128]{2,1,0:T(8,128)(2,1)S(1)} collective-permute-done((bf16[5,128,128]{2,1,0:T(8,128)(2,1)S(1)}, bf16[5,128,128]{2,1,0:T(8,128)(2,1)S(1)}, u32[]{:S(2)}, u32[]{:S(2)}) %collective-permute-start.19) | collective-permute-done | bytes 163872 | tf_op jit(solution)/shard_map/ppermute | solution.py:363
  146.5 3.8 %collective-permute-done.17 = bf16[5,128,128]{2,1,0:T(8,128)(2,1)S(1)} collective-permute-done((bf16[5,128,128]{2,1,0:T(8,128)(2,1)S(1)}, bf16[5,128,128]{2,1,0:T(8,128)(2,1)S(1)}, u32[]{:S(2)}, u32[]{:S(2)}) %collective-permute-start.17) | collective-permute-done | bytes 163872 | tf_op jit(solution)/shard_map/ppermute | solution.py:363
  150.3 0.1 pad_maximum_fusion.mine_ref
  150.4 0.9 collective-permute-start.20
  151.3 0.6 dynamic-slice.5
  152.6 0.5 collective-permute-done.20.other_ref
  153.0 3.9 %cross_part.1 = bf16[8,5,32,128]{3,2,1,0:T(8,128)(2,1)} custom-call(s32[4]{0:T(128)S(1)} %copy-done.9, bf16[8,5,32,128]{3,2,1,0:T(8,128)(2,1)S(1)} %copy-done.3, bf16[4,5,128,128]{3,2,1,0:T(8,128)(2,1)S(1)} %pad_maximum_fusion.mine_ref, bf16[4,5,128,128]{3,2,1,0:T(8,128)(2,1)S(1)} %collective-permute-done.20.other_ref, f32[1,512]{1,0:T(1,128)S(1)} %compare_convert_fusion.live_ref), custom_call_target="tpu_custom_call" | custom-call | tf_op jit(solution)/shard_map/cross_part/pallas_call | solution.py:286
  157.0 6.6 %all-to-all-start.4 = ((bf16[8,5,32,128]{3,2,1,0:T(8,128)(2,1)}), bf16[8,5,32,128]{3,2,1,0:T(8,128)(2,1)S(1)}, u32[]{:S(2)}, u32[]{:S(2)}) async-start(bf16[8,5,32,128]{3,2,1,0:T(8,128)(2,1)} %cross_part.1), calls=%async_computation.5 | async-start | bytes 655360 | tf_op jit(solution)/shard_map/all_to_all | solution.py:373
  163.6 1.0 copy-done.4
  164.6 1.0 last_part.1
  165.6 11.6 %all-to-all-done.4 = bf16[8,5,32,128]{3,2,1,0:T(8,128)(2,1)S(1)} async-done(((bf16[8,5,32,128]{3,2,1,0:T(8,128)(2,1)}), bf16[8,5,32,128]{3,2,1,0:T(8,128)(2,1)S(1)}, u32[]{:S(2)}, u32[]{:S(2)}) %all-to-all-start.4) | async-done | bytes 327712 | tf_op jit(solution)/shard_map/all_to_all | solution.py:373
  177.2 3.9 %all-to-all-start.3 = ((bf16[8,5,32,128]{3,2,1,0:T(8,128)(2,1)}), bf16[8,5,32,128]{3,2,1,0:T(8,128)(2,1)S(1)}, u32[]{:S(2)}, u32[]{:S(2)}) async-start(bf16[8,5,32,128]{3,2,1,0:T(8,128)(2,1)} %last_part.1), calls=%async_computation.4 | async-start | bytes 655360 | tf_op jit(solution)/shard_map/all_to_all | solution.py:375
  181.2 0.1 copy.28
  181.3 0.9 reshape.347
  182.2 6.1 %all-to-all-done.3 = bf16[8,5,32,128]{3,2,1,0:T(8,128)(2,1)S(1)} async-done(((bf16[8,5,32,128]{3,2,1,0:T(8,128)(2,1)}), bf16[8,5,32,128]{3,2,1,0:T(8,128)(2,1)S(1)}, u32[]{:S(2)}, u32[]{:S(2)}) %all-to-all-start.3) | async-done | bytes 327712 | tf_op jit(solution)/shard_map/all_to_all | solution.py:375
  188.3 0.1 copy.27
  188.4 0.9 reshape.344
  (67 shorter events, 0.6 us)
Async XLA Ops:
  7.2 33.7 %copy-start = (bf16[64,40,256]{2,1,0:T(8,128)(2,1)S(1)}, bf16[64,40,256]{2,1,0:T(8,128)(2,1)}, u32[]{:S(2)}) copy-start(bf16[64,40,256]{2,1,0:T(8,128)(2,1)} %param.15) | copy-start | bytes 3932164
  7.2 11.6 %copy-start.6 = (bf16[2,8,4096]{2,1,0:T(8,128)(2,1)S(1)}, bf16[2,8,4096]{2,1,0:T(8,128)(2,1)}, u32[]{:S(2)}) copy-start(bf16[2,8,4096]{2,1,0:T(8,128)(2,1)} %b0.1) | copy-start | bytes 393220
  7.2 11.6 %collective-permute-start.1 = (bf16[2,8,4096]{2,1,0:T(8,128)(2,1)}, bf16[2,8,4096]{2,1,0:T(8,128)(2,1)S(1)}, u32[]{:S(2)}, u32[]{:S(2)}) collective-permute-start(bf16[2,8,4096]{2,1,0:T(8,128)(2,1)} %b0.1), channel_id=1, source_target_pairs={{0,128},{64,192},{128,0},{192,64},{1,129},{65,193},{129,1},{193,65... | collective-permute-start | bytes 393224 | tf_op jit(solution)/shard_map/ppermute | solution.py:325
  11.0 7.8 %collective-permute-start = (bf16[2,8,4096]{2,1,0:T(8,128)(2,1)}, bf16[2,8,4096]{2,1,0:T(8,128)(2,1)S(1)}, u32[]{:S(2)}, u32[]{:S(2)}) collective-permute-start(bf16[2,8,4096]{2,1,0:T(8,128)(2,1)} %b0.1), channel_id=1, source_target_pairs={{0,64},{64,128},{128,192},{192,0},{1,65},{65,129},{129,193},{193,1... | collective-permute-start | bytes 393224 | tf_op jit(solution)/shard_map/ppermute | solution.py:325
  11.4 7.4 %collective-permute-start.2 = (bf16[2,8,4096]{2,1,0:T(8,128)(2,1)}, bf16[2,8,4096]{2,1,0:T(8,128)(2,1)S(1)}, u32[]{:S(2)}, u32[]{:S(2)}) collective-permute-start(bf16[2,8,4096]{2,1,0:T(8,128)(2,1)} %b0.1), channel_id=1, source_target_pairs={{0,192},{64,0},{128,64},{192,128},{1,193},{65,1},{129,65},{193,129... | collective-permute-start | bytes 393224 | tf_op jit(solution)/shard_map/ppermute | solution.py:325
  20.3 14.6 %all-to-all-start = ((bf16[8,224,128]{2,1,0:T(8,128)(2,1)}), bf16[8,224,128]{2,1,0:T(8,128)(2,1)S(1)}, u32[]{:S(2)}, u32[]{:S(2)}) async-start(bf16[8,224,128]{2,1,0:T(8,128)(2,1)} %pad_maximum_fusion.1), calls=%async_computation | async-start | bytes 917504 | tf_op jit(solution)/shard_map/all_to_all | solution.py:331
  26.1 2.4 %copy-start.8 = (f32[40,128]{1,0:T(8,128)S(1)}, f32[40,128]{1,0:T(8,128)}, u32[]{:S(2)}) copy-start(f32[40,128]{1,0:T(8,128)} %param.17) | copy-start | bytes 61444
  26.1 74.3 %all-gather.3.cloned.1.call-start = ((), (), s32[]{:S(2)}) async-start(), calls=%async_computation.7 | async-start | bytes 4128768 | tf_op jit(solution)/shard_map/all_gather | solution.py:339
  30.0 1.5 copy-start.1
  34.9 0.8 copy-start.10
  35.7 38.1 %all-to-all-start.1 = ((bf16[8,5,128,256]{3,2,1,0:T(8,128)(2,1)}), bf16[8,5,128,256]{3,2,1,0:T(8,128)(2,1)}, u32[]{:S(2)}, u32[]{:S(2)}) async-start(bf16[8,5,128,256]{3,2,1,0:T(8,128)(2,1)} %bitcast.71), calls=%async_computation.1 | async-start | bytes 5242880 | tf_op jit(solution)/shard_map/all_to_all | solution.py:338
  42.6 12.5 %collective-permute-start.3 = (bf16[5,16,256]{2,1,0:T(8,128)(2,1)S(1)}, bf16[5,16,256]{2,1,0:T(8,128)(2,1)S(1)}, u32[]{:S(2)}, u32[]{:S(2)}) collective-permute-start(bf16[5,16,256]{2,1,0:T(8,128)(2,1)S(1)} %get-tuple-element.44), channel_id=1, source_target_pairs={{0,2},{2,4},{4,6},{6,8},{8,10},{10,12},{12,14},{14,0},{1,3},{3,5},... | collective-permute-start | bytes 122888 | tf_op jit(solution)/shard_map/ppermute | solution.py:345
  44.3 25.5 %collective-permute-start.9 = (bf16[5,16,256]{2,1,0:T(8,128)(2,1)S(1)}, bf16[5,16,256]{2,1,0:T(8,128)(2,1)S(1)}, u32[]{:S(2)}, u32[]{:S(2)}) collective-permute-start(bf16[5,16,256]{2,1,0:T(8,128)(2,1)S(1)} %get-tuple-element.38), channel_id=1, source_target_pairs={{0,14},{2,0},{4,2},{6,4},{8,6},{10,8},{12,10},{14,12},{1,15},{3,1}... | collective-permute-start | bytes 122888 | tf_op jit(solution)/shard_map/ppermute | solution.py:345
  48.3 21.4 %collective-permute-start.8 = (bf16[5,16,256]{2,1,0:T(8,128)(2,1)S(1)}, bf16[5,16,256]{2,1,0:T(8,128)(2,1)S(1)}, u32[]{:S(2)}, u32[]{:S(2)}) collective-permute-start(bf16[5,16,256]{2,1,0:T(8,128)(2,1)S(1)} %get-tuple-element.39), channel_id=1, source_target_pairs={{0,12},{2,14},{4,0},{6,2},{8,4},{10,6},{12,8},{14,10},{1,13},{3,15... | collective-permute-start | bytes 122888 | tf_op jit(solution)/shard_map/ppermute | solution.py:345
  50.1 19.6 %collective-permute-start.7 = (bf16[5,16,256]{2,1,0:T(8,128)(2,1)S(1)}, bf16[5,16,256]{2,1,0:T(8,128)(2,1)S(1)}, u32[]{:S(2)}, u32[]{:S(2)}) collective-permute-start(bf16[5,16,256]{2,1,0:T(8,128)(2,1)S(1)} %get-tuple-element.40), channel_id=1, source_target_pairs={{0,10},{2,12},{4,14},{6,0},{8,2},{10,4},{12,6},{14,8},{1,11},{3,13... | collective-permute-start | bytes 122888 | tf_op jit(solution)/shard_map/ppermute | solution.py:345
  52.2 17.5 %collective-permute-start.6 = (bf16[5,16,256]{2,1,0:T(8,128)(2,1)S(1)}, bf16[5,16,256]{2,1,0:T(8,128)(2,1)S(1)}, u32[]{:S(2)}, u32[]{:S(2)}) collective-permute-start(bf16[5,16,256]{2,1,0:T(8,128)(2,1)S(1)} %get-tuple-element.41), channel_id=1, source_target_pairs={{0,8},{2,10},{4,12},{6,14},{8,0},{10,2},{12,4},{14,6},{1,9},{3,11}... | collective-permute-start | bytes 122888 | tf_op jit(solution)/shard_map/ppermute | solution.py:345
  55.1 7.7 %collective-permute-start.4 = (bf16[5,16,256]{2,1,0:T(8,128)(2,1)S(1)}, bf16[5,16,256]{2,1,0:T(8,128)(2,1)S(1)}, u32[]{:S(2)}, u32[]{:S(2)}) collective-permute-start(bf16[5,16,256]{2,1,0:T(8,128)(2,1)S(1)} %get-tuple-element.43), channel_id=1, source_target_pairs={{0,4},{2,6},{4,8},{6,10},{8,12},{10,14},{12,0},{14,2},{1,5},{3,7},... | collective-permute-start | bytes 122888 | tf_op jit(solution)/shard_map/ppermute | solution.py:345
  62.8 6.9 %collective-permute-start.5 = (bf16[5,16,256]{2,1,0:T(8,128)(2,1)S(1)}, bf16[5,16,256]{2,1,0:T(8,128)(2,1)S(1)}, u32[]{:S(2)}, u32[]{:S(2)}) collective-permute-start(bf16[5,16,256]{2,1,0:T(8,128)(2,1)S(1)} %get-tuple-element.42), channel_id=1, source_target_pairs={{0,6},{2,8},{4,10},{6,12},{8,14},{10,0},{12,2},{14,4},{1,7},{3,9},... | collective-permute-start | bytes 122888 | tf_op jit(solution)/shard_map/ppermute | solution.py:345
  69.8 11.3 %collective-permute-start.10 = (bf16[8,5,16,128]{3,2,1,0:T(8,128)(2,1)S(1)}, bf16[8,5,16,128]{3,2,1,0:T(8,128)(2,1)S(1)}, u32[]{:S(2)}, u32[]{:S(2)}) collective-permute-start(bf16[8,5,16,128]{3,2,1,0:T(8,128)(2,1)S(1)} %get-tuple-element.37), channel_id=1, source_target_pairs={{0,1},{1,0},{2,3},{3,2},{4,5},{5,4},{6,7},{7,6},{8,9},{9,8},{10,11... | collective-permute-start | bytes 491528 | tf_op jit(solution)/shard_map/ppermute | solution.py:349
  73.8 26.6 %all-to-all-start.2 = ((bf16[8,5,32,128]{3,2,1,0:T(8,128)(2,1)}), bf16[8,5,32,128]{3,2,1,0:T(8,128)(2,1)S(1)}, u32[]{:S(2)}, u32[]{:S(2)}) async-start(bf16[8,5,32,128]{3,2,1,0:T(8,128)(2,1)} %after.6), calls=%async_computation.2 | async-start | bytes 655360 | tf_op jit(solution)/shard_map/all_to_all | solution.py:354
  81.1 82.5 %reduce-scatter.2.cloned.1.call-start = ((), (), s32[]{:S(2)}) async-start(), calls=%async_computation.6 | async-start | bytes 3133440 | tf_op jit(solution)/shard_map/reduce_scatter | solution.py:367
  81.2 19.2 %copy-start.11 = (bf16[2,8,5,16,128]{4,3,2,1,0:T(8,128)(2,1)}, bf16[2,8,5,16,128]{4,3,2,1,0:T(8,128)(2,1)S(1)}, u32[]{:S(2)}) copy-start(bf16[2,8,5,16,128]{4,3,2,1,0:T(8,128)(2,1)S(1)} %pad_maximum_fusion.2.refs_2_.w0) | copy-start | bytes 983044
  81.2 8.2 %collective-permute-start.13 = (bf16[2,8,5,16,128]{4,3,2,1,0:T(8,128)(2,1)S(1)}, bf16[2,8,5,16,128]{4,3,2,1,0:T(8,128)(2,1)S(1)}, u32[]{:S(2)}, u32[]{:S(2)}) collective-permute-start(bf16[2,8,5,16,128]{4,3,2,1,0:T(8,128)(2,1)S(1)} %pad_maximum_fusion.2.refs_2_.w0), channel_id=1, source_target_pairs={{0,192},{64,0},{128,64},{192,128},{1,193},{65,1},{129,65},{193,129... | collective-permute-start | bytes 983048 | tf_op jit(solution)/shard_map/ppermute | solution.py:351
  82.7 9.4 %collective-permute-start.12 = (bf16[2,8,5,16,128]{4,3,2,1,0:T(8,128)(2,1)S(1)}, bf16[2,8,5,16,128]{4,3,2,1,0:T(8,128)(2,1)S(1)}, u32[]{:S(2)}, u32[]{:S(2)}) collective-permute-start(bf16[2,8,5,16,128]{4,3,2,1,0:T(8,128)(2,1)S(1)} %pad_maximum_fusion.2.refs_2_.w0), channel_id=1, source_target_pairs={{0,128},{64,192},{128,0},{192,64},{1,129},{65,193},{129,1},{193,65... | collective-permute-start | bytes 983048 | tf_op jit(solution)/shard_map/ppermute | solution.py:351
  82.7 17.6 %collective-permute-start.11 = (bf16[2,8,5,16,128]{4,3,2,1,0:T(8,128)(2,1)S(1)}, bf16[2,8,5,16,128]{4,3,2,1,0:T(8,128)(2,1)S(1)}, u32[]{:S(2)}, u32[]{:S(2)}) collective-permute-start(bf16[2,8,5,16,128]{4,3,2,1,0:T(8,128)(2,1)S(1)} %pad_maximum_fusion.2.refs_2_.w0), channel_id=1, source_target_pairs={{0,64},{64,128},{128,192},{192,0},{1,65},{65,129},{129,193},{193,1... | collective-permute-start | bytes 983048 | tf_op jit(solution)/shard_map/ppermute | solution.py:351
  89.4 11.0 %copy-start.12 = (bf16[2,8,5,16,128]{4,3,2,1,0:T(8,128)(2,1)}, bf16[2,8,5,16,128]{4,3,2,1,0:T(8,128)(2,1)S(1)}, u32[]{:S(2)}) copy-start(bf16[2,8,5,16,128]{4,3,2,1,0:T(8,128)(2,1)S(1)} %collective-permute-done.13.refs_5_.w3) | copy-start | bytes 983044
  92.0 8.4 %copy-start.13 = (bf16[2,8,5,16,128]{4,3,2,1,0:T(8,128)(2,1)}, bf16[2,8,5,16,128]{4,3,2,1,0:T(8,128)(2,1)S(1)}, u32[]{:S(2)}) copy-start(bf16[2,8,5,16,128]{4,3,2,1,0:T(8,128)(2,1)S(1)} %collective-permute-done.12.refs_4_.w2) | copy-start | bytes 983044
  100.3 0.7 copy-start.14
  100.4 0.8 copy-start.2
  117.7 17.0 %copy-start.7 = (f32[40,128]{1,0:T(8,128)S(1)}, f32[40,128]{1,0:T(8,128)}, u32[]{:S(2)}) copy-start(f32[40,128]{1,0:T(8,128)} %param.19) | copy-start | bytes 61444
  117.7 17.0 %copy-start.9 = (s32[4]{0:T(128)S(1)}, s32[4]{0:T(128)}, u32[]{:S(2)}) copy-start(s32[4]{0:T(128)} %pad_add_fusion.1.where_ref) | copy-start | bytes 52
  117.7 33.6 %copy-start.15 = (s32[8]{0:T(128)S(1)}, s32[8]{0:T(128)}, u32[]{:S(2)}) copy-start(s32[8]{0:T(128)} %param.13) | copy-start | bytes 100
  117.7 35.4 %copy-start.3 = (bf16[8,5,32,128]{3,2,1,0:T(8,128)(2,1)S(1)}, bf16[8,5,32,128]{3,2,1,0:T(8,128)(2,1)}, u32[]{:S(2)}) copy-start(bf16[8,5,32,128]{3,2,1,0:T(8,128)(2,1)} %copy-done.2) | copy-start | bytes 983044
  124.3 7.2 %collective-permute-start.14 = (bf16[5,128,128]{2,1,0:T(8,128)(2,1)}, bf16[5,128,128]{2,1,0:T(8,128)(2,1)S(1)}, u32[]{:S(2)}, u32[]{:S(2)}) collective-permute-start(bf16[5,128,128]{2,1,0:T(8,128)(2,1)} %get-tuple-element.7), channel_id=1, source_target_pairs={{0,16},{16,32},{32,48},{48,0},{1,17},{17,33},{33,49},{49,1},{2,18}... | collective-permute-start | bytes 491528 | tf_op jit(solution)/shard_map/ppermute | solution.py:363
  124.6 9.1 %collective-permute-start.15 = (bf16[5,128,128]{2,1,0:T(8,128)(2,1)}, bf16[5,128,128]{2,1,0:T(8,128)(2,1)S(1)}, u32[]{:S(2)}, u32[]{:S(2)}) collective-permute-start(bf16[5,128,128]{2,1,0:T(8,128)(2,1)} %get-tuple-element.8), channel_id=1, source_target_pairs={{0,32},{16,48},{32,0},{48,16},{1,33},{17,49},{33,1},{49,17},{2,34}... | collective-permute-start | bytes 491528 | tf_op jit(solution)/shard_map/ppermute | solution.py:363
  126.4 8.3 %collective-permute-start.16 = (bf16[5,128,128]{2,1,0:T(8,128)(2,1)}, bf16[5,128,128]{2,1,0:T(8,128)(2,1)S(1)}, u32[]{:S(2)}, u32[]{:S(2)}) collective-permute-start(bf16[5,128,128]{2,1,0:T(8,128)(2,1)} %get-tuple-element.9), channel_id=1, source_target_pairs={{0,48},{16,0},{32,16},{48,32},{1,49},{17,1},{33,17},{49,33},{2,50}... | collective-permute-start | bytes 491528 | tf_op jit(solution)/shard_map/ppermute | solution.py:363
  134.7 0.9 copy-start.5
  136.3 10.1 %collective-permute-start.19 = (bf16[5,128,128]{2,1,0:T(8,128)(2,1)S(1)}, bf16[5,128,128]{2,1,0:T(8,128)(2,1)S(1)}, u32[]{:S(2)}, u32[]{:S(2)}) collective-permute-start(bf16[5,128,128]{2,1,0:T(8,128)(2,1)S(1)} %text_sum.1), channel_id=1, source_target_pairs={{0,48},{16,0},{32,16},{48,32},{1,49},{17,1},{33,17},{49,33},{2,50}... | collective-permute-start | bytes 491528 | tf_op jit(solution)/shard_map/ppermute | solution.py:363
  139.8 6.7 %collective-permute-start.18 = (bf16[5,128,128]{2,1,0:T(8,128)(2,1)S(1)}, bf16[5,128,128]{2,1,0:T(8,128)(2,1)S(1)}, u32[]{:S(2)}, u32[]{:S(2)}) collective-permute-start(bf16[5,128,128]{2,1,0:T(8,128)(2,1)S(1)} %text_sum.1), channel_id=1, source_target_pairs={{0,32},{16,48},{32,0},{48,16},{1,33},{17,49},{33,1},{49,17},{2,34}... | collective-permute-start | bytes 491528 | tf_op jit(solution)/shard_map/ppermute | solution.py:363
  139.8 10.5 %collective-permute-start.17 = (bf16[5,128,128]{2,1,0:T(8,128)(2,1)S(1)}, bf16[5,128,128]{2,1,0:T(8,128)(2,1)S(1)}, u32[]{:S(2)}, u32[]{:S(2)}) collective-permute-start(bf16[5,128,128]{2,1,0:T(8,128)(2,1)S(1)} %text_sum.1), channel_id=1, source_target_pairs={{0,16},{16,32},{32,48},{48,0},{1,17},{17,33},{33,49},{49,1},{2,18}... | collective-permute-start | bytes 491528 | tf_op jit(solution)/shard_map/ppermute | solution.py:363
  150.4 2.6 %collective-permute-start.20 = (bf16[4,5,128,128]{3,2,1,0:T(8,128)(2,1)S(1)}, bf16[4,5,128,128]{3,2,1,0:T(8,128)(2,1)S(1)}, u32[]{:S(2)}, u32[]{:S(2)}) collective-permute-start(bf16[4,5,128,128]{3,2,1,0:T(8,128)(2,1)S(1)} %pad_maximum_fusion.mine_ref), channel_id=1, source_target_pairs={{0,1},{1,0},{2,3},{3,2},{4,5},{5,4},{6,7},{7,6},{8,9},{9,8},{10,11... | collective-permute-start | bytes 1966088 | tf_op jit(solution)/shard_map/ppermute | solution.py:371
  157.0 20.2 %all-to-all-start.4 = ((bf16[8,5,32,128]{3,2,1,0:T(8,128)(2,1)}), bf16[8,5,32,128]{3,2,1,0:T(8,128)(2,1)S(1)}, u32[]{:S(2)}, u32[]{:S(2)}) async-start(bf16[8,5,32,128]{3,2,1,0:T(8,128)(2,1)} %cross_part.1), calls=%async_computation.5 | async-start | bytes 655360 | tf_op jit(solution)/shard_map/all_to_all | solution.py:373
  163.6 1.0 copy-start.4
  177.2 11.1 %all-to-all-start.3 = ((bf16[8,5,32,128]{3,2,1,0:T(8,128)(2,1)}), bf16[8,5,32,128]{3,2,1,0:T(8,128)(2,1)S(1)}, u32[]{:S(2)}, u32[]{:S(2)}) async-start(bf16[8,5,32,128]{3,2,1,0:T(8,128)(2,1)} %last_part.1), calls=%async_computation.4 | async-start | bytes 655360 | tf_op jit(solution)/shard_map/all_to_all | solution.py:375
Sparse Core Ops, SparseCore 0:
  35.8 62.0 all-gather.2
  117.2 38.7 reduce-scatter.1

commit v3 on v2

--- a/solution.py
+++ b/solution.py
@@ -144,8 +144,11 @@
     )(value, *others)
 
 
-def pick_kernel(which_ref, b0, b1, b2, b3, out_ref):
-    plane, prompt = which_ref[0], which_ref[1]
+def pick_kernel(where_ref, requests_ref, b0, b1, b2, b3, out_ref):
+    wanted = requests_ref[where_ref[0]]
+    per_branch = b0.shape[0]
+    plane = lax.rem(where_ref[0] - wanted // per_branch + 4, 4)
+    prompt = lax.rem(wanted, per_branch)
     rows = None
     for k, ref in enumerate((b0, b1, b2, b3)):
         for p in range(ref.shape[0]):
@@ -162,20 +165,20 @@
                 out_ref[x * NC + c, at] = rows[:, first : first + 128]
 
 
-def pick_part(which, banks):
+def pick_part(where, requests, banks):
     per_branch, count, width = banks[0].shape
     return pl.pallas_call(
         pick_kernel,
         grid_spec=pltpu.PrefetchScalarGridSpec(
-            num_scalar_prefetch=1,
+            num_scalar_prefetch=2,
             grid=(1,),
-            in_specs=[pl.BlockSpec(banks[0].shape, lambda i, w: (0, 0, 0))] * 4,
-            out_specs=pl.BlockSpec((8, 8 * count, 128), lambda i, w: (0, 0, 0)),
+            in_specs=[pl.BlockSpec(banks[0].shape, lambda i, w, r: (0, 0, 0))] * 4,
+            out_specs=pl.BlockSpec((8, 8 * count, 128), lambda i, w, r: (0, 0, 0)),
         ),
         out_shape=jax.ShapeDtypeStruct((8, 8 * count, 128), BF16),
         compiler_params=pltpu.CompilerParams(vmem_limit_bytes=VMEM),
         name="pick_part",
-    )(which, *banks)
+    )(where, requests, *banks)
 
 
 def text_sum_kernel(where_ref, p0, p1, p2, p3, gain_ref, out_ref):
@@ -203,33 +206,30 @@
     )(where, *parts, gains.reshape(NZ, slots, 1, width))
 
 
-def text_kernel(where_ref, low_ref, high_ref, w0, w1, w2, w3, o0, o1, o2, o3, held, context):
+def text_kernel(where_ref, low_ref, high_ref, w0, w1, w2, w3, o0, o1, o2, o3, held, context, product):
     branch, z, x, c = where_ref[0], where_ref[1], where_ref[2], where_ref[3]
     for k, ref in enumerate((w0, w1, w2, w3)):
-        held[lax.rem(branch - k + 4, 4)] = ref[:, :, 0]
-    weights = jnp.concatenate(
-        [
-            held[plane, lax.rem(of_c + c, NC), lax.rem(z - of_z + NZ, NZ)]
-            for of_z in range(NZ)
-            for of_c in range(NC)
-            for plane in range(4)
-        ],
-        axis=0,
-    )
-
-    @pl.when(pl.program_id(0) == 0)
-    def _():
-        for i, ref in enumerate((low_ref, high_ref)):
-            rows = ref[...].astype(F32)
-            for j in range(4):
-                part = rows[:, :, j * 8 : (j + 1) * 8].reshape(512, 128)
-                first = (i * 4 + j) * 128
-                context[:, first : first + 128] = part.astype(BF16)
-
+        held[lax.rem(branch - k + 4, 4)] = ref[...]
+    for i, ref in enumerate((low_ref, high_ref)):
+        rows = ref[...].astype(F32)
+        for j in range(4):
+            part = rows[:, :, j * 8 : (j + 1) * 8].reshape(512, 128)
+            first = (i * 4 + j) * 128
+            context[:, first : first + 128] = part.astype(BF16)
+    for h in range(held.shape[3]):
+        weights = jnp.concatenate(
+            [
+                held[plane, lax.rem(of_c + c, NC), lax.rem(z - of_z + NZ, NZ), h]
+                for of_z in range(NZ)
+                for of_c in range(NC)
+                for plane in range(4)
+            ],
+            axis=0,
+        )
+        result = jnp.dot(context[...], weights, preferred_element_type=F32)
+        product[:, h] = result.astype(BF16).reshape(NX, 128, 128)
     for k, ref in enumerate((o0, o1, o2, o3)):
-        first = pl.multiple_of(lax.rem(x + k, NX) * 128, 128)
-        result = jnp.dot(context[pl.ds(first, 128)], weights, preferred_element_type=F32)
-        ref[0] = result.astype(BF16)
+        ref[...] = product[lax.rem(x + k, NX)]
 
 
 def text_part(where, gathered, weights):
@@ -237,14 +237,18 @@
     first = slots
     grid_spec = pltpu.PrefetchScalarGridSpec(
         num_scalar_prefetch=1,
-        grid=(slots,),
+        grid=(1,),
         in_specs=[
-            pl.BlockSpec((NZ, 8, 32, 128), lambda h, w: (0, 0, first, 0)),
-            pl.BlockSpec((NZ, 8, 32, 128), lambda h, w: (0, 0, first + 1, 0)),
+            pl.BlockSpec((NZ, 8, 32, 128), lambda i, w: (0, 0, first, 0)),
+            pl.BlockSpec((NZ, 8, 32, 128), lambda i, w: (0, 0, first + 1, 0)),
         ]
-        + [pl.BlockSpec((NC, NZ, 1, 16, 128), lambda h, w: (0, 0, h, 0, 0))] * 4,
-        out_specs=[pl.BlockSpec((1, 128, 128), lambda h, w: (h, 0, 0))] * NX,
-        scratch_shapes=[pltpu.VMEM((4, NC, NZ, 16, 128), BF16), pltpu.VMEM((512, 1024), BF16)],
+        + [pl.BlockSpec(weights[0].shape, lambda i, w: (0, 0, 0, 0, 0))] * 4,
+        out_specs=[pl.BlockSpec((slots, 128, 128), lambda i, w: (0, 0, 0))] * NX,
+        scratch_shapes=[
+            pltpu.VMEM((4,) + weights[0].shape, BF16),
+            pltpu.VMEM((512, 1024), BF16),
+            pltpu.VMEM((NX, slots, 128, 128), BF16),
+        ],
     )
     return pl.pallas_call(
         text_kernel,
@@ -255,7 +259,12 @@
     )(where, gathered, gathered, *weights)
 
 
-def cross_kernel(where_ref, q_ref, mine_ref, other_ref, live_ref, o_ref, *, scale):
+def cross_kernel(where_ref, requests_ref, lengths_ref, q_ref, mine_ref, other_ref, o_ref, *, scale):
+    entry = lax.broadcasted_iota(jnp.int32, (1, 512), 1)
+    of_z = 2 * jnp.bitwise_and(where_ref[2] - (entry >> 7) + NX, NX - 1) + ((entry >> 6) & 1)
+    of_x, of_c, of_row = (entry >> 4) & 3, (entry >> 3) & 1, entry & 7
+    text_row = ((of_x * NZ + of_z) * NC + of_c) * 8 + of_row
+    live = text_row < lengths_ref[requests_ref[where_ref[0]]]
     mine, other = mine_ref[...].reshape(512, 128), other_ref[...].reshape(512, 128)
     first = where_ref[3] == 0
     keys, values = jnp.where(first, mine, other), jnp.where(first, other, mine)
@@ -263,25 +272,22 @@
     scores = lax.dot_general(
         queries, keys, (((1,), (1,)), ((), ())), preferred_element_type=F32
     )
-    powers = jnp.where(live_ref[...] > 0.0, jnp.exp2(scores * scale), 0.0)
+    powers = jnp.where(live, jnp.exp2(scores * scale), 0.0)
     weights = powers / jnp.sum(powers, axis=1, keepdims=True)
     result = jnp.dot(weights.astype(BF16), values, preferred_element_type=F32)
-    o_ref[...] = result.astype(BF16).reshape(8, 1, 32, 128)
-
-
-def cross_part(where, queries, mine, other, live, scale):
+    result = result.astype(BF16).reshape(8, 32, 128)
+    for of_z in range(NZ):
+        o_ref[lax.rem(where_ref[1] - of_z + NZ, NZ), 0] = result[of_z]
+
+
+def cross_part(where, requests, lengths, queries, mine, other, scale):
     slots = queries.shape[1]
-    half = pl.BlockSpec((NX, 1, 128, 128), lambda h, w: (0, h, 0, 0))
+    half = pl.BlockSpec((NX, 1, 128, 128), lambda h, *refs: (0, h, 0, 0))
     grid_spec = pltpu.PrefetchScalarGridSpec(
-        num_scalar_prefetch=1,
+        num_scalar_prefetch=3,
         grid=(slots,),
-        in_specs=[
-            pl.BlockSpec((8, 1, 32, 128), lambda h, w: (0, h, 0, 0)),
-            half,
-            half,
-            pl.BlockSpec((1, 512), lambda h, w: (0, 0)),
-        ],
-        out_specs=pl.BlockSpec((8, 1, 32, 128), lambda h, w: (0, h, 0, 0)),
+        in_specs=[pl.BlockSpec((8, 1, 32, 128), lambda h, *refs: (0, h, 0, 0)), half, half],
+        out_specs=pl.BlockSpec((8, 1, 32, 128), lambda h, *refs: (0, h, 0, 0)),
     )
     return pl.pallas_call(
         functools.partial(cross_kernel, scale=scale),
@@ -289,7 +295,33 @@
         out_shape=jax.ShapeDtypeStruct(queries.shape, BF16),
         compiler_params=pltpu.CompilerParams(vmem_limit_bytes=VMEM),
         name="cross_part",
-    )(where, queries, mine, other, live)
+    )(where, requests, lengths, queries, mine, other)
+
+
+def place_kernel(where_ref, *refs):
+    out_ref = refs[-1]
+    slots, _, width = refs[0].shape
+    for k, ref in enumerate(refs[:-1]):
+        first = lax.rem(where_ref[1] + k, NZ) * (slots * width)
+        for h in range(slots):
+            at = pl.multiple_of(first + h * width, 128)
+            out_ref[:, pl.ds(at, width)] = ref[h]
+
+
+def place_part(where, pieces):
+    slots, rows, width = pieces[0].shape
+    return pl.pallas_call(
+        place_kernel,
+        grid_spec=pltpu.PrefetchScalarGridSpec(
+            num_scalar_prefetch=1,
+            grid=(1,),
+            in_specs=[pl.BlockSpec((slots, rows, width), lambda i, w: (0, 0, 0))] * NZ,
+            out_specs=pl.BlockSpec((rows, NZ * slots * width), lambda i, w: (0, 0)),
+        ),
+        out_shape=jax.ShapeDtypeStruct((rows, NZ * slots * width), BF16),
+        compiler_params=pltpu.CompilerParams(vmem_limit_bytes=VMEM),
+        name="place_part",
+    )(where, *pieces)
 
 
 def local(
@@ -320,10 +352,8 @@
             8, slots, values.shape[0], values.shape[2]
         )
 
-    wanted = jnp.take(requests, branch)
-    which = jnp.stack([(branch - wanted // per_branch) % 4, wanted % per_branch])
     banks = [prompt_bank] + [lax.ppermute(prompt_bank, "branch", ring(4, k)) for k in (1, 2, 3)]
-    columns = pick_part(which.astype(jnp.int32), banks)
+    columns = pick_part(where, requests, banks)
 
     local_queries = queries[0]
     self_queries = head_major(head_norm(local_queries[..., :head_dim], q_gain).astype(BF16))
@@ -350,27 +380,23 @@
     moved = jnp.stack([mine, other])
     weights = [moved] + [lax.ppermute(moved, "branch", ring(4, k)) for k in (1, 2, 3)]
 
-    cross_queries = head_major(head_norm(local_queries[..., head_dim:], cq_gain).astype(BF16))
-    cross_queries = lax.all_to_all(after(cross_queries, pairs), "z", 0, 0, tiled=True)
-
-    entry = jnp.arange(512, dtype=jnp.int32)
-    of_z = 2 * ((x - entry // 128 + NX) % NX) + entry % 128 // 64
-    of_x, of_c, of_row = entry // 16 % 4, entry // 8 % 2, entry % 8
-    text_row = ((of_x * NZ + of_z) * NC + of_c) * 8 + of_row
-    live = (text_row < jnp.take(prompt_lengths, wanted)).astype(F32)[None, :]
-
     def to_others(pieces):
         return [pieces[0]] + [lax.ppermute(pieces[k], "x", ring(NX, k)) for k in (1, 2, 3)]
 
-    gathered = after(gathered, cross_queries, *weights)
+    gathered = after(gathered, *weights)
     own = self_part(gathered, pairs, scale)
     total = lax.psum_scatter(own, "z", scatter_dimension=0)
 
+    cross_queries = head_major(head_norm(local_queries[..., head_dim:], cq_gain).astype(BF16))
+    cross_queries = lax.all_to_all(after(cross_queries, own), "z", 0, 0, tiled=True)
+
     parts = to_others(text_part(where, after(gathered, own), weights))
+    parts[0] = after(parts[0], cross_queries)
     text = jnp.stack(to_others([text_sum(where, parts, ck_gain)] * NX))
     other = lax.ppermute(text, "c", ring(NC, 1))
-    cross = cross_part(where, cross_queries, text, other, live, scale)
-    cross = lax.all_to_all(cross, "z", 0, 0, tiled=True)
+    cross = cross_part(where, requests, prompt_lengths, cross_queries, text, other, scale)
+    cross = [cross[0]] + [lax.ppermute(cross[k], "z", ring(NZ, -k)) for k in range(1, NZ)]
+    cross = place_part(where, cross)
     mine = last_part(total)
     mine = lax.all_to_all(mine, GROUP, 0, 0, tiled=True)
 
@@ -378,7 +404,7 @@
         values = values.reshape(heads, tokens, head_dim)
         return jnp.transpose(values, (1, 0, 2)).reshape(1, tokens, heads * head_dim)
 
-    return token_major(mine), token_major(cross)
+    return token_major(mine), cross[None]
 
 
 def solution(mesh):

time: 197 us -> 190 us (0.964)
  waiting for transfers between devices: 70.7 us -> 59.7 us
  starting transfers between devices: 61 us -> 68.7 us
    ppermute x0 -> x7, starting transfers between devices: none -> 13.6 us  [local(): lax.ppermute(cross[k], 'z', ring(NZ, -k))]
    all_to_all x2 -> x1, starting transfers between devices: 13.9 us -> 3.43 us  [local(): lax.all_to_all(after(cross_queries, own), 'z', 0, 0, tiled=True)]
    all_to_all x2 -> x1, waiting for transfers between devices: 11.6 us -> 1.85 us  [local(): lax.all_to_all(after(cross_queries, own), 'z', 0, 0, tiled=True)]
    all_to_all x1, waiting for transfers between devices: 6.14 us -> 0.01 us  [local(): mine = lax.all_to_all(mine, GROUP, 0, 0, tiled=True)]
    ppermute x6, waiting for transfers between devices: 17.4 us -> 13.2 us  [to_others(): lax.ppermute(pieces[k], 'x', ring(NX, k))]
    ppermute x0 -> x7, waiting for transfers between devices: none -> 4.1 us  [local(): lax.ppermute(cross[k], 'z', ring(NZ, -k))]
    all_to_all x1, starting transfers between devices: 3.95 us -> 7.62 us  [local(): mine = lax.all_to_all(mine, GROUP, 0, 0, tiled=True)]
    unnamed x39 -> x43, local copies, waits for them, and re-layouts: 7.37 us -> 8.98 us
  transfers between devices with their start and end apart: 28 -> 34, of which waited for: 14 -> 15; matrix products, arithmetic and copies ran while one was open for 6% -> 4% of each run, Pallas kernels for 7% -> 6%
where the time goes in v3:
time: 190 us; the launch traced here: 189 us
  starting transfers between devices  68.7 us (36%)
  waiting for transfers between devices  59.7 us (31%)
  Pallas kernels  29.2 us (15%)
  between operations  14.5 us (8%)
  local copies, waits for them, and re-layouts  12.6 us (7%)
  other arithmetic  4.03 us (2%)
    ppermute x3, waiting for transfers between devices, local(): lax.ppermute(moved, 'branch', ring(4, k))  17.1 us
    pallas_call x1, Pallas kernels, self_part(): pl.pallas_call(functools.partial(self_kernel, rows=512, keys=512, scale=s...  15.8 us
    ppermute x7, waiting for transfers between devices, local(): moved.append(lax.ppermute(piece, 'z', ring(NZ, k)))  15.6 us
    ppermute x7, starting transfers between devices, local(): lax.ppermute(cross[k], 'z', ring(NZ, -k))  13.6 us
    ppermute x6, waiting for transfers between devices, to_others(): lax.ppermute(pieces[k], 'x', ring(NX, k))  13.2 us
    ppermute x7, starting transfers between devices, local(): moved.append(lax.ppermute(piece, 'z', ring(NZ, k)))  12.5 us
    unnamed x43, local copies, waits for them, and re-layouts  8.98 us
    ppermute x6, starting transfers between devices, to_others(): lax.ppermute(pieces[k], 'x', ring(NX, k))  8.31 us
  transfers between devices with their start and end apart: 34, of which 15 were waited for; matrix products, arithmetic and copies ran while one was open for 4% of the time, Pallas kernels for 6%

profile of v3, /device:TPU:1, one launch (start us, length us, event | category | flops | bytes accessed | tf_op | source)
XLA Modules:
  0.0 188.7 jit_solution(11945508269967041808)
XLA Ops:
  7.2 3.8 %collective-permute-start.1 = (bf16[2,8,4096]{2,1,0:T(8,128)(2,1)}, bf16[2,8,4096]{2,1,0:T(8,128)(2,1)S(1)}, u32[]{:S(2)}, u32[]{:S(2)}) collective-permute-start(bf16[2,8,4096]{2,1,0:T(8,128)(2,1)} %b0.1), channel_id=1, source_target_pairs={{0,128},{64,192},{128,0},{192,64},{1,129},{65,193},{129,1},{193,65... | collective-permute-start | bytes 393224 | tf_op jit(solution)/shard_map/ppermute | solution.py:355
  11.4 2.3 %collective-permute-start.2 = (bf16[2,8,4096]{2,1,0:T(8,128)(2,1)}, bf16[2,8,4096]{2,1,0:T(8,128)(2,1)S(1)}, u32[]{:S(2)}, u32[]{:S(2)}) collective-permute-start(bf16[2,8,4096]{2,1,0:T(8,128)(2,1)} %b0.1), channel_id=1, source_target_pairs={{0,192},{64,0},{128,64},{192,128},{1,193},{65,1},{129,65},{193,129... | collective-permute-start | bytes 393224 | tf_op jit(solution)/shard_map/ppermute | solution.py:355
  13.7 1.5 fusion.3
  15.2 1.5 fusion.6
  16.9 1.7 collective-permute-done.b1
  18.6 0.6 pick_part.1
  19.3 0.8 pad_maximum_fusion.1
  20.1 4.6 %all-to-all-start = ((bf16[8,224,128]{2,1,0:T(8,128)(2,1)}), bf16[8,224,128]{2,1,0:T(8,128)(2,1)S(1)}, u32[]{:S(2)}, u32[]{:S(2)}) async-start(bf16[8,224,128]{2,1,0:T(8,128)(2,1)} %pad_maximum_fusion.1), calls=%async_computation | async-start | bytes 917504 | tf_op jit(solution)/shard_map/all_to_all | solution.py:361
  24.7 2.4 %copy.29 = bf16[1,128,40,256]{3,1,2,0:T(8,128)(2,1)S(1)} copy(bf16[1,128,40,256]{3,2,1,0:T(8,128)(2,1)} %param.11) | data formatting | bytes 5242880 | tf_op args[1]
  27.1 1.6 norm_keys.1.refs_1_
  28.6 1.5 copy-done.1
  30.1 3.3 %all-to-all-done.refs_0_ = bf16[8,224,128]{2,1,0:T(8,128)(2,1)S(1)} async-done(((bf16[8,224,128]{2,1,0:T(8,128)(2,1)}), bf16[8,224,128]{2,1,0:T(8,128)(2,1)S(1)}, u32[]{:S(2)}, u32[]{:S(2)}) %all-to-all-start) | async-done | bytes 458784 | tf_op jit(solution)/shard_map/all_to_all | solution.py:361
  33.5 0.8 copy-done.13
  34.4 0.8 copy.25
  35.2 0.9 dynamic-slice_bitcast_fusion.1
  36.1 1.7 collective-permute-start.3
  37.8 5.5 %all-to-all-start.1 = ((bf16[8,5,128,256]{3,2,1,0:T(8,128)(2,1)}), bf16[8,5,128,256]{3,2,1,0:T(8,128)(2,1)}, u32[]{:S(2)}, u32[]{:S(2)}) async-start(bf16[8,5,128,256]{3,2,1,0:T(8,128)(2,1)} %bitcast.79), calls=%async_computation.1 | async-start | bytes 5242880 | tf_op jit(solution)/shard_map/all_to_all | solution.py:368
  43.3 3.7 %collective-permute-start.9 = (bf16[5,16,256]{2,1,0:T(8,128)(2,1)S(1)}, bf16[5,16,256]{2,1,0:T(8,128)(2,1)S(1)}, u32[]{:S(2)}, u32[]{:S(2)}) collective-permute-start(bf16[5,16,256]{2,1,0:T(8,128)(2,1)S(1)} %get-tuple-element.24), channel_id=1, source_target_pairs={{0,14},{2,0},{4,2},{6,4},{8,6},{10,8},{12,10},{14,12},{1,15},{3,1}... | collective-permute-start | bytes 122888 | tf_op jit(solution)/shard_map/ppermute | solution.py:375
  47.0 2.2 %collective-permute-start.8 = (bf16[5,16,256]{2,1,0:T(8,128)(2,1)S(1)}, bf16[5,16,256]{2,1,0:T(8,128)(2,1)S(1)}, u32[]{:S(2)}, u32[]{:S(2)}) collective-permute-start(bf16[5,16,256]{2,1,0:T(8,128)(2,1)S(1)} %get-tuple-element.25), channel_id=1, source_target_pairs={{0,12},{2,14},{4,0},{6,2},{8,4},{10,6},{12,8},{14,10},{1,13},{3,15... | collective-permute-start | bytes 122888 | tf_op jit(solution)/shard_map/ppermute | solution.py:375
  49.2 2.2 %collective-permute-start.7 = (bf16[5,16,256]{2,1,0:T(8,128)(2,1)S(1)}, bf16[5,16,256]{2,1,0:T(8,128)(2,1)S(1)}, u32[]{:S(2)}, u32[]{:S(2)}) collective-permute-start(bf16[5,16,256]{2,1,0:T(8,128)(2,1)S(1)} %get-tuple-element.26), channel_id=1, source_target_pairs={{0,10},{2,12},{4,14},{6,0},{8,2},{10,4},{12,6},{14,8},{1,11},{3,13... | collective-permute-start | bytes 122888 | tf_op jit(solution)/shard_map/ppermute | solution.py:375
  51.3 2.7 %collective-permute-start.6 = (bf16[5,16,256]{2,1,0:T(8,128)(2,1)S(1)}, bf16[5,16,256]{2,1,0:T(8,128)(2,1)S(1)}, u32[]{:S(2)}, u32[]{:S(2)}) collective-permute-start(bf16[5,16,256]{2,1,0:T(8,128)(2,1)S(1)} %get-tuple-element.27), channel_id=1, source_target_pairs={{0,8},{2,10},{4,12},{6,14},{8,0},{10,2},{12,4},{14,6},{1,9},{3,11}... | collective-permute-start | bytes 122888 | tf_op jit(solution)/shard_map/ppermute | solution.py:375
  54.1 7.8 %collective-permute-done.4 = bf16[5,16,256]{2,1,0:T(8,128)(2,1)S(1)} collective-permute-done((bf16[5,16,256]{2,1,0:T(8,128)(2,1)S(1)}, bf16[5,16,256]{2,1,0:T(8,128)(2,1)S(1)}, u32[]{:S(2)}, u32[]{:S(2)}) %collective-permute-start.4) | collective-permute-done | bytes 40992 | tf_op jit(solution)/shard_map/ppermute | solution.py:375
  61.9 7.8 %collective-permute-done.5 = bf16[5,16,256]{2,1,0:T(8,128)(2,1)S(1)} collective-permute-done((bf16[5,16,256]{2,1,0:T(8,128)(2,1)S(1)}, bf16[5,16,256]{2,1,0:T(8,128)(2,1)S(1)}, u32[]{:S(2)}, u32[]{:S(2)}) %collective-permute-start.5) | collective-permute-done | bytes 40992 | tf_op jit(solution)/shard_map/ppermute | solution.py:375
  69.8 2.1 %collective-permute-start.10 = (bf16[8,5,16,128]{3,2,1,0:T(8,128)(2,1)S(1)}, bf16[8,5,16,128]{3,2,1,0:T(8,128)(2,1)S(1)}, u32[]{:S(2)}, u32[]{:S(2)}) collective-permute-start(bf16[8,5,16,128]{3,2,1,0:T(8,128)(2,1)S(1)} %get-tuple-element.23), channel_id=1, source_target_pairs={{0,1},{1,0},{2,3},{3,2},{4,5},{5,4},{6,7},{7,6},{8,9},{9,8},{10,11... | collective-permute-start | bytes 491528 | tf_op jit(solution)/shard_map/ppermute | solution.py:379
  71.9 1.0 collective-permute-done.10
  72.9 2.8 %collective-permute-start.13 = (bf16[2,8,5,16,128]{4,3,2,1,0:T(8,128)(2,1)S(1)}, bf16[2,8,5,16,128]{4,3,2,1,0:T(8,128)(2,1)S(1)}, u32[]{:S(2)}, u32[]{:S(2)}) collective-permute-start(bf16[2,8,5,16,128]{4,3,2,1,0:T(8,128)(2,1)S(1)} %pad_maximum_fusion.2.refs_1_.w0), channel_id=1, source_target_pairs={{0,192},{64,0},{128,64},{192,128},{1,193},{65,1},{129,65},{193,129... | collective-permute-start | bytes 983048 | tf_op jit(solution)/shard_map/ppermute | solution.py:381
  76.4 12.9 %collective-permute-done.13.refs_4_.w3 = bf16[2,8,5,16,128]{4,3,2,1,0:T(8,128)(2,1)S(1)} collective-permute-done((bf16[2,8,5,16,128]{4,3,2,1,0:T(8,128)(2,1)S(1)}, bf16[2,8,5,16,128]{4,3,2,1,0:T(8,128)(2,1)S(1)}, u32[]{:S(2)}, u32[]{:S(2)}) %collective-permute-start.13) | collective-permute-done | bytes 327712 | tf_op jit(solution)/shard_map/ppermute | solution.py:381
  89.3 4.2 %collective-permute-done.11.refs_2_.w1 = bf16[2,8,5,16,128]{4,3,2,1,0:T(8,128)(2,1)S(1)} collective-permute-done((bf16[2,8,5,16,128]{4,3,2,1,0:T(8,128)(2,1)S(1)}, bf16[2,8,5,16,128]{4,3,2,1,0:T(8,128)(2,1)S(1)}, u32[]{:S(2)}, u32[]{:S(2)}) %collective-permute-start.11) | collective-permute-done | bytes 327712 | tf_op jit(solution)/shard_map/ppermute | solution.py:381
  93.6 0.7 copy-done.17
  94.3 15.8 %self_part.1.refs_1_ = bf16[8,5,272,128]{3,2,1,0:T(8,128)(2,1)} custom-call(bf16[8,8,224,128]{3,2,1,0:T(8,128)(2,1)} %after.8.q_ref.refs_0_, bf16[8,5,128,256]{3,2,1,0:T(8,128)(2,1)} %all-to-all-done.1.kv_ref), custom_call_target="tpu_custom_call" | custom-call | flops 8053063680 | bytes 6291456 | tf_op jit(solution)/shard_map/self_part/pallas_call | solution.py:69
  110.1 0.8 copy.27
  110.9 3.4 %all-to-all-start.3 = ((bf16[8,5,32,128]{3,2,1,0:T(8,128)(2,1)}), bf16[8,5,32,128]{3,2,1,0:T(8,128)(2,1)S(1)}, u32[]{:S(2)}, u32[]{:S(2)}) async-start(bf16[8,5,32,128]{3,2,1,0:T(8,128)(2,1)} %after.9), calls=%async_computation.4 | async-start | bytes 655360 | tf_op jit(solution)/shard_map/all_to_all | solution.py:391
  114.4 5.0 %text_part.1 = (bf16[5,128,128]{2,1,0:T(8,128)(2,1)}, bf16[5,128,128]{2,1,0:T(8,128)(2,1)}, bf16[5,128,128]{2,1,0:T(8,128)(2,1)}, bf16[5,128,128]{2,1,0:T(8,128)(2,1)}) custom-call(s32[4]{0:T(128)} %copy-done.9, bf16[8,8,224,128]{3,2,1,0:T(8,128)(2,1)} %after.10.low_ref.high_ref, bf16[8,8,224,128]{3,2,1,0:T(8,128)(2,1)} %after.10.low_ref.high_ref, ...), custom_call_target="tpu_custom_call" | custom-call | tf_op jit(solution)/shard_map/text_part/pallas_call | solution.py:253
  119.4 1.5 collective-permute-start.14
  120.9 2.4 %collective-permute-start.15 = (bf16[5,128,128]{2,1,0:T(8,128)(2,1)}, bf16[5,128,128]{2,1,0:T(8,128)(2,1)S(1)}, u32[]{:S(2)}, u32[]{:S(2)}) collective-permute-start(bf16[5,128,128]{2,1,0:T(8,128)(2,1)} %get-tuple-element.8), channel_id=1, source_target_pairs={{0,32},{16,48},{32,0},{48,16},{1,33},{17,49},{33,1},{49,17},{2,34}... | collective-permute-start | bytes 491528 | tf_op jit(solution)/shard_map/ppermute | solution.py:384
  123.3 1.2 collective-permute-start.16
  124.5 1.8 all-to-all-done.3.refs_1_.q_ref
  126.4 0.7 copy-done.2
  127.1 3.5 %collective-permute-done.15.p2 = bf16[5,128,128]{2,1,0:T(8,128)(2,1)S(1)} collective-permute-done((bf16[5,128,128]{2,1,0:T(8,128)(2,1)}, bf16[5,128,128]{2,1,0:T(8,128)(2,1)S(1)}, u32[]{:S(2)}, u32[]{:S(2)}) %collective-permute-start.15) | collective-permute-done | bytes 163872 | tf_op jit(solution)/shard_map/ppermute | solution.py:384
  130.6 0.9 copy-done.4
  131.5 0.7 text_sum.1
  132.2 2.4 %collective-permute-start.19 = (bf16[5,128,128]{2,1,0:T(8,128)(2,1)S(1)}, bf16[5,128,128]{2,1,0:T(8,128)(2,1)S(1)}, u32[]{:S(2)}, u32[]{:S(2)}) collective-permute-start(bf16[5,128,128]{2,1,0:T(8,128)(2,1)S(1)} %text_sum.1), channel_id=1, source_target_pairs={{0,48},{16,0},{32,16},{48,32},{1,49},{17,1},{33,17},{49,33},{2,50}... | collective-permute-start | bytes 491528 | tf_op jit(solution)/shard_map/ppermute | solution.py:384
  134.6 0.9 collective-permute-start.18
  135.4 3.7 %collective-permute-done.19 = bf16[5,128,128]{2,1,0:T(8,128)(2,1)S(1)} collective-permute-done((bf16[5,128,128]{2,1,0:T(8,128)(2,1)S(1)}, bf16[5,128,128]{2,1,0:T(8,128)(2,1)S(1)}, u32[]{:S(2)}, u32[]{:S(2)}) %collective-permute-start.19) | collective-permute-done | bytes 163872 | tf_op jit(solution)/shard_map/ppermute | solution.py:384
  139.2 1.2 collective-permute-done.18
  140.3 4.8 %collective-permute-done.17 = bf16[5,128,128]{2,1,0:T(8,128)(2,1)S(1)} collective-permute-done((bf16[5,128,128]{2,1,0:T(8,128)(2,1)S(1)}, bf16[5,128,128]{2,1,0:T(8,128)(2,1)S(1)}, u32[]{:S(2)}, u32[]{:S(2)}) %collective-permute-start.17) | collective-permute-done | bytes 163872 | tf_op jit(solution)/shard_map/ppermute | solution.py:384
  145.2 1.2 collective-permute-start.20
  146.4 1.7 collective-permute-done.20.other_ref
  148.1 1.0 copy-done.3
  149.1 3.1 %cross_part.1 = bf16[8,5,32,128]{3,2,1,0:T(8,128)(2,1)S(1)} custom-call(s32[4]{0:T(128)S(1)} %copy-done.10, s32[4]{0:T(128)S(1)} %copy-done.11, s32[8]{0:T(128)S(1)} %copy-done.12, bf16[8,5,32,128]{3,2,1,0:T(8,128)(2,1)S(1)} %copy-done.3, bf16[4,5,128,128]{3,2,1,0:T(8,128)(2,1)S(1)} %pad_maximum_fusion.mine_ref, ...), custom_call_target="tpu_custom_call" | custom-call | tf_op jit(solution)/shard_map/cross_part/pallas_call | solution.py:292
  152.3 1.0 copy-done.5
  153.2 1.0 last_part.1
  154.2 7.6 %all-to-all-start.2 = ((bf16[8,5,32,128]{3,2,1,0:T(8,128)(2,1)}), bf16[8,5,32,128]{3,2,1,0:T(8,128)(2,1)S(1)}, u32[]{:S(2)}, u32[]{:S(2)}) async-start(bf16[8,5,32,128]{3,2,1,0:T(8,128)(2,1)} %last_part.1), calls=%async_computation.3 | async-start | bytes 655360 | tf_op jit(solution)/shard_map/all_to_all | solution.py:401
  161.9 1.0 collective-permute-start.27
  162.8 2.4 %collective-permute-start.26 = (bf16[5,32,128]{2,1,0:T(8,128)(2,1)S(1)}, bf16[5,32,128]{2,1,0:T(8,128)(2,1)S(1)}, u32[]{:S(2)}, u32[]{:S(2)}) collective-permute-start(bf16[5,32,128]{2,1,0:T(8,128)(2,1)S(1)} %get-tuple-element.15), channel_id=1, source_target_pairs={{0,4},{2,6},{4,8},{6,10},{8,12},{10,14},{12,0},{14,2},{1,5},{3,7},... | collective-permute-start | bytes 122888 | tf_op jit(solution)/shard_map/ppermute | solution.py:398
  165.2 1.0 collective-permute-start.25
  166.2 3.3 %collective-permute-start.24 = (bf16[5,32,128]{2,1,0:T(8,128)(2,1)S(1)}, bf16[5,32,128]{2,1,0:T(8,128)(2,1)S(1)}, u32[]{:S(2)}, u32[]{:S(2)}) collective-permute-start(bf16[5,32,128]{2,1,0:T(8,128)(2,1)S(1)} %get-tuple-element.17), channel_id=1, source_target_pairs={{0,8},{2,10},{4,12},{6,14},{8,0},{10,2},{12,4},{14,6},{1,9},{3,11}... | collective-permute-start | bytes 122888 | tf_op jit(solution)/shard_map/ppermute | solution.py:398
  169.5 1.4 collective-permute-start.23
  170.9 3.2 %collective-permute-start.22 = (bf16[5,32,128]{2,1,0:T(8,128)(2,1)S(1)}, bf16[5,32,128]{2,1,0:T(8,128)(2,1)S(1)}, u32[]{:S(2)}, u32[]{:S(2)}) collective-permute-start(bf16[5,32,128]{2,1,0:T(8,128)(2,1)S(1)} %get-tuple-element.19), channel_id=1, source_target_pairs={{0,12},{2,14},{4,0},{6,2},{8,4},{10,6},{12,8},{14,10},{1,13},{3,15... | collective-permute-start | bytes 122888 | tf_op jit(solution)/shard_map/ppermute | solution.py:398
  174.2 1.3 collective-permute-start.21
  175.5 3.3 %collective-permute-done.22.refs_2_ = bf16[5,32,128]{2,1,0:T(8,128)(2,1)S(1)} collective-permute-done((bf16[5,32,128]{2,1,0:T(8,128)(2,1)S(1)}, bf16[5,32,128]{2,1,0:T(8,128)(2,1)S(1)}, u32[]{:S(2)}, u32[]{:S(2)}) %collective-permute-start.22) | collective-permute-done | bytes 40992 | tf_op jit(solution)/shard_map/ppermute | solution.py:398
  178.8 0.8 collective-permute-done.21.refs_1_
  179.6 1.3 place_part.1
  181.0 0.9 reshape.43
  (80 shorter events, 1.8 us)
Async XLA Ops:
  7.2 27.2 %copy-start = (bf16[64,40,256]{2,1,0:T(8,128)(2,1)S(1)}, bf16[64,40,256]{2,1,0:T(8,128)(2,1)}, u32[]{:S(2)}) copy-start(bf16[64,40,256]{2,1,0:T(8,128)(2,1)} %param.15) | copy-start | bytes 3932164
  7.2 11.4 %copy-start.6 = (bf16[2,8,4096]{2,1,0:T(8,128)(2,1)S(1)}, bf16[2,8,4096]{2,1,0:T(8,128)(2,1)}, u32[]{:S(2)}) copy-start(bf16[2,8,4096]{2,1,0:T(8,128)(2,1)} %b0.1) | copy-start | bytes 393220
  7.2 11.4 %copy-start.11 = (s32[4]{0:T(128)S(1)}, s32[4]{0:T(128)}, u32[]{:S(2)}) copy-start(s32[4]{0:T(128)} %requests_ref.3) | copy-start | bytes 52
  7.2 9.7 %collective-permute-start.1 = (bf16[2,8,4096]{2,1,0:T(8,128)(2,1)}, bf16[2,8,4096]{2,1,0:T(8,128)(2,1)S(1)}, u32[]{:S(2)}, u32[]{:S(2)}) collective-permute-start(bf16[2,8,4096]{2,1,0:T(8,128)(2,1)} %b0.1), channel_id=1, source_target_pairs={{0,128},{64,192},{128,0},{192,64},{1,129},{65,193},{129,1},{193,65... | collective-permute-start | bytes 393224 | tf_op jit(solution)/shard_map/ppermute | solution.py:355
  11.0 7.6 %collective-permute-start = (bf16[2,8,4096]{2,1,0:T(8,128)(2,1)}, bf16[2,8,4096]{2,1,0:T(8,128)(2,1)S(1)}, u32[]{:S(2)}, u32[]{:S(2)}) collective-permute-start(bf16[2,8,4096]{2,1,0:T(8,128)(2,1)} %b0.1), channel_id=1, source_target_pairs={{0,64},{64,128},{128,192},{192,0},{1,65},{65,129},{129,193},{193,1... | collective-permute-start | bytes 393224 | tf_op jit(solution)/shard_map/ppermute | solution.py:355
  11.4 7.2 %collective-permute-start.2 = (bf16[2,8,4096]{2,1,0:T(8,128)(2,1)}, bf16[2,8,4096]{2,1,0:T(8,128)(2,1)S(1)}, u32[]{:S(2)}, u32[]{:S(2)}) collective-permute-start(bf16[2,8,4096]{2,1,0:T(8,128)(2,1)} %b0.1), channel_id=1, source_target_pairs={{0,192},{64,0},{128,64},{192,128},{1,193},{65,1},{129,65},{193,129... | collective-permute-start | bytes 393224 | tf_op jit(solution)/shard_map/ppermute | solution.py:355
  16.9 10.2 %copy-start.9 = (s32[4]{0:T(128)}, s32[4]{0:T(128)S(1)}, u32[]{:S(2)}) copy-start(s32[4]{0:T(128)S(1)} %pad_add_fusion.where_ref) | copy-start | bytes 52
  20.1 13.4 %all-to-all-start = ((bf16[8,224,128]{2,1,0:T(8,128)(2,1)}), bf16[8,224,128]{2,1,0:T(8,128)(2,1)S(1)}, u32[]{:S(2)}, u32[]{:S(2)}) async-start(bf16[8,224,128]{2,1,0:T(8,128)(2,1)} %pad_maximum_fusion.1), calls=%async_computation | async-start | bytes 917504 | tf_op jit(solution)/shard_map/all_to_all | solution.py:361
  24.7 2.4 %copy-start.8 = (f32[40,128]{1,0:T(8,128)S(1)}, f32[40,128]{1,0:T(8,128)}, u32[]{:S(2)}) copy-start(f32[40,128]{1,0:T(8,128)} %param.17) | copy-start | bytes 61444
  24.7 68.9 %all-gather.3.cloned.1.call-start = ((), (), s32[]{:S(2)}) async-start(), calls=%async_computation.6 | async-start | bytes 4128768 | tf_op jit(solution)/shard_map/all_gather | solution.py:369
  28.6 1.5 copy-start.1
  33.5 0.8 copy-start.13
  36.1 18.0 %collective-permute-start.3 = (bf16[5,16,256]{2,1,0:T(8,128)(2,1)S(1)}, bf16[5,16,256]{2,1,0:T(8,128)(2,1)S(1)}, u32[]{:S(2)}, u32[]{:S(2)}) collective-permute-start(bf16[5,16,256]{2,1,0:T(8,128)(2,1)S(1)} %get-tuple-element.30), channel_id=1, source_target_pairs={{0,2},{2,4},{4,6},{6,8},{8,10},{10,12},{12,14},{14,0},{1,3},{3,5},... | collective-permute-start | bytes 122888 | tf_op jit(solution)/shard_map/ppermute | solution.py:375
  37.8 56.4 %all-to-all-start.1 = ((bf16[8,5,128,256]{3,2,1,0:T(8,128)(2,1)}), bf16[8,5,128,256]{3,2,1,0:T(8,128)(2,1)}, u32[]{:S(2)}, u32[]{:S(2)}) async-start(bf16[8,5,128,256]{3,2,1,0:T(8,128)(2,1)} %bitcast.79), calls=%async_computation.1 | async-start | bytes 5242880 | tf_op jit(solution)/shard_map/all_to_all | solution.py:368
  43.3 108.9 %reduce-scatter.2.cloned.1.call-start = ((), (), s32[]{:S(2)}) async-start(), calls=%async_computation.5 | async-start | bytes 3133440 | tf_op jit(solution)/shard_map/reduce_scatter | solution.py:388
  43.3 26.4 %collective-permute-start.9 = (bf16[5,16,256]{2,1,0:T(8,128)(2,1)S(1)}, bf16[5,16,256]{2,1,0:T(8,128)(2,1)S(1)}, u32[]{:S(2)}, u32[]{:S(2)}) collective-permute-start(bf16[5,16,256]{2,1,0:T(8,128)(2,1)S(1)} %get-tuple-element.24), channel_id=1, source_target_pairs={{0,14},{2,0},{4,2},{6,4},{8,6},{10,8},{12,10},{14,12},{1,15},{3,1}... | collective-permute-start | bytes 122888 | tf_op jit(solution)/shard_map/ppermute | solution.py:375
  47.0 22.7 %collective-permute-start.8 = (bf16[5,16,256]{2,1,0:T(8,128)(2,1)S(1)}, bf16[5,16,256]{2,1,0:T(8,128)(2,1)S(1)}, u32[]{:S(2)}, u32[]{:S(2)}) collective-permute-start(bf16[5,16,256]{2,1,0:T(8,128)(2,1)S(1)} %get-tuple-element.25), channel_id=1, source_target_pairs={{0,12},{2,14},{4,0},{6,2},{8,4},{10,6},{12,8},{14,10},{1,13},{3,15... | collective-permute-start | bytes 122888 | tf_op jit(solution)/shard_map/ppermute | solution.py:375
  49.2 20.5 %collective-permute-start.7 = (bf16[5,16,256]{2,1,0:T(8,128)(2,1)S(1)}, bf16[5,16,256]{2,1,0:T(8,128)(2,1)S(1)}, u32[]{:S(2)}, u32[]{:S(2)}) collective-permute-start(bf16[5,16,256]{2,1,0:T(8,128)(2,1)S(1)} %get-tuple-element.26), channel_id=1, source_target_pairs={{0,10},{2,12},{4,14},{6,0},{8,2},{10,4},{12,6},{14,8},{1,11},{3,13... | collective-permute-start | bytes 122888 | tf_op jit(solution)/shard_map/ppermute | solution.py:375
  51.3 18.3 %collective-permute-start.6 = (bf16[5,16,256]{2,1,0:T(8,128)(2,1)S(1)}, bf16[5,16,256]{2,1,0:T(8,128)(2,1)S(1)}, u32[]{:S(2)}, u32[]{:S(2)}) collective-permute-start(bf16[5,16,256]{2,1,0:T(8,128)(2,1)S(1)} %get-tuple-element.27), channel_id=1, source_target_pairs={{0,8},{2,10},{4,12},{6,14},{8,0},{10,2},{12,4},{14,6},{1,9},{3,11}... | collective-permute-start | bytes 122888 | tf_op jit(solution)/shard_map/ppermute | solution.py:375
  54.1 7.8 %collective-permute-start.4 = (bf16[5,16,256]{2,1,0:T(8,128)(2,1)S(1)}, bf16[5,16,256]{2,1,0:T(8,128)(2,1)S(1)}, u32[]{:S(2)}, u32[]{:S(2)}) collective-permute-start(bf16[5,16,256]{2,1,0:T(8,128)(2,1)S(1)} %get-tuple-element.29), channel_id=1, source_target_pairs={{0,4},{2,6},{4,8},{6,10},{8,12},{10,14},{12,0},{14,2},{1,5},{3,7},... | collective-permute-start | bytes 122888 | tf_op jit(solution)/shard_map/ppermute | solution.py:375
  61.9 7.8 %collective-permute-start.5 = (bf16[5,16,256]{2,1,0:T(8,128)(2,1)S(1)}, bf16[5,16,256]{2,1,0:T(8,128)(2,1)S(1)}, u32[]{:S(2)}, u32[]{:S(2)}) collective-permute-start(bf16[5,16,256]{2,1,0:T(8,128)(2,1)S(1)} %get-tuple-element.28), channel_id=1, source_target_pairs={{0,6},{2,8},{4,10},{6,12},{8,14},{10,0},{12,2},{14,4},{1,7},{3,9},... | collective-permute-start | bytes 122888 | tf_op jit(solution)/shard_map/ppermute | solution.py:375
  69.8 3.1 %collective-permute-start.10 = (bf16[8,5,16,128]{3,2,1,0:T(8,128)(2,1)S(1)}, bf16[8,5,16,128]{3,2,1,0:T(8,128)(2,1)S(1)}, u32[]{:S(2)}, u32[]{:S(2)}) collective-permute-start(bf16[8,5,16,128]{3,2,1,0:T(8,128)(2,1)S(1)} %get-tuple-element.23), channel_id=1, source_target_pairs={{0,1},{1,0},{2,3},{3,2},{4,5},{5,4},{6,7},{7,6},{8,9},{9,8},{10,11... | collective-permute-start | bytes 491528 | tf_op jit(solution)/shard_map/ppermute | solution.py:379
  72.9 20.6 %copy-start.14 = (bf16[2,8,5,16,128]{4,3,2,1,0:T(8,128)(2,1)}, bf16[2,8,5,16,128]{4,3,2,1,0:T(8,128)(2,1)S(1)}, u32[]{:S(2)}) copy-start(bf16[2,8,5,16,128]{4,3,2,1,0:T(8,128)(2,1)S(1)} %pad_maximum_fusion.2.refs_1_.w0) | copy-start | bytes 983044
  72.9 16.4 %collective-permute-start.13 = (bf16[2,8,5,16,128]{4,3,2,1,0:T(8,128)(2,1)S(1)}, bf16[2,8,5,16,128]{4,3,2,1,0:T(8,128)(2,1)S(1)}, u32[]{:S(2)}, u32[]{:S(2)}) collective-permute-start(bf16[2,8,5,16,128]{4,3,2,1,0:T(8,128)(2,1)S(1)} %pad_maximum_fusion.2.refs_1_.w0), channel_id=1, source_target_pairs={{0,192},{64,0},{128,64},{192,128},{1,193},{65,1},{129,65},{193,129... | collective-permute-start | bytes 983048 | tf_op jit(solution)/shard_map/ppermute | solution.py:381
  75.7 13.6 %collective-permute-start.12 = (bf16[2,8,5,16,128]{4,3,2,1,0:T(8,128)(2,1)S(1)}, bf16[2,8,5,16,128]{4,3,2,1,0:T(8,128)(2,1)S(1)}, u32[]{:S(2)}, u32[]{:S(2)}) collective-permute-start(bf16[2,8,5,16,128]{4,3,2,1,0:T(8,128)(2,1)S(1)} %pad_maximum_fusion.2.refs_1_.w0), channel_id=1, source_target_pairs={{0,128},{64,192},{128,0},{192,64},{1,129},{65,193},{129,1},{193,65... | collective-permute-start | bytes 983048 | tf_op jit(solution)/shard_map/ppermute | solution.py:381
  75.8 17.7 %collective-permute-start.11 = (bf16[2,8,5,16,128]{4,3,2,1,0:T(8,128)(2,1)S(1)}, bf16[2,8,5,16,128]{4,3,2,1,0:T(8,128)(2,1)S(1)}, u32[]{:S(2)}, u32[]{:S(2)}) collective-permute-start(bf16[2,8,5,16,128]{4,3,2,1,0:T(8,128)(2,1)S(1)} %pad_maximum_fusion.2.refs_1_.w0), channel_id=1, source_target_pairs={{0,64},{64,128},{128,192},{192,0},{1,65},{65,129},{129,193},{193,1... | collective-permute-start | bytes 983048 | tf_op jit(solution)/shard_map/ppermute | solution.py:381
  89.3 4.2 %copy-start.15 = (bf16[2,8,5,16,128]{4,3,2,1,0:T(8,128)(2,1)}, bf16[2,8,5,16,128]{4,3,2,1,0:T(8,128)(2,1)S(1)}, u32[]{:S(2)}) copy-start(bf16[2,8,5,16,128]{4,3,2,1,0:T(8,128)(2,1)S(1)} %collective-permute-done.13.refs_4_.w3) | copy-start | bytes 983044
  89.3 4.2 %copy-start.16 = (bf16[2,8,5,16,128]{4,3,2,1,0:T(8,128)(2,1)}, bf16[2,8,5,16,128]{4,3,2,1,0:T(8,128)(2,1)S(1)}, u32[]{:S(2)}) copy-start(bf16[2,8,5,16,128]{4,3,2,1,0:T(8,128)(2,1)S(1)} %collective-permute-done.12.refs_3_.w2) | copy-start | bytes 983044
  93.5 0.7 copy-start.17
  110.9 15.4 %all-to-all-start.3 = ((bf16[8,5,32,128]{3,2,1,0:T(8,128)(2,1)}), bf16[8,5,32,128]{3,2,1,0:T(8,128)(2,1)S(1)}, u32[]{:S(2)}, u32[]{:S(2)}) async-start(bf16[8,5,32,128]{3,2,1,0:T(8,128)(2,1)} %after.9), calls=%async_computation.4 | async-start | bytes 655360 | tf_op jit(solution)/shard_map/all_to_all | solution.py:391
  114.4 16.2 %copy-start.7 = (f32[40,128]{1,0:T(8,128)S(1)}, f32[40,128]{1,0:T(8,128)}, u32[]{:S(2)}) copy-start(f32[40,128]{1,0:T(8,128)} %param.19) | copy-start | bytes 61444
  114.4 16.2 %copy-start.10 = (s32[4]{0:T(128)S(1)}, s32[4]{0:T(128)}, u32[]{:S(2)}) copy-start(s32[4]{0:T(128)} %copy-done.9) | copy-start | bytes 52
  119.4 28.7 %copy-start.12 = (s32[8]{0:T(128)S(1)}, s32[8]{0:T(128)}, u32[]{:S(2)}) copy-start(s32[8]{0:T(128)} %lengths_ref.1) | copy-start | bytes 100
  119.4 7.7 %collective-permute-start.14 = (bf16[5,128,128]{2,1,0:T(8,128)(2,1)}, bf16[5,128,128]{2,1,0:T(8,128)(2,1)S(1)}, u32[]{:S(2)}, u32[]{:S(2)}) collective-permute-start(bf16[5,128,128]{2,1,0:T(8,128)(2,1)} %get-tuple-element.7), channel_id=1, source_target_pairs={{0,16},{16,32},{32,48},{48,0},{1,17},{17,33},{33,49},{49,1},{2,18}... | collective-permute-start | bytes 491528 | tf_op jit(solution)/shard_map/ppermute | solution.py:384
  120.9 9.7 %collective-permute-start.15 = (bf16[5,128,128]{2,1,0:T(8,128)(2,1)}, bf16[5,128,128]{2,1,0:T(8,128)(2,1)S(1)}, u32[]{:S(2)}, u32[]{:S(2)}) collective-permute-start(bf16[5,128,128]{2,1,0:T(8,128)(2,1)} %get-tuple-element.8), channel_id=1, source_target_pairs={{0,32},{16,48},{32,0},{48,16},{1,33},{17,49},{33,1},{49,17},{2,34}... | collective-permute-start | bytes 491528 | tf_op jit(solution)/shard_map/ppermute | solution.py:384
  123.3 7.2 %collective-permute-start.16 = (bf16[5,128,128]{2,1,0:T(8,128)(2,1)}, bf16[5,128,128]{2,1,0:T(8,128)(2,1)S(1)}, u32[]{:S(2)}, u32[]{:S(2)}) collective-permute-start(bf16[5,128,128]{2,1,0:T(8,128)(2,1)} %get-tuple-element.9), channel_id=1, source_target_pairs={{0,48},{16,0},{32,16},{48,32},{1,49},{17,1},{33,17},{49,33},{2,50}... | collective-permute-start | bytes 491528 | tf_op jit(solution)/shard_map/ppermute | solution.py:384
  126.4 0.7 copy-start.2
  130.6 0.9 copy-start.4
  132.2 6.9 %collective-permute-start.19 = (bf16[5,128,128]{2,1,0:T(8,128)(2,1)S(1)}, bf16[5,128,128]{2,1,0:T(8,128)(2,1)S(1)}, u32[]{:S(2)}, u32[]{:S(2)}) collective-permute-start(bf16[5,128,128]{2,1,0:T(8,128)(2,1)S(1)} %text_sum.1), channel_id=1, source_target_pairs={{0,48},{16,0},{32,16},{48,32},{1,49},{17,1},{33,17},{49,33},{2,50}... | collective-permute-start | bytes 491528 | tf_op jit(solution)/shard_map/ppermute | solution.py:384
  134.6 5.8 %collective-permute-start.18 = (bf16[5,128,128]{2,1,0:T(8,128)(2,1)S(1)}, bf16[5,128,128]{2,1,0:T(8,128)(2,1)S(1)}, u32[]{:S(2)}, u32[]{:S(2)}) collective-permute-start(bf16[5,128,128]{2,1,0:T(8,128)(2,1)S(1)} %text_sum.1), channel_id=1, source_target_pairs={{0,32},{16,48},{32,0},{48,16},{1,33},{17,49},{33,1},{49,17},{2,34}... | collective-permute-start | bytes 491528 | tf_op jit(solution)/shard_map/ppermute | solution.py:384
  135.4 9.7 %collective-permute-start.17 = (bf16[5,128,128]{2,1,0:T(8,128)(2,1)S(1)}, bf16[5,128,128]{2,1,0:T(8,128)(2,1)S(1)}, u32[]{:S(2)}, u32[]{:S(2)}) collective-permute-start(bf16[5,128,128]{2,1,0:T(8,128)(2,1)S(1)} %text_sum.1), channel_id=1, source_target_pairs={{0,16},{16,32},{32,48},{48,0},{1,17},{17,33},{33,49},{49,1},{2,18}... | collective-permute-start | bytes 491528 | tf_op jit(solution)/shard_map/ppermute | solution.py:384
  145.2 2.9 %collective-permute-start.20 = (bf16[4,5,128,128]{3,2,1,0:T(8,128)(2,1)S(1)}, bf16[4,5,128,128]{3,2,1,0:T(8,128)(2,1)S(1)}, u32[]{:S(2)}, u32[]{:S(2)}) collective-permute-start(bf16[4,5,128,128]{3,2,1,0:T(8,128)(2,1)S(1)} %pad_maximum_fusion.mine_ref), channel_id=1, source_target_pairs={{0,1},{1,0},{2,3},{3,2},{4,5},{5,4},{6,7},{7,6},{8,9},{9,8},{10,11... | collective-permute-start | bytes 1966088 | tf_op jit(solution)/shard_map/ppermute | solution.py:396
  148.1 1.0 copy-start.3
  152.3 1.0 copy-start.5
  154.2 26.7 %all-to-all-start.2 = ((bf16[8,5,32,128]{3,2,1,0:T(8,128)(2,1)}), bf16[8,5,32,128]{3,2,1,0:T(8,128)(2,1)S(1)}, u32[]{:S(2)}, u32[]{:S(2)}) async-start(bf16[8,5,32,128]{3,2,1,0:T(8,128)(2,1)} %last_part.1), calls=%async_computation.3 | async-start | bytes 655360 | tf_op jit(solution)/shard_map/all_to_all | solution.py:401
  161.9 9.1 %collective-permute-start.27 = (bf16[5,32,128]{2,1,0:T(8,128)(2,1)S(1)}, bf16[5,32,128]{2,1,0:T(8,128)(2,1)S(1)}, u32[]{:S(2)}, u32[]{:S(2)}) collective-permute-start(bf16[5,32,128]{2,1,0:T(8,128)(2,1)S(1)} %get-tuple-element.14), channel_id=1, source_target_pairs={{0,2},{2,4},{4,6},{6,8},{8,10},{10,12},{12,14},{14,0},{1,3},{3,5},... | collective-permute-start | bytes 122888 | tf_op jit(solution)/shard_map/ppermute | solution.py:398
  162.8 11.3 %collective-permute-start.26 = (bf16[5,32,128]{2,1,0:T(8,128)(2,1)S(1)}, bf16[5,32,128]{2,1,0:T(8,128)(2,1)S(1)}, u32[]{:S(2)}, u32[]{:S(2)}) collective-permute-start(bf16[5,32,128]{2,1,0:T(8,128)(2,1)S(1)} %get-tuple-element.15), channel_id=1, source_target_pairs={{0,4},{2,6},{4,8},{6,10},{8,12},{10,14},{12,0},{14,2},{1,5},{3,7},... | collective-permute-start | bytes 122888 | tf_op jit(solution)/shard_map/ppermute | solution.py:398
  165.2 10.2 %collective-permute-start.25 = (bf16[5,32,128]{2,1,0:T(8,128)(2,1)S(1)}, bf16[5,32,128]{2,1,0:T(8,128)(2,1)S(1)}, u32[]{:S(2)}, u32[]{:S(2)}) collective-permute-start(bf16[5,32,128]{2,1,0:T(8,128)(2,1)S(1)} %get-tuple-element.16), channel_id=1, source_target_pairs={{0,6},{2,8},{4,10},{6,12},{8,14},{10,0},{12,2},{14,4},{1,7},{3,9},... | collective-permute-start | bytes 122888 | tf_op jit(solution)/shard_map/ppermute | solution.py:398
  166.2 9.2 %collective-permute-start.24 = (bf16[5,32,128]{2,1,0:T(8,128)(2,1)S(1)}, bf16[5,32,128]{2,1,0:T(8,128)(2,1)S(1)}, u32[]{:S(2)}, u32[]{:S(2)}) collective-permute-start(bf16[5,32,128]{2,1,0:T(8,128)(2,1)S(1)} %get-tuple-element.17), channel_id=1, source_target_pairs={{0,8},{2,10},{4,12},{6,14},{8,0},{10,2},{12,4},{14,6},{1,9},{3,11}... | collective-permute-start | bytes 122888 | tf_op jit(solution)/shard_map/ppermute | solution.py:398
  169.5 6.0 %collective-permute-start.23 = (bf16[5,32,128]{2,1,0:T(8,128)(2,1)S(1)}, bf16[5,32,128]{2,1,0:T(8,128)(2,1)S(1)}, u32[]{:S(2)}, u32[]{:S(2)}) collective-permute-start(bf16[5,32,128]{2,1,0:T(8,128)(2,1)S(1)} %get-tuple-element.18), channel_id=1, source_target_pairs={{0,10},{2,12},{4,14},{6,0},{8,2},{10,4},{12,6},{14,8},{1,11},{3,13... | collective-permute-start | bytes 122888 | tf_op jit(solution)/shard_map/ppermute | solution.py:398
  170.9 7.8 %collective-permute-start.22 = (bf16[5,32,128]{2,1,0:T(8,128)(2,1)S(1)}, bf16[5,32,128]{2,1,0:T(8,128)(2,1)S(1)}, u32[]{:S(2)}, u32[]{:S(2)}) collective-permute-start(bf16[5,32,128]{2,1,0:T(8,128)(2,1)S(1)} %get-tuple-element.19), channel_id=1, source_target_pairs={{0,12},{2,14},{4,0},{6,2},{8,4},{10,6},{12,8},{14,10},{1,13},{3,15... | collective-permute-start | bytes 122888 | tf_op jit(solution)/shard_map/ppermute | solution.py:398
  174.2 5.4 %collective-permute-start.21 = (bf16[5,32,128]{2,1,0:T(8,128)(2,1)S(1)}, bf16[5,32,128]{2,1,0:T(8,128)(2,1)S(1)}, u32[]{:S(2)}, u32[]{:S(2)}) collective-permute-start(bf16[5,32,128]{2,1,0:T(8,128)(2,1)S(1)} %get-tuple-element.20), channel_id=1, source_target_pairs={{0,14},{2,0},{4,2},{6,4},{8,6},{10,8},{12,10},{14,12},{1,15},{3,1}... | collective-permute-start | bytes 122888 | tf_op jit(solution)/shard_map/ppermute | solution.py:398
Sparse Core Ops, SparseCore 0:
  34.4 56.6 all-gather.2
  110.3 41.2 reduce-scatter.1

commit v4 on v3

--- a/solution.py
+++ b/solution.py
@@ -67,7 +67,7 @@
     slots = pairs.shape[1]
     pairs_count = slots * NZ * ROWS * 1024
     return pl.pallas_call(
-        functools.partial(self_kernel, rows=512, keys=512, scale=scale),
+        functools.partial(self_kernel, rows=1024, keys=1024, scale=scale),
         grid=(slots,),
         in_specs=[
             pl.BlockSpec((NZ, 8, 32, 128), lambda h: (0, 0, h, 0)),
@@ -101,7 +101,7 @@
     return pl.pallas_call(
         last_kernel,
         out_shape=jax.ShapeDtypeStruct((8, slots, 32, 128), BF16),
-        compiler_params=pltpu.CompilerParams(vmem_limit_bytes=VMEM),
+        compiler_params=pltpu.CompilerParams(vmem_limit_bytes=ALL_VMEM),
         name="last_part",
     )(total)
 
@@ -206,10 +206,12 @@
     )(where, *parts, gains.reshape(NZ, slots, 1, width))
 
 
-def text_kernel(where_ref, low_ref, high_ref, w0, w1, w2, w3, o0, o1, o2, o3, held, context, product):
+def text_kernel(where_ref, low_ref, high_ref, w0, w1, w2, w4, w3, o0, o1, o2, o3, held, context, product):
     branch, z, x, c = where_ref[0], where_ref[1], where_ref[2], where_ref[3]
-    for k, ref in enumerate((w0, w1, w2, w3)):
+    for k, ref in ((0, w0), (1, w1), (3, w3)):
         held[lax.rem(branch - k + 4, 4)] = ref[...]
+    for i, ref in enumerate((w2, w4)):
+        held[lax.rem(branch + 2, 4), i] = ref[...]
     for i, ref in enumerate((low_ref, high_ref)):
         rows = ref[...].astype(F32)
         for j in range(4):
@@ -242,7 +244,9 @@
             pl.BlockSpec((NZ, 8, 32, 128), lambda i, w: (0, 0, first, 0)),
             pl.BlockSpec((NZ, 8, 32, 128), lambda i, w: (0, 0, first + 1, 0)),
         ]
-        + [pl.BlockSpec(weights[0].shape, lambda i, w: (0, 0, 0, 0, 0))] * 4,
+        + [
+            pl.BlockSpec(value.shape, lambda i, w, n=value.ndim: (0,) * n) for value in weights
+        ],
         out_specs=[pl.BlockSpec((slots, 128, 128), lambda i, w: (0, 0, 0))] * NX,
         scratch_shapes=[
             pltpu.VMEM((4,) + weights[0].shape, BF16),
@@ -377,8 +381,13 @@
     halves = moved[..., :head_dim], moved[..., head_dim:]
     mine = jnp.where(c == 0, halves[0], halves[1])
     other = lax.ppermute(jnp.where(c == 0, halves[1], halves[0]), "c", ring(NC, 1))
-    moved = jnp.stack([mine, other])
-    weights = [moved] + [lax.ppermute(moved, "branch", ring(4, k)) for k in (1, 2, 3)]
+    both = jnp.stack([mine, other])
+    next_plane, last_plane = (lax.ppermute(both, "branch", ring(4, k)) for k in (1, -1))
+    far_planes = (
+        lax.ppermute(next_plane[0], "branch", ring(4, 1)),
+        lax.ppermute(last_plane[1], "branch", ring(4, -1)),
+    )
+    weights = (both, next_plane, *far_planes, last_plane)
 
     def to_others(pieces):
         return [pieces[0]] + [lax.ppermute(pieces[k], "x", ring(NX, k)) for k in (1, 2, 3)]
@@ -391,8 +400,8 @@
     cross_queries = lax.all_to_all(after(cross_queries, own), "z", 0, 0, tiled=True)
 
     parts = to_others(text_part(where, after(gathered, own), weights))
-    parts[0] = after(parts[0], cross_queries)
     text = jnp.stack(to_others([text_sum(where, parts, ck_gain)] * NX))
+    text = after(text, cross_queries)
     other = lax.ppermute(text, "c", ring(NC, 1))
     cross = cross_part(where, requests, prompt_lengths, cross_queries, text, other, scale)
     cross = [cross[0]] + [lax.ppermute(cross[k], "z", ring(NZ, -k)) for k in range(1, NZ)]

time: 190 us -> 188 us (0.989)
  waiting for transfers between devices: 59.7 us -> 55.1 us
  starting transfers between devices: 68.7 us -> 71.2 us
    ppermute x3 -> x4, waiting for transfers between devices: 17.1 us -> 12.1 us  [the longest x2 6.73 us: local(): lax.ppermute(both, 'branch', ring(4, k))]
    ppermute x3 -> x4, starting transfers between devices: 3.48 us -> 6.69 us  [the longest x1 3.77 us: local(): lax.ppermute(last_plane[1], 'branch', ring(4, -1))]
    all_to_all x1, starting transfers between devices: 7.62 us -> 5.15 us  [local(): mine = lax.all_to_all(mine, GROUP, 0, 0, tiled=True)]
    ppermute x6, waiting for transfers between devices: 13.2 us -> 15.3 us  [to_others(): lax.ppermute(pieces[k], 'x', ring(NX, k))]
    unnamed x43 -> x45, local copies, waits for them, and re-layouts: 8.98 us -> 9.06 us
  transfers between devices with their start and end apart: 34 -> 35, of which waited for: 15 -> 15; matrix products, arithmetic and copies ran while one was open for 4% -> 5% of each run, Pallas kernels for 6% -> 6%
where the time goes in v4:
time: 188 us; the launch traced here: 187 us
  starting transfers between devices  71.2 us (38%)
  waiting for transfers between devices  55.1 us (29%)
  Pallas kernels  28.8 us (15%)
  between operations  14.5 us (8%)
  local copies, waits for them, and re-layouts  12.7 us (7%)
  other arithmetic  4.89 us (3%)
    ppermute x7, waiting for transfers between devices, local(): moved.append(lax.ppermute(piece, 'z', ring(NZ, k)))  15.5 us
    ppermute x6, waiting for transfers between devices, to_others(): lax.ppermute(pieces[k], 'x', ring(NX, k))  15.3 us
    pallas_call x1, Pallas kernels, self_part(): pl.pallas_call(functools.partial(self_kernel, rows=1024, keys=1024, scale...  14.5 us
    ppermute x7, starting transfers between devices, local(): lax.ppermute(cross[k], 'z', ring(NZ, -k))  13.5 us
    ppermute x7, starting transfers between devices, local(): moved.append(lax.ppermute(piece, 'z', ring(NZ, k)))  12.5 us
    unnamed x45, local copies, waits for them, and re-layouts  9.06 us
    ppermute x6, starting transfers between devices, to_others(): lax.ppermute(pieces[k], 'x', ring(NX, k))  8.43 us
    ppermute x2, waiting for transfers between devices, local(): lax.ppermute(both, 'branch', ring(4, k))  6.73 us
  transfers between devices with their start and end apart: 35, of which 15 were waited for; matrix products, arithmetic and copies ran while one was open for 5% of the time, Pallas kernels for 6%

profile of v4, /device:TPU:1, one launch (start us, length us, event | category | flops | bytes accessed | tf_op | source)
XLA Modules:
  0.0 187.0 jit_solution(14498469821859917931)
XLA Ops:
  7.2 3.8 %collective-permute-start.1 = (bf16[2,8,4096]{2,1,0:T(8,128)(2,1)}, bf16[2,8,4096]{2,1,0:T(8,128)(2,1)S(1)}, u32[]{:S(2)}, u32[]{:S(2)}) collective-permute-start(bf16[2,8,4096]{2,1,0:T(8,128)(2,1)} %b0.1), channel_id=1, source_target_pairs={{0,128},{64,192},{128,0},{192,64},{1,129},{65,193},{129,1},{193,65... | collective-permute-start | bytes 393224 | tf_op jit(solution)/shard_map/ppermute | solution.py:359
  11.4 2.3 %collective-permute-start.2 = (bf16[2,8,4096]{2,1,0:T(8,128)(2,1)}, bf16[2,8,4096]{2,1,0:T(8,128)(2,1)S(1)}, u32[]{:S(2)}, u32[]{:S(2)}) collective-permute-start(bf16[2,8,4096]{2,1,0:T(8,128)(2,1)} %b0.1), channel_id=1, source_target_pairs={{0,192},{64,0},{128,64},{192,128},{1,193},{65,1},{129,65},{193,129... | collective-permute-start | bytes 393224 | tf_op jit(solution)/shard_map/ppermute | solution.py:359
  13.7 1.5 fusion.3
  15.2 1.5 fusion.6
  16.9 1.7 collective-permute-done.b1
  19.3 0.8 pad_maximum_fusion.1
  20.1 4.6 %all-to-all-start = ((bf16[8,224,128]{2,1,0:T(8,128)(2,1)}), bf16[8,224,128]{2,1,0:T(8,128)(2,1)S(1)}, u32[]{:S(2)}, u32[]{:S(2)}) async-start(bf16[8,224,128]{2,1,0:T(8,128)(2,1)} %pad_maximum_fusion.1), calls=%async_computation | async-start | bytes 917504 | tf_op jit(solution)/shard_map/all_to_all | solution.py:365
  24.7 2.4 %copy.29 = bf16[1,128,40,256]{3,1,2,0:T(8,128)(2,1)S(1)} copy(bf16[1,128,40,256]{3,2,1,0:T(8,128)(2,1)} %param.11) | data formatting | bytes 5242880 | tf_op args[1]
  27.1 1.6 norm_keys.1.refs_1_
  28.6 1.5 copy-done.1
  30.2 3.3 %all-to-all-done.refs_0_ = bf16[8,224,128]{2,1,0:T(8,128)(2,1)S(1)} async-done(((bf16[8,224,128]{2,1,0:T(8,128)(2,1)}), bf16[8,224,128]{2,1,0:T(8,128)(2,1)S(1)}, u32[]{:S(2)}, u32[]{:S(2)}) %all-to-all-start) | async-done | bytes 458784 | tf_op jit(solution)/shard_map/all_to_all | solution.py:365
  33.5 0.8 copy-done.13
  34.4 0.8 copy.25
  35.2 0.9 dynamic-slice_bitcast_fusion.1
  36.1 1.7 collective-permute-start.3
  37.8 5.4 %all-to-all-start.1 = ((bf16[8,5,128,256]{3,2,1,0:T(8,128)(2,1)}), bf16[8,5,128,256]{3,2,1,0:T(8,128)(2,1)}, u32[]{:S(2)}, u32[]{:S(2)}) async-start(bf16[8,5,128,256]{3,2,1,0:T(8,128)(2,1)} %bitcast.83), calls=%async_computation.1 | async-start | bytes 5242880 | tf_op jit(solution)/shard_map/all_to_all | solution.py:372
  43.3 3.7 %collective-permute-start.9 = (bf16[5,16,256]{2,1,0:T(8,128)(2,1)S(1)}, bf16[5,16,256]{2,1,0:T(8,128)(2,1)S(1)}, u32[]{:S(2)}, u32[]{:S(2)}) collective-permute-start(bf16[5,16,256]{2,1,0:T(8,128)(2,1)S(1)} %get-tuple-element.24), channel_id=1, source_target_pairs={{0,14},{2,0},{4,2},{6,4},{8,6},{10,8},{12,10},{14,12},{1,15},{3,1}... | collective-permute-start | bytes 122888 | tf_op jit(solution)/shard_map/ppermute | solution.py:379
  46.9 2.2 %collective-permute-start.8 = (bf16[5,16,256]{2,1,0:T(8,128)(2,1)S(1)}, bf16[5,16,256]{2,1,0:T(8,128)(2,1)S(1)}, u32[]{:S(2)}, u32[]{:S(2)}) collective-permute-start(bf16[5,16,256]{2,1,0:T(8,128)(2,1)S(1)} %get-tuple-element.25), channel_id=1, source_target_pairs={{0,12},{2,14},{4,0},{6,2},{8,4},{10,6},{12,8},{14,10},{1,13},{3,15... | collective-permute-start | bytes 122888 | tf_op jit(solution)/shard_map/ppermute | solution.py:379
  49.1 2.2 %collective-permute-start.7 = (bf16[5,16,256]{2,1,0:T(8,128)(2,1)S(1)}, bf16[5,16,256]{2,1,0:T(8,128)(2,1)S(1)}, u32[]{:S(2)}, u32[]{:S(2)}) collective-permute-start(bf16[5,16,256]{2,1,0:T(8,128)(2,1)S(1)} %get-tuple-element.26), channel_id=1, source_target_pairs={{0,10},{2,12},{4,14},{6,0},{8,2},{10,4},{12,6},{14,8},{1,11},{3,13... | collective-permute-start | bytes 122888 | tf_op jit(solution)/shard_map/ppermute | solution.py:379
  51.3 2.7 %collective-permute-start.6 = (bf16[5,16,256]{2,1,0:T(8,128)(2,1)S(1)}, bf16[5,16,256]{2,1,0:T(8,128)(2,1)S(1)}, u32[]{:S(2)}, u32[]{:S(2)}) collective-permute-start(bf16[5,16,256]{2,1,0:T(8,128)(2,1)S(1)} %get-tuple-element.27), channel_id=1, source_target_pairs={{0,8},{2,10},{4,12},{6,14},{8,0},{10,2},{12,4},{14,6},{1,9},{3,11}... | collective-permute-start | bytes 122888 | tf_op jit(solution)/shard_map/ppermute | solution.py:379
  54.1 7.8 %collective-permute-done.4 = bf16[5,16,256]{2,1,0:T(8,128)(2,1)S(1)} collective-permute-done((bf16[5,16,256]{2,1,0:T(8,128)(2,1)S(1)}, bf16[5,16,256]{2,1,0:T(8,128)(2,1)S(1)}, u32[]{:S(2)}, u32[]{:S(2)}) %collective-permute-start.4) | collective-permute-done | bytes 40992 | tf_op jit(solution)/shard_map/ppermute | solution.py:379
  61.8 7.7 %collective-permute-done.5 = bf16[5,16,256]{2,1,0:T(8,128)(2,1)S(1)} collective-permute-done((bf16[5,16,256]{2,1,0:T(8,128)(2,1)S(1)}, bf16[5,16,256]{2,1,0:T(8,128)(2,1)S(1)}, u32[]{:S(2)}, u32[]{:S(2)}) %collective-permute-start.5) | collective-permute-done | bytes 40992 | tf_op jit(solution)/shard_map/ppermute | solution.py:379
  69.7 2.1 %collective-permute-start.10 = (bf16[8,5,16,128]{3,2,1,0:T(8,128)(2,1)S(1)}, bf16[8,5,16,128]{3,2,1,0:T(8,128)(2,1)S(1)}, u32[]{:S(2)}, u32[]{:S(2)}) collective-permute-start(bf16[8,5,16,128]{3,2,1,0:T(8,128)(2,1)S(1)} %get-tuple-element.23), channel_id=1, source_target_pairs={{0,1},{1,0},{2,3},{3,2},{4,5},{5,4},{6,7},{7,6},{8,9},{9,8},{10,11... | collective-permute-start | bytes 491528 | tf_op jit(solution)/shard_map/ppermute | solution.py:383
  71.8 1.0 collective-permute-done.10
  72.9 2.8 %collective-permute-start.13 = (bf16[2,8,5,16,128]{4,3,2,1,0:T(8,128)(2,1)S(1)}, bf16[2,8,5,16,128]{4,3,2,1,0:T(8,128)(2,1)S(1)}, u32[]{:S(2)}, u32[]{:S(2)}) collective-permute-start(bf16[2,8,5,16,128]{4,3,2,1,0:T(8,128)(2,1)S(1)} %pad_maximum_fusion.2.refs_1_.w0), channel_id=1, source_target_pairs={{0,192},{64,0},{128,64},{192,128},{1,193},{65,1},{129,65},{193,129... | collective-permute-start | bytes 983048 | tf_op jit(solution)/shard_map/ppermute | solution.py:385
  75.7 6.7 %collective-permute-done.13.refs_5_.w3 = bf16[2,8,5,16,128]{4,3,2,1,0:T(8,128)(2,1)S(1)} collective-permute-done((bf16[2,8,5,16,128]{4,3,2,1,0:T(8,128)(2,1)S(1)}, bf16[2,8,5,16,128]{4,3,2,1,0:T(8,128)(2,1)S(1)}, u32[]{:S(2)}, u32[]{:S(2)}) %collective-permute-start.13) | collective-permute-done | bytes 327712 | tf_op jit(solution)/shard_map/ppermute | solution.py:385
  82.5 3.8 %collective-permute-start.14 = (bf16[8,5,16,128]{3,2,1,0:T(8,128)(2,1)S(1)}, bf16[8,5,16,128]{3,2,1,0:T(8,128)(2,1)S(1)}, u32[]{:S(2)}, u32[]{:S(2)}) collective-permute-start(bf16[8,5,16,128]{3,2,1,0:T(8,128)(2,1)S(1)} %slice_bitcast_fusion), channel_id=1, source_target_pairs={{0,192},{64,0},{128,64},{192,128},{1,193},{65,1},{129,65},{193,129... | collective-permute-start | bytes 491528 | tf_op jit(solution)/shard_map/ppermute | solution.py:388
  86.3 2.2 %collective-permute-done.14.refs_4_.w4 = bf16[8,5,16,128]{3,2,1,0:T(8,128)(2,1)S(1)} collective-permute-done((bf16[8,5,16,128]{3,2,1,0:T(8,128)(2,1)S(1)}, bf16[8,5,16,128]{3,2,1,0:T(8,128)(2,1)S(1)}, u32[]{:S(2)}, u32[]{:S(2)}) %collective-permute-start.14) | collective-permute-done | bytes 163872 | tf_op jit(solution)/shard_map/ppermute | solution.py:388
  88.5 3.2 %collective-permute-done.12.refs_3_.w2 = bf16[8,5,16,128]{3,2,1,0:T(8,128)(2,1)S(1)} collective-permute-done((bf16[8,5,16,128]{3,2,1,0:T(8,128)(2,1)S(1)}, bf16[8,5,16,128]{3,2,1,0:T(8,128)(2,1)S(1)}, u32[]{:S(2)}, u32[]{:S(2)}) %collective-permute-start.12) | collective-permute-done | bytes 163872 | tf_op jit(solution)/shard_map/ppermute | solution.py:387
  92.4 14.5 %self_part.1.refs_1_ = bf16[8,5,272,128]{3,2,1,0:T(8,128)(2,1)} custom-call(bf16[8,8,224,128]{3,2,1,0:T(8,128)(2,1)} %after.8.q_ref.refs_0_, bf16[8,5,128,256]{3,2,1,0:T(8,128)(2,1)} %all-to-all-done.1.kv_ref), custom_call_target="tpu_custom_call" | custom-call | flops 8053063680 | bytes 6291456 | tf_op jit(solution)/shard_map/self_part/pallas_call | solution.py:69
  106.9 0.8 copy.27
  107.7 5.0 %all-to-all-start.3 = ((bf16[8,5,32,128]{3,2,1,0:T(8,128)(2,1)}), bf16[8,5,32,128]{3,2,1,0:T(8,128)(2,1)S(1)}, u32[]{:S(2)}, u32[]{:S(2)}) async-start(bf16[8,5,32,128]{3,2,1,0:T(8,128)(2,1)} %after.9), calls=%async_computation.4 | async-start | bytes 655360 | tf_op jit(solution)/shard_map/all_to_all | solution.py:400
  112.7 4.9 %text_part.1 = (bf16[5,128,128]{2,1,0:T(8,128)(2,1)}, bf16[5,128,128]{2,1,0:T(8,128)(2,1)}, bf16[5,128,128]{2,1,0:T(8,128)(2,1)}, bf16[5,128,128]{2,1,0:T(8,128)(2,1)}) custom-call(s32[4]{0:T(128)} %copy-done.9, bf16[8,8,224,128]{3,2,1,0:T(8,128)(2,1)} %after.10.low_ref.high_ref, bf16[8,8,224,128]{3,2,1,0:T(8,128)(2,1)} %after.10.low_ref.high_ref, ...), custom_call_target="tpu_custom_call" | custom-call | tf_op jit(solution)/shard_map/text_part/pallas_call | solution.py:257
  117.6 1.4 collective-permute-start.15
  119.0 2.4 %collective-permute-start.16 = (bf16[5,128,128]{2,1,0:T(8,128)(2,1)}, bf16[5,128,128]{2,1,0:T(8,128)(2,1)S(1)}, u32[]{:S(2)}, u32[]{:S(2)}) collective-permute-start(bf16[5,128,128]{2,1,0:T(8,128)(2,1)} %get-tuple-element.8), channel_id=1, source_target_pairs={{0,32},{16,48},{32,0},{48,16},{1,33},{17,49},{33,1},{49,17},{2,34}... | collective-permute-start | bytes 491528 | tf_op jit(solution)/shard_map/ppermute | solution.py:393
  121.5 1.2 collective-permute-start.17
  122.6 1.0 collective-permute-done.15.p1
  123.7 4.5 %collective-permute-done.16.p2 = bf16[5,128,128]{2,1,0:T(8,128)(2,1)S(1)} collective-permute-done((bf16[5,128,128]{2,1,0:T(8,128)(2,1)}, bf16[5,128,128]{2,1,0:T(8,128)(2,1)S(1)}, u32[]{:S(2)}, u32[]{:S(2)}) %collective-permute-start.16) | collective-permute-done | bytes 163872 | tf_op jit(solution)/shard_map/ppermute | solution.py:393
  128.3 0.9 copy-done.5
  129.2 0.7 text_sum.1
  129.9 2.7 %collective-permute-start.20 = (bf16[5,128,128]{2,1,0:T(8,128)(2,1)S(1)}, bf16[5,128,128]{2,1,0:T(8,128)(2,1)S(1)}, u32[]{:S(2)}, u32[]{:S(2)}) collective-permute-start(bf16[5,128,128]{2,1,0:T(8,128)(2,1)S(1)} %text_sum.1), channel_id=1, source_target_pairs={{0,48},{16,0},{32,16},{48,32},{1,49},{17,1},{33,17},{49,33},{2,50}... | collective-permute-start | bytes 491528 | tf_op jit(solution)/shard_map/ppermute | solution.py:393
  132.6 0.7 collective-permute-start.19
  133.3 5.8 %collective-permute-done.20 = bf16[5,128,128]{2,1,0:T(8,128)(2,1)S(1)} collective-permute-done((bf16[5,128,128]{2,1,0:T(8,128)(2,1)S(1)}, bf16[5,128,128]{2,1,0:T(8,128)(2,1)S(1)}, u32[]{:S(2)}, u32[]{:S(2)}) %collective-permute-start.20) | collective-permute-done | bytes 163872 | tf_op jit(solution)/shard_map/ppermute | solution.py:393
  139.2 3.9 %collective-permute-done.18 = bf16[5,128,128]{2,1,0:T(8,128)(2,1)S(1)} collective-permute-done((bf16[5,128,128]{2,1,0:T(8,128)(2,1)S(1)}, bf16[5,128,128]{2,1,0:T(8,128)(2,1)S(1)}, u32[]{:S(2)}, u32[]{:S(2)}) %collective-permute-start.18) | collective-permute-done | bytes 163872 | tf_op jit(solution)/shard_map/ppermute | solution.py:393
  143.0 0.9 pad_maximum_fusion.refs_0_
  144.0 0.7 copy-done.3
  144.7 1.2 collective-permute-start.21
  145.9 1.9 %collective-permute-done.21.other_ref = bf16[4,5,128,128]{3,2,1,0:T(8,128)(2,1)S(1)} collective-permute-done((bf16[4,5,128,128]{3,2,1,0:T(8,128)(2,1)}, bf16[4,5,128,128]{3,2,1,0:T(8,128)(2,1)S(1)}, u32[]{:S(2)}, u32[]{:S(2)}) %collective-permute-start.21) | collective-permute-done | bytes 655392 | tf_op jit(solution)/shard_map/ppermute | solution.py:405
  147.8 1.1 copy-done.2
  148.9 1.0 copy-done.4
  149.9 3.1 %cross_part.1 = bf16[8,5,32,128]{3,2,1,0:T(8,128)(2,1)S(1)} custom-call(s32[4]{0:T(128)S(1)} %copy-done.10, s32[4]{0:T(128)S(1)} %copy-done.11, s32[8]{0:T(128)S(1)} %copy-done.12, bf16[8,5,32,128]{3,2,1,0:T(8,128)(2,1)S(1)} %copy-done.4, bf16[4,5,128,128]{3,2,1,0:T(8,128)(2,1)S(1)} %copy-done.2, bf16[4,5,128,128]{3,2,1,0:T(8,128)(2,1)S(1)} %collective-permute-done.21.other_ref), custom_call_target="tpu_custom_call" | custom-call | tf_op jit(solution)/shard_map/cross_part/pallas_call | solution.py:296
  153.1 2.0 %last_part.1 = bf16[8,5,32,128]{3,2,1,0:T(8,128)(2,1)} custom-call(bf16[5,272,128]{2,1,0:T(8,128)(2,1)} %bitcast.95), custom_call_target="tpu_custom_call" | custom-call | tf_op jit(solution)/shard_map/last_part/pallas_call | solution.py:101
  155.0 5.2 %all-to-all-start.2 = ((bf16[8,5,32,128]{3,2,1,0:T(8,128)(2,1)}), bf16[8,5,32,128]{3,2,1,0:T(8,128)(2,1)S(1)}, u32[]{:S(2)}, u32[]{:S(2)}) async-start(bf16[8,5,32,128]{3,2,1,0:T(8,128)(2,1)} %last_part.1), calls=%async_computation.3 | async-start | bytes 655360 | tf_op jit(solution)/shard_map/all_to_all | solution.py:410
  160.2 0.7 collective-permute-start.28
  161.0 2.4 %collective-permute-start.27 = (bf16[5,32,128]{2,1,0:T(8,128)(2,1)S(1)}, bf16[5,32,128]{2,1,0:T(8,128)(2,1)S(1)}, u32[]{:S(2)}, u32[]{:S(2)}) collective-permute-start(bf16[5,32,128]{2,1,0:T(8,128)(2,1)S(1)} %get-tuple-element.15), channel_id=1, source_target_pairs={{0,4},{2,6},{4,8},{6,10},{8,12},{10,14},{12,0},{14,2},{1,5},{3,7},... | collective-permute-start | bytes 122888 | tf_op jit(solution)/shard_map/ppermute | solution.py:407
  163.4 1.3 collective-permute-start.26
  164.7 3.1 %collective-permute-start.25 = (bf16[5,32,128]{2,1,0:T(8,128)(2,1)S(1)}, bf16[5,32,128]{2,1,0:T(8,128)(2,1)S(1)}, u32[]{:S(2)}, u32[]{:S(2)}) collective-permute-start(bf16[5,32,128]{2,1,0:T(8,128)(2,1)S(1)} %get-tuple-element.17), channel_id=1, source_target_pairs={{0,8},{2,10},{4,12},{6,14},{8,0},{10,2},{12,4},{14,6},{1,9},{3,11}... | collective-permute-start | bytes 122888 | tf_op jit(solution)/shard_map/ppermute | solution.py:407
  167.8 1.3 collective-permute-start.24
  169.1 3.5 %collective-permute-start.23 = (bf16[5,32,128]{2,1,0:T(8,128)(2,1)S(1)}, bf16[5,32,128]{2,1,0:T(8,128)(2,1)S(1)}, u32[]{:S(2)}, u32[]{:S(2)}) collective-permute-start(bf16[5,32,128]{2,1,0:T(8,128)(2,1)S(1)} %get-tuple-element.19), channel_id=1, source_target_pairs={{0,12},{2,14},{4,0},{6,2},{8,4},{10,6},{12,8},{14,10},{1,13},{3,15... | collective-permute-start | bytes 122888 | tf_op jit(solution)/shard_map/ppermute | solution.py:407
  172.6 1.2 collective-permute-start.22
  173.8 3.3 %collective-permute-done.23.refs_2_ = bf16[5,32,128]{2,1,0:T(8,128)(2,1)S(1)} collective-permute-done((bf16[5,32,128]{2,1,0:T(8,128)(2,1)S(1)}, bf16[5,32,128]{2,1,0:T(8,128)(2,1)S(1)}, u32[]{:S(2)}, u32[]{:S(2)}) %collective-permute-start.23) | collective-permute-done | bytes 40992 | tf_op jit(solution)/shard_map/ppermute | solution.py:407
  177.1 0.8 collective-permute-done.22.refs_1_
  177.9 1.3 place_part.1
  179.3 0.9 reshape.43
  (86 shorter events, 2.4 us)
Async XLA Ops:
  7.2 27.2 %copy-start = (bf16[64,40,256]{2,1,0:T(8,128)(2,1)S(1)}, bf16[64,40,256]{2,1,0:T(8,128)(2,1)}, u32[]{:S(2)}) copy-start(bf16[64,40,256]{2,1,0:T(8,128)(2,1)} %param.15) | copy-start | bytes 3932164
  7.2 11.4 %copy-start.6 = (bf16[2,8,4096]{2,1,0:T(8,128)(2,1)S(1)}, bf16[2,8,4096]{2,1,0:T(8,128)(2,1)}, u32[]{:S(2)}) copy-start(bf16[2,8,4096]{2,1,0:T(8,128)(2,1)} %b0.1) | copy-start | bytes 393220
  7.2 11.4 %copy-start.11 = (s32[4]{0:T(128)S(1)}, s32[4]{0:T(128)}, u32[]{:S(2)}) copy-start(s32[4]{0:T(128)} %requests_ref.3) | copy-start | bytes 52
  7.2 9.7 %collective-permute-start.1 = (bf16[2,8,4096]{2,1,0:T(8,128)(2,1)}, bf16[2,8,4096]{2,1,0:T(8,128)(2,1)S(1)}, u32[]{:S(2)}, u32[]{:S(2)}) collective-permute-start(bf16[2,8,4096]{2,1,0:T(8,128)(2,1)} %b0.1), channel_id=1, source_target_pairs={{0,128},{64,192},{128,0},{192,64},{1,129},{65,193},{129,1},{193,65... | collective-permute-start | bytes 393224 | tf_op jit(solution)/shard_map/ppermute | solution.py:359
  11.0 7.6 %collective-permute-start = (bf16[2,8,4096]{2,1,0:T(8,128)(2,1)}, bf16[2,8,4096]{2,1,0:T(8,128)(2,1)S(1)}, u32[]{:S(2)}, u32[]{:S(2)}) collective-permute-start(bf16[2,8,4096]{2,1,0:T(8,128)(2,1)} %b0.1), channel_id=1, source_target_pairs={{0,64},{64,128},{128,192},{192,0},{1,65},{65,129},{129,193},{193,1... | collective-permute-start | bytes 393224 | tf_op jit(solution)/shard_map/ppermute | solution.py:359
  11.4 7.2 %collective-permute-start.2 = (bf16[2,8,4096]{2,1,0:T(8,128)(2,1)}, bf16[2,8,4096]{2,1,0:T(8,128)(2,1)S(1)}, u32[]{:S(2)}, u32[]{:S(2)}) collective-permute-start(bf16[2,8,4096]{2,1,0:T(8,128)(2,1)} %b0.1), channel_id=1, source_target_pairs={{0,192},{64,0},{128,64},{192,128},{1,193},{65,1},{129,65},{193,129... | collective-permute-start | bytes 393224 | tf_op jit(solution)/shard_map/ppermute | solution.py:359
  16.9 10.2 %copy-start.9 = (s32[4]{0:T(128)}, s32[4]{0:T(128)S(1)}, u32[]{:S(2)}) copy-start(s32[4]{0:T(128)S(1)} %pad_add_fusion.where_ref) | copy-start | bytes 52
  20.1 13.4 %all-to-all-start = ((bf16[8,224,128]{2,1,0:T(8,128)(2,1)}), bf16[8,224,128]{2,1,0:T(8,128)(2,1)S(1)}, u32[]{:S(2)}, u32[]{:S(2)}) async-start(bf16[8,224,128]{2,1,0:T(8,128)(2,1)} %pad_maximum_fusion.1), calls=%async_computation | async-start | bytes 917504 | tf_op jit(solution)/shard_map/all_to_all | solution.py:365
  24.7 2.4 %copy-start.8 = (f32[40,128]{1,0:T(8,128)S(1)}, f32[40,128]{1,0:T(8,128)}, u32[]{:S(2)}) copy-start(f32[40,128]{1,0:T(8,128)} %param.17) | copy-start | bytes 61444
  24.7 67.0 %all-gather.3.cloned.1.call-start = ((), (), s32[]{:S(2)}) async-start(), calls=%async_computation.6 | async-start | bytes 4128768 | tf_op jit(solution)/shard_map/all_gather | solution.py:373
  28.6 1.5 copy-start.1
  33.5 0.8 copy-start.13
  36.1 17.9 %collective-permute-start.3 = (bf16[5,16,256]{2,1,0:T(8,128)(2,1)S(1)}, bf16[5,16,256]{2,1,0:T(8,128)(2,1)S(1)}, u32[]{:S(2)}, u32[]{:S(2)}) collective-permute-start(bf16[5,16,256]{2,1,0:T(8,128)(2,1)S(1)} %get-tuple-element.30), channel_id=1, source_target_pairs={{0,2},{2,4},{4,6},{6,8},{8,10},{10,12},{12,14},{14,0},{1,3},{3,5},... | collective-permute-start | bytes 122888 | tf_op jit(solution)/shard_map/ppermute | solution.py:379
  37.8 54.5 %all-to-all-start.1 = ((bf16[8,5,128,256]{3,2,1,0:T(8,128)(2,1)}), bf16[8,5,128,256]{3,2,1,0:T(8,128)(2,1)}, u32[]{:S(2)}, u32[]{:S(2)}) async-start(bf16[8,5,128,256]{3,2,1,0:T(8,128)(2,1)} %bitcast.83), calls=%async_computation.1 | async-start | bytes 5242880 | tf_op jit(solution)/shard_map/all_to_all | solution.py:372
  43.3 109.8 %reduce-scatter.2.cloned.1.call-start = ((), (), s32[]{:S(2)}) async-start(), calls=%async_computation.5 | async-start | bytes 3133440 | tf_op jit(solution)/shard_map/reduce_scatter | solution.py:397
  43.3 26.4 %collective-permute-start.9 = (bf16[5,16,256]{2,1,0:T(8,128)(2,1)S(1)}, bf16[5,16,256]{2,1,0:T(8,128)(2,1)S(1)}, u32[]{:S(2)}, u32[]{:S(2)}) collective-permute-start(bf16[5,16,256]{2,1,0:T(8,128)(2,1)S(1)} %get-tuple-element.24), channel_id=1, source_target_pairs={{0,14},{2,0},{4,2},{6,4},{8,6},{10,8},{12,10},{14,12},{1,15},{3,1}... | collective-permute-start | bytes 122888 | tf_op jit(solution)/shard_map/ppermute | solution.py:379
  46.9 22.7 %collective-permute-start.8 = (bf16[5,16,256]{2,1,0:T(8,128)(2,1)S(1)}, bf16[5,16,256]{2,1,0:T(8,128)(2,1)S(1)}, u32[]{:S(2)}, u32[]{:S(2)}) collective-permute-start(bf16[5,16,256]{2,1,0:T(8,128)(2,1)S(1)} %get-tuple-element.25), channel_id=1, source_target_pairs={{0,12},{2,14},{4,0},{6,2},{8,4},{10,6},{12,8},{14,10},{1,13},{3,15... | collective-permute-start | bytes 122888 | tf_op jit(solution)/shard_map/ppermute | solution.py:379
  49.1 20.5 %collective-permute-start.7 = (bf16[5,16,256]{2,1,0:T(8,128)(2,1)S(1)}, bf16[5,16,256]{2,1,0:T(8,128)(2,1)S(1)}, u32[]{:S(2)}, u32[]{:S(2)}) collective-permute-start(bf16[5,16,256]{2,1,0:T(8,128)(2,1)S(1)} %get-tuple-element.26), channel_id=1, source_target_pairs={{0,10},{2,12},{4,14},{6,0},{8,2},{10,4},{12,6},{14,8},{1,11},{3,13... | collective-permute-start | bytes 122888 | tf_op jit(solution)/shard_map/ppermute | solution.py:379
  51.3 18.3 %collective-permute-start.6 = (bf16[5,16,256]{2,1,0:T(8,128)(2,1)S(1)}, bf16[5,16,256]{2,1,0:T(8,128)(2,1)S(1)}, u32[]{:S(2)}, u32[]{:S(2)}) collective-permute-start(bf16[5,16,256]{2,1,0:T(8,128)(2,1)S(1)} %get-tuple-element.27), channel_id=1, source_target_pairs={{0,8},{2,10},{4,12},{6,14},{8,0},{10,2},{12,4},{14,6},{1,9},{3,11}... | collective-permute-start | bytes 122888 | tf_op jit(solution)/shard_map/ppermute | solution.py:379
  54.0 7.8 %collective-permute-start.4 = (bf16[5,16,256]{2,1,0:T(8,128)(2,1)S(1)}, bf16[5,16,256]{2,1,0:T(8,128)(2,1)S(1)}, u32[]{:S(2)}, u32[]{:S(2)}) collective-permute-start(bf16[5,16,256]{2,1,0:T(8,128)(2,1)S(1)} %get-tuple-element.29), channel_id=1, source_target_pairs={{0,4},{2,6},{4,8},{6,10},{8,12},{10,14},{12,0},{14,2},{1,5},{3,7},... | collective-permute-start | bytes 122888 | tf_op jit(solution)/shard_map/ppermute | solution.py:379
  61.8 7.7 %collective-permute-start.5 = (bf16[5,16,256]{2,1,0:T(8,128)(2,1)S(1)}, bf16[5,16,256]{2,1,0:T(8,128)(2,1)S(1)}, u32[]{:S(2)}, u32[]{:S(2)}) collective-permute-start(bf16[5,16,256]{2,1,0:T(8,128)(2,1)S(1)} %get-tuple-element.28), channel_id=1, source_target_pairs={{0,6},{2,8},{4,10},{6,12},{8,14},{10,0},{12,2},{14,4},{1,7},{3,9},... | collective-permute-start | bytes 122888 | tf_op jit(solution)/shard_map/ppermute | solution.py:379
  69.7 3.1 %collective-permute-start.10 = (bf16[8,5,16,128]{3,2,1,0:T(8,128)(2,1)S(1)}, bf16[8,5,16,128]{3,2,1,0:T(8,128)(2,1)S(1)}, u32[]{:S(2)}, u32[]{:S(2)}) collective-permute-start(bf16[8,5,16,128]{3,2,1,0:T(8,128)(2,1)S(1)} %get-tuple-element.23), channel_id=1, source_target_pairs={{0,1},{1,0},{2,3},{3,2},{4,5},{5,4},{6,7},{7,6},{8,9},{9,8},{10,11... | collective-permute-start | bytes 491528 | tf_op jit(solution)/shard_map/ppermute | solution.py:383
  72.9 18.9 %copy-start.14 = (bf16[2,8,5,16,128]{4,3,2,1,0:T(8,128)(2,1)}, bf16[2,8,5,16,128]{4,3,2,1,0:T(8,128)(2,1)S(1)}, u32[]{:S(2)}) copy-start(bf16[2,8,5,16,128]{4,3,2,1,0:T(8,128)(2,1)S(1)} %pad_maximum_fusion.2.refs_1_.w0) | copy-start | bytes 983044
  72.9 9.6 %collective-permute-start.13 = (bf16[2,8,5,16,128]{4,3,2,1,0:T(8,128)(2,1)S(1)}, bf16[2,8,5,16,128]{4,3,2,1,0:T(8,128)(2,1)S(1)}, u32[]{:S(2)}, u32[]{:S(2)}) collective-permute-start(bf16[2,8,5,16,128]{4,3,2,1,0:T(8,128)(2,1)S(1)} %pad_maximum_fusion.2.refs_1_.w0), channel_id=1, source_target_pairs={{0,192},{64,0},{128,64},{192,128},{1,193},{65,1},{129,65},{193,129... | collective-permute-start | bytes 983048 | tf_op jit(solution)/shard_map/ppermute | solution.py:385
  75.7 10.5 %collective-permute-start.11 = (bf16[2,8,5,16,128]{4,3,2,1,0:T(8,128)(2,1)S(1)}, bf16[2,8,5,16,128]{4,3,2,1,0:T(8,128)(2,1)S(1)}, u32[]{:S(2)}, u32[]{:S(2)}) collective-permute-start(bf16[2,8,5,16,128]{4,3,2,1,0:T(8,128)(2,1)S(1)} %pad_maximum_fusion.2.refs_1_.w0), channel_id=1, source_target_pairs={{0,64},{64,128},{128,192},{192,0},{1,65},{65,129},{129,193},{193,1... | collective-permute-start | bytes 983048 | tf_op jit(solution)/shard_map/ppermute | solution.py:385
  82.4 9.3 %copy-start.15 = (bf16[2,8,5,16,128]{4,3,2,1,0:T(8,128)(2,1)}, bf16[2,8,5,16,128]{4,3,2,1,0:T(8,128)(2,1)S(1)}, u32[]{:S(2)}) copy-start(bf16[2,8,5,16,128]{4,3,2,1,0:T(8,128)(2,1)S(1)} %collective-permute-done.13.refs_5_.w3) | copy-start | bytes 983044
  82.5 6.0 %collective-permute-start.14 = (bf16[8,5,16,128]{3,2,1,0:T(8,128)(2,1)S(1)}, bf16[8,5,16,128]{3,2,1,0:T(8,128)(2,1)S(1)}, u32[]{:S(2)}, u32[]{:S(2)}) collective-permute-start(bf16[8,5,16,128]{3,2,1,0:T(8,128)(2,1)S(1)} %slice_bitcast_fusion), channel_id=1, source_target_pairs={{0,192},{64,0},{128,64},{192,128},{1,193},{65,1},{129,65},{193,129... | collective-permute-start | bytes 491528 | tf_op jit(solution)/shard_map/ppermute | solution.py:388
  86.2 5.5 %copy-start.16 = (bf16[2,8,5,16,128]{4,3,2,1,0:T(8,128)(2,1)}, bf16[2,8,5,16,128]{4,3,2,1,0:T(8,128)(2,1)S(1)}, u32[]{:S(2)}) copy-start(bf16[2,8,5,16,128]{4,3,2,1,0:T(8,128)(2,1)S(1)} %collective-permute-done.11.refs_2_.w1) | copy-start | bytes 983044
  86.2 5.5 %collective-permute-start.12 = (bf16[8,5,16,128]{3,2,1,0:T(8,128)(2,1)S(1)}, bf16[8,5,16,128]{3,2,1,0:T(8,128)(2,1)S(1)}, u32[]{:S(2)}, u32[]{:S(2)}) collective-permute-start(bf16[8,5,16,128]{3,2,1,0:T(8,128)(2,1)S(1)} %slice_bitcast_fusion.1), channel_id=1, source_target_pairs={{0,64},{64,128},{128,192},{192,0},{1,65},{65,129},{129,193},{193,1... | collective-permute-start | bytes 491528 | tf_op jit(solution)/shard_map/ppermute | solution.py:387
  88.5 3.2 %copy-start.17 = (bf16[8,5,16,128]{3,2,1,0:T(8,128)(2,1)}, bf16[8,5,16,128]{3,2,1,0:T(8,128)(2,1)S(1)}, u32[]{:S(2)}) copy-start(bf16[8,5,16,128]{3,2,1,0:T(8,128)(2,1)S(1)} %collective-permute-done.14.refs_4_.w4) | copy-start | bytes 491524
  91.7 0.7 copy-start.18
  107.7 36.3 %all-to-all-start.3 = ((bf16[8,5,32,128]{3,2,1,0:T(8,128)(2,1)}), bf16[8,5,32,128]{3,2,1,0:T(8,128)(2,1)S(1)}, u32[]{:S(2)}, u32[]{:S(2)}) async-start(bf16[8,5,32,128]{3,2,1,0:T(8,128)(2,1)} %after.9), calls=%async_computation.4 | async-start | bytes 655360 | tf_op jit(solution)/shard_map/all_to_all | solution.py:400
  112.7 15.6 %copy-start.7 = (f32[40,128]{1,0:T(8,128)S(1)}, f32[40,128]{1,0:T(8,128)}, u32[]{:S(2)}) copy-start(f32[40,128]{1,0:T(8,128)} %param.19) | copy-start | bytes 61444
  112.7 15.5 %copy-start.10 = (s32[4]{0:T(128)S(1)}, s32[4]{0:T(128)}, u32[]{:S(2)}) copy-start(s32[4]{0:T(128)} %copy-done.9) | copy-start | bytes 52
  117.6 30.2 %copy-start.12 = (s32[8]{0:T(128)S(1)}, s32[8]{0:T(128)}, u32[]{:S(2)}) copy-start(s32[8]{0:T(128)} %lengths_ref.1) | copy-start | bytes 100
  117.6 6.0 %collective-permute-start.15 = (bf16[5,128,128]{2,1,0:T(8,128)(2,1)}, bf16[5,128,128]{2,1,0:T(8,128)(2,1)S(1)}, u32[]{:S(2)}, u32[]{:S(2)}) collective-permute-start(bf16[5,128,128]{2,1,0:T(8,128)(2,1)} %get-tuple-element.7), channel_id=1, source_target_pairs={{0,16},{16,32},{32,48},{48,0},{1,17},{17,33},{33,49},{49,1},{2,18}... | collective-permute-start | bytes 491528 | tf_op jit(solution)/shard_map/ppermute | solution.py:393
  119.0 9.2 %collective-permute-start.16 = (bf16[5,128,128]{2,1,0:T(8,128)(2,1)}, bf16[5,128,128]{2,1,0:T(8,128)(2,1)S(1)}, u32[]{:S(2)}, u32[]{:S(2)}) collective-permute-start(bf16[5,128,128]{2,1,0:T(8,128)(2,1)} %get-tuple-element.8), channel_id=1, source_target_pairs={{0,32},{16,48},{32,0},{48,16},{1,33},{17,49},{33,1},{49,17},{2,34}... | collective-permute-start | bytes 491528 | tf_op jit(solution)/shard_map/ppermute | solution.py:393
  121.5 6.8 %collective-permute-start.17 = (bf16[5,128,128]{2,1,0:T(8,128)(2,1)}, bf16[5,128,128]{2,1,0:T(8,128)(2,1)S(1)}, u32[]{:S(2)}, u32[]{:S(2)}) collective-permute-start(bf16[5,128,128]{2,1,0:T(8,128)(2,1)} %get-tuple-element.9), channel_id=1, source_target_pairs={{0,48},{16,0},{32,16},{48,32},{1,49},{17,1},{33,17},{49,33},{2,50}... | collective-permute-start | bytes 491528 | tf_op jit(solution)/shard_map/ppermute | solution.py:393
  128.2 0.9 copy-start.5
  129.9 9.3 %collective-permute-start.20 = (bf16[5,128,128]{2,1,0:T(8,128)(2,1)S(1)}, bf16[5,128,128]{2,1,0:T(8,128)(2,1)S(1)}, u32[]{:S(2)}, u32[]{:S(2)}) collective-permute-start(bf16[5,128,128]{2,1,0:T(8,128)(2,1)S(1)} %text_sum.1), channel_id=1, source_target_pairs={{0,48},{16,0},{32,16},{48,32},{1,49},{17,1},{33,17},{49,33},{2,50}... | collective-permute-start | bytes 491528 | tf_op jit(solution)/shard_map/ppermute | solution.py:393
  132.6 6.5 %collective-permute-start.19 = (bf16[5,128,128]{2,1,0:T(8,128)(2,1)S(1)}, bf16[5,128,128]{2,1,0:T(8,128)(2,1)S(1)}, u32[]{:S(2)}, u32[]{:S(2)}) collective-permute-start(bf16[5,128,128]{2,1,0:T(8,128)(2,1)S(1)} %text_sum.1), channel_id=1, source_target_pairs={{0,32},{16,48},{32,0},{48,16},{1,33},{17,49},{33,1},{49,17},{2,34}... | collective-permute-start | bytes 491528 | tf_op jit(solution)/shard_map/ppermute | solution.py:393
  133.3 9.7 %collective-permute-start.18 = (bf16[5,128,128]{2,1,0:T(8,128)(2,1)S(1)}, bf16[5,128,128]{2,1,0:T(8,128)(2,1)S(1)}, u32[]{:S(2)}, u32[]{:S(2)}) collective-permute-start(bf16[5,128,128]{2,1,0:T(8,128)(2,1)S(1)} %text_sum.1), channel_id=1, source_target_pairs={{0,16},{16,32},{32,48},{48,0},{1,17},{17,33},{33,49},{49,1},{2,18}... | collective-permute-start | bytes 491528 | tf_op jit(solution)/shard_map/ppermute | solution.py:393
  144.0 0.7 copy-start.3
  144.7 3.1 %collective-permute-start.21 = (bf16[4,5,128,128]{3,2,1,0:T(8,128)(2,1)}, bf16[4,5,128,128]{3,2,1,0:T(8,128)(2,1)S(1)}, u32[]{:S(2)}, u32[]{:S(2)}) collective-permute-start(bf16[4,5,128,128]{3,2,1,0:T(8,128)(2,1)} %after.11.mine_ref), channel_id=1, source_target_pairs={{0,1},{1,0},{2,3},{3,2},{4,5},{5,4},{6,7},{7,6},{8,9},{9,8},{10,11... | collective-permute-start | bytes 1966088 | tf_op jit(solution)/shard_map/ppermute | solution.py:405
  147.8 1.1 copy-start.2
  148.9 1.0 copy-start.4
  155.0 24.2 %all-to-all-start.2 = ((bf16[8,5,32,128]{3,2,1,0:T(8,128)(2,1)}), bf16[8,5,32,128]{3,2,1,0:T(8,128)(2,1)S(1)}, u32[]{:S(2)}, u32[]{:S(2)}) async-start(bf16[8,5,32,128]{3,2,1,0:T(8,128)(2,1)} %last_part.1), calls=%async_computation.3 | async-start | bytes 655360 | tf_op jit(solution)/shard_map/all_to_all | solution.py:410
  160.2 8.9 %collective-permute-start.28 = (bf16[5,32,128]{2,1,0:T(8,128)(2,1)S(1)}, bf16[5,32,128]{2,1,0:T(8,128)(2,1)S(1)}, u32[]{:S(2)}, u32[]{:S(2)}) collective-permute-start(bf16[5,32,128]{2,1,0:T(8,128)(2,1)S(1)} %get-tuple-element.14), channel_id=1, source_target_pairs={{0,2},{2,4},{4,6},{6,8},{8,10},{10,12},{12,14},{14,0},{1,3},{3,5},... | collective-permute-start | bytes 122888 | tf_op jit(solution)/shard_map/ppermute | solution.py:407
  161.0 11.7 %collective-permute-start.27 = (bf16[5,32,128]{2,1,0:T(8,128)(2,1)S(1)}, bf16[5,32,128]{2,1,0:T(8,128)(2,1)S(1)}, u32[]{:S(2)}, u32[]{:S(2)}) collective-permute-start(bf16[5,32,128]{2,1,0:T(8,128)(2,1)S(1)} %get-tuple-element.15), channel_id=1, source_target_pairs={{0,4},{2,6},{4,8},{6,10},{8,12},{10,14},{12,0},{14,2},{1,5},{3,7},... | collective-permute-start | bytes 122888 | tf_op jit(solution)/shard_map/ppermute | solution.py:407
  163.4 10.4 %collective-permute-start.26 = (bf16[5,32,128]{2,1,0:T(8,128)(2,1)S(1)}, bf16[5,32,128]{2,1,0:T(8,128)(2,1)S(1)}, u32[]{:S(2)}, u32[]{:S(2)}) collective-permute-start(bf16[5,32,128]{2,1,0:T(8,128)(2,1)S(1)} %get-tuple-element.16), channel_id=1, source_target_pairs={{0,6},{2,8},{4,10},{6,12},{8,14},{10,0},{12,2},{14,4},{1,7},{3,9},... | collective-permute-start | bytes 122888 | tf_op jit(solution)/shard_map/ppermute | solution.py:407
  164.7 9.1 %collective-permute-start.25 = (bf16[5,32,128]{2,1,0:T(8,128)(2,1)S(1)}, bf16[5,32,128]{2,1,0:T(8,128)(2,1)S(1)}, u32[]{:S(2)}, u32[]{:S(2)}) collective-permute-start(bf16[5,32,128]{2,1,0:T(8,128)(2,1)S(1)} %get-tuple-element.17), channel_id=1, source_target_pairs={{0,8},{2,10},{4,12},{6,14},{8,0},{10,2},{12,4},{14,6},{1,9},{3,11}... | collective-permute-start | bytes 122888 | tf_op jit(solution)/shard_map/ppermute | solution.py:407
  167.8 6.0 %collective-permute-start.24 = (bf16[5,32,128]{2,1,0:T(8,128)(2,1)S(1)}, bf16[5,32,128]{2,1,0:T(8,128)(2,1)S(1)}, u32[]{:S(2)}, u32[]{:S(2)}) collective-permute-start(bf16[5,32,128]{2,1,0:T(8,128)(2,1)S(1)} %get-tuple-element.18), channel_id=1, source_target_pairs={{0,10},{2,12},{4,14},{6,0},{8,2},{10,4},{12,6},{14,8},{1,11},{3,13... | collective-permute-start | bytes 122888 | tf_op jit(solution)/shard_map/ppermute | solution.py:407
  169.1 7.9 %collective-permute-start.23 = (bf16[5,32,128]{2,1,0:T(8,128)(2,1)S(1)}, bf16[5,32,128]{2,1,0:T(8,128)(2,1)S(1)}, u32[]{:S(2)}, u32[]{:S(2)}) collective-permute-start(bf16[5,32,128]{2,1,0:T(8,128)(2,1)S(1)} %get-tuple-element.19), channel_id=1, source_target_pairs={{0,12},{2,14},{4,0},{6,2},{8,4},{10,6},{12,8},{14,10},{1,13},{3,15... | collective-permute-start | bytes 122888 | tf_op jit(solution)/shard_map/ppermute | solution.py:407
  172.6 5.3 %collective-permute-start.22 = (bf16[5,32,128]{2,1,0:T(8,128)(2,1)S(1)}, bf16[5,32,128]{2,1,0:T(8,128)(2,1)S(1)}, u32[]{:S(2)}, u32[]{:S(2)}) collective-permute-start(bf16[5,32,128]{2,1,0:T(8,128)(2,1)S(1)} %get-tuple-element.20), channel_id=1, source_target_pairs={{0,14},{2,0},{4,2},{6,4},{8,6},{10,8},{12,10},{14,12},{1,15},{3,1}... | collective-permute-start | bytes 122888 | tf_op jit(solution)/shard_map/ppermute | solution.py:407
Sparse Core Ops, SparseCore 0:
  34.4 56.6 all-gather.2
  107.0 42.8 reduce-scatter.1

commit v5 on v4

--- a/solution.py
+++ b/solution.py
@@ -155,14 +155,11 @@
             value = ref[p].astype(F32)
             here = jnp.logical_and(plane == k, prompt == p)
             rows = value if rows is None else jnp.where(here, value, rows)
-    count = rows.shape[0]
-    rows = rows.astype(BF16)
     for x in range(NX):
-        for block in range(8):
-            first = (x * 8 + block) * 128
-            for c in range(NC):
-                at = slice(block * count, (block + 1) * count)
-                out_ref[x * NC + c, at] = rows[:, first : first + 128]
+        blocks = [rows[:, (x * 8 + block) * 128 : (x * 8 + block + 1) * 128] for block in range(8)]
+        blocks = jnp.concatenate(blocks, axis=0).astype(BF16)
+        for c in range(NC):
+            out_ref[x * NC + c] = blocks
 
 
 def pick_part(where, requests, banks):
@@ -179,6 +176,26 @@
         compiler_params=pltpu.CompilerParams(vmem_limit_bytes=VMEM),
         name="pick_part",
     )(where, requests, *banks)
+
+
+def slice_kernel(where_ref, value_ref, *out_refs):
+    for k, ref in enumerate(out_refs):
+        ref[...] = value_ref[lax.rem(where_ref[1] + k, NZ)]
+
+
+def slice_part(where, value):
+    return pl.pallas_call(
+        slice_kernel,
+        grid_spec=pltpu.PrefetchScalarGridSpec(
+            num_scalar_prefetch=1,
+            grid=(1,),
+            in_specs=[pl.BlockSpec(value.shape, lambda i, w: (0, 0, 0, 0))],
+            out_specs=[pl.BlockSpec(value.shape[1:], lambda i, w: (0, 0, 0))] * NZ,
+        ),
+        out_shape=[jax.ShapeDtypeStruct(value.shape[1:], BF16)] * NZ,
+        compiler_params=pltpu.CompilerParams(vmem_limit_bytes=ALL_VMEM),
+        name="slice_part",
+    )(where, value)
 
 
 def text_sum_kernel(where_ref, p0, p1, p2, p3, gain_ref, out_ref):
@@ -302,30 +319,36 @@
     )(where, requests, lengths, queries, mine, other)
 
 
-def place_kernel(where_ref, *refs):
-    out_ref = refs[-1]
-    slots, _, width = refs[0].shape
-    for k, ref in enumerate(refs[:-1]):
+def place_kernel(where_ref, self_ref, *refs):
+    self_out, cross_out = refs[NZ:]
+    groups, slots, _, width = self_ref.shape
+    for g in range(groups):
+        for h in range(slots):
+            at = (g * slots + h) * width
+            self_out[0, :, at : at + width] = self_ref[g, h]
+    for k in range(NZ):
         first = lax.rem(where_ref[1] + k, NZ) * (slots * width)
         for h in range(slots):
             at = pl.multiple_of(first + h * width, 128)
-            out_ref[:, pl.ds(at, width)] = ref[h]
-
-
-def place_part(where, pieces):
-    slots, rows, width = pieces[0].shape
+            cross_out[0, :, pl.ds(at, width)] = refs[k][h]
+
+
+def place_part(where, mine, pieces):
+    groups, slots, rows, width = mine.shape
+    shape = (1, rows, groups * slots * width)
     return pl.pallas_call(
         place_kernel,
         grid_spec=pltpu.PrefetchScalarGridSpec(
             num_scalar_prefetch=1,
             grid=(1,),
-            in_specs=[pl.BlockSpec((slots, rows, width), lambda i, w: (0, 0, 0))] * NZ,
-            out_specs=pl.BlockSpec((rows, NZ * slots * width), lambda i, w: (0, 0)),
+            in_specs=[pl.BlockSpec(mine.shape, lambda i, w: (0, 0, 0, 0))]
+            + [pl.BlockSpec((slots, rows, width), lambda i, w: (0, 0, 0))] * NZ,
+            out_specs=[pl.BlockSpec(shape, lambda i, w: (0, 0, 0))] * 2,
         ),
-        out_shape=jax.ShapeDtypeStruct((rows, NZ * slots * width), BF16),
+        out_shape=[jax.ShapeDtypeStruct(shape, BF16)] * 2,
         compiler_params=pltpu.CompilerParams(vmem_limit_bytes=VMEM),
         name="place_part",
-    )(where, *pieces)
+    )(where, mine, *pieces)
 
 
 def local(
@@ -372,11 +395,11 @@
     pairs = lax.all_to_all(pairs, GROUP, 0, 0, tiled=True)
     gathered = lax.all_gather(got, "z", axis=0)
 
-    part = after(head_major(lax.dynamic_slice_in_dim(w_text, branch * 16, 16, 0)), got)
-    moved = [lax.dynamic_index_in_dim(part, z, 0, keepdims=False)]
-    for k in range(1, NZ):
-        piece = lax.dynamic_index_in_dim(part, (z + k) % NZ, 0, keepdims=False)
-        moved.append(lax.ppermute(piece, "z", ring(NZ, k)))
+    part = head_major(lax.dynamic_slice_in_dim(w_text, branch * 16, 16, 0))
+    moved = slice_part(where, part)
+    moved = [moved[0]] + [
+        lax.ppermute(after(moved[k], got), "z", ring(NZ, k)) for k in range(1, NZ)
+    ]
     moved = jnp.stack(moved)
     halves = moved[..., :head_dim], moved[..., head_dim:]
     mine = jnp.where(c == 0, halves[0], halves[1])
@@ -405,15 +428,10 @@
     other = lax.ppermute(text, "c", ring(NC, 1))
     cross = cross_part(where, requests, prompt_lengths, cross_queries, text, other, scale)
     cross = [cross[0]] + [lax.ppermute(cross[k], "z", ring(NZ, -k)) for k in range(1, NZ)]
-    cross = place_part(where, cross)
     mine = last_part(total)
     mine = lax.all_to_all(mine, GROUP, 0, 0, tiled=True)
 
-    def token_major(values):
-        values = values.reshape(heads, tokens, head_dim)
-        return jnp.transpose(values, (1, 0, 2)).reshape(1, tokens, heads * head_dim)
-
-    return token_major(mine), cross[None]
+    return tuple(place_part(where, mine, cross))
 
 
 def solution(mesh):

time: 188 us -> 186 us (0.989)
  waiting for transfers between devices: 55.1 us -> 50.5 us
  Pallas kernels: 28.8 us -> 31.4 us
  starting transfers between devices: 71.2 us -> 73.4 us
    ppermute x7, waiting for transfers between devices: 15.5 us -> 6.9 us  [local(): lax.ppermute(after(moved[k], got), 'z', ring(NZ, k))]
    ppermute x7, starting transfers between devices: 12.5 us -> 16.6 us  [local(): lax.ppermute(after(moved[k], got), 'z', ring(NZ, k))]
    all_gather x1, waiting for transfers between devices: 0.01 us -> 3.45 us  [local(): gathered = lax.all_gather(got, 'z', axis=0)]
    pallas_call x0 -> x1, Pallas kernels: none -> 2.37 us  [slice_part(): pl.pallas_call(slice_kernel, grid_spec=pltpu.PrefetchScalarGridSpec(num_s...]
    unnamed x45 -> x48, local copies, waits for them, and re-layouts: 9.06 us -> 9.2 us
  transfers between devices with their start and end apart: 35 -> 35, of which waited for: 15 -> 18; matrix products, arithmetic and copies ran while one was open for 5% -> 5% of each run, Pallas kernels for 6% -> 7%
where the time goes in v5:
time: 186 us; the launch traced here: 185 us
  starting transfers between devices  73.4 us (39%)
  waiting for transfers between devices  50.5 us (27%)
  Pallas kernels  31.4 us (17%)
  between operations  14.3 us (8%)
  local copies, waits for them, and re-layouts  10.9 us (6%)
  other arithmetic  4.89 us (3%)
    ppermute x7, starting transfers between devices, local(): lax.ppermute(after(moved[k], got), 'z', ring(NZ, k))  16.6 us
    ppermute x6, waiting for transfers between devices, to_others(): lax.ppermute(pieces[k], 'x', ring(NX, k))  16 us
    pallas_call x1, Pallas kernels, self_part(): pl.pallas_call(functools.partial(self_kernel, rows=1024, keys=1024, scale...  14.5 us
    ppermute x7, starting transfers between devices, local(): lax.ppermute(cross[k], 'z', ring(NZ, -k))  13.7 us
    unnamed x48, local copies, waits for them, and re-layouts  9.2 us
    ppermute x6, starting transfers between devices, to_others(): lax.ppermute(pieces[k], 'x', ring(NX, k))  8.59 us
    ppermute x7, waiting for transfers between devices, local(): lax.ppermute(after(moved[k], got), 'z', ring(NZ, k))  6.9 us
    ppermute x2, waiting for transfers between devices, local(): lax.ppermute(both, 'branch', ring(4, k))  6.73 us
  transfers between devices with their start and end apart: 35, of which 18 were waited for; matrix products, arithmetic and copies ran while one was open for 5% of the time, Pallas kernels for 7%

profile of v5, /device:TPU:1, one launch (start us, length us, event | category | flops | bytes accessed | tf_op | source)
XLA Modules:
  0.0 185.4 jit_solution(7829835376014138901)
XLA Ops:
  7.2 3.8 %collective-permute-start.1 = (bf16[2,8,4096]{2,1,0:T(8,128)(2,1)}, bf16[2,8,4096]{2,1,0:T(8,128)(2,1)S(1)}, u32[]{:S(2)}, u32[]{:S(2)}) collective-permute-start(bf16[2,8,4096]{2,1,0:T(8,128)(2,1)} %b0.1), channel_id=1, source_target_pairs={{0,128},{64,192},{128,0},{192,64},{1,129},{65,193},{129,1},{193,65... | collective-permute-start | bytes 393224 | tf_op jit(solution)/shard_map/ppermute | solution.py:382
  11.4 2.3 %collective-permute-start.2 = (bf16[2,8,4096]{2,1,0:T(8,128)(2,1)}, bf16[2,8,4096]{2,1,0:T(8,128)(2,1)S(1)}, u32[]{:S(2)}, u32[]{:S(2)}) collective-permute-start(bf16[2,8,4096]{2,1,0:T(8,128)(2,1)} %b0.1), channel_id=1, source_target_pairs={{0,192},{64,0},{128,64},{192,128},{1,193},{65,1},{129,65},{193,129... | collective-permute-start | bytes 393224 | tf_op jit(solution)/shard_map/ppermute | solution.py:382
  13.7 1.5 fusion.3
  15.2 1.5 fusion.6
  16.9 1.7 collective-permute-done.b1
  19.3 0.8 pad_maximum_fusion.1
  20.1 4.6 %all-to-all-start = ((bf16[8,224,128]{2,1,0:T(8,128)(2,1)}), bf16[8,224,128]{2,1,0:T(8,128)(2,1)S(1)}, u32[]{:S(2)}, u32[]{:S(2)}) async-start(bf16[8,224,128]{2,1,0:T(8,128)(2,1)} %pad_maximum_fusion.1), calls=%async_computation | async-start | bytes 917504 | tf_op jit(solution)/shard_map/all_to_all | solution.py:388
  24.7 2.4 %copy.33 = bf16[1,128,40,256]{3,1,2,0:T(8,128)(2,1)S(1)} copy(bf16[1,128,40,256]{3,2,1,0:T(8,128)(2,1)} %param.11) | data formatting | bytes 5242880 | tf_op args[1]
  27.1 1.6 norm_keys.1.refs_1_
  28.6 1.5 copy-done.1
  30.1 3.3 %all-to-all-done.refs_0_ = bf16[8,224,128]{2,1,0:T(8,128)(2,1)S(1)} async-done(((bf16[8,224,128]{2,1,0:T(8,128)(2,1)}), bf16[8,224,128]{2,1,0:T(8,128)(2,1)S(1)}, u32[]{:S(2)}, u32[]{:S(2)}) %all-to-all-start) | async-done | bytes 458784 | tf_op jit(solution)/shard_map/all_to_all | solution.py:388
  33.5 0.8 copy-done.13
  34.2 5.1 %all-to-all-start.1 = ((bf16[8,5,128,256]{3,2,1,0:T(8,128)(2,1)}), bf16[8,5,128,256]{3,2,1,0:T(8,128)(2,1)}, u32[]{:S(2)}, u32[]{:S(2)}) async-start(bf16[8,5,128,256]{3,2,1,0:T(8,128)(2,1)} %bitcast.67), calls=%async_computation.1 | async-start | bytes 5242880 | tf_op jit(solution)/shard_map/all_to_all | solution.py:395
  39.4 0.8 copy.30
  40.2 2.4 %slice_part.1 = (bf16[5,16,256]{2,1,0:T(8,128)(2,1)}, bf16[5,16,256]{2,1,0:T(8,128)(2,1)}, bf16[5,16,256]{2,1,0:T(8,128)(2,1)}, bf16[5,16,256]{2,1,0:T(8,128)(2,...) custom-call(s32[4]{0:T(128)} %copy-done.7, ...), custom_call_target="tpu_custom_call" | custom-call | tf_op jit(solution)/shard_map/slice_part/pallas_call | solution.py:187
  42.6 1.7 collective-permute-start.3
  44.3 0.8 bitcast_dynamic-update-slice_fusion.7
  45.1 3.1 %collective-permute-start.4 = (bf16[5,16,256]{2,1,0:T(8,128)(2,1)}, bf16[5,16,256]{2,1,0:T(8,128)(2,1)S(1)}, u32[]{:S(2)}, u32[]{:S(2)}) collective-permute-start(bf16[5,16,256]{2,1,0:T(8,128)(2,1)} %after.14), channel_id=1, source_target_pairs={{0,4},{2,6},{4,8},{6,10},{8,12},{10,14},{12,0},{14,2},{1,5},{3,7},... | collective-permute-start | bytes 122888 | tf_op jit(solution)/shard_map/ppermute | solution.py:401
  48.1 3.8 %collective-permute-start.5 = (bf16[5,16,256]{2,1,0:T(8,128)(2,1)}, bf16[5,16,256]{2,1,0:T(8,128)(2,1)S(1)}, u32[]{:S(2)}, u32[]{:S(2)}) collective-permute-start(bf16[5,16,256]{2,1,0:T(8,128)(2,1)} %after.15), channel_id=1, source_target_pairs={{0,6},{2,8},{4,10},{6,12},{8,14},{10,0},{12,2},{14,4},{1,7},{3,9},... | collective-permute-start | bytes 122888 | tf_op jit(solution)/shard_map/ppermute | solution.py:401
  52.4 4.5 %collective-permute-start.7 = (bf16[5,16,256]{2,1,0:T(8,128)(2,1)}, bf16[5,16,256]{2,1,0:T(8,128)(2,1)S(1)}, u32[]{:S(2)}, u32[]{:S(2)}) collective-permute-start(bf16[5,16,256]{2,1,0:T(8,128)(2,1)} %after.17), channel_id=1, source_target_pairs={{0,10},{2,12},{4,14},{6,0},{8,2},{10,4},{12,6},{14,8},{1,11},{3,13... | collective-permute-start | bytes 122888 | tf_op jit(solution)/shard_map/ppermute | solution.py:401
  56.8 2.4 %collective-permute-start.8 = (bf16[5,16,256]{2,1,0:T(8,128)(2,1)}, bf16[5,16,256]{2,1,0:T(8,128)(2,1)S(1)}, u32[]{:S(2)}, u32[]{:S(2)}) collective-permute-start(bf16[5,16,256]{2,1,0:T(8,128)(2,1)} %after.18), channel_id=1, source_target_pairs={{0,12},{2,14},{4,0},{6,2},{8,4},{10,6},{12,8},{14,10},{1,13},{3,15... | collective-permute-start | bytes 122888 | tf_op jit(solution)/shard_map/ppermute | solution.py:401
  59.2 0.8 collective-permute-start.9
  60.8 2.2 %collective-permute-done.7 = bf16[5,16,256]{2,1,0:T(8,128)(2,1)S(1)} collective-permute-done((bf16[5,16,256]{2,1,0:T(8,128)(2,1)}, bf16[5,16,256]{2,1,0:T(8,128)(2,1)S(1)}, u32[]{:S(2)}, u32[]{:S(2)}) %collective-permute-start.7) | collective-permute-done | bytes 40992 | tf_op jit(solution)/shard_map/ppermute | solution.py:401
  63.0 1.3 collective-permute-done.8
  64.3 2.7 %collective-permute-done.9 = bf16[5,16,256]{2,1,0:T(8,128)(2,1)S(1)} collective-permute-done((bf16[5,16,256]{2,1,0:T(8,128)(2,1)S(1)}, bf16[5,16,256]{2,1,0:T(8,128)(2,1)S(1)}, u32[]{:S(2)}, u32[]{:S(2)}) %collective-permute-start.9) | collective-permute-done | bytes 40992 | tf_op jit(solution)/shard_map/ppermute | solution.py:401
  67.0 0.9 collective-permute-start.10
  67.9 1.0 collective-permute-done.10
  69.0 2.9 %collective-permute-start.13 = (bf16[2,8,5,16,128]{4,3,2,1,0:T(8,128)(2,1)S(1)}, bf16[2,8,5,16,128]{4,3,2,1,0:T(8,128)(2,1)S(1)}, u32[]{:S(2)}, u32[]{:S(2)}) collective-permute-start(bf16[2,8,5,16,128]{4,3,2,1,0:T(8,128)(2,1)S(1)} %pad_maximum_fusion.2.refs_1_.w0), channel_id=1, source_target_pairs={{0,192},{64,0},{128,64},{192,128},{1,193},{65,1},{129,65},{193,129... | collective-permute-start | bytes 983048 | tf_op jit(solution)/shard_map/ppermute | solution.py:408
  71.8 6.7 %collective-permute-done.13.refs_5_.w3 = bf16[2,8,5,16,128]{4,3,2,1,0:T(8,128)(2,1)S(1)} collective-permute-done((bf16[2,8,5,16,128]{4,3,2,1,0:T(8,128)(2,1)S(1)}, bf16[2,8,5,16,128]{4,3,2,1,0:T(8,128)(2,1)S(1)}, u32[]{:S(2)}, u32[]{:S(2)}) %collective-permute-start.13) | collective-permute-done | bytes 327712 | tf_op jit(solution)/shard_map/ppermute | solution.py:408
  78.6 3.8 %collective-permute-start.14 = (bf16[8,5,16,128]{3,2,1,0:T(8,128)(2,1)S(1)}, bf16[8,5,16,128]{3,2,1,0:T(8,128)(2,1)S(1)}, u32[]{:S(2)}, u32[]{:S(2)}) collective-permute-start(bf16[8,5,16,128]{3,2,1,0:T(8,128)(2,1)S(1)} %slice_bitcast_fusion), channel_id=1, source_target_pairs={{0,192},{64,0},{128,64},{192,128},{1,193},{65,1},{129,65},{193,129... | collective-permute-start | bytes 491528 | tf_op jit(solution)/shard_map/ppermute | solution.py:411
  82.5 2.2 %collective-permute-done.14.refs_4_.w4 = bf16[8,5,16,128]{3,2,1,0:T(8,128)(2,1)S(1)} collective-permute-done((bf16[8,5,16,128]{3,2,1,0:T(8,128)(2,1)S(1)}, bf16[8,5,16,128]{3,2,1,0:T(8,128)(2,1)S(1)}, u32[]{:S(2)}, u32[]{:S(2)}) %collective-permute-start.14) | collective-permute-done | bytes 163872 | tf_op jit(solution)/shard_map/ppermute | solution.py:411
  84.6 3.6 %collective-permute-done.12.refs_3_.w2 = bf16[8,5,16,128]{3,2,1,0:T(8,128)(2,1)S(1)} collective-permute-done((bf16[8,5,16,128]{3,2,1,0:T(8,128)(2,1)S(1)}, bf16[8,5,16,128]{3,2,1,0:T(8,128)(2,1)S(1)}, u32[]{:S(2)}, u32[]{:S(2)}) %collective-permute-start.12) | collective-permute-done | bytes 163872 | tf_op jit(solution)/shard_map/ppermute | solution.py:410
  88.2 3.5 %all-gather.3.cloned.1.call-done = bf16[64,224,128]{2,1,0:T(8,128)(2,1)} async-done(((bf16[8,224,128]{2,1,0:T(8,128)(2,1)}), bf16[64,224,128]{2,1,0:T(8,128)(2,1)}) %all-gather.3.cloned.1.call-update) | async-done | bytes 3670032 | tf_op jit(solution)/shard_map/all_gather | solution.py:396
  91.7 14.5 %self_part.1.refs_1_ = bf16[8,5,272,128]{3,2,1,0:T(8,128)(2,1)} custom-call(bf16[8,8,224,128]{3,2,1,0:T(8,128)(2,1)} %after.20.q_ref.refs_0_, bf16[8,5,128,256]{3,2,1,0:T(8,128)(2,1)} %all-to-all-done.1.kv_ref), custom_call_target="tpu_custom_call" | custom-call | flops 8053063680 | bytes 6291456 | tf_op jit(solution)/shard_map/self_part/pallas_call | solution.py:69
  106.2 0.8 copy.31
  107.0 5.0 %all-to-all-start.3 = ((bf16[8,5,32,128]{3,2,1,0:T(8,128)(2,1)}), bf16[8,5,32,128]{3,2,1,0:T(8,128)(2,1)S(1)}, u32[]{:S(2)}, u32[]{:S(2)}) async-start(bf16[8,5,32,128]{3,2,1,0:T(8,128)(2,1)} %after.21), calls=%async_computation.4 | async-start | bytes 655360 | tf_op jit(solution)/shard_map/all_to_all | solution.py:423
  112.0 5.0 %text_part.1 = (bf16[5,128,128]{2,1,0:T(8,128)(2,1)}, bf16[5,128,128]{2,1,0:T(8,128)(2,1)}, bf16[5,128,128]{2,1,0:T(8,128)(2,1)}, bf16[5,128,128]{2,1,0:T(8,128)(2,1)}) custom-call(s32[4]{0:T(128)} %copy-done.7, bf16[8,8,224,128]{3,2,1,0:T(8,128)(2,1)} %after.22.low_ref.high_ref, bf16[8,8,224,128]{3,2,1,0:T(8,128)(2,1)} %after.22.low_ref.high_ref, ...), custom_call_target="tpu_custom_call" | custom-call | tf_op jit(solution)/shard_map/text_part/pallas_call | solution.py:274
  117.0 1.7 collective-permute-start.15
  118.8 2.4 %collective-permute-start.16 = (bf16[5,128,128]{2,1,0:T(8,128)(2,1)}, bf16[5,128,128]{2,1,0:T(8,128)(2,1)S(1)}, u32[]{:S(2)}, u32[]{:S(2)}) collective-permute-start(bf16[5,128,128]{2,1,0:T(8,128)(2,1)} %get-tuple-element.24), channel_id=1, source_target_pairs={{0,32},{16,48},{32,0},{48,16},{1,33},{17,49},{33,1},{49,17},{2,34}... | collective-permute-start | bytes 491528 | tf_op jit(solution)/shard_map/ppermute | solution.py:416
  121.2 1.2 collective-permute-start.17
  122.4 1.6 collective-permute-done.15.p1
  124.0 4.4 %collective-permute-done.16.p2 = bf16[5,128,128]{2,1,0:T(8,128)(2,1)S(1)} collective-permute-done((bf16[5,128,128]{2,1,0:T(8,128)(2,1)}, bf16[5,128,128]{2,1,0:T(8,128)(2,1)S(1)}, u32[]{:S(2)}, u32[]{:S(2)}) %collective-permute-start.16) | collective-permute-done | bytes 163872 | tf_op jit(solution)/shard_map/ppermute | solution.py:416
  128.5 0.9 copy-done.5
  130.1 2.5 %collective-permute-start.20 = (bf16[5,128,128]{2,1,0:T(8,128)(2,1)S(1)}, bf16[5,128,128]{2,1,0:T(8,128)(2,1)S(1)}, u32[]{:S(2)}, u32[]{:S(2)}) collective-permute-start(bf16[5,128,128]{2,1,0:T(8,128)(2,1)S(1)} %text_sum.1), channel_id=1, source_target_pairs={{0,48},{16,0},{32,16},{48,32},{1,49},{17,1},{33,17},{49,33},{2,50}... | collective-permute-start | bytes 491528 | tf_op jit(solution)/shard_map/ppermute | solution.py:416
  133.3 3.9 %collective-permute-done.20 = bf16[5,128,128]{2,1,0:T(8,128)(2,1)S(1)} collective-permute-done((bf16[5,128,128]{2,1,0:T(8,128)(2,1)S(1)}, bf16[5,128,128]{2,1,0:T(8,128)(2,1)S(1)}, u32[]{:S(2)}, u32[]{:S(2)}) %collective-permute-start.20) | collective-permute-done | bytes 163872 | tf_op jit(solution)/shard_map/ppermute | solution.py:416
  137.3 1.1 collective-permute-done.19
  138.4 4.9 %collective-permute-done.18 = bf16[5,128,128]{2,1,0:T(8,128)(2,1)S(1)} collective-permute-done((bf16[5,128,128]{2,1,0:T(8,128)(2,1)S(1)}, bf16[5,128,128]{2,1,0:T(8,128)(2,1)S(1)}, u32[]{:S(2)}, u32[]{:S(2)}) %collective-permute-start.18) | collective-permute-done | bytes 163872 | tf_op jit(solution)/shard_map/ppermute | solution.py:416
  143.3 0.9 pad_maximum_fusion.refs_0_
  144.2 0.7 copy-done.3
  145.0 0.9 collective-permute-start.21
  145.9 1.9 %collective-permute-done.21.other_ref = bf16[4,5,128,128]{3,2,1,0:T(8,128)(2,1)S(1)} collective-permute-done((bf16[4,5,128,128]{3,2,1,0:T(8,128)(2,1)}, bf16[4,5,128,128]{3,2,1,0:T(8,128)(2,1)S(1)}, u32[]{:S(2)}, u32[]{:S(2)}) %collective-permute-start.21) | collective-permute-done | bytes 655392 | tf_op jit(solution)/shard_map/ppermute | solution.py:428
  147.8 1.1 copy-done.2
  148.9 1.0 copy-done.4
  149.9 3.1 %cross_part.1 = bf16[8,5,32,128]{3,2,1,0:T(8,128)(2,1)S(1)} custom-call(s32[4]{0:T(128)S(1)} %copy-done.8, s32[4]{0:T(128)S(1)} %copy-done.11, s32[8]{0:T(128)S(1)} %copy-done.12, bf16[8,5,32,128]{3,2,1,0:T(8,128)(2,1)S(1)} %copy-done.4, bf16[4,5,128,128]{3,2,1,0:T(8,128)(2,1)S(1)} %copy-done.2, bf16[4,5,128,128]{3,2,1,0:T(8,128)(2,1)S(1)} %collective-permute-done.21.other_ref), custom_call_target="tpu_custom_call" | custom-call | tf_op jit(solution)/shard_map/cross_part/pallas_call | solution.py:313
  153.1 2.0 %last_part.1 = bf16[8,5,32,128]{3,2,1,0:T(8,128)(2,1)} custom-call(bf16[5,272,128]{2,1,0:T(8,128)(2,1)} %bitcast.78), custom_call_target="tpu_custom_call" | custom-call | tf_op jit(solution)/shard_map/last_part/pallas_call | solution.py:101
  155.0 4.8 %all-to-all-start.2 = ((bf16[8,5,32,128]{3,2,1,0:T(8,128)(2,1)}), bf16[8,5,32,128]{3,2,1,0:T(8,128)(2,1)S(1)}, u32[]{:S(2)}, u32[]{:S(2)}) async-start(bf16[8,5,32,128]{3,2,1,0:T(8,128)(2,1)} %last_part.1), calls=%async_computation.3 | async-start | bytes 655360 | tf_op jit(solution)/shard_map/all_to_all | solution.py:432
  160.4 2.4 %collective-permute-start.27 = (bf16[5,32,128]{2,1,0:T(8,128)(2,1)S(1)}, bf16[5,32,128]{2,1,0:T(8,128)(2,1)S(1)}, u32[]{:S(2)}, u32[]{:S(2)}) collective-permute-start(bf16[5,32,128]{2,1,0:T(8,128)(2,1)S(1)} %get-tuple-element.31), channel_id=1, source_target_pairs={{0,4},{2,6},{4,8},{6,10},{8,12},{10,14},{12,0},{14,2},{1,5},{3,7},... | collective-permute-start | bytes 122888 | tf_op jit(solution)/shard_map/ppermute | solution.py:430
  162.8 1.7 collective-permute-start.26
  164.4 3.1 %collective-permute-start.25 = (bf16[5,32,128]{2,1,0:T(8,128)(2,1)S(1)}, bf16[5,32,128]{2,1,0:T(8,128)(2,1)S(1)}, u32[]{:S(2)}, u32[]{:S(2)}) collective-permute-start(bf16[5,32,128]{2,1,0:T(8,128)(2,1)S(1)} %get-tuple-element.33), channel_id=1, source_target_pairs={{0,8},{2,10},{4,12},{6,14},{8,0},{10,2},{12,4},{14,6},{1,9},{3,11}... | collective-permute-start | bytes 122888 | tf_op jit(solution)/shard_map/ppermute | solution.py:430
  167.5 1.5 collective-permute-start.24
  169.0 3.3 %collective-permute-start.23 = (bf16[5,32,128]{2,1,0:T(8,128)(2,1)S(1)}, bf16[5,32,128]{2,1,0:T(8,128)(2,1)S(1)}, u32[]{:S(2)}, u32[]{:S(2)}) collective-permute-start(bf16[5,32,128]{2,1,0:T(8,128)(2,1)S(1)} %get-tuple-element.35), channel_id=1, source_target_pairs={{0,12},{2,14},{4,0},{6,2},{8,4},{10,6},{12,8},{14,10},{1,13},{3,15... | collective-permute-start | bytes 122888 | tf_op jit(solution)/shard_map/ppermute | solution.py:430
  172.3 1.2 collective-permute-start.22
  173.5 3.6 %collective-permute-done.23.refs_2_ = bf16[5,32,128]{2,1,0:T(8,128)(2,1)S(1)} collective-permute-done((bf16[5,32,128]{2,1,0:T(8,128)(2,1)S(1)}, bf16[5,32,128]{2,1,0:T(8,128)(2,1)S(1)}, u32[]{:S(2)}, u32[]{:S(2)}) %collective-permute-start.23) | collective-permute-done | bytes 40992 | tf_op jit(solution)/shard_map/ppermute | solution.py:430
  177.1 1.5 place_part.1
  (93 shorter events, 4.8 us)
Async XLA Ops:
  7.2 32.2 %copy-start = (bf16[64,40,256]{2,1,0:T(8,128)(2,1)S(1)}, bf16[64,40,256]{2,1,0:T(8,128)(2,1)}, u32[]{:S(2)}) copy-start(bf16[64,40,256]{2,1,0:T(8,128)(2,1)} %param.15) | copy-start | bytes 3932164
  7.2 11.4 %copy-start.6 = (bf16[2,8,4096]{2,1,0:T(8,128)(2,1)S(1)}, bf16[2,8,4096]{2,1,0:T(8,128)(2,1)}, u32[]{:S(2)}) copy-start(bf16[2,8,4096]{2,1,0:T(8,128)(2,1)} %b0.1) | copy-start | bytes 393220
  7.2 11.4 %copy-start.11 = (s32[4]{0:T(128)S(1)}, s32[4]{0:T(128)}, u32[]{:S(2)}) copy-start(s32[4]{0:T(128)} %requests_ref.3) | copy-start | bytes 52
  7.2 9.7 %collective-permute-start.1 = (bf16[2,8,4096]{2,1,0:T(8,128)(2,1)}, bf16[2,8,4096]{2,1,0:T(8,128)(2,1)S(1)}, u32[]{:S(2)}, u32[]{:S(2)}) collective-permute-start(bf16[2,8,4096]{2,1,0:T(8,128)(2,1)} %b0.1), channel_id=1, source_target_pairs={{0,128},{64,192},{128,0},{192,64},{1,129},{65,193},{129,1},{193,65... | collective-permute-start | bytes 393224 | tf_op jit(solution)/shard_map/ppermute | solution.py:382
  11.0 7.6 %collective-permute-start = (bf16[2,8,4096]{2,1,0:T(8,128)(2,1)}, bf16[2,8,4096]{2,1,0:T(8,128)(2,1)S(1)}, u32[]{:S(2)}, u32[]{:S(2)}) collective-permute-start(bf16[2,8,4096]{2,1,0:T(8,128)(2,1)} %b0.1), channel_id=1, source_target_pairs={{0,64},{64,128},{128,192},{192,0},{1,65},{65,129},{129,193},{193,1... | collective-permute-start | bytes 393224 | tf_op jit(solution)/shard_map/ppermute | solution.py:382
  11.4 7.2 %collective-permute-start.2 = (bf16[2,8,4096]{2,1,0:T(8,128)(2,1)}, bf16[2,8,4096]{2,1,0:T(8,128)(2,1)S(1)}, u32[]{:S(2)}, u32[]{:S(2)}) collective-permute-start(bf16[2,8,4096]{2,1,0:T(8,128)(2,1)} %b0.1), channel_id=1, source_target_pairs={{0,192},{64,0},{128,64},{192,128},{1,193},{65,1},{129,65},{193,129... | collective-permute-start | bytes 393224 | tf_op jit(solution)/shard_map/ppermute | solution.py:382
  16.9 10.2 %copy-start.7 = (s32[4]{0:T(128)}, s32[4]{0:T(128)S(1)}, u32[]{:S(2)}) copy-start(s32[4]{0:T(128)S(1)} %pad_add_fusion.where_ref) | copy-start | bytes 52
  20.1 13.4 %all-to-all-start = ((bf16[8,224,128]{2,1,0:T(8,128)(2,1)}), bf16[8,224,128]{2,1,0:T(8,128)(2,1)S(1)}, u32[]{:S(2)}, u32[]{:S(2)}) async-start(bf16[8,224,128]{2,1,0:T(8,128)(2,1)} %pad_maximum_fusion.1), calls=%async_computation | async-start | bytes 917504 | tf_op jit(solution)/shard_map/all_to_all | solution.py:388
  24.7 2.4 %copy-start.10 = (f32[40,128]{1,0:T(8,128)S(1)}, f32[40,128]{1,0:T(8,128)}, u32[]{:S(2)}) copy-start(f32[40,128]{1,0:T(8,128)} %param.17) | copy-start | bytes 61444
  24.7 67.0 %all-gather.3.cloned.1.call-start = ((), (), s32[]{:S(2)}) async-start(), calls=%async_computation.6 | async-start | bytes 4128768 | tf_op jit(solution)/shard_map/all_gather | solution.py:396
  28.6 1.5 copy-start.1
  33.5 0.8 copy-start.13
  34.2 57.5 %all-to-all-start.1 = ((bf16[8,5,128,256]{3,2,1,0:T(8,128)(2,1)}), bf16[8,5,128,256]{3,2,1,0:T(8,128)(2,1)}, u32[]{:S(2)}, u32[]{:S(2)}) async-start(bf16[8,5,128,256]{3,2,1,0:T(8,128)(2,1)} %bitcast.67), calls=%async_computation.1 | async-start | bytes 5242880 | tf_op jit(solution)/shard_map/all_to_all | solution.py:395
  39.4 113.7 %reduce-scatter.2.cloned.1.call-start = ((), (), s32[]{:S(2)}) async-start(), calls=%async_computation.5 | async-start | bytes 3133440 | tf_op jit(solution)/shard_map/reduce_scatter | solution.py:420
  42.6 14.2 %collective-permute-start.3 = (bf16[5,16,256]{2,1,0:T(8,128)(2,1)}, bf16[5,16,256]{2,1,0:T(8,128)(2,1)S(1)}, u32[]{:S(2)}, u32[]{:S(2)}) collective-permute-start(bf16[5,16,256]{2,1,0:T(8,128)(2,1)} %after.13), channel_id=1, source_target_pairs={{0,2},{2,4},{4,6},{6,8},{8,10},{10,12},{12,14},{14,0},{1,3},{3,5},... | collective-permute-start | bytes 122888 | tf_op jit(solution)/shard_map/ppermute | solution.py:401
  45.0 14.2 %copy-start.19 = (bf16[5,16,256]{2,1,0:T(8,128)(2,1)S(1)}, bf16[5,16,256]{2,1,0:T(8,128)(2,1)}, u32[]{:S(2)}) copy-start(bf16[5,16,256]{2,1,0:T(8,128)(2,1)} %after.19) | copy-start | bytes 122884
  45.1 14.2 %collective-permute-start.4 = (bf16[5,16,256]{2,1,0:T(8,128)(2,1)}, bf16[5,16,256]{2,1,0:T(8,128)(2,1)S(1)}, u32[]{:S(2)}, u32[]{:S(2)}) collective-permute-start(bf16[5,16,256]{2,1,0:T(8,128)(2,1)} %after.14), channel_id=1, source_target_pairs={{0,4},{2,6},{4,8},{6,10},{8,12},{10,14},{12,0},{14,2},{1,5},{3,7},... | collective-permute-start | bytes 122888 | tf_op jit(solution)/shard_map/ppermute | solution.py:401
  48.1 11.9 %collective-permute-start.5 = (bf16[5,16,256]{2,1,0:T(8,128)(2,1)}, bf16[5,16,256]{2,1,0:T(8,128)(2,1)S(1)}, u32[]{:S(2)}, u32[]{:S(2)}) collective-permute-start(bf16[5,16,256]{2,1,0:T(8,128)(2,1)} %after.15), channel_id=1, source_target_pairs={{0,6},{2,8},{4,10},{6,12},{8,14},{10,0},{12,2},{14,4},{1,7},{3,9},... | collective-permute-start | bytes 122888 | tf_op jit(solution)/shard_map/ppermute | solution.py:401
  51.9 8.9 %collective-permute-start.6 = (bf16[5,16,256]{2,1,0:T(8,128)(2,1)}, bf16[5,16,256]{2,1,0:T(8,128)(2,1)S(1)}, u32[]{:S(2)}, u32[]{:S(2)}) collective-permute-start(bf16[5,16,256]{2,1,0:T(8,128)(2,1)} %after.16), channel_id=1, source_target_pairs={{0,8},{2,10},{4,12},{6,14},{8,0},{10,2},{12,4},{14,6},{1,9},{3,11}... | collective-permute-start | bytes 122888 | tf_op jit(solution)/shard_map/ppermute | solution.py:401
  52.4 10.7 %collective-permute-start.7 = (bf16[5,16,256]{2,1,0:T(8,128)(2,1)}, bf16[5,16,256]{2,1,0:T(8,128)(2,1)S(1)}, u32[]{:S(2)}, u32[]{:S(2)}) collective-permute-start(bf16[5,16,256]{2,1,0:T(8,128)(2,1)} %after.17), channel_id=1, source_target_pairs={{0,10},{2,12},{4,14},{6,0},{8,2},{10,4},{12,6},{14,8},{1,11},{3,13... | collective-permute-start | bytes 122888 | tf_op jit(solution)/shard_map/ppermute | solution.py:401
  56.8 7.5 %collective-permute-start.8 = (bf16[5,16,256]{2,1,0:T(8,128)(2,1)}, bf16[5,16,256]{2,1,0:T(8,128)(2,1)S(1)}, u32[]{:S(2)}, u32[]{:S(2)}) collective-permute-start(bf16[5,16,256]{2,1,0:T(8,128)(2,1)} %after.18), channel_id=1, source_target_pairs={{0,12},{2,14},{4,0},{6,2},{8,4},{10,6},{12,8},{14,10},{1,13},{3,15... | collective-permute-start | bytes 122888 | tf_op jit(solution)/shard_map/ppermute | solution.py:401
  59.2 7.7 %collective-permute-start.9 = (bf16[5,16,256]{2,1,0:T(8,128)(2,1)S(1)}, bf16[5,16,256]{2,1,0:T(8,128)(2,1)S(1)}, u32[]{:S(2)}, u32[]{:S(2)}) collective-permute-start(bf16[5,16,256]{2,1,0:T(8,128)(2,1)S(1)} %copy-done.19), channel_id=1, source_target_pairs={{0,14},{2,0},{4,2},{6,4},{8,6},{10,8},{12,10},{14,12},{1,15},{3,1}... | collective-permute-start | bytes 122888 | tf_op jit(solution)/shard_map/ppermute | solution.py:401
  67.0 2.0 %collective-permute-start.10 = (bf16[8,5,16,128]{3,2,1,0:T(8,128)(2,1)S(1)}, bf16[8,5,16,128]{3,2,1,0:T(8,128)(2,1)S(1)}, u32[]{:S(2)}, u32[]{:S(2)}) collective-permute-start(bf16[8,5,16,128]{3,2,1,0:T(8,128)(2,1)S(1)} %get-tuple-element.39), channel_id=1, source_target_pairs={{0,1},{1,0},{2,3},{3,2},{4,5},{5,4},{6,7},{7,6},{8,9},{9,8},{10,11... | collective-permute-start | bytes 491528 | tf_op jit(solution)/shard_map/ppermute | solution.py:406
  69.0 22.7 %copy-start.14 = (bf16[2,8,5,16,128]{4,3,2,1,0:T(8,128)(2,1)}, bf16[2,8,5,16,128]{4,3,2,1,0:T(8,128)(2,1)S(1)}, u32[]{:S(2)}) copy-start(bf16[2,8,5,16,128]{4,3,2,1,0:T(8,128)(2,1)S(1)} %pad_maximum_fusion.2.refs_1_.w0) | copy-start | bytes 983044
  69.0 9.6 %collective-permute-start.13 = (bf16[2,8,5,16,128]{4,3,2,1,0:T(8,128)(2,1)S(1)}, bf16[2,8,5,16,128]{4,3,2,1,0:T(8,128)(2,1)S(1)}, u32[]{:S(2)}, u32[]{:S(2)}) collective-permute-start(bf16[2,8,5,16,128]{4,3,2,1,0:T(8,128)(2,1)S(1)} %pad_maximum_fusion.2.refs_1_.w0), channel_id=1, source_target_pairs={{0,192},{64,0},{128,64},{192,128},{1,193},{65,1},{129,65},{193,129... | collective-permute-start | bytes 983048 | tf_op jit(solution)/shard_map/ppermute | solution.py:408
  71.8 10.5 %collective-permute-start.11 = (bf16[2,8,5,16,128]{4,3,2,1,0:T(8,128)(2,1)S(1)}, bf16[2,8,5,16,128]{4,3,2,1,0:T(8,128)(2,1)S(1)}, u32[]{:S(2)}, u32[]{:S(2)}) collective-permute-start(bf16[2,8,5,16,128]{4,3,2,1,0:T(8,128)(2,1)S(1)} %pad_maximum_fusion.2.refs_1_.w0), channel_id=1, source_target_pairs={{0,64},{64,128},{128,192},{192,0},{1,65},{65,129},{129,193},{193,1... | collective-permute-start | bytes 983048 | tf_op jit(solution)/shard_map/ppermute | solution.py:408
  78.6 13.1 %copy-start.15 = (bf16[2,8,5,16,128]{4,3,2,1,0:T(8,128)(2,1)}, bf16[2,8,5,16,128]{4,3,2,1,0:T(8,128)(2,1)S(1)}, u32[]{:S(2)}) copy-start(bf16[2,8,5,16,128]{4,3,2,1,0:T(8,128)(2,1)S(1)} %collective-permute-done.13.refs_5_.w3) | copy-start | bytes 983044
  78.6 6.0 %collective-permute-start.14 = (bf16[8,5,16,128]{3,2,1,0:T(8,128)(2,1)S(1)}, bf16[8,5,16,128]{3,2,1,0:T(8,128)(2,1)S(1)}, u32[]{:S(2)}, u32[]{:S(2)}) collective-permute-start(bf16[8,5,16,128]{3,2,1,0:T(8,128)(2,1)S(1)} %slice_bitcast_fusion), channel_id=1, source_target_pairs={{0,192},{64,0},{128,64},{192,128},{1,193},{65,1},{129,65},{193,129... | collective-permute-start | bytes 491528 | tf_op jit(solution)/shard_map/ppermute | solution.py:411
  82.4 9.3 %copy-start.16 = (bf16[2,8,5,16,128]{4,3,2,1,0:T(8,128)(2,1)}, bf16[2,8,5,16,128]{4,3,2,1,0:T(8,128)(2,1)S(1)}, u32[]{:S(2)}) copy-start(bf16[2,8,5,16,128]{4,3,2,1,0:T(8,128)(2,1)S(1)} %collective-permute-done.11.refs_2_.w1) | copy-start | bytes 983044
  82.4 5.9 %collective-permute-start.12 = (bf16[8,5,16,128]{3,2,1,0:T(8,128)(2,1)S(1)}, bf16[8,5,16,128]{3,2,1,0:T(8,128)(2,1)S(1)}, u32[]{:S(2)}, u32[]{:S(2)}) collective-permute-start(bf16[8,5,16,128]{3,2,1,0:T(8,128)(2,1)S(1)} %slice_bitcast_fusion.1), channel_id=1, source_target_pairs={{0,64},{64,128},{128,192},{192,0},{1,65},{65,129},{129,193},{193,1... | collective-permute-start | bytes 491528 | tf_op jit(solution)/shard_map/ppermute | solution.py:410
  84.6 7.1 %copy-start.17 = (bf16[8,5,16,128]{3,2,1,0:T(8,128)(2,1)}, bf16[8,5,16,128]{3,2,1,0:T(8,128)(2,1)S(1)}, u32[]{:S(2)}) copy-start(bf16[8,5,16,128]{3,2,1,0:T(8,128)(2,1)S(1)} %collective-permute-done.14.refs_4_.w4) | copy-start | bytes 491524
  88.2 3.5 %copy-start.18 = (bf16[8,5,16,128]{3,2,1,0:T(8,128)(2,1)}, bf16[8,5,16,128]{3,2,1,0:T(8,128)(2,1)S(1)}, u32[]{:S(2)}) copy-start(bf16[8,5,16,128]{3,2,1,0:T(8,128)(2,1)S(1)} %collective-permute-done.12.refs_3_.w2) | copy-start | bytes 491524
  107.0 37.2 %all-to-all-start.3 = ((bf16[8,5,32,128]{3,2,1,0:T(8,128)(2,1)}), bf16[8,5,32,128]{3,2,1,0:T(8,128)(2,1)S(1)}, u32[]{:S(2)}, u32[]{:S(2)}) async-start(bf16[8,5,32,128]{3,2,1,0:T(8,128)(2,1)} %after.21), calls=%async_computation.4 | async-start | bytes 655360 | tf_op jit(solution)/shard_map/all_to_all | solution.py:423
  112.0 16.5 %copy-start.8 = (s32[4]{0:T(128)S(1)}, s32[4]{0:T(128)}, u32[]{:S(2)}) copy-start(s32[4]{0:T(128)} %copy-done.7) | copy-start | bytes 52
  112.0 16.5 %copy-start.9 = (f32[40,128]{1,0:T(8,128)S(1)}, f32[40,128]{1,0:T(8,128)}, u32[]{:S(2)}) copy-start(f32[40,128]{1,0:T(8,128)} %param.19) | copy-start | bytes 61444
  117.0 30.8 %copy-start.12 = (s32[8]{0:T(128)S(1)}, s32[8]{0:T(128)}, u32[]{:S(2)}) copy-start(s32[8]{0:T(128)} %lengths_ref.1) | copy-start | bytes 100
  117.0 7.0 %collective-permute-start.15 = (bf16[5,128,128]{2,1,0:T(8,128)(2,1)}, bf16[5,128,128]{2,1,0:T(8,128)(2,1)S(1)}, u32[]{:S(2)}, u32[]{:S(2)}) collective-permute-start(bf16[5,128,128]{2,1,0:T(8,128)(2,1)} %get-tuple-element.23), channel_id=1, source_target_pairs={{0,16},{16,32},{32,48},{48,0},{1,17},{17,33},{33,49},{49,1},{2,18}... | collective-permute-start | bytes 491528 | tf_op jit(solution)/shard_map/ppermute | solution.py:416
  118.8 9.7 %collective-permute-start.16 = (bf16[5,128,128]{2,1,0:T(8,128)(2,1)}, bf16[5,128,128]{2,1,0:T(8,128)(2,1)S(1)}, u32[]{:S(2)}, u32[]{:S(2)}) collective-permute-start(bf16[5,128,128]{2,1,0:T(8,128)(2,1)} %get-tuple-element.24), channel_id=1, source_target_pairs={{0,32},{16,48},{32,0},{48,16},{1,33},{17,49},{33,1},{49,17},{2,34}... | collective-permute-start | bytes 491528 | tf_op jit(solution)/shard_map/ppermute | solution.py:416
  121.2 7.2 %collective-permute-start.17 = (bf16[5,128,128]{2,1,0:T(8,128)(2,1)}, bf16[5,128,128]{2,1,0:T(8,128)(2,1)S(1)}, u32[]{:S(2)}, u32[]{:S(2)}) collective-permute-start(bf16[5,128,128]{2,1,0:T(8,128)(2,1)} %get-tuple-element.25), channel_id=1, source_target_pairs={{0,48},{16,0},{32,16},{48,32},{1,49},{17,1},{33,17},{49,33},{2,50}... | collective-permute-start | bytes 491528 | tf_op jit(solution)/shard_map/ppermute | solution.py:416
  128.5 0.9 copy-start.5
  130.1 7.2 %collective-permute-start.20 = (bf16[5,128,128]{2,1,0:T(8,128)(2,1)S(1)}, bf16[5,128,128]{2,1,0:T(8,128)(2,1)S(1)}, u32[]{:S(2)}, u32[]{:S(2)}) collective-permute-start(bf16[5,128,128]{2,1,0:T(8,128)(2,1)S(1)} %text_sum.1), channel_id=1, source_target_pairs={{0,48},{16,0},{32,16},{48,32},{1,49},{17,1},{33,17},{49,33},{2,50}... | collective-permute-start | bytes 491528 | tf_op jit(solution)/shard_map/ppermute | solution.py:416
  132.6 5.8 %collective-permute-start.19 = (bf16[5,128,128]{2,1,0:T(8,128)(2,1)S(1)}, bf16[5,128,128]{2,1,0:T(8,128)(2,1)S(1)}, u32[]{:S(2)}, u32[]{:S(2)}) collective-permute-start(bf16[5,128,128]{2,1,0:T(8,128)(2,1)S(1)} %text_sum.1), channel_id=1, source_target_pairs={{0,32},{16,48},{32,0},{48,16},{1,33},{17,49},{33,1},{49,17},{2,34}... | collective-permute-start | bytes 491528 | tf_op jit(solution)/shard_map/ppermute | solution.py:416
  133.3 10.0 %collective-permute-start.18 = (bf16[5,128,128]{2,1,0:T(8,128)(2,1)S(1)}, bf16[5,128,128]{2,1,0:T(8,128)(2,1)S(1)}, u32[]{:S(2)}, u32[]{:S(2)}) collective-permute-start(bf16[5,128,128]{2,1,0:T(8,128)(2,1)S(1)} %text_sum.1), channel_id=1, source_target_pairs={{0,16},{16,32},{32,48},{48,0},{1,17},{17,33},{33,49},{49,1},{2,18}... | collective-permute-start | bytes 491528 | tf_op jit(solution)/shard_map/ppermute | solution.py:416
  144.2 0.7 copy-start.3
  145.0 2.8 %collective-permute-start.21 = (bf16[4,5,128,128]{3,2,1,0:T(8,128)(2,1)}, bf16[4,5,128,128]{3,2,1,0:T(8,128)(2,1)S(1)}, u32[]{:S(2)}, u32[]{:S(2)}) collective-permute-start(bf16[4,5,128,128]{3,2,1,0:T(8,128)(2,1)} %after.23.mine_ref), channel_id=1, source_target_pairs={{0,1},{1,0},{2,3},{3,2},{4,5},{5,4},{6,7},{7,6},{8,9},{9,8},{10,11... | collective-permute-start | bytes 1966088 | tf_op jit(solution)/shard_map/ppermute | solution.py:428
  147.8 1.1 copy-start.2
  148.9 1.0 copy-start.4
  155.0 22.1 %all-to-all-start.2 = ((bf16[8,5,32,128]{3,2,1,0:T(8,128)(2,1)}), bf16[8,5,32,128]{3,2,1,0:T(8,128)(2,1)S(1)}, u32[]{:S(2)}, u32[]{:S(2)}) async-start(bf16[8,5,32,128]{3,2,1,0:T(8,128)(2,1)} %last_part.1), calls=%async_computation.3 | async-start | bytes 655360 | tf_op jit(solution)/shard_map/all_to_all | solution.py:432
  159.8 9.2 %collective-permute-start.28 = (bf16[5,32,128]{2,1,0:T(8,128)(2,1)S(1)}, bf16[5,32,128]{2,1,0:T(8,128)(2,1)S(1)}, u32[]{:S(2)}, u32[]{:S(2)}) collective-permute-start(bf16[5,32,128]{2,1,0:T(8,128)(2,1)S(1)} %get-tuple-element.30), channel_id=1, source_target_pairs={{0,2},{2,4},{4,6},{6,8},{8,10},{10,12},{12,14},{14,0},{1,3},{3,5},... | collective-permute-start | bytes 122888 | tf_op jit(solution)/shard_map/ppermute | solution.py:430
  160.4 12.0 %collective-permute-start.27 = (bf16[5,32,128]{2,1,0:T(8,128)(2,1)S(1)}, bf16[5,32,128]{2,1,0:T(8,128)(2,1)S(1)}, u32[]{:S(2)}, u32[]{:S(2)}) collective-permute-start(bf16[5,32,128]{2,1,0:T(8,128)(2,1)S(1)} %get-tuple-element.31), channel_id=1, source_target_pairs={{0,4},{2,6},{4,8},{6,10},{8,12},{10,14},{12,0},{14,2},{1,5},{3,7},... | collective-permute-start | bytes 122888 | tf_op jit(solution)/shard_map/ppermute | solution.py:430
  162.8 10.7 %collective-permute-start.26 = (bf16[5,32,128]{2,1,0:T(8,128)(2,1)S(1)}, bf16[5,32,128]{2,1,0:T(8,128)(2,1)S(1)}, u32[]{:S(2)}, u32[]{:S(2)}) collective-permute-start(bf16[5,32,128]{2,1,0:T(8,128)(2,1)S(1)} %get-tuple-element.32), channel_id=1, source_target_pairs={{0,6},{2,8},{4,10},{6,12},{8,14},{10,0},{12,2},{14,4},{1,7},{3,9},... | collective-permute-start | bytes 122888 | tf_op jit(solution)/shard_map/ppermute | solution.py:430
  164.4 9.1 %collective-permute-start.25 = (bf16[5,32,128]{2,1,0:T(8,128)(2,1)S(1)}, bf16[5,32,128]{2,1,0:T(8,128)(2,1)S(1)}, u32[]{:S(2)}, u32[]{:S(2)}) collective-permute-start(bf16[5,32,128]{2,1,0:T(8,128)(2,1)S(1)} %get-tuple-element.33), channel_id=1, source_target_pairs={{0,8},{2,10},{4,12},{6,14},{8,0},{10,2},{12,4},{14,6},{1,9},{3,11}... | collective-permute-start | bytes 122888 | tf_op jit(solution)/shard_map/ppermute | solution.py:430
  167.5 6.0 %collective-permute-start.24 = (bf16[5,32,128]{2,1,0:T(8,128)(2,1)S(1)}, bf16[5,32,128]{2,1,0:T(8,128)(2,1)S(1)}, u32[]{:S(2)}, u32[]{:S(2)}) collective-permute-start(bf16[5,32,128]{2,1,0:T(8,128)(2,1)S(1)} %get-tuple-element.34), channel_id=1, source_target_pairs={{0,10},{2,12},{4,14},{6,0},{8,2},{10,4},{12,6},{14,8},{1,11},{3,13... | collective-permute-start | bytes 122888 | tf_op jit(solution)/shard_map/ppermute | solution.py:430
  169.0 8.1 %collective-permute-start.23 = (bf16[5,32,128]{2,1,0:T(8,128)(2,1)S(1)}, bf16[5,32,128]{2,1,0:T(8,128)(2,1)S(1)}, u32[]{:S(2)}, u32[]{:S(2)}) collective-permute-start(bf16[5,32,128]{2,1,0:T(8,128)(2,1)S(1)} %get-tuple-element.35), channel_id=1, source_target_pairs={{0,12},{2,14},{4,0},{6,2},{8,4},{10,6},{12,8},{14,10},{1,13},{3,15... | collective-permute-start | bytes 122888 | tf_op jit(solution)/shard_map/ppermute | solution.py:430
  172.3 4.8 %collective-permute-start.22 = (bf16[5,32,128]{2,1,0:T(8,128)(2,1)S(1)}, bf16[5,32,128]{2,1,0:T(8,128)(2,1)S(1)}, u32[]{:S(2)}, u32[]{:S(2)}) collective-permute-start(bf16[5,32,128]{2,1,0:T(8,128)(2,1)S(1)} %get-tuple-element.36), channel_id=1, source_target_pairs={{0,14},{2,0},{4,2},{6,4},{8,6},{10,8},{12,10},{14,12},{1,15},{3,1}... | collective-permute-start | bytes 122888 | tf_op jit(solution)/shard_map/ppermute | solution.py:430
Sparse Core Ops, SparseCore 0:
  34.4 57.2 all-gather.2
  106.4 42.7 reduce-scatter.1

commit v6 on v5

--- a/solution.py
+++ b/solution.py
@@ -144,17 +144,38 @@
     )(value, *others)
 
 
-def pick_kernel(where_ref, requests_ref, b0, b1, b2, b3, out_ref):
+def choose_kernel(where_ref, requests_ref, bank_ref, *out_refs):
+    per_branch = bank_ref.shape[0]
+    for k, ref in enumerate(out_refs):
+        prompt = lax.rem(requests_ref[lax.rem(where_ref[0] + k, 4)], per_branch)
+        rows = bank_ref[0].astype(F32)
+        for p in range(1, per_branch):
+            rows = jnp.where(prompt == p, bank_ref[p].astype(F32), rows)
+        ref[...] = rows.astype(BF16)
+
+
+def choose_part(where, requests, bank):
+    _, count, width = bank.shape
+    return pl.pallas_call(
+        choose_kernel,
+        grid_spec=pltpu.PrefetchScalarGridSpec(
+            num_scalar_prefetch=2,
+            grid=(1,),
+            in_specs=[pl.BlockSpec(bank.shape, lambda i, w, r: (0, 0, 0))],
+            out_specs=[pl.BlockSpec((count, width), lambda i, w, r: (0, 0))] * 4,
+        ),
+        out_shape=[jax.ShapeDtypeStruct((count, width), BF16)] * 4,
+        compiler_params=pltpu.CompilerParams(vmem_limit_bytes=VMEM),
+        name="choose_part",
+    )(where, requests, bank)
+
+
+def pick_kernel(where_ref, requests_ref, b0, b1, b2, b3, out_ref, *, per_branch):
     wanted = requests_ref[where_ref[0]]
-    per_branch = b0.shape[0]
     plane = lax.rem(where_ref[0] - wanted // per_branch + 4, 4)
-    prompt = lax.rem(wanted, per_branch)
-    rows = None
-    for k, ref in enumerate((b0, b1, b2, b3)):
-        for p in range(ref.shape[0]):
-            value = ref[p].astype(F32)
-            here = jnp.logical_and(plane == k, prompt == p)
-            rows = value if rows is None else jnp.where(here, value, rows)
+    rows = b0[...].astype(F32)
+    for k, ref in ((1, b1), (2, b2), (3, b3)):
+        rows = jnp.where(plane == k, ref[...].astype(F32), rows)
     for x in range(NX):
         blocks = [rows[:, (x * 8 + block) * 128 : (x * 8 + block + 1) * 128] for block in range(8)]
         blocks = jnp.concatenate(blocks, axis=0).astype(BF16)
@@ -162,14 +183,14 @@
             out_ref[x * NC + c] = blocks
 
 
-def pick_part(where, requests, banks):
-    per_branch, count, width = banks[0].shape
-    return pl.pallas_call(
-        pick_kernel,
+def pick_part(where, requests, banks, per_branch):
+    count, width = banks[0].shape
+    return pl.pallas_call(
+        functools.partial(pick_kernel, per_branch=per_branch),
         grid_spec=pltpu.PrefetchScalarGridSpec(
             num_scalar_prefetch=2,
             grid=(1,),
-            in_specs=[pl.BlockSpec(banks[0].shape, lambda i, w, r: (0, 0, 0))] * 4,
+            in_specs=[pl.BlockSpec((count, width), lambda i, w, r: (0, 0))] * 4,
             out_specs=pl.BlockSpec((8, 8 * count, 128), lambda i, w, r: (0, 0, 0)),
         ),
         out_shape=jax.ShapeDtypeStruct((8, 8 * count, 128), BF16),
@@ -319,6 +340,23 @@
     )(where, requests, lengths, queries, mine, other)
 
 
+def queries_kernel(q_ref, self_gain_ref, cross_gain_ref, self_out, cross_out):
+    for gain_ref, out_ref, first in ((self_gain_ref, self_out, 0), (cross_gain_ref, cross_out, 128)):
+        value = head_norm(q_ref[:, :, first : first + 128], gain_ref[...])
+        out_ref[...] = jnp.swapaxes(value, 0, 1).astype(BF16)
+
+
+def queries_part(queries, self_gain, cross_gain):
+    tokens, heads, width = queries.shape
+    shape = jax.ShapeDtypeStruct((heads, tokens, width // 2), BF16)
+    return pl.pallas_call(
+        queries_kernel,
+        out_shape=[shape, shape],
+        compiler_params=pltpu.CompilerParams(vmem_limit_bytes=ALL_VMEM),
+        name="queries_part",
+    )(queries, self_gain, cross_gain)
+
+
 def place_kernel(where_ref, self_ref, *refs):
     self_out, cross_out = refs[NZ:]
     groups, slots, _, width = self_ref.shape
@@ -379,11 +417,12 @@
             8, slots, values.shape[0], values.shape[2]
         )
 
-    banks = [prompt_bank] + [lax.ppermute(prompt_bank, "branch", ring(4, k)) for k in (1, 2, 3)]
-    columns = pick_part(where, requests, banks)
+    banks = choose_part(where, requests, prompt_bank)
+    banks = [banks[0]] + [lax.ppermute(banks[k], "branch", ring(4, k)) for k in (1, 2, 3)]
+    columns = pick_part(where, requests, banks, per_branch)
 
     local_queries = queries[0]
-    self_queries = head_major(head_norm(local_queries[..., :head_dim], q_gain).astype(BF16))
+    self_queries, cross_queries = queries_part(local_queries, q_gain, cq_gain)
     self_queries = self_queries.reshape(8, slots * tokens, 128)
     got = lax.all_to_all(
         jnp.concatenate([self_queries, columns], axis=1), GROUP, 0, 0, tiled=True
@@ -419,7 +458,7 @@
     own = self_part(gathered, pairs, scale)
     total = lax.psum_scatter(own, "z", scatter_dimension=0)
 
-    cross_queries = head_major(head_norm(local_queries[..., head_dim:], cq_gain).astype(BF16))
+    cross_queries = cross_queries.reshape(8, slots, tokens, head_dim)
     cross_queries = lax.all_to_all(after(cross_queries, own), "z", 0, 0, tiled=True)
 
     parts = to_others(text_part(where, after(gathered, own), weights))

time: 186 us -> 188 us (1.011)
  Pallas kernels: 31.4 us -> 34.5 us
  other arithmetic: 4.89 us -> 2.88 us
    pallas_call x1 -> x3, Pallas kernels: 0.63 us -> 3.62 us  [the longest x1 2.43 us: queries_part(): pl.pallas_call(queries_kernel, out_shape=[shape, shape], compiler_params=...]
    unnamed x48 -> x52, local copies, waits for them, and re-layouts: 9.2 us -> 11.5 us
  transfers between devices with their start and end apart: 35 -> 35, of which waited for: 18 -> 18; matrix products, arithmetic and copies ran while one was open for 5% -> 3% of each run, Pallas kernels for 7% -> 8%
where the time goes in v6:
time: 188 us; the launch traced here: 187 us
  starting transfers between devices  74.3 us (40%)
  waiting for transfers between devices  48.8 us (26%)
  Pallas kernels  34.5 us (18%)
  between operations  14.3 us (8%)
  local copies, waits for them, and re-layouts  12.4 us (7%)
  other arithmetic  2.88 us (2%)
    ppermute x7, starting transfers between devices, local(): lax.ppermute(after(moved[k], got), 'z', ring(NZ, k))  16.6 us
    ppermute x6, waiting for transfers between devices, to_others(): lax.ppermute(pieces[k], 'x', ring(NX, k))  15.5 us
    pallas_call x1, Pallas kernels, self_part(): pl.pallas_call(functools.partial(self_kernel, rows=1024, keys=1024, scale...  14.5 us
    ppermute x7, starting transfers between devices, local(): lax.ppermute(cross[k], 'z', ring(NZ, -k))  13.5 us
    unnamed x52, local copies, waits for them, and re-layouts  11.5 us
    ppermute x6, starting transfers between devices, to_others(): lax.ppermute(pieces[k], 'x', ring(NX, k))  8.4 us
    ppermute x7, waiting for transfers between devices, local(): lax.ppermute(after(moved[k], got), 'z', ring(NZ, k))  6.89 us
    ppermute x2, waiting for transfers between devices, local(): lax.ppermute(both, 'branch', ring(4, k))  6.79 us
  transfers between devices with their start and end apart: 35, of which 18 were waited for; matrix products, arithmetic and copies ran while one was open for 3% of the time, Pallas kernels for 8%

profile of v6, /device:TPU:1, one launch (start us, length us, event | category | flops | bytes accessed | tf_op | source)
XLA Modules:
  0.0 187.2 jit_solution(12661492668050158460)
XLA Ops:
  7.3 1.0 copy-done.6
  9.5 2.2 %collective-permute-start = (bf16[8,4096]{1,0:T(8,128)(2,1)S(1)}, bf16[8,4096]{1,0:T(8,128)(2,1)S(1)}, u32[]{:S(2)}, u32[]{:S(2)}) collective-permute-start(bf16[8,4096]{1,0:T(8,128)(2,1)S(1)} %get-tuple-element.22), channel_id=1, source_target_pairs={{0,64},{64,128},{128,192},{192,0},{1,65},{65,129},{129,193},{193,1... | collective-permute-start | bytes 196616 | tf_op jit(solution)/shard_map/ppermute | solution.py:421
  11.7 2.6 %collective-permute-start.1 = (bf16[8,4096]{1,0:T(8,128)(2,1)S(1)}, bf16[8,4096]{1,0:T(8,128)(2,1)S(1)}, u32[]{:S(2)}, u32[]{:S(2)}) collective-permute-start(bf16[8,4096]{1,0:T(8,128)(2,1)S(1)} %get-tuple-element.23), channel_id=1, source_target_pairs={{0,128},{64,192},{128,0},{192,64},{1,129},{65,193},{129,1},{193,65... | collective-permute-start | bytes 196616 | tf_op jit(solution)/shard_map/ppermute | solution.py:421
  14.3 1.1 collective-permute-start.2
  15.4 2.4 %queries_part.1 = (bf16[40,32,128]{2,1,0:T(8,128)(2,1)}, bf16[40,32,128]{2,1,0:T(8,128)(2,1)}) custom-call(bf16[32,40,256]{2,1,0:T(8,128)(2,1)} %bitcast.71, f32[40,128]{1,0:T(8,128)} %self_gain_ref.1, f32[40,128]{1,0:T(8,128)} %cross_gain_ref.1), custom_call_target="tpu_custom_call" | custom-call | tf_op jit(solution)/shard_map/queries_part/pallas_call | solution.py:352
  19.1 1.8 pad_maximum_fusion.1
  20.9 6.3 %all-to-all-start = ((bf16[8,224,128]{2,1,0:T(8,128)(2,1)}), bf16[8,224,128]{2,1,0:T(8,128)(2,1)S(1)}, u32[]{:S(2)}, u32[]{:S(2)}) async-start(bf16[8,224,128]{2,1,0:T(8,128)(2,1)} %pad_maximum_fusion.1), calls=%async_computation | async-start | bytes 917504 | tf_op jit(solution)/shard_map/all_to_all | solution.py:427
  27.2 2.4 %copy.29 = bf16[1,128,40,256]{3,1,2,0:T(8,128)(2,1)S(1)} copy(bf16[1,128,40,256]{3,2,1,0:T(8,128)(2,1)} %param.11) | data formatting | bytes 5242880 | tf_op args[1]
  29.6 1.6 norm_keys.1.refs_1_
  31.1 1.5 copy-done.1
  32.7 3.3 %all-to-all-done.refs_0_ = bf16[8,224,128]{2,1,0:T(8,128)(2,1)S(1)} async-done(((bf16[8,224,128]{2,1,0:T(8,128)(2,1)}), bf16[8,224,128]{2,1,0:T(8,128)(2,1)S(1)}, u32[]{:S(2)}, u32[]{:S(2)}) %all-to-all-start) | async-done | bytes 458784 | tf_op jit(solution)/shard_map/all_to_all | solution.py:427
  36.0 0.8 copy-done.15
  36.8 5.2 %all-to-all-start.1 = ((bf16[8,5,128,256]{3,2,1,0:T(8,128)(2,1)}), bf16[8,5,128,256]{3,2,1,0:T(8,128)(2,1)}, u32[]{:S(2)}, u32[]{:S(2)}) async-start(bf16[8,5,128,256]{3,2,1,0:T(8,128)(2,1)} %bitcast.63), calls=%async_computation.1 | async-start | bytes 5242880 | tf_op jit(solution)/shard_map/all_to_all | solution.py:434
  42.0 0.8 copy.27
  42.8 2.4 %slice_part.1 = (bf16[5,16,256]{2,1,0:T(8,128)(2,1)}, bf16[5,16,256]{2,1,0:T(8,128)(2,1)}, bf16[5,16,256]{2,1,0:T(8,128)(2,1)}, bf16[5,16,256]{2,1,0:T(8,128)(2,...) custom-call(s32[4]{0:T(128)} %copy-done.7, ...), custom_call_target="tpu_custom_call" | custom-call | tf_op jit(solution)/shard_map/slice_part/pallas_call | solution.py:208
  45.1 1.7 collective-permute-start.3
  46.8 0.8 bitcast_dynamic-update-slice_fusion.7
  47.6 3.1 %collective-permute-start.4 = (bf16[5,16,256]{2,1,0:T(8,128)(2,1)}, bf16[5,16,256]{2,1,0:T(8,128)(2,1)S(1)}, u32[]{:S(2)}, u32[]{:S(2)}) collective-permute-start(bf16[5,16,256]{2,1,0:T(8,128)(2,1)} %after.14), channel_id=1, source_target_pairs={{0,4},{2,6},{4,8},{6,10},{8,12},{10,14},{12,0},{14,2},{1,5},{3,7},... | collective-permute-start | bytes 122888 | tf_op jit(solution)/shard_map/ppermute | solution.py:440
  50.7 3.8 %collective-permute-start.5 = (bf16[5,16,256]{2,1,0:T(8,128)(2,1)}, bf16[5,16,256]{2,1,0:T(8,128)(2,1)S(1)}, u32[]{:S(2)}, u32[]{:S(2)}) collective-permute-start(bf16[5,16,256]{2,1,0:T(8,128)(2,1)} %after.15), channel_id=1, source_target_pairs={{0,6},{2,8},{4,10},{6,12},{8,14},{10,0},{12,2},{14,4},{1,7},{3,9},... | collective-permute-start | bytes 122888 | tf_op jit(solution)/shard_map/ppermute | solution.py:440
  54.9 4.5 %collective-permute-start.7 = (bf16[5,16,256]{2,1,0:T(8,128)(2,1)}, bf16[5,16,256]{2,1,0:T(8,128)(2,1)S(1)}, u32[]{:S(2)}, u32[]{:S(2)}) collective-permute-start(bf16[5,16,256]{2,1,0:T(8,128)(2,1)} %after.17), channel_id=1, source_target_pairs={{0,10},{2,12},{4,14},{6,0},{8,2},{10,4},{12,6},{14,8},{1,11},{3,13... | collective-permute-start | bytes 122888 | tf_op jit(solution)/shard_map/ppermute | solution.py:440
  59.4 2.4 %collective-permute-start.8 = (bf16[5,16,256]{2,1,0:T(8,128)(2,1)}, bf16[5,16,256]{2,1,0:T(8,128)(2,1)S(1)}, u32[]{:S(2)}, u32[]{:S(2)}) collective-permute-start(bf16[5,16,256]{2,1,0:T(8,128)(2,1)} %after.18), channel_id=1, source_target_pairs={{0,12},{2,14},{4,0},{6,2},{8,4},{10,6},{12,8},{14,10},{1,13},{3,15... | collective-permute-start | bytes 122888 | tf_op jit(solution)/shard_map/ppermute | solution.py:440
  61.8 0.8 collective-permute-start.9
  62.6 0.8 collective-permute-done.6
  63.4 1.3 collective-permute-done.7
  64.7 2.5 %collective-permute-done.8 = bf16[5,16,256]{2,1,0:T(8,128)(2,1)S(1)} collective-permute-done((bf16[5,16,256]{2,1,0:T(8,128)(2,1)}, bf16[5,16,256]{2,1,0:T(8,128)(2,1)S(1)}, u32[]{:S(2)}, u32[]{:S(2)}) %collective-permute-start.8) | collective-permute-done | bytes 40992 | tf_op jit(solution)/shard_map/ppermute | solution.py:440
  67.2 2.3 %collective-permute-done.9 = bf16[5,16,256]{2,1,0:T(8,128)(2,1)S(1)} collective-permute-done((bf16[5,16,256]{2,1,0:T(8,128)(2,1)S(1)}, bf16[5,16,256]{2,1,0:T(8,128)(2,1)S(1)}, u32[]{:S(2)}, u32[]{:S(2)}) %collective-permute-start.9) | collective-permute-done | bytes 40992 | tf_op jit(solution)/shard_map/ppermute | solution.py:440
  69.5 0.9 collective-permute-start.10
  70.5 1.0 collective-permute-done.10
  71.5 2.3 %collective-permute-start.13 = (bf16[2,8,5,16,128]{4,3,2,1,0:T(8,128)(2,1)S(1)}, bf16[2,8,5,16,128]{4,3,2,1,0:T(8,128)(2,1)S(1)}, u32[]{:S(2)}, u32[]{:S(2)}) collective-permute-start(bf16[2,8,5,16,128]{4,3,2,1,0:T(8,128)(2,1)S(1)} %pad_maximum_fusion.2.refs_1_.w0), channel_id=1, source_target_pairs={{0,192},{64,0},{128,64},{192,128},{1,193},{65,1},{129,65},{193,129... | collective-permute-start | bytes 983048 | tf_op jit(solution)/shard_map/ppermute | solution.py:447
  73.9 6.8 %collective-permute-done.13.refs_5_.w3 = bf16[2,8,5,16,128]{4,3,2,1,0:T(8,128)(2,1)S(1)} collective-permute-done((bf16[2,8,5,16,128]{4,3,2,1,0:T(8,128)(2,1)S(1)}, bf16[2,8,5,16,128]{4,3,2,1,0:T(8,128)(2,1)S(1)}, u32[]{:S(2)}, u32[]{:S(2)}) %collective-permute-start.13) | collective-permute-done | bytes 327712 | tf_op jit(solution)/shard_map/ppermute | solution.py:447
  80.7 3.7 %collective-permute-start.14 = (bf16[8,5,16,128]{3,2,1,0:T(8,128)(2,1)S(1)}, bf16[8,5,16,128]{3,2,1,0:T(8,128)(2,1)S(1)}, u32[]{:S(2)}, u32[]{:S(2)}) collective-permute-start(bf16[8,5,16,128]{3,2,1,0:T(8,128)(2,1)S(1)} %slice_bitcast_fusion), channel_id=1, source_target_pairs={{0,192},{64,0},{128,64},{192,128},{1,193},{65,1},{129,65},{193,129... | collective-permute-start | bytes 491528 | tf_op jit(solution)/shard_map/ppermute | solution.py:450
  84.5 2.2 %collective-permute-done.14.refs_4_.w4 = bf16[8,5,16,128]{3,2,1,0:T(8,128)(2,1)S(1)} collective-permute-done((bf16[8,5,16,128]{3,2,1,0:T(8,128)(2,1)S(1)}, bf16[8,5,16,128]{3,2,1,0:T(8,128)(2,1)S(1)}, u32[]{:S(2)}, u32[]{:S(2)}) %collective-permute-start.14) | collective-permute-done | bytes 163872 | tf_op jit(solution)/shard_map/ppermute | solution.py:450
  86.6 3.6 %collective-permute-done.12.refs_3_.w2 = bf16[8,5,16,128]{3,2,1,0:T(8,128)(2,1)S(1)} collective-permute-done((bf16[8,5,16,128]{3,2,1,0:T(8,128)(2,1)S(1)}, bf16[8,5,16,128]{3,2,1,0:T(8,128)(2,1)S(1)}, u32[]{:S(2)}, u32[]{:S(2)}) %collective-permute-start.12) | collective-permute-done | bytes 163872 | tf_op jit(solution)/shard_map/ppermute | solution.py:449
  90.3 3.8 %all-gather.3.cloned.1.call-done = bf16[64,224,128]{2,1,0:T(8,128)(2,1)} async-done(((bf16[8,224,128]{2,1,0:T(8,128)(2,1)}), bf16[64,224,128]{2,1,0:T(8,128)(2,1)}) %all-gather.3.cloned.1.call-update) | async-done | bytes 3670032 | tf_op jit(solution)/shard_map/all_gather | solution.py:435
  94.1 14.5 %self_part.1.refs_1_ = bf16[8,5,272,128]{3,2,1,0:T(8,128)(2,1)} custom-call(bf16[8,8,224,128]{3,2,1,0:T(8,128)(2,1)} %after.20.q_ref.refs_0_, bf16[8,5,128,256]{3,2,1,0:T(8,128)(2,1)} %all-to-all-done.1.kv_ref), custom_call_target="tpu_custom_call" | custom-call | flops 8053063680 | bytes 6291456 | tf_op jit(solution)/shard_map/self_part/pallas_call | solution.py:69
  108.6 5.3 %all-to-all-start.3 = ((bf16[8,5,32,128]{3,2,1,0:T(8,128)(2,1)}), bf16[8,5,32,128]{3,2,1,0:T(8,128)(2,1)S(1)}, u32[]{:S(2)}, u32[]{:S(2)}) async-start(bf16[8,5,32,128]{3,2,1,0:T(8,128)(2,1)} %after.21), calls=%async_computation.4 | async-start | bytes 655360 | tf_op jit(solution)/shard_map/all_to_all | solution.py:462
  114.0 5.0 %text_part.1 = (bf16[5,128,128]{2,1,0:T(8,128)(2,1)}, bf16[5,128,128]{2,1,0:T(8,128)(2,1)}, bf16[5,128,128]{2,1,0:T(8,128)(2,1)}, bf16[5,128,128]{2,1,0:T(8,128)(2,1)}) custom-call(s32[4]{0:T(128)} %copy-done.7, bf16[8,8,224,128]{3,2,1,0:T(8,128)(2,1)} %after.22.low_ref.high_ref, bf16[8,8,224,128]{3,2,1,0:T(8,128)(2,1)} %after.22.low_ref.high_ref, ...), custom_call_target="tpu_custom_call" | custom-call | tf_op jit(solution)/shard_map/text_part/pallas_call | solution.py:295
  119.0 1.1 collective-permute-start.15
  120.2 2.4 %collective-permute-start.16 = (bf16[5,128,128]{2,1,0:T(8,128)(2,1)}, bf16[5,128,128]{2,1,0:T(8,128)(2,1)S(1)}, u32[]{:S(2)}, u32[]{:S(2)}) collective-permute-start(bf16[5,128,128]{2,1,0:T(8,128)(2,1)} %get-tuple-element.36), channel_id=1, source_target_pairs={{0,32},{16,48},{32,0},{48,16},{1,33},{17,49},{33,1},{49,17},{2,34}... | collective-permute-start | bytes 491528 | tf_op jit(solution)/shard_map/ppermute | solution.py:455
  122.6 1.2 collective-permute-start.17
  123.8 1.8 collective-permute-done.15.p1
  125.6 4.3 %collective-permute-done.16.p2 = bf16[5,128,128]{2,1,0:T(8,128)(2,1)S(1)} collective-permute-done((bf16[5,128,128]{2,1,0:T(8,128)(2,1)}, bf16[5,128,128]{2,1,0:T(8,128)(2,1)S(1)}, u32[]{:S(2)}, u32[]{:S(2)}) %collective-permute-start.16) | collective-permute-done | bytes 163872 | tf_op jit(solution)/shard_map/ppermute | solution.py:455
  129.9 0.9 copy-done.5
  131.5 2.6 %collective-permute-start.20 = (bf16[5,128,128]{2,1,0:T(8,128)(2,1)S(1)}, bf16[5,128,128]{2,1,0:T(8,128)(2,1)S(1)}, u32[]{:S(2)}, u32[]{:S(2)}) collective-permute-start(bf16[5,128,128]{2,1,0:T(8,128)(2,1)S(1)} %text_sum.1), channel_id=1, source_target_pairs={{0,48},{16,0},{32,16},{48,32},{1,49},{17,1},{33,17},{49,33},{2,50}... | collective-permute-start | bytes 491528 | tf_op jit(solution)/shard_map/ppermute | solution.py:455
  134.1 1.1 collective-permute-start.19
  135.2 2.6 %collective-permute-done.20 = bf16[5,128,128]{2,1,0:T(8,128)(2,1)S(1)} collective-permute-done((bf16[5,128,128]{2,1,0:T(8,128)(2,1)S(1)}, bf16[5,128,128]{2,1,0:T(8,128)(2,1)S(1)}, u32[]{:S(2)}, u32[]{:S(2)}) %collective-permute-start.20) | collective-permute-done | bytes 163872 | tf_op jit(solution)/shard_map/ppermute | solution.py:455
  137.8 2.0 %collective-permute-done.19 = bf16[5,128,128]{2,1,0:T(8,128)(2,1)S(1)} collective-permute-done((bf16[5,128,128]{2,1,0:T(8,128)(2,1)S(1)}, bf16[5,128,128]{2,1,0:T(8,128)(2,1)S(1)}, u32[]{:S(2)}, u32[]{:S(2)}) %collective-permute-start.19) | collective-permute-done | bytes 163872 | tf_op jit(solution)/shard_map/ppermute | solution.py:455
  139.9 4.7 %collective-permute-done.18 = bf16[5,128,128]{2,1,0:T(8,128)(2,1)S(1)} collective-permute-done((bf16[5,128,128]{2,1,0:T(8,128)(2,1)S(1)}, bf16[5,128,128]{2,1,0:T(8,128)(2,1)S(1)}, u32[]{:S(2)}, u32[]{:S(2)}) %collective-permute-start.18) | collective-permute-done | bytes 163872 | tf_op jit(solution)/shard_map/ppermute | solution.py:455
  144.6 0.9 pad_maximum_fusion.refs_0_
  146.3 1.1 collective-permute-start.21
  147.4 1.9 %collective-permute-done.21.other_ref = bf16[4,5,128,128]{3,2,1,0:T(8,128)(2,1)S(1)} collective-permute-done((bf16[4,5,128,128]{3,2,1,0:T(8,128)(2,1)}, bf16[4,5,128,128]{3,2,1,0:T(8,128)(2,1)S(1)}, u32[]{:S(2)}, u32[]{:S(2)}) %collective-permute-start.21) | collective-permute-done | bytes 655392 | tf_op jit(solution)/shard_map/ppermute | solution.py:467
  149.4 1.1 copy-done.2
  150.5 1.0 copy-done.4
  151.4 3.1 %cross_part.1 = bf16[8,5,32,128]{3,2,1,0:T(8,128)(2,1)S(1)} custom-call(s32[4]{0:T(128)S(1)} %copy-done.8, s32[4]{0:T(128)S(1)} %copy-done.13, s32[8]{0:T(128)S(1)} %copy-done.14, bf16[8,5,32,128]{3,2,1,0:T(8,128)(2,1)S(1)} %copy-done.4, bf16[4,5,128,128]{3,2,1,0:T(8,128)(2,1)S(1)} %copy-done.2, bf16[4,5,128,128]{3,2,1,0:T(8,128)(2,1)S(1)} %collective-permute-done.21.other_ref), custom_call_target="tpu_custom_call" | custom-call | tf_op jit(solution)/shard_map/cross_part/pallas_call | solution.py:334
  154.6 2.0 %last_part.1 = bf16[8,5,32,128]{3,2,1,0:T(8,128)(2,1)} custom-call(bf16[5,272,128]{2,1,0:T(8,128)(2,1)} %bitcast.72), custom_call_target="tpu_custom_call" | custom-call | tf_op jit(solution)/shard_map/last_part/pallas_call | solution.py:101
  156.6 5.0 %all-to-all-start.2 = ((bf16[8,5,32,128]{3,2,1,0:T(8,128)(2,1)}), bf16[8,5,32,128]{3,2,1,0:T(8,128)(2,1)S(1)}, u32[]{:S(2)}, u32[]{:S(2)}) async-start(bf16[8,5,32,128]{3,2,1,0:T(8,128)(2,1)} %last_part.1), calls=%async_computation.3 | async-start | bytes 655360 | tf_op jit(solution)/shard_map/all_to_all | solution.py:471
  162.0 2.4 %collective-permute-start.27 = (bf16[5,32,128]{2,1,0:T(8,128)(2,1)S(1)}, bf16[5,32,128]{2,1,0:T(8,128)(2,1)S(1)}, u32[]{:S(2)}, u32[]{:S(2)}) collective-permute-start(bf16[5,32,128]{2,1,0:T(8,128)(2,1)S(1)} %get-tuple-element.39), channel_id=1, source_target_pairs={{0,4},{2,6},{4,8},{6,10},{8,12},{10,14},{12,0},{14,2},{1,5},{3,7},... | collective-permute-start | bytes 122888 | tf_op jit(solution)/shard_map/ppermute | solution.py:469
  164.4 1.6 collective-permute-start.26
  166.1 2.7 %collective-permute-start.25 = (bf16[5,32,128]{2,1,0:T(8,128)(2,1)S(1)}, bf16[5,32,128]{2,1,0:T(8,128)(2,1)S(1)}, u32[]{:S(2)}, u32[]{:S(2)}) collective-permute-start(bf16[5,32,128]{2,1,0:T(8,128)(2,1)S(1)} %get-tuple-element.41), channel_id=1, source_target_pairs={{0,8},{2,10},{4,12},{6,14},{8,0},{10,2},{12,4},{14,6},{1,9},{3,11}... | collective-permute-start | bytes 122888 | tf_op jit(solution)/shard_map/ppermute | solution.py:469
  168.8 1.8 collective-permute-start.24
  170.6 3.3 %collective-permute-start.23 = (bf16[5,32,128]{2,1,0:T(8,128)(2,1)S(1)}, bf16[5,32,128]{2,1,0:T(8,128)(2,1)S(1)}, u32[]{:S(2)}, u32[]{:S(2)}) collective-permute-start(bf16[5,32,128]{2,1,0:T(8,128)(2,1)S(1)} %get-tuple-element.43), channel_id=1, source_target_pairs={{0,12},{2,14},{4,0},{6,2},{8,4},{10,6},{12,8},{14,10},{1,13},{3,15... | collective-permute-start | bytes 122888 | tf_op jit(solution)/shard_map/ppermute | solution.py:469
  173.9 1.2 collective-permute-start.22
  175.1 3.4 %collective-permute-done.23.refs_2_ = bf16[5,32,128]{2,1,0:T(8,128)(2,1)S(1)} collective-permute-done((bf16[5,32,128]{2,1,0:T(8,128)(2,1)S(1)}, bf16[5,32,128]{2,1,0:T(8,128)(2,1)S(1)}, u32[]{:S(2)}, u32[]{:S(2)}) %collective-permute-start.23) | collective-permute-done | bytes 40992 | tf_op jit(solution)/shard_map/ppermute | solution.py:469
  178.9 1.5 place_part.1
  (94 shorter events, 5.6 us)
Async XLA Ops:
  7.2 34.8 %copy-start = (bf16[64,40,256]{2,1,0:T(8,128)(2,1)S(1)}, bf16[64,40,256]{2,1,0:T(8,128)(2,1)}, u32[]{:S(2)}) copy-start(bf16[64,40,256]{2,1,0:T(8,128)(2,1)} %param.15) | copy-start | bytes 3932164
  7.3 1.0 copy-start.6
  8.3 0.7 copy-start.11
  8.9 20.6 %copy-start.7 = (s32[4]{0:T(128)}, s32[4]{0:T(128)S(1)}, u32[]{:S(2)}) copy-start(s32[4]{0:T(128)S(1)} %pad_add_fusion.where_ref) | copy-start | bytes 52
  9.5 8.3 %collective-permute-start = (bf16[8,4096]{1,0:T(8,128)(2,1)S(1)}, bf16[8,4096]{1,0:T(8,128)(2,1)S(1)}, u32[]{:S(2)}, u32[]{:S(2)}) collective-permute-start(bf16[8,4096]{1,0:T(8,128)(2,1)S(1)} %get-tuple-element.22), channel_id=1, source_target_pairs={{0,64},{64,128},{128,192},{192,0},{1,65},{65,129},{129,193},{193,1... | collective-permute-start | bytes 196616 | tf_op jit(solution)/shard_map/ppermute | solution.py:421
  11.7 6.1 %collective-permute-start.1 = (bf16[8,4096]{1,0:T(8,128)(2,1)S(1)}, bf16[8,4096]{1,0:T(8,128)(2,1)S(1)}, u32[]{:S(2)}, u32[]{:S(2)}) collective-permute-start(bf16[8,4096]{1,0:T(8,128)(2,1)S(1)} %get-tuple-element.23), channel_id=1, source_target_pairs={{0,128},{64,192},{128,0},{192,64},{1,129},{65,193},{129,1},{193,65... | collective-permute-start | bytes 196616 | tf_op jit(solution)/shard_map/ppermute | solution.py:421
  14.3 3.5 %collective-permute-start.2 = (bf16[8,4096]{1,0:T(8,128)(2,1)S(1)}, bf16[8,4096]{1,0:T(8,128)(2,1)S(1)}, u32[]{:S(2)}, u32[]{:S(2)}) collective-permute-start(bf16[8,4096]{1,0:T(8,128)(2,1)S(1)} %get-tuple-element.24), channel_id=1, source_target_pairs={{0,192},{64,0},{128,64},{192,128},{1,193},{65,1},{129,65},{193,129... | collective-permute-start | bytes 196616 | tf_op jit(solution)/shard_map/ppermute | solution.py:421
  17.9 0.7 copy-start.12
  20.9 15.1 %all-to-all-start = ((bf16[8,224,128]{2,1,0:T(8,128)(2,1)}), bf16[8,224,128]{2,1,0:T(8,128)(2,1)S(1)}, u32[]{:S(2)}, u32[]{:S(2)}) async-start(bf16[8,224,128]{2,1,0:T(8,128)(2,1)} %pad_maximum_fusion.1), calls=%async_computation | async-start | bytes 917504 | tf_op jit(solution)/shard_map/all_to_all | solution.py:427
  27.2 2.4 %copy-start.10 = (f32[40,128]{1,0:T(8,128)S(1)}, f32[40,128]{1,0:T(8,128)}, u32[]{:S(2)}) copy-start(f32[40,128]{1,0:T(8,128)} %param.17) | copy-start | bytes 61444
  27.2 66.8 %all-gather.3.cloned.1.call-start = ((), (), s32[]{:S(2)}) async-start(), calls=%async_computation.6 | async-start | bytes 4128768 | tf_op jit(solution)/shard_map/all_gather | solution.py:435
  31.1 1.5 copy-start.1
  36.0 0.8 copy-start.15
  36.8 57.3 %all-to-all-start.1 = ((bf16[8,5,128,256]{3,2,1,0:T(8,128)(2,1)}), bf16[8,5,128,256]{3,2,1,0:T(8,128)(2,1)}, u32[]{:S(2)}, u32[]{:S(2)}) async-start(bf16[8,5,128,256]{3,2,1,0:T(8,128)(2,1)} %bitcast.63), calls=%async_computation.1 | async-start | bytes 5242880 | tf_op jit(solution)/shard_map/all_to_all | solution.py:434
  41.9 112.7 %reduce-scatter.2.cloned.1.call-start = ((), (), s32[]{:S(2)}) async-start(), calls=%async_computation.5 | async-start | bytes 3133440 | tf_op jit(solution)/shard_map/reduce_scatter | solution.py:459
  45.1 14.2 %collective-permute-start.3 = (bf16[5,16,256]{2,1,0:T(8,128)(2,1)}, bf16[5,16,256]{2,1,0:T(8,128)(2,1)S(1)}, u32[]{:S(2)}, u32[]{:S(2)}) collective-permute-start(bf16[5,16,256]{2,1,0:T(8,128)(2,1)} %after.13), channel_id=1, source_target_pairs={{0,2},{2,4},{4,6},{6,8},{8,10},{10,12},{12,14},{14,0},{1,3},{3,5},... | collective-permute-start | bytes 122888 | tf_op jit(solution)/shard_map/ppermute | solution.py:440
  47.6 14.2 %copy-start.21 = (bf16[5,16,256]{2,1,0:T(8,128)(2,1)S(1)}, bf16[5,16,256]{2,1,0:T(8,128)(2,1)}, u32[]{:S(2)}) copy-start(bf16[5,16,256]{2,1,0:T(8,128)(2,1)} %after.19) | copy-start | bytes 122884
  47.6 14.2 %collective-permute-start.4 = (bf16[5,16,256]{2,1,0:T(8,128)(2,1)}, bf16[5,16,256]{2,1,0:T(8,128)(2,1)S(1)}, u32[]{:S(2)}, u32[]{:S(2)}) collective-permute-start(bf16[5,16,256]{2,1,0:T(8,128)(2,1)} %after.14), channel_id=1, source_target_pairs={{0,4},{2,6},{4,8},{6,10},{8,12},{10,14},{12,0},{14,2},{1,5},{3,7},... | collective-permute-start | bytes 122888 | tf_op jit(solution)/shard_map/ppermute | solution.py:440
  50.7 11.9 %collective-permute-start.5 = (bf16[5,16,256]{2,1,0:T(8,128)(2,1)}, bf16[5,16,256]{2,1,0:T(8,128)(2,1)S(1)}, u32[]{:S(2)}, u32[]{:S(2)}) collective-permute-start(bf16[5,16,256]{2,1,0:T(8,128)(2,1)} %after.15), channel_id=1, source_target_pairs={{0,6},{2,8},{4,10},{6,12},{8,14},{10,0},{12,2},{14,4},{1,7},{3,9},... | collective-permute-start | bytes 122888 | tf_op jit(solution)/shard_map/ppermute | solution.py:440
  54.4 9.0 %collective-permute-start.6 = (bf16[5,16,256]{2,1,0:T(8,128)(2,1)}, bf16[5,16,256]{2,1,0:T(8,128)(2,1)S(1)}, u32[]{:S(2)}, u32[]{:S(2)}) collective-permute-start(bf16[5,16,256]{2,1,0:T(8,128)(2,1)} %after.16), channel_id=1, source_target_pairs={{0,8},{2,10},{4,12},{6,14},{8,0},{10,2},{12,4},{14,6},{1,9},{3,11}... | collective-permute-start | bytes 122888 | tf_op jit(solution)/shard_map/ppermute | solution.py:440
  54.9 9.8 %collective-permute-start.7 = (bf16[5,16,256]{2,1,0:T(8,128)(2,1)}, bf16[5,16,256]{2,1,0:T(8,128)(2,1)S(1)}, u32[]{:S(2)}, u32[]{:S(2)}) collective-permute-start(bf16[5,16,256]{2,1,0:T(8,128)(2,1)} %after.17), channel_id=1, source_target_pairs={{0,10},{2,12},{4,14},{6,0},{8,2},{10,4},{12,6},{14,8},{1,11},{3,13... | collective-permute-start | bytes 122888 | tf_op jit(solution)/shard_map/ppermute | solution.py:440
  59.4 7.8 %collective-permute-start.8 = (bf16[5,16,256]{2,1,0:T(8,128)(2,1)}, bf16[5,16,256]{2,1,0:T(8,128)(2,1)S(1)}, u32[]{:S(2)}, u32[]{:S(2)}) collective-permute-start(bf16[5,16,256]{2,1,0:T(8,128)(2,1)} %after.18), channel_id=1, source_target_pairs={{0,12},{2,14},{4,0},{6,2},{8,4},{10,6},{12,8},{14,10},{1,13},{3,15... | collective-permute-start | bytes 122888 | tf_op jit(solution)/shard_map/ppermute | solution.py:440
  61.8 7.7 %collective-permute-start.9 = (bf16[5,16,256]{2,1,0:T(8,128)(2,1)S(1)}, bf16[5,16,256]{2,1,0:T(8,128)(2,1)S(1)}, u32[]{:S(2)}, u32[]{:S(2)}) collective-permute-start(bf16[5,16,256]{2,1,0:T(8,128)(2,1)S(1)} %copy-done.21), channel_id=1, source_target_pairs={{0,14},{2,0},{4,2},{6,4},{8,6},{10,8},{12,10},{14,12},{1,15},{3,1}... | collective-permute-start | bytes 122888 | tf_op jit(solution)/shard_map/ppermute | solution.py:440
  69.5 2.0 %collective-permute-start.10 = (bf16[8,5,16,128]{3,2,1,0:T(8,128)(2,1)S(1)}, bf16[8,5,16,128]{3,2,1,0:T(8,128)(2,1)S(1)}, u32[]{:S(2)}, u32[]{:S(2)}) collective-permute-start(bf16[8,5,16,128]{3,2,1,0:T(8,128)(2,1)S(1)} %get-tuple-element.47), channel_id=1, source_target_pairs={{0,1},{1,0},{2,3},{3,2},{4,5},{5,4},{6,7},{7,6},{8,9},{9,8},{10,11... | collective-permute-start | bytes 491528 | tf_op jit(solution)/shard_map/ppermute | solution.py:445
  71.5 22.5 %copy-start.16 = (bf16[2,8,5,16,128]{4,3,2,1,0:T(8,128)(2,1)}, bf16[2,8,5,16,128]{4,3,2,1,0:T(8,128)(2,1)S(1)}, u32[]{:S(2)}) copy-start(bf16[2,8,5,16,128]{4,3,2,1,0:T(8,128)(2,1)S(1)} %pad_maximum_fusion.2.refs_1_.w0) | copy-start | bytes 983044
  71.5 9.1 %collective-permute-start.13 = (bf16[2,8,5,16,128]{4,3,2,1,0:T(8,128)(2,1)S(1)}, bf16[2,8,5,16,128]{4,3,2,1,0:T(8,128)(2,1)S(1)}, u32[]{:S(2)}, u32[]{:S(2)}) collective-permute-start(bf16[2,8,5,16,128]{4,3,2,1,0:T(8,128)(2,1)S(1)} %pad_maximum_fusion.2.refs_1_.w0), channel_id=1, source_target_pairs={{0,192},{64,0},{128,64},{192,128},{1,193},{65,1},{129,65},{193,129... | collective-permute-start | bytes 983048 | tf_op jit(solution)/shard_map/ppermute | solution.py:447
  73.9 10.5 %collective-permute-start.11 = (bf16[2,8,5,16,128]{4,3,2,1,0:T(8,128)(2,1)S(1)}, bf16[2,8,5,16,128]{4,3,2,1,0:T(8,128)(2,1)S(1)}, u32[]{:S(2)}, u32[]{:S(2)}) collective-permute-start(bf16[2,8,5,16,128]{4,3,2,1,0:T(8,128)(2,1)S(1)} %pad_maximum_fusion.2.refs_1_.w0), channel_id=1, source_target_pairs={{0,64},{64,128},{128,192},{192,0},{1,65},{65,129},{129,193},{193,1... | collective-permute-start | bytes 983048 | tf_op jit(solution)/shard_map/ppermute | solution.py:447
  80.6 13.4 %copy-start.17 = (bf16[2,8,5,16,128]{4,3,2,1,0:T(8,128)(2,1)}, bf16[2,8,5,16,128]{4,3,2,1,0:T(8,128)(2,1)S(1)}, u32[]{:S(2)}) copy-start(bf16[2,8,5,16,128]{4,3,2,1,0:T(8,128)(2,1)S(1)} %collective-permute-done.13.refs_5_.w3) | copy-start | bytes 983044
  80.7 6.0 %collective-permute-start.14 = (bf16[8,5,16,128]{3,2,1,0:T(8,128)(2,1)S(1)}, bf16[8,5,16,128]{3,2,1,0:T(8,128)(2,1)S(1)}, u32[]{:S(2)}, u32[]{:S(2)}) collective-permute-start(bf16[8,5,16,128]{3,2,1,0:T(8,128)(2,1)S(1)} %slice_bitcast_fusion), channel_id=1, source_target_pairs={{0,192},{64,0},{128,64},{192,128},{1,193},{65,1},{129,65},{193,129... | collective-permute-start | bytes 491528 | tf_op jit(solution)/shard_map/ppermute | solution.py:450
  84.4 9.7 %copy-start.18 = (bf16[2,8,5,16,128]{4,3,2,1,0:T(8,128)(2,1)}, bf16[2,8,5,16,128]{4,3,2,1,0:T(8,128)(2,1)S(1)}, u32[]{:S(2)}) copy-start(bf16[2,8,5,16,128]{4,3,2,1,0:T(8,128)(2,1)S(1)} %collective-permute-done.11.refs_2_.w1) | copy-start | bytes 983044
  84.4 5.9 %collective-permute-start.12 = (bf16[8,5,16,128]{3,2,1,0:T(8,128)(2,1)S(1)}, bf16[8,5,16,128]{3,2,1,0:T(8,128)(2,1)S(1)}, u32[]{:S(2)}, u32[]{:S(2)}) collective-permute-start(bf16[8,5,16,128]{3,2,1,0:T(8,128)(2,1)S(1)} %slice_bitcast_fusion.1), channel_id=1, source_target_pairs={{0,64},{64,128},{128,192},{192,0},{1,65},{65,129},{129,193},{193,1... | collective-permute-start | bytes 491528 | tf_op jit(solution)/shard_map/ppermute | solution.py:449
  86.6 7.4 %copy-start.19 = (bf16[8,5,16,128]{3,2,1,0:T(8,128)(2,1)}, bf16[8,5,16,128]{3,2,1,0:T(8,128)(2,1)S(1)}, u32[]{:S(2)}) copy-start(bf16[8,5,16,128]{3,2,1,0:T(8,128)(2,1)S(1)} %collective-permute-done.14.refs_4_.w4) | copy-start | bytes 491524
  90.3 3.8 %copy-start.20 = (bf16[8,5,16,128]{3,2,1,0:T(8,128)(2,1)}, bf16[8,5,16,128]{3,2,1,0:T(8,128)(2,1)S(1)}, u32[]{:S(2)}) copy-start(bf16[8,5,16,128]{3,2,1,0:T(8,128)(2,1)S(1)} %collective-permute-done.12.refs_3_.w2) | copy-start | bytes 491524
  108.6 36.9 %all-to-all-start.3 = ((bf16[8,5,32,128]{3,2,1,0:T(8,128)(2,1)}), bf16[8,5,32,128]{3,2,1,0:T(8,128)(2,1)S(1)}, u32[]{:S(2)}, u32[]{:S(2)}) async-start(bf16[8,5,32,128]{3,2,1,0:T(8,128)(2,1)} %after.21), calls=%async_computation.4 | async-start | bytes 655360 | tf_op jit(solution)/shard_map/all_to_all | solution.py:462
  114.0 15.9 %copy-start.8 = (s32[4]{0:T(128)S(1)}, s32[4]{0:T(128)}, u32[]{:S(2)}) copy-start(s32[4]{0:T(128)} %copy-done.7) | copy-start | bytes 52
  114.0 15.9 %copy-start.9 = (f32[40,128]{1,0:T(8,128)S(1)}, f32[40,128]{1,0:T(8,128)}, u32[]{:S(2)}) copy-start(f32[40,128]{1,0:T(8,128)} %param.19) | copy-start | bytes 61444
  119.0 30.3 %copy-start.13 = (s32[4]{0:T(128)S(1)}, s32[4]{0:T(128)}, u32[]{:S(2)}) copy-start(s32[4]{0:T(128)} %requests_ref.5) | copy-start | bytes 52
  119.0 30.3 %copy-start.14 = (s32[8]{0:T(128)S(1)}, s32[8]{0:T(128)}, u32[]{:S(2)}) copy-start(s32[8]{0:T(128)} %lengths_ref.1) | copy-start | bytes 100
  119.0 6.6 %collective-permute-start.15 = (bf16[5,128,128]{2,1,0:T(8,128)(2,1)}, bf16[5,128,128]{2,1,0:T(8,128)(2,1)S(1)}, u32[]{:S(2)}, u32[]{:S(2)}) collective-permute-start(bf16[5,128,128]{2,1,0:T(8,128)(2,1)} %get-tuple-element.35), channel_id=1, source_target_pairs={{0,16},{16,32},{32,48},{48,0},{1,17},{17,33},{33,49},{49,1},{2,18}... | collective-permute-start | bytes 491528 | tf_op jit(solution)/shard_map/ppermute | solution.py:455
  120.2 9.7 %collective-permute-start.16 = (bf16[5,128,128]{2,1,0:T(8,128)(2,1)}, bf16[5,128,128]{2,1,0:T(8,128)(2,1)S(1)}, u32[]{:S(2)}, u32[]{:S(2)}) collective-permute-start(bf16[5,128,128]{2,1,0:T(8,128)(2,1)} %get-tuple-element.36), channel_id=1, source_target_pairs={{0,32},{16,48},{32,0},{48,16},{1,33},{17,49},{33,1},{49,17},{2,34}... | collective-permute-start | bytes 491528 | tf_op jit(solution)/shard_map/ppermute | solution.py:455
  122.6 7.3 %collective-permute-start.17 = (bf16[5,128,128]{2,1,0:T(8,128)(2,1)}, bf16[5,128,128]{2,1,0:T(8,128)(2,1)S(1)}, u32[]{:S(2)}, u32[]{:S(2)}) collective-permute-start(bf16[5,128,128]{2,1,0:T(8,128)(2,1)} %get-tuple-element.37), channel_id=1, source_target_pairs={{0,48},{16,0},{32,16},{48,32},{1,49},{17,1},{33,17},{49,33},{2,50}... | collective-permute-start | bytes 491528 | tf_op jit(solution)/shard_map/ppermute | solution.py:455
  129.9 0.9 copy-start.5
  131.5 6.3 %collective-permute-start.20 = (bf16[5,128,128]{2,1,0:T(8,128)(2,1)S(1)}, bf16[5,128,128]{2,1,0:T(8,128)(2,1)S(1)}, u32[]{:S(2)}, u32[]{:S(2)}) collective-permute-start(bf16[5,128,128]{2,1,0:T(8,128)(2,1)S(1)} %text_sum.1), channel_id=1, source_target_pairs={{0,48},{16,0},{32,16},{48,32},{1,49},{17,1},{33,17},{49,33},{2,50}... | collective-permute-start | bytes 491528 | tf_op jit(solution)/shard_map/ppermute | solution.py:455
  134.1 5.8 %collective-permute-start.19 = (bf16[5,128,128]{2,1,0:T(8,128)(2,1)S(1)}, bf16[5,128,128]{2,1,0:T(8,128)(2,1)S(1)}, u32[]{:S(2)}, u32[]{:S(2)}) collective-permute-start(bf16[5,128,128]{2,1,0:T(8,128)(2,1)S(1)} %text_sum.1), channel_id=1, source_target_pairs={{0,32},{16,48},{32,0},{48,16},{1,33},{17,49},{33,1},{49,17},{2,34}... | collective-permute-start | bytes 491528 | tf_op jit(solution)/shard_map/ppermute | solution.py:455
  135.2 9.4 %collective-permute-start.18 = (bf16[5,128,128]{2,1,0:T(8,128)(2,1)S(1)}, bf16[5,128,128]{2,1,0:T(8,128)(2,1)S(1)}, u32[]{:S(2)}, u32[]{:S(2)}) collective-permute-start(bf16[5,128,128]{2,1,0:T(8,128)(2,1)S(1)} %text_sum.1), channel_id=1, source_target_pairs={{0,16},{16,32},{32,48},{48,0},{1,17},{17,33},{33,49},{49,1},{2,18}... | collective-permute-start | bytes 491528 | tf_op jit(solution)/shard_map/ppermute | solution.py:455
  145.6 0.7 copy-start.3
  146.3 3.1 %collective-permute-start.21 = (bf16[4,5,128,128]{3,2,1,0:T(8,128)(2,1)}, bf16[4,5,128,128]{3,2,1,0:T(8,128)(2,1)S(1)}, u32[]{:S(2)}, u32[]{:S(2)}) collective-permute-start(bf16[4,5,128,128]{3,2,1,0:T(8,128)(2,1)} %after.23.mine_ref), channel_id=1, source_target_pairs={{0,1},{1,0},{2,3},{3,2},{4,5},{5,4},{6,7},{7,6},{8,9},{9,8},{10,11... | collective-permute-start | bytes 1966088 | tf_op jit(solution)/shard_map/ppermute | solution.py:467
  149.4 1.1 copy-start.2
  150.4 1.0 copy-start.4
  156.6 22.3 %all-to-all-start.2 = ((bf16[8,5,32,128]{3,2,1,0:T(8,128)(2,1)}), bf16[8,5,32,128]{3,2,1,0:T(8,128)(2,1)S(1)}, u32[]{:S(2)}, u32[]{:S(2)}) async-start(bf16[8,5,32,128]{3,2,1,0:T(8,128)(2,1)} %last_part.1), calls=%async_computation.3 | async-start | bytes 655360 | tf_op jit(solution)/shard_map/all_to_all | solution.py:471
  161.6 8.9 %collective-permute-start.28 = (bf16[5,32,128]{2,1,0:T(8,128)(2,1)S(1)}, bf16[5,32,128]{2,1,0:T(8,128)(2,1)S(1)}, u32[]{:S(2)}, u32[]{:S(2)}) collective-permute-start(bf16[5,32,128]{2,1,0:T(8,128)(2,1)S(1)} %get-tuple-element.38), channel_id=1, source_target_pairs={{0,2},{2,4},{4,6},{6,8},{8,10},{10,12},{12,14},{14,0},{1,3},{3,5},... | collective-permute-start | bytes 122888 | tf_op jit(solution)/shard_map/ppermute | solution.py:469
  162.0 11.9 %collective-permute-start.27 = (bf16[5,32,128]{2,1,0:T(8,128)(2,1)S(1)}, bf16[5,32,128]{2,1,0:T(8,128)(2,1)S(1)}, u32[]{:S(2)}, u32[]{:S(2)}) collective-permute-start(bf16[5,32,128]{2,1,0:T(8,128)(2,1)S(1)} %get-tuple-element.39), channel_id=1, source_target_pairs={{0,4},{2,6},{4,8},{6,10},{8,12},{10,14},{12,0},{14,2},{1,5},{3,7},... | collective-permute-start | bytes 122888 | tf_op jit(solution)/shard_map/ppermute | solution.py:469
  164.4 10.7 %collective-permute-start.26 = (bf16[5,32,128]{2,1,0:T(8,128)(2,1)S(1)}, bf16[5,32,128]{2,1,0:T(8,128)(2,1)S(1)}, u32[]{:S(2)}, u32[]{:S(2)}) collective-permute-start(bf16[5,32,128]{2,1,0:T(8,128)(2,1)S(1)} %get-tuple-element.40), channel_id=1, source_target_pairs={{0,6},{2,8},{4,10},{6,12},{8,14},{10,0},{12,2},{14,4},{1,7},{3,9},... | collective-permute-start | bytes 122888 | tf_op jit(solution)/shard_map/ppermute | solution.py:469
  166.1 9.1 %collective-permute-start.25 = (bf16[5,32,128]{2,1,0:T(8,128)(2,1)S(1)}, bf16[5,32,128]{2,1,0:T(8,128)(2,1)S(1)}, u32[]{:S(2)}, u32[]{:S(2)}) collective-permute-start(bf16[5,32,128]{2,1,0:T(8,128)(2,1)S(1)} %get-tuple-element.41), channel_id=1, source_target_pairs={{0,8},{2,10},{4,12},{6,14},{8,0},{10,2},{12,4},{14,6},{1,9},{3,11}... | collective-permute-start | bytes 122888 | tf_op jit(solution)/shard_map/ppermute | solution.py:469
  168.8 6.4 %collective-permute-start.24 = (bf16[5,32,128]{2,1,0:T(8,128)(2,1)S(1)}, bf16[5,32,128]{2,1,0:T(8,128)(2,1)S(1)}, u32[]{:S(2)}, u32[]{:S(2)}) collective-permute-start(bf16[5,32,128]{2,1,0:T(8,128)(2,1)S(1)} %get-tuple-element.42), channel_id=1, source_target_pairs={{0,10},{2,12},{4,14},{6,0},{8,2},{10,4},{12,6},{14,8},{1,11},{3,13... | collective-permute-start | bytes 122888 | tf_op jit(solution)/shard_map/ppermute | solution.py:469
  170.6 8.0 %collective-permute-start.23 = (bf16[5,32,128]{2,1,0:T(8,128)(2,1)S(1)}, bf16[5,32,128]{2,1,0:T(8,128)(2,1)S(1)}, u32[]{:S(2)}, u32[]{:S(2)}) collective-permute-start(bf16[5,32,128]{2,1,0:T(8,128)(2,1)S(1)} %get-tuple-element.43), channel_id=1, source_target_pairs={{0,12},{2,14},{4,0},{6,2},{8,4},{10,6},{12,8},{14,10},{1,13},{3,15... | collective-permute-start | bytes 122888 | tf_op jit(solution)/shard_map/ppermute | solution.py:469
  173.9 5.0 %collective-permute-start.22 = (bf16[5,32,128]{2,1,0:T(8,128)(2,1)S(1)}, bf16[5,32,128]{2,1,0:T(8,128)(2,1)S(1)}, u32[]{:S(2)}, u32[]{:S(2)}) collective-permute-start(bf16[5,32,128]{2,1,0:T(8,128)(2,1)S(1)} %get-tuple-element.44), channel_id=1, source_target_pairs={{0,14},{2,0},{4,2},{6,4},{8,6},{10,8},{12,10},{14,12},{1,15},{3,1}... | collective-permute-start | bytes 122888 | tf_op jit(solution)/shard_map/ppermute | solution.py:469
Sparse Core Ops, SparseCore 0:
  36.9 57.0 all-gather.2
  108.8 42.5 reduce-scatter.1

commit v7 on v5

--- a/solution.py
+++ b/solution.py
@@ -218,7 +218,7 @@
             out_specs=pl.BlockSpec((slots, rows, width), lambda i, w: (0, 0, 0)),
         ),
         out_shape=jax.ShapeDtypeStruct((slots, rows, width), BF16),
-        compiler_params=pltpu.CompilerParams(vmem_limit_bytes=VMEM),
+        compiler_params=pltpu.CompilerParams(vmem_limit_bytes=ALL_VMEM),
         name="text_sum",
     )(where, *parts, gains.reshape(NZ, slots, 1, width))
 
@@ -314,7 +314,7 @@
         functools.partial(cross_kernel, scale=scale),
         grid_spec=grid_spec,
         out_shape=jax.ShapeDtypeStruct(queries.shape, BF16),
-        compiler_params=pltpu.CompilerParams(vmem_limit_bytes=VMEM),
+        compiler_params=pltpu.CompilerParams(vmem_limit_bytes=ALL_VMEM),
         name="cross_part",
     )(where, requests, lengths, queries, mine, other)
 

time: 186 us -> 191 us (1.027)
  Pallas kernels: 31.4 us -> 35.9 us
    pallas_call x1, Pallas kernels: 3.14 us -> 5.84 us  [cross_part(): pl.pallas_call(functools.partial(cross_kernel, scale=scale), grid_spec=gr...]
    pallas_call x1, Pallas kernels: 0.72 us -> 2.68 us  [text_sum(): pl.pallas_call(text_sum_kernel, grid_spec=pltpu.PrefetchScalarGridSpec(nu...]
    unnamed x48 -> x46, local copies, waits for them, and re-layouts: 9.2 us -> 7.76 us
  transfers between devices with their start and end apart: 35 -> 35, of which waited for: 18 -> 18; matrix products, arithmetic and copies ran while one was open for 5% -> 6% of each run, Pallas kernels for 7% -> 9%
where the time goes in v7:
time: 191 us; the launch traced here: 190 us
  starting transfers between devices  73.4 us (38%)
  waiting for transfers between devices  50.6 us (26%)
  Pallas kernels  35.9 us (19%)
  between operations  14.3 us (7%)
  local copies, waits for them, and re-layouts  10.4 us (5%)
  other arithmetic  5.8 us (3%)
    ppermute x7, starting transfers between devices, local(): lax.ppermute(after(moved[k], got), 'z', ring(NZ, k))  16.6 us
    ppermute x6, waiting for transfers between devices, to_others(): lax.ppermute(pieces[k], 'x', ring(NX, k))  16 us
    ppermute x7, starting transfers between devices, local(): lax.ppermute(cross[k], 'z', ring(NZ, -k))  14.8 us
    pallas_call x1, Pallas kernels, self_part(): pl.pallas_call(functools.partial(self_kernel, rows=1024, keys=1024, scale...  14.5 us
    ppermute x6, starting transfers between devices, to_others(): lax.ppermute(pieces[k], 'x', ring(NX, k))  8.43 us
    unnamed x46, local copies, waits for them, and re-layouts  7.76 us
    ppermute x7, waiting for transfers between devices, local(): lax.ppermute(after(moved[k], got), 'z', ring(NZ, k))  6.88 us
    ppermute x2, waiting for transfers between devices, local(): lax.ppermute(both, 'branch', ring(4, k))  6.73 us
  transfers between devices with their start and end apart: 35, of which 18 were waited for; matrix products, arithmetic and copies ran while one was open for 6% of the time, Pallas kernels for 9%

profile of v7, /device:TPU:1, one launch (start us, length us, event | category | flops | bytes accessed | tf_op | source)
XLA Modules:
  0.0 190.4 jit_solution(8997768584087498968)
XLA Ops:
  7.2 3.8 %collective-permute-start.1 = (bf16[2,8,4096]{2,1,0:T(8,128)(2,1)}, bf16[2,8,4096]{2,1,0:T(8,128)(2,1)S(1)}, u32[]{:S(2)}, u32[]{:S(2)}) collective-permute-start(bf16[2,8,4096]{2,1,0:T(8,128)(2,1)} %b0.1), channel_id=1, source_target_pairs={{0,128},{64,192},{128,0},{192,64},{1,129},{65,193},{129,1},{193,65... | collective-permute-start | bytes 393224 | tf_op jit(solution)/shard_map/ppermute | solution.py:382
  11.4 2.3 %collective-permute-start.2 = (bf16[2,8,4096]{2,1,0:T(8,128)(2,1)}, bf16[2,8,4096]{2,1,0:T(8,128)(2,1)S(1)}, u32[]{:S(2)}, u32[]{:S(2)}) collective-permute-start(bf16[2,8,4096]{2,1,0:T(8,128)(2,1)} %b0.1), channel_id=1, source_target_pairs={{0,192},{64,0},{128,64},{192,128},{1,193},{65,1},{129,65},{193,129... | collective-permute-start | bytes 393224 | tf_op jit(solution)/shard_map/ppermute | solution.py:382
  13.7 1.5 fusion.3
  15.2 1.5 fusion.6
  16.9 1.7 collective-permute-done.b1
  19.3 0.8 pad_maximum_fusion.1
  20.1 4.6 %all-to-all-start = ((bf16[8,224,128]{2,1,0:T(8,128)(2,1)}), bf16[8,224,128]{2,1,0:T(8,128)(2,1)S(1)}, u32[]{:S(2)}, u32[]{:S(2)}) async-start(bf16[8,224,128]{2,1,0:T(8,128)(2,1)} %pad_maximum_fusion.1), calls=%async_computation | async-start | bytes 917504 | tf_op jit(solution)/shard_map/all_to_all | solution.py:388
  24.7 2.4 %copy.33 = bf16[1,128,40,256]{3,1,2,0:T(8,128)(2,1)S(1)} copy(bf16[1,128,40,256]{3,2,1,0:T(8,128)(2,1)} %param.11) | data formatting | bytes 5242880 | tf_op args[1]
  27.1 1.6 norm_keys.1.refs_1_
  28.6 1.5 copy-done.1
  30.2 3.3 %all-to-all-done.refs_0_ = bf16[8,224,128]{2,1,0:T(8,128)(2,1)S(1)} async-done(((bf16[8,224,128]{2,1,0:T(8,128)(2,1)}), bf16[8,224,128]{2,1,0:T(8,128)(2,1)S(1)}, u32[]{:S(2)}, u32[]{:S(2)}) %all-to-all-start) | async-done | bytes 458784 | tf_op jit(solution)/shard_map/all_to_all | solution.py:388
  33.5 0.8 copy-done.7
  34.2 5.1 %all-to-all-start.1 = ((bf16[8,5,128,256]{3,2,1,0:T(8,128)(2,1)}), bf16[8,5,128,256]{3,2,1,0:T(8,128)(2,1)}, u32[]{:S(2)}, u32[]{:S(2)}) async-start(bf16[8,5,128,256]{3,2,1,0:T(8,128)(2,1)} %bitcast.67), calls=%async_computation.1 | async-start | bytes 5242880 | tf_op jit(solution)/shard_map/all_to_all | solution.py:395
  39.4 0.8 copy.30
  40.2 2.4 %slice_part.1 = (bf16[5,16,256]{2,1,0:T(8,128)(2,1)}, bf16[5,16,256]{2,1,0:T(8,128)(2,1)}, bf16[5,16,256]{2,1,0:T(8,128)(2,1)}, bf16[5,16,256]{2,1,0:T(8,128)(2,...) custom-call(s32[4]{0:T(128)} %copy-done.3, ...), custom_call_target="tpu_custom_call" | custom-call | tf_op jit(solution)/shard_map/slice_part/pallas_call | solution.py:187
  42.6 1.7 collective-permute-start.3
  44.3 0.8 bitcast_dynamic-update-slice_fusion.7
  45.1 3.1 %collective-permute-start.4 = (bf16[5,16,256]{2,1,0:T(8,128)(2,1)}, bf16[5,16,256]{2,1,0:T(8,128)(2,1)S(1)}, u32[]{:S(2)}, u32[]{:S(2)}) collective-permute-start(bf16[5,16,256]{2,1,0:T(8,128)(2,1)} %after.14), channel_id=1, source_target_pairs={{0,4},{2,6},{4,8},{6,10},{8,12},{10,14},{12,0},{14,2},{1,5},{3,7},... | collective-permute-start | bytes 122888 | tf_op jit(solution)/shard_map/ppermute | solution.py:401
  48.1 3.8 %collective-permute-start.5 = (bf16[5,16,256]{2,1,0:T(8,128)(2,1)}, bf16[5,16,256]{2,1,0:T(8,128)(2,1)S(1)}, u32[]{:S(2)}, u32[]{:S(2)}) collective-permute-start(bf16[5,16,256]{2,1,0:T(8,128)(2,1)} %after.15), channel_id=1, source_target_pairs={{0,6},{2,8},{4,10},{6,12},{8,14},{10,0},{12,2},{14,4},{1,7},{3,9},... | collective-permute-start | bytes 122888 | tf_op jit(solution)/shard_map/ppermute | solution.py:401
  52.4 4.5 %collective-permute-start.7 = (bf16[5,16,256]{2,1,0:T(8,128)(2,1)}, bf16[5,16,256]{2,1,0:T(8,128)(2,1)S(1)}, u32[]{:S(2)}, u32[]{:S(2)}) collective-permute-start(bf16[5,16,256]{2,1,0:T(8,128)(2,1)} %after.17), channel_id=1, source_target_pairs={{0,10},{2,12},{4,14},{6,0},{8,2},{10,4},{12,6},{14,8},{1,11},{3,13... | collective-permute-start | bytes 122888 | tf_op jit(solution)/shard_map/ppermute | solution.py:401
  56.8 2.4 %collective-permute-start.8 = (bf16[5,16,256]{2,1,0:T(8,128)(2,1)}, bf16[5,16,256]{2,1,0:T(8,128)(2,1)S(1)}, u32[]{:S(2)}, u32[]{:S(2)}) collective-permute-start(bf16[5,16,256]{2,1,0:T(8,128)(2,1)} %after.18), channel_id=1, source_target_pairs={{0,12},{2,14},{4,0},{6,2},{8,4},{10,6},{12,8},{14,10},{1,13},{3,15... | collective-permute-start | bytes 122888 | tf_op jit(solution)/shard_map/ppermute | solution.py:401
  59.2 0.8 collective-permute-start.9
  60.8 2.6 %collective-permute-done.7 = bf16[5,16,256]{2,1,0:T(8,128)(2,1)S(1)} collective-permute-done((bf16[5,16,256]{2,1,0:T(8,128)(2,1)}, bf16[5,16,256]{2,1,0:T(8,128)(2,1)S(1)}, u32[]{:S(2)}, u32[]{:S(2)}) %collective-permute-start.7) | collective-permute-done | bytes 40992 | tf_op jit(solution)/shard_map/ppermute | solution.py:401
  63.4 1.0 collective-permute-done.8
  64.4 2.5 %collective-permute-done.9 = bf16[5,16,256]{2,1,0:T(8,128)(2,1)S(1)} collective-permute-done((bf16[5,16,256]{2,1,0:T(8,128)(2,1)S(1)}, bf16[5,16,256]{2,1,0:T(8,128)(2,1)S(1)}, u32[]{:S(2)}, u32[]{:S(2)}) %collective-permute-start.9) | collective-permute-done | bytes 40992 | tf_op jit(solution)/shard_map/ppermute | solution.py:401
  67.0 1.0 collective-permute-start.10
  67.9 1.0 collective-permute-done.10
  69.0 2.8 %collective-permute-start.13 = (bf16[2,8,5,16,128]{4,3,2,1,0:T(8,128)(2,1)S(1)}, bf16[2,8,5,16,128]{4,3,2,1,0:T(8,128)(2,1)S(1)}, u32[]{:S(2)}, u32[]{:S(2)}) collective-permute-start(bf16[2,8,5,16,128]{4,3,2,1,0:T(8,128)(2,1)S(1)} %pad_maximum_fusion.2.refs_1_.w0), channel_id=1, source_target_pairs={{0,192},{64,0},{128,64},{192,128},{1,193},{65,1},{129,65},{193,129... | collective-permute-start | bytes 983048 | tf_op jit(solution)/shard_map/ppermute | solution.py:408
  71.8 6.7 %collective-permute-done.13.refs_5_.w3 = bf16[2,8,5,16,128]{4,3,2,1,0:T(8,128)(2,1)S(1)} collective-permute-done((bf16[2,8,5,16,128]{4,3,2,1,0:T(8,128)(2,1)S(1)}, bf16[2,8,5,16,128]{4,3,2,1,0:T(8,128)(2,1)S(1)}, u32[]{:S(2)}, u32[]{:S(2)}) %collective-permute-start.13) | collective-permute-done | bytes 327712 | tf_op jit(solution)/shard_map/ppermute | solution.py:408
  78.6 3.8 %collective-permute-start.14 = (bf16[8,5,16,128]{3,2,1,0:T(8,128)(2,1)S(1)}, bf16[8,5,16,128]{3,2,1,0:T(8,128)(2,1)S(1)}, u32[]{:S(2)}, u32[]{:S(2)}) collective-permute-start(bf16[8,5,16,128]{3,2,1,0:T(8,128)(2,1)S(1)} %slice_bitcast_fusion), channel_id=1, source_target_pairs={{0,192},{64,0},{128,64},{192,128},{1,193},{65,1},{129,65},{193,129... | collective-permute-start | bytes 491528 | tf_op jit(solution)/shard_map/ppermute | solution.py:411
  82.5 2.2 %collective-permute-done.14.refs_4_.w4 = bf16[8,5,16,128]{3,2,1,0:T(8,128)(2,1)S(1)} collective-permute-done((bf16[8,5,16,128]{3,2,1,0:T(8,128)(2,1)S(1)}, bf16[8,5,16,128]{3,2,1,0:T(8,128)(2,1)S(1)}, u32[]{:S(2)}, u32[]{:S(2)}) %collective-permute-start.14) | collective-permute-done | bytes 163872 | tf_op jit(solution)/shard_map/ppermute | solution.py:411
  84.6 3.6 %collective-permute-done.12.refs_3_.w2 = bf16[8,5,16,128]{3,2,1,0:T(8,128)(2,1)S(1)} collective-permute-done((bf16[8,5,16,128]{3,2,1,0:T(8,128)(2,1)S(1)}, bf16[8,5,16,128]{3,2,1,0:T(8,128)(2,1)S(1)}, u32[]{:S(2)}, u32[]{:S(2)}) %collective-permute-start.12) | collective-permute-done | bytes 163872 | tf_op jit(solution)/shard_map/ppermute | solution.py:410
  88.2 3.5 %all-gather.3.cloned.1.call-done = bf16[64,224,128]{2,1,0:T(8,128)(2,1)} async-done(((bf16[8,224,128]{2,1,0:T(8,128)(2,1)}), bf16[64,224,128]{2,1,0:T(8,128)(2,1)}) %all-gather.3.cloned.1.call-update) | async-done | bytes 3670032 | tf_op jit(solution)/shard_map/all_gather | solution.py:396
  91.8 14.5 %self_part.1.refs_1_ = bf16[8,5,272,128]{3,2,1,0:T(8,128)(2,1)} custom-call(bf16[8,8,224,128]{3,2,1,0:T(8,128)(2,1)} %after.20.q_ref.refs_0_, bf16[8,5,128,256]{3,2,1,0:T(8,128)(2,1)} %all-to-all-done.1.kv_ref), custom_call_target="tpu_custom_call" | custom-call | flops 8053063680 | bytes 6291456 | tf_op jit(solution)/shard_map/self_part/pallas_call | solution.py:69
  106.3 0.8 copy.31
  107.1 4.9 %all-to-all-start.3 = ((bf16[8,5,32,128]{3,2,1,0:T(8,128)(2,1)}), bf16[8,5,32,128]{3,2,1,0:T(8,128)(2,1)S(1)}, u32[]{:S(2)}, u32[]{:S(2)}) async-start(bf16[8,5,32,128]{3,2,1,0:T(8,128)(2,1)} %after.21), calls=%async_computation.4 | async-start | bytes 655360 | tf_op jit(solution)/shard_map/all_to_all | solution.py:423
  112.0 4.9 %text_part.1 = (bf16[5,128,128]{2,1,0:T(8,128)(2,1)}, bf16[5,128,128]{2,1,0:T(8,128)(2,1)}, bf16[5,128,128]{2,1,0:T(8,128)(2,1)}, bf16[5,128,128]{2,1,0:T(8,128)(2,1)}) custom-call(s32[4]{0:T(128)} %copy-done.3, bf16[8,8,224,128]{3,2,1,0:T(8,128)(2,1)} %after.22.low_ref.high_ref, bf16[8,8,224,128]{3,2,1,0:T(8,128)(2,1)} %after.22.low_ref.high_ref, ...), custom_call_target="tpu_custom_call" | custom-call | tf_op jit(solution)/shard_map/text_part/pallas_call | solution.py:274
  116.9 1.8 collective-permute-start.15
  118.6 2.4 %collective-permute-start.16 = (bf16[5,128,128]{2,1,0:T(8,128)(2,1)}, bf16[5,128,128]{2,1,0:T(8,128)(2,1)S(1)}, u32[]{:S(2)}, u32[]{:S(2)}) collective-permute-start(bf16[5,128,128]{2,1,0:T(8,128)(2,1)} %get-tuple-element.24), channel_id=1, source_target_pairs={{0,32},{16,48},{32,0},{48,16},{1,33},{17,49},{33,1},{49,17},{2,34}... | collective-permute-start | bytes 491528 | tf_op jit(solution)/shard_map/ppermute | solution.py:416
  121.1 1.2 collective-permute-start.17
  122.2 1.6 collective-permute-done.15.p1
  123.9 4.4 %collective-permute-done.16.p2 = bf16[5,128,128]{2,1,0:T(8,128)(2,1)S(1)} collective-permute-done((bf16[5,128,128]{2,1,0:T(8,128)(2,1)}, bf16[5,128,128]{2,1,0:T(8,128)(2,1)S(1)}, u32[]{:S(2)}, u32[]{:S(2)}) %collective-permute-start.16) | collective-permute-done | bytes 163872 | tf_op jit(solution)/shard_map/ppermute | solution.py:416
  129.0 2.7 %text_sum.1 = bf16[5,128,128]{2,1,0:T(8,128)(2,1)} custom-call(s32[4]{0:T(128)} %copy-done.3, bf16[5,128,128]{2,1,0:T(8,128)(2,1)} %get-tuple-element.22.p0, bf16[5,128,128]{2,1,0:T(8,128)(2,1)} %copy-done.15, bf16[5,128,128]{2,1,0:T(8,128)(2,1)} %copy-done.16, bf16[5,128,128]{2,1,0:T(8,128)(2,1)} %copy-done.17, f32[8,5,1,128]{3,2,1,0:T(1,128)} %bitcast.82), custom_call_target="tpu_custom_call" | custom-call | tf_op jit(solution)/shard_map/text_sum/pallas_call | solution.py:211
  131.7 2.2 %collective-permute-start.20 = (bf16[5,128,128]{2,1,0:T(8,128)(2,1)}, bf16[5,128,128]{2,1,0:T(8,128)(2,1)S(1)}, u32[]{:S(2)}, u32[]{:S(2)}) collective-permute-start(bf16[5,128,128]{2,1,0:T(8,128)(2,1)} %text_sum.1), channel_id=1, source_target_pairs={{0,48},{16,0},{32,16},{48,32},{1,49},{17,1},{33,17},{49,33},{2,50}... | collective-permute-start | bytes 491528 | tf_op jit(solution)/shard_map/ppermute | solution.py:416
  134.8 3.9 %collective-permute-done.20 = bf16[5,128,128]{2,1,0:T(8,128)(2,1)S(1)} collective-permute-done((bf16[5,128,128]{2,1,0:T(8,128)(2,1)}, bf16[5,128,128]{2,1,0:T(8,128)(2,1)S(1)}, u32[]{:S(2)}, u32[]{:S(2)}) %collective-permute-start.20) | collective-permute-done | bytes 163872 | tf_op jit(solution)/shard_map/ppermute | solution.py:416
  138.7 1.2 collective-permute-done.19
  139.9 4.9 %collective-permute-done.18 = bf16[5,128,128]{2,1,0:T(8,128)(2,1)S(1)} collective-permute-done((bf16[5,128,128]{2,1,0:T(8,128)(2,1)}, bf16[5,128,128]{2,1,0:T(8,128)(2,1)S(1)}, u32[]{:S(2)}, u32[]{:S(2)}) %collective-permute-start.18) | collective-permute-done | bytes 163872 | tf_op jit(solution)/shard_map/ppermute | solution.py:416
  144.7 1.9 pad_maximum_fusion.refs_0_
  147.3 1.0 collective-permute-start.21
  148.3 1.9 %collective-permute-done.21.other_ref = bf16[4,5,128,128]{3,2,1,0:T(8,128)(2,1)S(1)} collective-permute-done((bf16[4,5,128,128]{3,2,1,0:T(8,128)(2,1)}, bf16[4,5,128,128]{3,2,1,0:T(8,128)(2,1)S(1)}, u32[]{:S(2)}, u32[]{:S(2)}) %collective-permute-start.21) | collective-permute-done | bytes 655392 | tf_op jit(solution)/shard_map/ppermute | solution.py:428
  150.3 0.8 copy-done.12
  151.1 5.8 %cross_part.1 = bf16[8,5,32,128]{3,2,1,0:T(8,128)(2,1)} custom-call(s32[4]{0:T(128)} %copy-done.3, s32[4]{0:T(128)} %requests_ref.3, s32[8]{0:T(128)} %lengths_ref.1, bf16[8,5,32,128]{3,2,1,0:T(8,128)(2,1)} %copy-done.9, bf16[4,5,128,128]{3,2,1,0:T(8,128)(2,1)} %after.23.mine_ref, bf16[4,5,128,128]{3,2,1,0:T(8,128)(2,1)} %copy-done.12), custom_call_target="tpu_custom_call" | custom-call | tf_op jit(solution)/shard_map/cross_part/pallas_call | solution.py:313
  156.9 2.0 %last_part.1 = bf16[8,5,32,128]{3,2,1,0:T(8,128)(2,1)} custom-call(bf16[5,272,128]{2,1,0:T(8,128)(2,1)} %bitcast.77), custom_call_target="tpu_custom_call" | custom-call | tf_op jit(solution)/shard_map/last_part/pallas_call | solution.py:101
  158.9 3.7 %all-to-all-start.2 = ((bf16[8,5,32,128]{3,2,1,0:T(8,128)(2,1)}), bf16[8,5,32,128]{3,2,1,0:T(8,128)(2,1)S(1)}, u32[]{:S(2)}, u32[]{:S(2)}) async-start(bf16[8,5,32,128]{3,2,1,0:T(8,128)(2,1)} %last_part.1), calls=%async_computation.3 | async-start | bytes 655360 | tf_op jit(solution)/shard_map/all_to_all | solution.py:432
  162.6 0.9 slice_bitcast_fusion.2
  163.6 1.3 collective-permute-start.28
  164.8 2.2 %collective-permute-start.27 = (bf16[5,32,128]{2,1,0:T(8,128)(2,1)S(1)}, bf16[5,32,128]{2,1,0:T(8,128)(2,1)S(1)}, u32[]{:S(2)}, u32[]{:S(2)}) collective-permute-start(bf16[5,32,128]{2,1,0:T(8,128)(2,1)S(1)} %get-tuple-element.31), channel_id=1, source_target_pairs={{0,4},{2,6},{4,8},{6,10},{8,12},{10,14},{12,0},{14,2},{1,5},{3,7},... | collective-permute-start | bytes 122888 | tf_op jit(solution)/shard_map/ppermute | solution.py:430
  167.0 2.3 %collective-permute-start.26 = (bf16[5,32,128]{2,1,0:T(8,128)(2,1)S(1)}, bf16[5,32,128]{2,1,0:T(8,128)(2,1)S(1)}, u32[]{:S(2)}, u32[]{:S(2)}) collective-permute-start(bf16[5,32,128]{2,1,0:T(8,128)(2,1)S(1)} %get-tuple-element.32), channel_id=1, source_target_pairs={{0,6},{2,8},{4,10},{6,12},{8,14},{10,0},{12,2},{14,4},{1,7},{3,9},... | collective-permute-start | bytes 122888 | tf_op jit(solution)/shard_map/ppermute | solution.py:430
  169.3 2.1 %collective-permute-start.25 = (bf16[5,32,128]{2,1,0:T(8,128)(2,1)S(1)}, bf16[5,32,128]{2,1,0:T(8,128)(2,1)S(1)}, u32[]{:S(2)}, u32[]{:S(2)}) collective-permute-start(bf16[5,32,128]{2,1,0:T(8,128)(2,1)S(1)} %get-tuple-element.33), channel_id=1, source_target_pairs={{0,8},{2,10},{4,12},{6,14},{8,0},{10,2},{12,4},{14,6},{1,9},{3,11}... | collective-permute-start | bytes 122888 | tf_op jit(solution)/shard_map/ppermute | solution.py:430
  171.4 2.5 %collective-permute-start.24 = (bf16[5,32,128]{2,1,0:T(8,128)(2,1)S(1)}, bf16[5,32,128]{2,1,0:T(8,128)(2,1)S(1)}, u32[]{:S(2)}, u32[]{:S(2)}) collective-permute-start(bf16[5,32,128]{2,1,0:T(8,128)(2,1)S(1)} %get-tuple-element.34), channel_id=1, source_target_pairs={{0,10},{2,12},{4,14},{6,0},{8,2},{10,4},{12,6},{14,8},{1,11},{3,13... | collective-permute-start | bytes 122888 | tf_op jit(solution)/shard_map/ppermute | solution.py:430
  173.9 3.3 %collective-permute-start.23 = (bf16[5,32,128]{2,1,0:T(8,128)(2,1)S(1)}, bf16[5,32,128]{2,1,0:T(8,128)(2,1)S(1)}, u32[]{:S(2)}, u32[]{:S(2)}) collective-permute-start(bf16[5,32,128]{2,1,0:T(8,128)(2,1)S(1)} %get-tuple-element.35), channel_id=1, source_target_pairs={{0,12},{2,14},{4,0},{6,2},{8,4},{10,6},{12,8},{14,10},{1,13},{3,15... | collective-permute-start | bytes 122888 | tf_op jit(solution)/shard_map/ppermute | solution.py:430
  177.2 1.2 collective-permute-start.22
  178.4 3.7 %collective-permute-done.23.refs_2_ = bf16[5,32,128]{2,1,0:T(8,128)(2,1)S(1)} collective-permute-done((bf16[5,32,128]{2,1,0:T(8,128)(2,1)S(1)}, bf16[5,32,128]{2,1,0:T(8,128)(2,1)S(1)}, u32[]{:S(2)}, u32[]{:S(2)}) %collective-permute-start.23) | collective-permute-done | bytes 40992 | tf_op jit(solution)/shard_map/ppermute | solution.py:430
  182.1 1.5 place_part.1
  (91 shorter events, 5.0 us)
Async XLA Ops:
  7.2 32.2 %copy-start = (bf16[64,40,256]{2,1,0:T(8,128)(2,1)S(1)}, bf16[64,40,256]{2,1,0:T(8,128)(2,1)}, u32[]{:S(2)}) copy-start(bf16[64,40,256]{2,1,0:T(8,128)(2,1)} %param.15) | copy-start | bytes 3932164
  7.2 11.4 %copy-start.2 = (bf16[2,8,4096]{2,1,0:T(8,128)(2,1)S(1)}, bf16[2,8,4096]{2,1,0:T(8,128)(2,1)}, u32[]{:S(2)}) copy-start(bf16[2,8,4096]{2,1,0:T(8,128)(2,1)} %b0.1) | copy-start | bytes 393220
  7.2 11.4 %copy-start.6 = (s32[4]{0:T(128)S(1)}, s32[4]{0:T(128)}, u32[]{:S(2)}) copy-start(s32[4]{0:T(128)} %requests_ref.3) | copy-start | bytes 52
  7.2 9.7 %collective-permute-start.1 = (bf16[2,8,4096]{2,1,0:T(8,128)(2,1)}, bf16[2,8,4096]{2,1,0:T(8,128)(2,1)S(1)}, u32[]{:S(2)}, u32[]{:S(2)}) collective-permute-start(bf16[2,8,4096]{2,1,0:T(8,128)(2,1)} %b0.1), channel_id=1, source_target_pairs={{0,128},{64,192},{128,0},{192,64},{1,129},{65,193},{129,1},{193,65... | collective-permute-start | bytes 393224 | tf_op jit(solution)/shard_map/ppermute | solution.py:382
  11.0 7.6 %collective-permute-start = (bf16[2,8,4096]{2,1,0:T(8,128)(2,1)}, bf16[2,8,4096]{2,1,0:T(8,128)(2,1)S(1)}, u32[]{:S(2)}, u32[]{:S(2)}) collective-permute-start(bf16[2,8,4096]{2,1,0:T(8,128)(2,1)} %b0.1), channel_id=1, source_target_pairs={{0,64},{64,128},{128,192},{192,0},{1,65},{65,129},{129,193},{193,1... | collective-permute-start | bytes 393224 | tf_op jit(solution)/shard_map/ppermute | solution.py:382
  11.4 7.2 %collective-permute-start.2 = (bf16[2,8,4096]{2,1,0:T(8,128)(2,1)}, bf16[2,8,4096]{2,1,0:T(8,128)(2,1)S(1)}, u32[]{:S(2)}, u32[]{:S(2)}) collective-permute-start(bf16[2,8,4096]{2,1,0:T(8,128)(2,1)} %b0.1), channel_id=1, source_target_pairs={{0,192},{64,0},{128,64},{192,128},{1,193},{65,1},{129,65},{193,129... | collective-permute-start | bytes 393224 | tf_op jit(solution)/shard_map/ppermute | solution.py:382
  16.9 10.2 %copy-start.3 = (s32[4]{0:T(128)}, s32[4]{0:T(128)S(1)}, u32[]{:S(2)}) copy-start(s32[4]{0:T(128)S(1)} %pad_add_fusion.where_ref) | copy-start | bytes 52
  20.1 13.4 %all-to-all-start = ((bf16[8,224,128]{2,1,0:T(8,128)(2,1)}), bf16[8,224,128]{2,1,0:T(8,128)(2,1)S(1)}, u32[]{:S(2)}, u32[]{:S(2)}) async-start(bf16[8,224,128]{2,1,0:T(8,128)(2,1)} %pad_maximum_fusion.1), calls=%async_computation | async-start | bytes 917504 | tf_op jit(solution)/shard_map/all_to_all | solution.py:388
  24.7 2.4 %copy-start.5 = (f32[40,128]{1,0:T(8,128)S(1)}, f32[40,128]{1,0:T(8,128)}, u32[]{:S(2)}) copy-start(f32[40,128]{1,0:T(8,128)} %param.17) | copy-start | bytes 61444
  24.7 67.0 %all-gather.3.cloned.1.call-start = ((), (), s32[]{:S(2)}) async-start(), calls=%async_computation.6 | async-start | bytes 4128768 | tf_op jit(solution)/shard_map/all_gather | solution.py:396
  28.6 1.5 copy-start.1
  33.5 0.8 copy-start.7
  34.2 57.5 %all-to-all-start.1 = ((bf16[8,5,128,256]{3,2,1,0:T(8,128)(2,1)}), bf16[8,5,128,256]{3,2,1,0:T(8,128)(2,1)}, u32[]{:S(2)}, u32[]{:S(2)}) async-start(bf16[8,5,128,256]{3,2,1,0:T(8,128)(2,1)} %bitcast.67), calls=%async_computation.1 | async-start | bytes 5242880 | tf_op jit(solution)/shard_map/all_to_all | solution.py:395
  39.4 117.5 %reduce-scatter.2.cloned.1.call-start = ((), (), s32[]{:S(2)}) async-start(), calls=%async_computation.5 | async-start | bytes 3133440 | tf_op jit(solution)/shard_map/reduce_scatter | solution.py:420
  42.6 14.2 %collective-permute-start.3 = (bf16[5,16,256]{2,1,0:T(8,128)(2,1)}, bf16[5,16,256]{2,1,0:T(8,128)(2,1)S(1)}, u32[]{:S(2)}, u32[]{:S(2)}) collective-permute-start(bf16[5,16,256]{2,1,0:T(8,128)(2,1)} %after.13), channel_id=1, source_target_pairs={{0,2},{2,4},{4,6},{6,8},{8,10},{10,12},{12,14},{14,0},{1,3},{3,5},... | collective-permute-start | bytes 122888 | tf_op jit(solution)/shard_map/ppermute | solution.py:401
  45.0 14.2 %copy-start.18 = (bf16[5,16,256]{2,1,0:T(8,128)(2,1)S(1)}, bf16[5,16,256]{2,1,0:T(8,128)(2,1)}, u32[]{:S(2)}) copy-start(bf16[5,16,256]{2,1,0:T(8,128)(2,1)} %after.19) | copy-start | bytes 122884
  45.1 14.2 %collective-permute-start.4 = (bf16[5,16,256]{2,1,0:T(8,128)(2,1)}, bf16[5,16,256]{2,1,0:T(8,128)(2,1)S(1)}, u32[]{:S(2)}, u32[]{:S(2)}) collective-permute-start(bf16[5,16,256]{2,1,0:T(8,128)(2,1)} %after.14), channel_id=1, source_target_pairs={{0,4},{2,6},{4,8},{6,10},{8,12},{10,14},{12,0},{14,2},{1,5},{3,7},... | collective-permute-start | bytes 122888 | tf_op jit(solution)/shard_map/ppermute | solution.py:401
  48.1 11.9 %collective-permute-start.5 = (bf16[5,16,256]{2,1,0:T(8,128)(2,1)}, bf16[5,16,256]{2,1,0:T(8,128)(2,1)S(1)}, u32[]{:S(2)}, u32[]{:S(2)}) collective-permute-start(bf16[5,16,256]{2,1,0:T(8,128)(2,1)} %after.15), channel_id=1, source_target_pairs={{0,6},{2,8},{4,10},{6,12},{8,14},{10,0},{12,2},{14,4},{1,7},{3,9},... | collective-permute-start | bytes 122888 | tf_op jit(solution)/shard_map/ppermute | solution.py:401
  51.9 8.9 %collective-permute-start.6 = (bf16[5,16,256]{2,1,0:T(8,128)(2,1)}, bf16[5,16,256]{2,1,0:T(8,128)(2,1)S(1)}, u32[]{:S(2)}, u32[]{:S(2)}) collective-permute-start(bf16[5,16,256]{2,1,0:T(8,128)(2,1)} %after.16), channel_id=1, source_target_pairs={{0,8},{2,10},{4,12},{6,14},{8,0},{10,2},{12,4},{14,6},{1,9},{3,11}... | collective-permute-start | bytes 122888 | tf_op jit(solution)/shard_map/ppermute | solution.py:401
  52.4 11.0 %collective-permute-start.7 = (bf16[5,16,256]{2,1,0:T(8,128)(2,1)}, bf16[5,16,256]{2,1,0:T(8,128)(2,1)S(1)}, u32[]{:S(2)}, u32[]{:S(2)}) collective-permute-start(bf16[5,16,256]{2,1,0:T(8,128)(2,1)} %after.17), channel_id=1, source_target_pairs={{0,10},{2,12},{4,14},{6,0},{8,2},{10,4},{12,6},{14,8},{1,11},{3,13... | collective-permute-start | bytes 122888 | tf_op jit(solution)/shard_map/ppermute | solution.py:401
  56.8 7.6 %collective-permute-start.8 = (bf16[5,16,256]{2,1,0:T(8,128)(2,1)}, bf16[5,16,256]{2,1,0:T(8,128)(2,1)S(1)}, u32[]{:S(2)}, u32[]{:S(2)}) collective-permute-start(bf16[5,16,256]{2,1,0:T(8,128)(2,1)} %after.18), channel_id=1, source_target_pairs={{0,12},{2,14},{4,0},{6,2},{8,4},{10,6},{12,8},{14,10},{1,13},{3,15... | collective-permute-start | bytes 122888 | tf_op jit(solution)/shard_map/ppermute | solution.py:401
  59.2 7.7 %collective-permute-start.9 = (bf16[5,16,256]{2,1,0:T(8,128)(2,1)S(1)}, bf16[5,16,256]{2,1,0:T(8,128)(2,1)S(1)}, u32[]{:S(2)}, u32[]{:S(2)}) collective-permute-start(bf16[5,16,256]{2,1,0:T(8,128)(2,1)S(1)} %copy-done.18), channel_id=1, source_target_pairs={{0,14},{2,0},{4,2},{6,4},{8,6},{10,8},{12,10},{14,12},{1,15},{3,1}... | collective-permute-start | bytes 122888 | tf_op jit(solution)/shard_map/ppermute | solution.py:401
  67.0 2.0 %collective-permute-start.10 = (bf16[8,5,16,128]{3,2,1,0:T(8,128)(2,1)S(1)}, bf16[8,5,16,128]{3,2,1,0:T(8,128)(2,1)S(1)}, u32[]{:S(2)}, u32[]{:S(2)}) collective-permute-start(bf16[8,5,16,128]{3,2,1,0:T(8,128)(2,1)S(1)} %get-tuple-element.39), channel_id=1, source_target_pairs={{0,1},{1,0},{2,3},{3,2},{4,5},{5,4},{6,7},{7,6},{8,9},{9,8},{10,11... | collective-permute-start | bytes 491528 | tf_op jit(solution)/shard_map/ppermute | solution.py:406
  69.0 22.7 %copy-start.8 = (bf16[2,8,5,16,128]{4,3,2,1,0:T(8,128)(2,1)}, bf16[2,8,5,16,128]{4,3,2,1,0:T(8,128)(2,1)S(1)}, u32[]{:S(2)}) copy-start(bf16[2,8,5,16,128]{4,3,2,1,0:T(8,128)(2,1)S(1)} %pad_maximum_fusion.2.refs_1_.w0) | copy-start | bytes 983044
  69.0 9.6 %collective-permute-start.13 = (bf16[2,8,5,16,128]{4,3,2,1,0:T(8,128)(2,1)S(1)}, bf16[2,8,5,16,128]{4,3,2,1,0:T(8,128)(2,1)S(1)}, u32[]{:S(2)}, u32[]{:S(2)}) collective-permute-start(bf16[2,8,5,16,128]{4,3,2,1,0:T(8,128)(2,1)S(1)} %pad_maximum_fusion.2.refs_1_.w0), channel_id=1, source_target_pairs={{0,192},{64,0},{128,64},{192,128},{1,193},{65,1},{129,65},{193,129... | collective-permute-start | bytes 983048 | tf_op jit(solution)/shard_map/ppermute | solution.py:408
  71.8 10.5 %collective-permute-start.11 = (bf16[2,8,5,16,128]{4,3,2,1,0:T(8,128)(2,1)S(1)}, bf16[2,8,5,16,128]{4,3,2,1,0:T(8,128)(2,1)S(1)}, u32[]{:S(2)}, u32[]{:S(2)}) collective-permute-start(bf16[2,8,5,16,128]{4,3,2,1,0:T(8,128)(2,1)S(1)} %pad_maximum_fusion.2.refs_1_.w0), channel_id=1, source_target_pairs={{0,64},{64,128},{128,192},{192,0},{1,65},{65,129},{129,193},{193,1... | collective-permute-start | bytes 983048 | tf_op jit(solution)/shard_map/ppermute | solution.py:408
  78.6 13.1 %copy-start.10 = (bf16[2,8,5,16,128]{4,3,2,1,0:T(8,128)(2,1)}, bf16[2,8,5,16,128]{4,3,2,1,0:T(8,128)(2,1)S(1)}, u32[]{:S(2)}) copy-start(bf16[2,8,5,16,128]{4,3,2,1,0:T(8,128)(2,1)S(1)} %collective-permute-done.13.refs_5_.w3) | copy-start | bytes 983044
  78.6 6.0 %collective-permute-start.14 = (bf16[8,5,16,128]{3,2,1,0:T(8,128)(2,1)S(1)}, bf16[8,5,16,128]{3,2,1,0:T(8,128)(2,1)S(1)}, u32[]{:S(2)}, u32[]{:S(2)}) collective-permute-start(bf16[8,5,16,128]{3,2,1,0:T(8,128)(2,1)S(1)} %slice_bitcast_fusion), channel_id=1, source_target_pairs={{0,192},{64,0},{128,64},{192,128},{1,193},{65,1},{129,65},{193,129... | collective-permute-start | bytes 491528 | tf_op jit(solution)/shard_map/ppermute | solution.py:411
  82.4 9.4 %copy-start.11 = (bf16[2,8,5,16,128]{4,3,2,1,0:T(8,128)(2,1)}, bf16[2,8,5,16,128]{4,3,2,1,0:T(8,128)(2,1)S(1)}, u32[]{:S(2)}) copy-start(bf16[2,8,5,16,128]{4,3,2,1,0:T(8,128)(2,1)S(1)} %collective-permute-done.11.refs_2_.w1) | copy-start | bytes 983044
  82.4 5.9 %collective-permute-start.12 = (bf16[8,5,16,128]{3,2,1,0:T(8,128)(2,1)S(1)}, bf16[8,5,16,128]{3,2,1,0:T(8,128)(2,1)S(1)}, u32[]{:S(2)}, u32[]{:S(2)}) collective-permute-start(bf16[8,5,16,128]{3,2,1,0:T(8,128)(2,1)S(1)} %slice_bitcast_fusion.1), channel_id=1, source_target_pairs={{0,64},{64,128},{128,192},{192,0},{1,65},{65,129},{129,193},{193,1... | collective-permute-start | bytes 491528 | tf_op jit(solution)/shard_map/ppermute | solution.py:410
  84.6 7.1 %copy-start.13 = (bf16[8,5,16,128]{3,2,1,0:T(8,128)(2,1)}, bf16[8,5,16,128]{3,2,1,0:T(8,128)(2,1)S(1)}, u32[]{:S(2)}) copy-start(bf16[8,5,16,128]{3,2,1,0:T(8,128)(2,1)S(1)} %collective-permute-done.14.refs_4_.w4) | copy-start | bytes 491524
  88.2 3.5 %copy-start.14 = (bf16[8,5,16,128]{3,2,1,0:T(8,128)(2,1)}, bf16[8,5,16,128]{3,2,1,0:T(8,128)(2,1)S(1)}, u32[]{:S(2)}) copy-start(bf16[8,5,16,128]{3,2,1,0:T(8,128)(2,1)S(1)} %collective-permute-done.12.refs_3_.w2) | copy-start | bytes 491524
  107.1 39.5 %all-to-all-start.3 = ((bf16[8,5,32,128]{3,2,1,0:T(8,128)(2,1)}), bf16[8,5,32,128]{3,2,1,0:T(8,128)(2,1)S(1)}, u32[]{:S(2)}, u32[]{:S(2)}) async-start(bf16[8,5,32,128]{3,2,1,0:T(8,128)(2,1)} %after.21), calls=%async_computation.4 | async-start | bytes 655360 | tf_op jit(solution)/shard_map/all_to_all | solution.py:423
  116.9 7.0 %collective-permute-start.15 = (bf16[5,128,128]{2,1,0:T(8,128)(2,1)}, bf16[5,128,128]{2,1,0:T(8,128)(2,1)S(1)}, u32[]{:S(2)}, u32[]{:S(2)}) collective-permute-start(bf16[5,128,128]{2,1,0:T(8,128)(2,1)} %get-tuple-element.23), channel_id=1, source_target_pairs={{0,16},{16,32},{32,48},{48,0},{1,17},{17,33},{33,49},{49,1},{2,18}... | collective-permute-start | bytes 491528 | tf_op jit(solution)/shard_map/ppermute | solution.py:416
  118.6 9.7 %collective-permute-start.16 = (bf16[5,128,128]{2,1,0:T(8,128)(2,1)}, bf16[5,128,128]{2,1,0:T(8,128)(2,1)S(1)}, u32[]{:S(2)}, u32[]{:S(2)}) collective-permute-start(bf16[5,128,128]{2,1,0:T(8,128)(2,1)} %get-tuple-element.24), channel_id=1, source_target_pairs={{0,32},{16,48},{32,0},{48,16},{1,33},{17,49},{33,1},{49,17},{2,34}... | collective-permute-start | bytes 491528 | tf_op jit(solution)/shard_map/ppermute | solution.py:416
  121.1 7.3 %collective-permute-start.17 = (bf16[5,128,128]{2,1,0:T(8,128)(2,1)}, bf16[5,128,128]{2,1,0:T(8,128)(2,1)S(1)}, u32[]{:S(2)}, u32[]{:S(2)}) collective-permute-start(bf16[5,128,128]{2,1,0:T(8,128)(2,1)} %get-tuple-element.25), channel_id=1, source_target_pairs={{0,48},{16,0},{32,16},{48,32},{1,49},{17,1},{33,17},{49,33},{2,50}... | collective-permute-start | bytes 491528 | tf_op jit(solution)/shard_map/ppermute | solution.py:416
  123.9 4.5 %copy-start.15 = (bf16[5,128,128]{2,1,0:T(8,128)(2,1)}, bf16[5,128,128]{2,1,0:T(8,128)(2,1)S(1)}, u32[]{:S(2)}) copy-start(bf16[5,128,128]{2,1,0:T(8,128)(2,1)S(1)} %collective-permute-done.15.p1) | copy-start | bytes 491524
  128.3 0.7 copy-start.16
  128.3 0.7 copy-start.17
  131.7 7.0 %collective-permute-start.20 = (bf16[5,128,128]{2,1,0:T(8,128)(2,1)}, bf16[5,128,128]{2,1,0:T(8,128)(2,1)S(1)}, u32[]{:S(2)}, u32[]{:S(2)}) collective-permute-start(bf16[5,128,128]{2,1,0:T(8,128)(2,1)} %text_sum.1), channel_id=1, source_target_pairs={{0,48},{16,0},{32,16},{48,32},{1,49},{17,1},{33,17},{49,33},{2,50}... | collective-permute-start | bytes 491528 | tf_op jit(solution)/shard_map/ppermute | solution.py:416
  133.9 6.0 %collective-permute-start.19 = (bf16[5,128,128]{2,1,0:T(8,128)(2,1)}, bf16[5,128,128]{2,1,0:T(8,128)(2,1)S(1)}, u32[]{:S(2)}, u32[]{:S(2)}) collective-permute-start(bf16[5,128,128]{2,1,0:T(8,128)(2,1)} %text_sum.1), channel_id=1, source_target_pairs={{0,32},{16,48},{32,0},{48,16},{1,33},{17,49},{33,1},{49,17},{2,34}... | collective-permute-start | bytes 491528 | tf_op jit(solution)/shard_map/ppermute | solution.py:416
  134.6 10.1 %collective-permute-start.18 = (bf16[5,128,128]{2,1,0:T(8,128)(2,1)}, bf16[5,128,128]{2,1,0:T(8,128)(2,1)S(1)}, u32[]{:S(2)}, u32[]{:S(2)}) collective-permute-start(bf16[5,128,128]{2,1,0:T(8,128)(2,1)} %text_sum.1), channel_id=1, source_target_pairs={{0,16},{16,32},{32,48},{48,0},{1,17},{17,33},{33,49},{49,1},{2,18}... | collective-permute-start | bytes 491528 | tf_op jit(solution)/shard_map/ppermute | solution.py:416
  146.6 35.5 %copy-start.4 = (s32[4]{0:T(128)S(1)}, s32[4]{0:T(128)}, u32[]{:S(2)}) copy-start(s32[4]{0:T(128)} %copy-done.3) | copy-start | bytes 52
  146.6 0.7 copy-start.9
  147.3 2.9 %collective-permute-start.21 = (bf16[4,5,128,128]{3,2,1,0:T(8,128)(2,1)}, bf16[4,5,128,128]{3,2,1,0:T(8,128)(2,1)S(1)}, u32[]{:S(2)}, u32[]{:S(2)}) collective-permute-start(bf16[4,5,128,128]{3,2,1,0:T(8,128)(2,1)} %after.23.mine_ref), channel_id=1, source_target_pairs={{0,1},{1,0},{2,3},{3,2},{4,5},{5,4},{6,7},{7,6},{8,9},{9,8},{10,11... | collective-permute-start | bytes 1966088 | tf_op jit(solution)/shard_map/ppermute | solution.py:428
  150.3 0.8 copy-start.12
  158.9 23.2 %all-to-all-start.2 = ((bf16[8,5,32,128]{3,2,1,0:T(8,128)(2,1)}), bf16[8,5,32,128]{3,2,1,0:T(8,128)(2,1)S(1)}, u32[]{:S(2)}, u32[]{:S(2)}) async-start(bf16[8,5,32,128]{3,2,1,0:T(8,128)(2,1)} %last_part.1), calls=%async_computation.3 | async-start | bytes 655360 | tf_op jit(solution)/shard_map/all_to_all | solution.py:432
  163.6 10.4 %collective-permute-start.28 = (bf16[5,32,128]{2,1,0:T(8,128)(2,1)S(1)}, bf16[5,32,128]{2,1,0:T(8,128)(2,1)S(1)}, u32[]{:S(2)}, u32[]{:S(2)}) collective-permute-start(bf16[5,32,128]{2,1,0:T(8,128)(2,1)S(1)} %get-tuple-element.30), channel_id=1, source_target_pairs={{0,2},{2,4},{4,6},{6,8},{8,10},{10,12},{12,14},{14,0},{1,3},{3,5},... | collective-permute-start | bytes 122888 | tf_op jit(solution)/shard_map/ppermute | solution.py:430
  164.8 12.3 %collective-permute-start.27 = (bf16[5,32,128]{2,1,0:T(8,128)(2,1)S(1)}, bf16[5,32,128]{2,1,0:T(8,128)(2,1)S(1)}, u32[]{:S(2)}, u32[]{:S(2)}) collective-permute-start(bf16[5,32,128]{2,1,0:T(8,128)(2,1)S(1)} %get-tuple-element.31), channel_id=1, source_target_pairs={{0,4},{2,6},{4,8},{6,10},{8,12},{10,14},{12,0},{14,2},{1,5},{3,7},... | collective-permute-start | bytes 122888 | tf_op jit(solution)/shard_map/ppermute | solution.py:430
  167.0 11.3 %collective-permute-start.26 = (bf16[5,32,128]{2,1,0:T(8,128)(2,1)S(1)}, bf16[5,32,128]{2,1,0:T(8,128)(2,1)S(1)}, u32[]{:S(2)}, u32[]{:S(2)}) collective-permute-start(bf16[5,32,128]{2,1,0:T(8,128)(2,1)S(1)} %get-tuple-element.32), channel_id=1, source_target_pairs={{0,6},{2,8},{4,10},{6,12},{8,14},{10,0},{12,2},{14,4},{1,7},{3,9},... | collective-permute-start | bytes 122888 | tf_op jit(solution)/shard_map/ppermute | solution.py:430
  169.3 9.1 %collective-permute-start.25 = (bf16[5,32,128]{2,1,0:T(8,128)(2,1)S(1)}, bf16[5,32,128]{2,1,0:T(8,128)(2,1)S(1)}, u32[]{:S(2)}, u32[]{:S(2)}) collective-permute-start(bf16[5,32,128]{2,1,0:T(8,128)(2,1)S(1)} %get-tuple-element.33), channel_id=1, source_target_pairs={{0,8},{2,10},{4,12},{6,14},{8,0},{10,2},{12,4},{14,6},{1,9},{3,11}... | collective-permute-start | bytes 122888 | tf_op jit(solution)/shard_map/ppermute | solution.py:430
  171.4 7.0 %collective-permute-start.24 = (bf16[5,32,128]{2,1,0:T(8,128)(2,1)S(1)}, bf16[5,32,128]{2,1,0:T(8,128)(2,1)S(1)}, u32[]{:S(2)}, u32[]{:S(2)}) collective-permute-start(bf16[5,32,128]{2,1,0:T(8,128)(2,1)S(1)} %get-tuple-element.34), channel_id=1, source_target_pairs={{0,10},{2,12},{4,14},{6,0},{8,2},{10,4},{12,6},{14,8},{1,11},{3,13... | collective-permute-start | bytes 122888 | tf_op jit(solution)/shard_map/ppermute | solution.py:430
  173.9 8.2 %collective-permute-start.23 = (bf16[5,32,128]{2,1,0:T(8,128)(2,1)S(1)}, bf16[5,32,128]{2,1,0:T(8,128)(2,1)S(1)}, u32[]{:S(2)}, u32[]{:S(2)}) collective-permute-start(bf16[5,32,128]{2,1,0:T(8,128)(2,1)S(1)} %get-tuple-element.35), channel_id=1, source_target_pairs={{0,12},{2,14},{4,0},{6,2},{8,4},{10,6},{12,8},{14,10},{1,13},{3,15... | collective-permute-start | bytes 122888 | tf_op jit(solution)/shard_map/ppermute | solution.py:430
  177.2 4.9 %collective-permute-start.22 = (bf16[5,32,128]{2,1,0:T(8,128)(2,1)S(1)}, bf16[5,32,128]{2,1,0:T(8,128)(2,1)S(1)}, u32[]{:S(2)}, u32[]{:S(2)}) collective-permute-start(bf16[5,32,128]{2,1,0:T(8,128)(2,1)S(1)} %get-tuple-element.36), channel_id=1, source_target_pairs={{0,14},{2,0},{4,2},{6,4},{8,6},{10,8},{12,10},{14,12},{1,15},{3,1}... | collective-permute-start | bytes 122888 | tf_op jit(solution)/shard_map/ppermute | solution.py:430
Sparse Core Ops, SparseCore 0:
  34.4 57.2 all-gather.2
  106.4 42.8 reduce-scatter.1
